TPU v7x, 32 devices: a whole 2x2x4 slice. The times are simulated.
32 devices in a mesh: groups: 2 (over y), tm: 4 (over z), chan: 2 (over x), pol: 2 (over core).
Axes of the slice: x: 2, y: 2, z: 4, core: 2. Of those that a mesh axis runs over, the one named last changes fastest.
Arguments:
- voltages: bfloat16 [1024, 2, 8, 2, 512], P(('groups', 'tm'), 'pol', 'chan'), parts along dimension 0, may hold values from -60 to 60
- start_block: float32 [2, 8, 2, 8, 512], P('pol', 'chan'), may hold values from -6 to 6
- flags: int32 [16], P(('groups', 'chan')), parts along dimension 0, may hold values 0 or 1
- ranks: int32 [16], P(('groups', 'chan')), parts along dimension 0, may hold values from 1 to 8
- phase_index: int32 [256, 512], replicated, may hold values from 0 to 1023
Outputs:
- power: float32 [1024, 8, 256], P(('groups', 'tm'), 'chan', 'pol'), parts along dimension 0
There are 2 independent parts, one for each index of `groups`. A program takes and returns all parts, laid end to end along the dimension named above; an argument that names none is the same for every part. Nothing has to cross between parts.
All inputs are finite; a program needn't handle non-finite values. No bound on the sum of `flags` on one device may be relied on, other than what follows from the above.
Results may differ from a plain program's by a relative error of at most 0.008.
Values may be sent and summed in bfloat16 or wider, within the bound.
No kernel may reach another device: no remote copies, remote signals or barrier semaphores. Data moves between devices by JAX's collectives and lax.ppermute only.
A program may use at most 128 MiB of HBM per device.

v0:
```python
import jax
import jax.numpy as jnp
from jax import lax
from jax.sharding import PartitionSpec as P

ITERS = 4
PHASES = 1024


HIGH = lax.Precision.HIGHEST


def block_cov(piece, factor):
    real_part = piece[:, :, 0]
    imag_part = piece[:, :, 1]
    stacked = jnp.concatenate([real_part, imag_part], axis=0)
    rotated = jnp.concatenate([imag_part, -real_part], axis=0)
    left_side = jnp.stack([stacked, rotated], axis=2)
    return (
        jnp.einsum("scja,sck->cjak", left_side, stacked, preferred_element_type=jnp.float32)
        * factor
    )


def apply_cov(cov, real_q, imag_q):

    def times_matrix(vectors, matrix):
        return jnp.einsum("cmk,cjk->cmj", vectors, matrix, precision=HIGH)

    cov_real = cov[:, 0]
    cov_imag = cov[:, 1]
    new_real = times_matrix(real_q, cov_real) - times_matrix(imag_q, cov_imag)
    new_imag = times_matrix(imag_q, cov_real) + times_matrix(real_q, cov_imag)
    return (new_real, new_imag)


def orthonormalize(real_z, imag_z):
    done_real = []
    done_imag = []
    for column in range(real_z.shape[1]):
        vec_real = real_z[:, column]
        vec_imag = imag_z[:, column]
        if column > 0:
            base_real = jnp.stack(done_real, axis=1)
            base_imag = jnp.stack(done_imag, axis=1)
            dot_real = jnp.sum(
                base_real * vec_real[:, None] + base_imag * vec_imag[:, None],
                axis=-1,
                keepdims=True,
            )
            dot_imag = jnp.sum(
                base_real * vec_imag[:, None] - base_imag * vec_real[:, None],
                axis=-1,
                keepdims=True,
            )
            vec_real = vec_real - jnp.sum(dot_real * base_real - dot_imag * base_imag, axis=1)
            vec_imag = vec_imag - jnp.sum(dot_real * base_imag + dot_imag * base_real, axis=1)
        factor = 1.0 / jnp.sqrt(
            jnp.sum(vec_real * vec_real + vec_imag * vec_imag, axis=-1, keepdims=True) + 1e-06
        )
        done_real.append(vec_real * factor)
        done_imag.append(vec_imag * factor)
    return (jnp.stack(done_real, axis=1), jnp.stack(done_imag, axis=1))


def subspace(cov, real_q, imag_q):
    for sweep in range(ITERS):
        real_z, imag_z = apply_cov(cov, real_q, imag_q)
        real_q, imag_q = orthonormalize(real_z, imag_z)
    return (real_q, imag_q)


def projector(real_u, imag_u):

    def outer_sum(left_vec, right_vec):
        return jnp.einsum("cmj,cmk->cjk", left_vec, right_vec, precision=HIGH)

    identity = jnp.eye(real_u.shape[2], dtype=jnp.float32)[None]
    proj_real = identity - (outer_sum(real_u, real_u) + outer_sum(imag_u, imag_u))
    proj_imag = outer_sum(real_u, imag_u) - outer_sum(imag_u, real_u)
    return jnp.stack([proj_real, proj_imag], axis=1).astype(jnp.bfloat16)


def project(series, proj):

    def apply_one(vectors, matrix):
        return jnp.einsum("sck,cjk->scj", vectors, matrix, preferred_element_type=jnp.float32)

    in_real = series[:, :, 0]
    in_imag = series[:, :, 1]
    proj_real = proj[:, 0]
    proj_imag = proj[:, 1]
    out_real = apply_one(in_real, proj_real) - apply_one(in_imag, proj_imag)
    out_imag = apply_one(in_imag, proj_real) + apply_one(in_real, proj_imag)
    return jnp.stack([out_real, out_imag], axis=2).astype(jnp.bfloat16)


def steering(chan_ids, phase_index):
    turn = phase_index[None] * (chan_ids[:, None, None] + 1) % PHASES
    angle = turn.astype(jnp.float32) * (2.0 * jnp.pi / PHASES)
    norm_factor = 1.0 / jnp.sqrt(jnp.float32(phase_index.shape[1]))
    return (
        (jnp.cos(angle) * norm_factor).astype(jnp.bfloat16),
        (jnp.sin(angle) * norm_factor).astype(jnp.bfloat16),
    )


def beam_power(cleaned, weight_real, weight_imag):

    def form(vectors, weights):
        return jnp.einsum("sca,cba->scb", vectors, weights, preferred_element_type=jnp.float32)

    out_real = cleaned[:, :, 0]
    out_imag = cleaned[:, :, 1]
    beam_real = form(out_real, weight_real) - form(out_imag, weight_imag)
    beam_imag = form(out_real, weight_imag) + form(out_imag, weight_real)
    return beam_real * beam_real + beam_imag * beam_imag


def local(voltages, start_block, flags, ranks, phase_index):
    tm_count = lax.axis_size("tm")
    tm_index = lax.axis_index("tm")
    series = voltages[:, 0]
    samples = series.shape[0]
    chan_dev = series.shape[1]
    width = series.shape[3]
    own = chan_dev // tm_count
    vec_count = start_block.shape[3]
    factor = 1.0 / (samples * tm_count)
    moved = lax.all_to_all(series, "tm", split_axis=1, concat_axis=0, tiled=True)
    blocks = moved.reshape(tm_count, samples, own, 2, width)

    def add_block(carry, piece):
        rounded = lax.optimization_barrier(block_cov(piece, factor).astype(jnp.bfloat16))
        return (carry + rounded.astype(jnp.float32), None)

    cov, unused = lax.scan(add_block, jnp.zeros((own, 2, width, width), jnp.float32), blocks)
    first_own = tm_index * own
    mine = lax.dynamic_slice_in_dim(start_block[0], first_own, own, 0)
    rank_all = flags * ranks
    rank_mine = lax.dynamic_slice_in_dim(rank_all, first_own, own, 0)
    keep = (jnp.arange(vec_count, dtype=jnp.int32)[None, :] < rank_mine[:, None]).astype(
        jnp.float32
    )[:, :, None]
    real_q, imag_q = subspace(cov, mine[:, 0], mine[:, 1])
    basis = jnp.stack([real_q * keep, imag_q * keep], axis=1)
    every = lax.all_gather(basis.astype(jnp.bfloat16), "tm", axis=0, tiled=True).astype(basis.dtype)
    proj = projector(every[:, 0], every[:, 1])
    cleaned = project(series, proj)
    chan_ids = lax.axis_index("chan") * chan_dev + jnp.arange(chan_dev, dtype=jnp.int32)
    weight_real, weight_imag = steering(chan_ids, phase_index)
    power_term = beam_power(cleaned, weight_real, weight_imag)
    return lax.psum_scatter(
        power_term.astype(jnp.bfloat16), "pol", scatter_dimension=2, tiled=True
    ).astype(jnp.float32)


def solution(mesh):
    placed = (
        P(("groups", "tm"), "pol", "chan", None, None),
        P("pol", "chan", None, None, None),
        P(("groups", "chan")),
        P(("groups", "chan")),
        P(),
    )
    return jax.shard_map(
        local,
        mesh=mesh,
        in_specs=placed,
        out_specs=P(("groups", "tm"), "chan", "pol"),
        check_vma=False,
    )
```

profile of v0, /device:TPU:0, one launch (start us, length us, event | category | flops | bytes accessed | tf_op | source)
XLA Modules:
  0.0 199.3 jit_solution(10578678874605304417)
XLA Ops:
  6.5 2.6 %copy.46 = bf16[128,1,4,2,512]{4,0,3,2,1:T(8,128)(2,1)} copy(bf16[128,1,4,2,512]{4,3,2,1,0:T(2,128)(2,1)} %param.7) | data formatting | bytes 2097152 | tf_op jit(solution)/shard_map/squeeze | solution.py:123
  9.2 6.4 %all-to-all-start = ((bf16[128,4,2,512]{3,0,2,1:T(8,128)(2,1)}), bf16[128,4,2,512]{3,0,2,1:T(8,128)(2,1)}, u32[]{:S(2)}, u32[]{:S(2)}) async-start(bf16[128,4,2,512]{3,0,2,1:T(8,128)(2,1)} %bitcast.689), calls=%async_computation | async-start | bytes 2097152 | tf_op jit(solution)/shard_map/all_to_all | solution.py:130
  15.6 1.3 copy.47
  16.9 0.7 dynamic_slice.14
  17.6 0.7 compare_convert_fusion
  18.3 1.2 fusion.51
  19.5 21.9 %all-to-all-done = bf16[128,4,2,512]{3,0,2,1:T(8,128)(2,1)} async-done(((bf16[128,4,2,512]{3,0,2,1:T(8,128)(2,1)}), bf16[128,4,2,512]{3,0,2,1:T(8,128)(2,1)}, u32[]{:S(2)}, u32[]{:S(2)}) %all-to-all-start) | async-done | bytes 1048608 | tf_op jit(solution)/shard_map/all_to_all | solution.py:130
  41.4 9.2 %while.11 = (s32[]{:T(128)}, f32[1,2,512,512]{3,2,1,0:T(8,128)S(1)}, bf16[4,128,1,2,512]{4,1,3,2,0:T(8,128)(2,1)}, s32[]{:T(128)}, s32[]{:T(128)}) while((s32[]{:T(128)}, f32[1,2,512,512]{3,2,1,0:T(8,128)S(1)}, bf16[4,128,1,2,512]{4,1,3,2,0:T(8,128)(2,1)}, s32[]{:T(128)}, s32[]{:T(128)}) %tuple.149), condition=%wide.region_1.2_spmd.clone, body=%wide.region_0.1_spmd.clone.sunk | while | flops 272957440 | bytes 9306187 | solution.py:137
  41.4 1.0 dynamic-slice_bitcast_fusion.3
  43.0 0.7 select_add_fusion.2
  43.7 1.0 dynamic-slice_bitcast_fusion.3
  45.3 0.7 select_add_fusion.2
  46.0 1.0 dynamic-slice_bitcast_fusion.3
  47.5 0.7 select_add_fusion.2
  48.2 1.0 dynamic-slice_bitcast_fusion.3
  49.8 0.7 select_add_fusion.2
  50.6 1.0 fusion.49
  51.6 1.0 fusion.47
  52.6 1.0 fusion.26
  53.5 1.0 fusion.25
  54.5 0.6 add_reduce_fusion.59
  55.8 0.6 add_reduce_fusion.58
  56.5 1.9 add_reduce_fusion.57
  60.9 0.6 fusion.161
  65.8 0.6 fusion.164
  68.8 1.0 fusion.45
  69.8 1.0 fusion.43
  70.8 1.0 fusion.24
  71.8 1.0 fusion.23
  72.8 0.6 add_reduce_fusion.56
  74.1 0.6 add_reduce_fusion.55
  74.7 1.9 add_reduce_fusion.54
  84.0 0.6 fusion.170
  85.7 0.6 fusion.171
  87.1 1.0 fusion.41
  88.1 1.0 fusion.39
  89.1 1.0 fusion.22
  90.0 1.0 fusion.21
  91.0 0.6 add_reduce_fusion.53
  92.3 0.6 add_reduce_fusion.52
  92.9 1.9 add_reduce_fusion.51
  105.7 1.0 fusion.37
  106.7 1.0 fusion.35
  107.7 1.0 fusion.20
  108.7 1.0 fusion.19
  109.7 0.6 add_reduce_fusion.50
  111.0 0.6 add_reduce_fusion.49
  111.6 1.9 add_reduce_fusion.48
  117.6 0.6 fusion.180
  124.1 13.1 %all_gather.3 = bf16[4,2,8,512]{3,2,1,0:T(8,128)(2,1)S(1)} all-gather(bf16[1,2,8,512]{3,2,1,0:T(8,128)(2,1)S(1)} %pad_maximum_fusion.2), channel_id=1, replica_groups=mesh['groups'=2,'tm'=4,'chan'=2,'pol'=2] {'tm'}, dimensions={0}, use_global_device_ids=true | all-gather | bytes 81920 | tf_op jit(solution)/shard_map/all_gather | solution.py:147
  137.2 0.8 fusion.72
  138.0 0.7 fusion.73
  139.2 0.8 subtract_convert_fusion.1
  140.4 0.7 fusion.71
  141.1 0.7 fusion.70
  141.9 0.8 subtract_convert_fusion
  142.6 0.7 fusion.13
  143.7 10.1 %fusion.53 = f32[4,256,128]{2,1,0:T(8,128)S(1)} fusion(bf16[128,4,512]{0,2,1:T(8,128)(2,1)S(1)} %fusion.13, s32[4]{0:T(128)S(1)} %add_add_fusion, s32[256,512]{1,0:T(8,128)S(1)} %copy-done.4), kind=kOutput, calls=%fused_computation.85 | convolution fusion | flops 142606336 | bytes 1572880 | tf_op jit(solution)/shard_map/sca,cba->scb/dot_general | solution.py:111
  153.7 10.1 %fusion.52 = f32[4,256,128]{2,1,0:T(8,128)S(1)} fusion(bf16[128,4,512]{0,2,1:T(8,128)(2,1)S(1)} %fusion.13, s32[4]{0:T(128)S(1)} %add_add_fusion, s32[256,512]{1,0:T(8,128)S(1)} %copy-done.4), kind=kOutput, calls=%fused_computation.84 | convolution fusion | flops 142606336 | bytes 1572880 | tf_op jit(solution)/shard_map/sca,cba->scb/dot_general | solution.py:111
  163.9 0.7 fusion.12
  164.6 9.9 %fusion.14 = f32[4,256,128]{2,1,0:T(8,128)S(1)} fusion(f32[4,256,128]{2,1,0:T(8,128)S(1)} %fusion.53, bf16[128,4,512]{0,2,1:T(8,128)(2,1)S(1)} %fusion.12, s32[4]{0:T(128)S(1)} %add_add_fusion, s32[256,512]{1,0:T(8,128)S(1)} %copy-done.4), kind=kOutput, calls=%fused_computation.34 | convolution fusion | flops 142868480 | bytes 2097168 | tf_op jit(solution)/shard_map/sca,cba->scb/dot_general | solution.py:111
  174.5 9.1 %fusion.18 = bf16[128,4,256]{0,2,1:T(8,128)(2,1)} fusion(f32[4,256,128]{2,1,0:T(8,128)S(1)} %fusion.14, f32[4,256,128]{2,1,0:T(8,128)S(1)} %fusion.52, bf16[128,4,512]{0,2,1:T(8,128)(2,1)S(1)} %fusion.12, s32[4]{0:T(128)S(1)} %add_add_fusion, s32[256,512]{1,0:T(8,128)S(1)} %copy-done.4), kind=kOutput, calls=%fused_computation.39 | convolution fusion | flops 143130624 | bytes 2359312 | tf_op jit(solution)/shard_map/sca,cba->scb/dot_general | solution.py:111
  183.6 6.9 %reduce-scatter.2.cloned.1.call-done = bf16[128,4,128]{0,2,1:T(8,128)(2,1)} async-done(((bf16[128,4,256]{0,2,1:T(8,128)(2,1)}), bf16[128,4,128]{0,2,1:T(8,128)(2,1)}) %reduce-scatter.2.cloned.1.call-update) | async-done | bytes 131088 | tf_op jit(solution)/shard_map/reduce_scatter | solution.py:153
  190.5 1.7 copy.35
  (192 shorter events, 23.3 us)
Async XLA Ops:
  6.5 11.8 %copy-start = (f32[1,4,2,8,512]{4,3,2,1,0:T(8,128)S(1)}, f32[1,4,2,8,512]{4,3,2,1,0:T(8,128)}, u32[]{:S(2)}) copy-start(f32[1,4,2,8,512]{4,3,2,1,0:T(8,128)} %param.8) | copy-start | bytes 393220
  6.5 9.1 %copy-start.3 = (bf16[128,1,4,2,512]{4,3,2,1,0:T(2,128)(2,1)S(1)}, bf16[128,1,4,2,512]{4,3,2,1,0:T(2,128)(2,1)}, u32[]{:S(2)}) copy-start(bf16[128,1,4,2,512]{4,3,2,1,0:T(2,128)(2,1)} %param.7) | copy-start | bytes 3145732
  9.2 7.8 %copy-start.5 = (s32[4]{0:T(128)S(1)}, s32[4]{0:T(128)}, u32[]{:S(2)}) copy-start(s32[4]{0:T(128)} %param.9) | copy-start | bytes 52
  9.2 7.8 %copy-start.6 = (s32[4]{0:T(128)S(1)}, s32[4]{0:T(128)}, u32[]{:S(2)}) copy-start(s32[4]{0:T(128)} %param.10) | copy-start | bytes 52
  9.2 32.3 %all-to-all-start = ((bf16[128,4,2,512]{3,0,2,1:T(8,128)(2,1)}), bf16[128,4,2,512]{3,0,2,1:T(8,128)(2,1)}, u32[]{:S(2)}, u32[]{:S(2)}) async-start(bf16[128,4,2,512]{3,0,2,1:T(8,128)(2,1)} %bitcast.689), calls=%async_computation | async-start | bytes 2097152 | tf_op jit(solution)/shard_map/all_to_all | solution.py:130
  15.6 174.9 %reduce-scatter.2.cloned.1.call-start = ((), (), s32[]{:S(2)}) async-start(), calls=%async_computation.2 | async-start | bytes 393216 | tf_op jit(solution)/shard_map/reduce_scatter | solution.py:153
  138.0 1.2 copy-start.2
  139.2 1.2 copy-start.1
  142.6 1.0 copy-start.4
Sparse Core Ops, SparseCore 0:
  183.7 6.7 reduce-scatter.1
where the time goes:
time: 203 us; the launch traced here: 199 us
  matrix products  62.4 us (31%)
  other arithmetic  38.6 us (19%)
  between operations  36.4 us (18%)
  waiting for transfers between devices  28.9 us (14%)
  blocking collectives  13.1 us (6%)
  local copies, waits for them, and re-layouts  13 us (6%)
  starting transfers between devices  6.45 us (3%)
    dot_general x4, matrix products, form(): jnp.einsum('sca,cba->scb', vectors, weights, preferred_element_type=jnp.f...  39.2 us
    reduce_sum x32, other arithmetic, orthonormalize(): jnp.sum(vec_real * vec_real + vec_imag * vec_imag, axis=-1, keepdims=True)  24.8 us
    all_to_all x1, waiting for transfers between devices, local(): lax.all_to_all(series, 'tm', split_axis=1, concat_axis=0, tiled=True)  21.9 us
    dot_general x16, matrix products, times_matrix(): return jnp.einsum('cmk,cjk->cmj', vectors, matrix, precision=HIGH)  15.5 us
    all_gather x1, blocking collectives, local(): lax.all_gather(basis.astype(jnp.bfloat16), 'tm', axis=0, tiled=True)  13.1 us
    reduce_scatter x1, waiting for transfers between devices, local(): lax.psum_scatter(power_term.astype(jnp.bfloat16), 'pol', scatter_dimensio...  6.91 us
    all_to_all x1, starting transfers between devices, local(): lax.all_to_all(series, 'tm', split_axis=1, concat_axis=0, tiled=True)  6.45 us
    reduce_sum x28, other arithmetic, orthonormalize(): jnp.sum(base_real * vec_real[:, None] + base_imag * vec_imag[:, None], ax...  6.23 us
  transfers between devices with their start and end apart: 2, of which 2 were waited for; matrix products, arithmetic and copies ran while one was open for 2% of the time, Pallas kernels for 0%

commit v1 on v0

v1 whole, which is shorter than its diff:
```python
import functools

import jax
import jax.numpy as jnp
from jax import lax
from jax.experimental import pallas as pl
from jax.experimental.pallas import tpu as pltpu
from jax.sharding import PartitionSpec as P

ITERS = 4
PHASES = 1024
QUARTER = PHASES // 4
EPS = 1e-06
F32 = jnp.float32
BF16 = jnp.bfloat16
NT = (((1,), (1,)), ((), ()))
NN = (((1,), (0,)), ((), ()))
TN = (((0,), (0,)), ((), ()))
VMEM_LIMIT = 48 * 1024 * 1024


def dot(left, right, dims):
    return lax.dot_general(left, right, dims, preferred_element_type=F32)


def split(values):
    high = values.astype(BF16)
    low = (values - high.astype(F32)).astype(BF16)
    return high, low


def steer(phase, step, norm):
    turn = (phase * step) & (PHASES - 1)
    quadrant = (turn + QUARTER // 2) // QUARTER
    angle = (turn - quadrant * QUARTER).astype(F32) * (2.0 * jnp.pi / PHASES)
    sq = angle * angle
    sine = angle * (1.0 + sq * (-1.0 / 6 + sq * (1.0 / 120 + sq * (-1.0 / 5040 + sq / 362880))))
    cosine = 1.0 + sq * (-0.5 + sq * (1.0 / 24 + sq * (-1.0 / 720 + sq / 40320)))
    odd = (quadrant & 1) == 1
    real = jnp.where(odd, sine, cosine) * norm
    imag = jnp.where(odd, cosine, sine) * norm
    real = jnp.where(((quadrant + 1) & 2) == 2, -real, real)
    imag = jnp.where((quadrant & 2) == 2, -imag, imag)
    return real.astype(BF16), imag.astype(BF16)


def fill_weights(phase_ref, first, rows, step, out):
    norm = 1.0 / (phase_ref.shape[1] ** 0.5)
    chunk = 32

    def body(i, carry):
        at = pl.multiple_of(i * chunk, chunk)
        real, imag = steer(phase_ref[pl.ds(first + at, chunk), :], step, norm)
        out[pl.ds(at, chunk), :] = real
        out[pl.ds(rows + at, chunk), :] = imag
        return carry

    lax.fori_loop(0, rows // chunk, body, 0)


def own_weights_kernel(own, chan_dev, phase_ref, out_ref):
    beams = phase_ref.shape[0]
    first = lax.axis_index("chan") * chan_dev + lax.axis_index("tm") * own
    for o in range(own):
        fill_weights(phase_ref, 0, beams, first + o + 1, out_ref.at[o])


def raw_beams_kernel(chan_dev, phase_ref, mine_ref, other_ref, out_ref, weights):
    half = phase_ref.shape[0] // 2
    width = phase_ref.shape[1]
    chan_id = lax.axis_index("chan") * chan_dev + pl.program_id(0)
    first = pl.multiple_of(lax.axis_index("pol") * half, half)
    fill_weights(phase_ref, first, half, chan_id + 1, weights)
    for slot, ref in enumerate((mine_ref, other_ref)):
        by_real = dot(ref[0, :, :width], weights[...], NT)
        by_imag = dot(ref[0, :, width:], weights[...], NT)
        out_ref[0, slot, :, :half] = by_real[:, :half] - by_imag[:, half:]
        out_ref[0, slot, :, half:] = by_real[:, half:] + by_imag[:, :half]


def correlate(real, imag, x_ref):
    rows = jnp.concatenate(
        [jnp.concatenate([real, imag], axis=1), jnp.concatenate([imag, -real], axis=1)], axis=0
    )
    count = rows.shape[0]
    product = dot(jnp.concatenate(split(rows), axis=0), x_ref[...], NT)
    return product[:count] + product[count:]


def cov_times(real, imag, x_ref, factor):
    vectors, width = real.shape
    series = correlate(real, imag, x_ref)
    count = series.shape[0]
    product = dot(jnp.concatenate(split(series), axis=0), x_ref[...], NN)
    product = (product[:count] + product[count:]) * factor
    real_z = product[:vectors, :width] - product[vectors:, width:]
    imag_z = product[vectors:, :width] + product[:vectors, width:]
    return real_z, imag_z


def orthonormalize(real_z, imag_z):
    vectors = real_z.shape[0]
    row = lax.broadcasted_iota(jnp.int32, real_z.shape, 0)
    real_v, imag_v = real_z, imag_z
    scale = jnp.zeros((vectors, 1), F32)
    for n in range(vectors):
        here = row == n
        real_a, imag_a = real_v[n : n + 1], imag_v[n : n + 1]
        real_z = jnp.where(here, real_v, real_z)
        imag_z = jnp.where(here, imag_v, imag_z)
        real_d = jnp.sum(real_a * real_z + imag_a * imag_z, axis=1, keepdims=True)
        norm = real_d[n : n + 1] + EPS
        scale = jnp.where(row[:, :1] == n, norm, scale)
        if n + 1 < vectors:
            imag_d = jnp.sum(real_a * imag_z - imag_a * real_z, axis=1, keepdims=True)
            inverse = 1.0 / norm
            later = row[:, :1] > n
            real_c = jnp.where(later, real_d * inverse, 0.0)
            imag_c = jnp.where(later, imag_d * inverse, 0.0)
            real_v = real_v - (real_c * real_a - imag_c * imag_a)
            imag_v = imag_v - (real_c * imag_a + imag_c * real_a)
    factor = 1.0 / jnp.sqrt(scale)
    return real_v * factor, imag_v * factor


def subspace_kernel(tm, own, samples, factor, x_ref, start_ref, flags_ref, ranks_ref, weights_ref, *rest):
    outs, series_ref, steered_ref = rest[:-2], rest[-2], rest[-1]
    vectors, width = start_ref.shape[3], start_ref.shape[4]
    tm_index = lax.axis_index("tm")
    pol_index = lax.axis_index("pol")
    half = steered_ref.shape[1] // 2
    for o in range(own):
        chan = tm_index * own + o
        real_q = start_ref[0, chan, 0]
        imag_q = start_ref[0, chan, 1]
        x = x_ref.at[o]
        for sweep in range(ITERS):
            real_z, imag_z = cov_times(real_q, imag_q, x, factor)
            real_q, imag_q = orthonormalize(real_z, imag_z)
        rank = flags_ref[chan] * ranks_ref[chan]
        keep = lax.broadcasted_iota(jnp.int32, (vectors, width), 0) < rank
        real_u = jnp.where(keep, real_q, 0.0)
        imag_u = jnp.where(keep, imag_q, 0.0)
        series = correlate(real_u, imag_u, x)
        series_ref[:vectors] = series[:vectors]
        series_ref[vectors:] = -series[vectors:]
        rows = jnp.concatenate([real_u, imag_u], axis=0)
        product = dot(jnp.concatenate(split(rows), axis=0), weights_ref[o], NT)
        product = product[: 2 * vectors] + product[2 * vectors :]
        beams = product.shape[1] // 2
        steered_ref[:vectors] = product[:vectors, :beams] - product[vectors:, beams:]
        steered_ref[vectors:] = product[:vectors, beams:] + product[vectors:, :beams]
        for d in range(tm):
            to = lax.rem(tm_index + d, tm)
            part = series_ref[:, pl.ds(pl.multiple_of(to * samples, samples), samples)]
            for swap in range(2):
                core = lax.rem(pol_index + swap, 2)
                out = outs[2 * d + swap]
                out[o, :, :samples] = part
                out[o, :, samples:] = steered_ref[:, pl.ds(pl.multiple_of(core * half, half), half)]


def finish_kernel(tm, own, raw_ref, *rest):
    arrived, out_ref, powers = rest[:-2], rest[-2], rest[-1]
    samples = raw_ref.shape[2]
    half = raw_ref.shape[3] // 2
    tm_index = lax.axis_index("tm")
    for d in range(tm):
        source = lax.rem(tm_index + tm - d, tm)
        for o in range(own):
            chan = source * own + o
            total = jnp.zeros((samples, half), F32)
            for swap in range(2):
                ref = arrived[2 * d + swap]
                series = ref[o, :, :samples]
                steered = ref[o, :, samples:]
                vectors = steered.shape[0] // 2
                real_w, imag_w = steered[:vectors], steered[vectors:]
                right = jnp.concatenate(
                    [
                        jnp.concatenate([real_w, imag_w], axis=1),
                        jnp.concatenate([-imag_w, real_w], axis=1),
                    ],
                    axis=0,
                )
                high_s, low_s = split(series)
                high_w, low_w = split(right)
                left = jnp.concatenate([high_s, high_s, low_s], axis=0)
                right = jnp.concatenate([high_w, low_w, high_w], axis=0)
                beam = raw_ref[chan, swap] - dot(left, right, TN)
                total = total + beam[:, :half] * beam[:, :half] + beam[:, half:] * beam[:, half:]
            powers[chan] = total
    for chan in range(powers.shape[0]):
        out_ref[:, chan, :] = powers[chan]


def local(voltages, start_block, flags, ranks, phase_index):
    tm = lax.axis_size("tm")
    samples, chan_dev, width = voltages.shape[0], voltages.shape[2], voltages.shape[4]
    own = chan_dev // tm
    vectors = start_block.shape[3]
    beams = phase_index.shape[0]
    half = beams // 2
    factor = 1.0 / (samples * tm)
    params = pltpu.CompilerParams(vmem_limit_bytes=VMEM_LIMIT)
    whole = pl.BlockSpec(memory_space=pltpu.VMEM)
    scalars = pl.BlockSpec(memory_space=pltpu.SMEM)

    series = voltages[:, 0].transpose(1, 0, 2, 3).reshape(chan_dev, samples, 2 * width)
    moved = lax.all_to_all(series, "tm", split_axis=0, concat_axis=0, tiled=True)
    other = lax.ppermute(series, "pol", [(0, 1), (1, 0)])

    own_weights = pl.pallas_call(
        functools.partial(own_weights_kernel, own, chan_dev),
        out_shape=jax.ShapeDtypeStruct((own, 2 * beams, width), BF16),
        in_specs=[whole],
        out_specs=whole,
        compiler_params=params,
        cost_estimate=pl.CostEstimate(
            flops=40 * own * beams * width, bytes_accessed=8 * own * beams * width, transcendentals=0
        ),
    )(phase_index)

    raw = pl.pallas_call(
        functools.partial(raw_beams_kernel, chan_dev),
        grid=(chan_dev,),
        out_shape=jax.ShapeDtypeStruct((chan_dev, 2, samples, beams), F32),
        in_specs=[
            pl.BlockSpec((beams, width), lambda c: (0, 0)),
            pl.BlockSpec((1, samples, 2 * width), lambda c: (c, 0, 0)),
            pl.BlockSpec((1, samples, 2 * width), lambda c: (c, 0, 0)),
        ],
        out_specs=pl.BlockSpec((1, 2, samples, beams), lambda c: (c, 0, 0, 0)),
        scratch_shapes=[pltpu.VMEM((beams, width), BF16)],
        compiler_params=params,
        cost_estimate=pl.CostEstimate(
            flops=8 * chan_dev * samples * 2 * width * beams,
            bytes_accessed=8 * chan_dev * samples * width,
            transcendentals=0,
        ),
    )(phase_index, series, other)

    blocks = moved.reshape(tm, own, samples, 2 * width)
    blocks = blocks.transpose(1, 0, 2, 3).reshape(own, tm * samples, 2 * width)
    packet = jax.ShapeDtypeStruct((own, 2 * vectors, samples + half), F32)
    packets = pl.pallas_call(
        functools.partial(subspace_kernel, tm, own, samples, factor),
        out_shape=[packet] * (2 * tm),
        in_specs=[whole, whole, scalars, scalars, whole],
        out_specs=[whole] * (2 * tm),
        scratch_shapes=[
            pltpu.VMEM((2 * vectors, tm * samples), F32),
            pltpu.VMEM((2 * vectors, beams), F32),
        ],
        compiler_params=params,
        cost_estimate=pl.CostEstimate(
            flops=64 * own * vectors * tm * samples * width * ITERS,
            bytes_accessed=4 * own * tm * samples * width,
            transcendentals=0,
        ),
    )(blocks, start_block, flags, ranks, own_weights)

    arrived = []
    for d in range(tm):
        for swap in range(2):
            packet = packets[2 * d + swap]
            if d or swap:
                route = [
                    (z * 2 + p, (z + d) % tm * 2 + (p + swap) % 2) for z in range(tm) for p in range(2)
                ]
                packet = lax.ppermute(packet, ("tm", "pol"), route)
            arrived.append(packet)

    return pl.pallas_call(
        functools.partial(finish_kernel, tm, own),
        out_shape=jax.ShapeDtypeStruct((samples, chan_dev, half), F32),
        in_specs=[whole] * (1 + 2 * tm),
        out_specs=whole,
        scratch_shapes=[pltpu.VMEM((chan_dev, samples, half), F32)],
        compiler_params=params,
    )(raw, *arrived)


def solution(mesh):
    placed = (
        P(("groups", "tm"), "pol", "chan", None, None),
        P("pol", "chan", None, None, None),
        P(("groups", "chan")),
        P(("groups", "chan")),
        P(),
    )
    return jax.shard_map(
        local,
        mesh=mesh,
        in_specs=placed,
        out_specs=P(("groups", "tm"), "chan", "pol"),
        check_vma=False,
    )
```

time: 203 us -> 56.6 us (0.28); the launches traced: 199 us -> 56.3 us
  matrix products: 62.4 us -> 0 us
  other arithmetic: 38.6 us -> 0 us
  between operations: 36.4 us -> 0.13 us
  Pallas kernels: 0 us -> 13.9 us
  blocking collectives: 13.1 us -> 0 us
  local copies, waits for them, and re-layouts: 13 us -> 3.05 us
  starting transfers between devices: 6.45 us -> 14.6 us
  waiting for transfers between devices: 28.9 us -> 24.6 us
    dot_general x32 -> x0, matrix products: 62.4 us -> none  [the longest x4 39.2 us: form(): jnp.einsum('sca,cba->scb', vectors, weights, preferred_element_type=jnp.f...]
    reduce_sum x84 -> x0, other arithmetic: 33.3 us -> none  [the longest x32 24.8 us: orthonormalize(): jnp.sum(vec_real * vec_real + vec_imag * vec_imag, axis=-1, keepdims=True)]
    pallas_call x0 -> x4, Pallas kernels: none -> 13.9 us  [the longest x1 6.63 us: local(): pl.pallas_call(functools.partial(subspace_kernel, tm, own, samples, facto...]
    all_gather x1 -> x0, blocking collectives: 13.1 us -> none  [local(): lax.all_gather(basis.astype(jnp.bfloat16), 'tm', axis=0, tiled=True)]
    ppermute x0 -> x8, starting transfers between devices: none -> 8.14 us  [the longest x7 8.14 us: local(): packet = lax.ppermute(packet, ('tm', 'pol'), route)]
    reduce_scatter x1 -> x0, waiting for transfers between devices: 6.91 us -> none  [local(): lax.psum_scatter(power_term.astype(jnp.bfloat16), 'pol', scatter_dimensio...]
    squeeze x9 -> x0, local copies, waits for them, and re-layouts: 6.57 us -> none  [the longest x4 3.88 us: local(): lax.scan(add_block, jnp.zeros((own, 2, width, width), jnp.float32), blocks)]
    reshape x0 -> x2, local copies, waits for them, and re-layouts: none -> 3.03 us  [local(): voltages[:, 0].transpose(1, 0, 2, 3).reshape(chan_dev, samples, 2 * width)]
  transfers between devices with their start and end apart: 2 -> 9, of which waited for: 2 -> 1; matrix products, arithmetic and copies ran while one was open for 2% -> 0% of each run, Pallas kernels for 0% -> 23%
where the time goes in v1:
time: 56.6 us; the launch traced here: 56.3 us
  waiting for transfers between devices  24.6 us (43%)
  starting transfers between devices  14.6 us (26%)
  Pallas kernels  13.9 us (25%)
  local copies, waits for them, and re-layouts  3.05 us (5%)
    all_to_all x1, waiting for transfers between devices, local(): lax.all_to_all(series, 'tm', split_axis=0, concat_axis=0, tiled=True)  24.6 us
    ppermute x7, starting transfers between devices, local(): packet = lax.ppermute(packet, ('tm', 'pol'), route)  8.14 us
    pallas_call x1, Pallas kernels, local(): pl.pallas_call(functools.partial(subspace_kernel, tm, own, samples, facto...  6.63 us
    all_to_all x1, starting transfers between devices, local(): lax.all_to_all(series, 'tm', split_axis=0, concat_axis=0, tiled=True)  6.45 us
    pallas_call x1, Pallas kernels, local(): pl.pallas_call(functools.partial(raw_beams_kernel, chan_dev), grid=(chan_...  5.03 us
    reshape x2, local copies, waits for them, and re-layouts, local(): voltages[:, 0].transpose(1, 0, 2, 3).reshape(chan_dev, samples, 2 * width)  3.03 us
    pallas_call x1, Pallas kernels, local(): pl.pallas_call(functools.partial(finish_kernel, tm, own), out_shape=jax.S...  1.19 us
  transfers between devices with their start and end apart: 9, of which 1 were waited for; matrix products, arithmetic and copies ran while one was open for 0% of the time, Pallas kernels for 23%

profile of v1, /device:TPU:0, one launch (start us, length us, event | category | flops | bytes accessed | tf_op | source)
XLA Modules:
  0.0 56.3 jit_solution(12803467071858947761)
XLA Ops:
  0.0 1.7 %reshape.4 = bf16[4,128,1024]{2,0,1:T(4,128)(2,1)S(1)} reshape(bf16[4,128,2,512]{3,2,0,1:T(2,128)(2,1)} %bitcast.7) | data formatting | bytes 2097152 | tf_op jit(solution)/shard_map/reshape | solution.py:209
  1.7 1.3 %copy.7.mine_ref = bf16[4,128,1024]{2,1,0:T(8,128)(2,1)} copy(bf16[4,128,1024]{2,0,1:T(4,128)(2,1)S(1)} %reshape.4) | data formatting | bytes 2097152 | tf_op jit(solution)/shard_map/reshape | solution.py:209
  3.0 0.0 copy-start
  3.0 6.4 %all-to-all-start = ((bf16[4,128,1024]{2,1,0:T(8,128)(2,1)}), bf16[4,128,1024]{2,1,0:T(8,128)(2,1)S(1)}, u32[]{:S(2)}, u32[]{:S(2)}) async-start(bf16[4,128,1024]{2,1,0:T(8,128)(2,1)} %copy.7.mine_ref), calls=%async_computation | async-start | bytes 2097152 | tf_op jit(solution)/shard_map/all_to_all | solution.py:210
  9.5 0.0 copy-start.1
  9.5 0.0 collective-permute-start
  9.5 0.0 copy-done
  9.5 1.1 %shard_map.56.weights_ref = bf16[1,512,512]{2,1,0:T(8,128)(2,1)S(1)} custom-call(s32[256,512]{1,0:T(8,128)S(1)} %copy-done), custom_call_target="tpu_custom_call" | custom-call | flops 5242880 | bytes 1048576 | tf_op jit(solution)/shard_map/pallas_call | solution.py:213
  10.6 0.0 copy-start.2
  10.6 0.0 copy-start.3
  10.6 24.6 %all-to-all-done = bf16[4,128,1024]{2,1,0:T(8,128)(2,1)S(1)} async-done(((bf16[4,128,1024]{2,1,0:T(8,128)(2,1)}), bf16[4,128,1024]{2,1,0:T(8,128)(2,1)S(1)}, u32[]{:S(2)}, u32[]{:S(2)}) %all-to-all-start) | async-done | bytes 1048608 | tf_op jit(solution)/shard_map/all_to_all | solution.py:210
  35.2 0.0 copy-done.1
  35.2 0.0 copy-done.2
  35.2 0.0 copy-done.3
  35.2 6.6 %shard_map.57 = (f32[1,16,256]{2,1,0:T(8,128)S(1)}, f32[1,16,256]{2,1,0:T(8,128)S(1)}, f32[1,16,256]{2,1,0:T(8,128)S(1)}, f32[1,16,256]{2,1,0:T(8,128)S(1)}, f32...) custom-call(bf16[1,512,1024]{2,1,0:T(8,128)(2,1)S(1)} %bitcast.6, ...), custom_call_target="tpu_custom_call" | custom-call | flops 536870912 | bytes 1048576 | tf_op jit(solution)/shard_map/pallas_call | solution.py:246
  41.9 0.1 collective-permute-start.1
  41.9 0.1 collective-permute-start.2
  42.0 0.1 collective-permute-start.3
  42.1 4.1 %collective-permute-start.4 = (f32[1,16,256]{2,1,0:T(8,128)S(1)}, f32[1,16,256]{2,1,0:T(8,128)S(1)}, u32[]{:S(2)}, u32[]{:S(2)}) collective-permute-start(f32[1,16,256]{2,1,0:T(8,128)S(1)} %get-tuple-element.17), channel_id=1, source_target_pairs={{0,8},{1,9},{4,12},{5,13},{8,0},{9,1},{12,4},{13,5},{2,10},{3,11},... | collective-permute-start | bytes 49160 | tf_op jit(solution)/shard_map/ppermute | solution.py:271
  46.2 0.0 collective-permute-done.other_ref
  46.2 0.0 collective-permute-start.5
  46.2 0.0 collective-permute-done.1.rest_1_
  46.2 2.1 %collective-permute-start.6 = (f32[1,16,256]{2,1,0:T(8,128)S(1)}, f32[1,16,256]{2,1,0:T(8,128)S(1)}, u32[]{:S(2)}, u32[]{:S(2)}) collective-permute-start(f32[1,16,256]{2,1,0:T(8,128)S(1)} %get-tuple-element.19), channel_id=1, source_target_pairs={{0,12},{1,13},{4,0},{5,1},{8,4},{9,5},{12,8},{13,9},{2,14},{3,15},... | collective-permute-start | bytes 49160 | tf_op jit(solution)/shard_map/ppermute | solution.py:271
  48.3 0.0 collective-permute-done.2.rest_2_
  48.3 1.7 %collective-permute-start.7 = (f32[1,16,256]{2,1,0:T(8,128)S(1)}, f32[1,16,256]{2,1,0:T(8,128)S(1)}, u32[]{:S(2)}, u32[]{:S(2)}) collective-permute-start(f32[1,16,256]{2,1,0:T(8,128)S(1)} %get-tuple-element.20), channel_id=1, source_target_pairs={{0,13},{1,12},{4,1},{5,0},{8,5},{9,4},{12,9},{13,8},{2,15},{3,14},... | collective-permute-start | bytes 49160 | tf_op jit(solution)/shard_map/ppermute | solution.py:271
  50.0 5.0 %shard_map.55.raw_ref = f32[4,2,128,256]{3,2,1,0:T(8,128)S(1)} custom-call(s32[256,512]{1,0:T(8,128)S(1)} %copy-done, bf16[4,128,1024]{2,1,0:T(8,128)(2,1)} %copy.7.mine_ref, bf16[4,128,1024]{2,1,0:T(8,128)(2,1)S(1)} %collective-permute-done.other_ref), custom_call_target="tpu_custom_call" | custom-call | flops 1073741824 | bytes 2097152 | tf_op jit(solution)/shard_map/pallas_call | solution.py:224
  55.1 0.0 collective-permute-done.3.rest_3_
  55.1 0.0 collective-permute-done.4.rest_4_
  55.1 0.0 collective-permute-done.5.rest_5_
  55.1 0.0 collective-permute-done.6.rest_6_
  55.1 0.0 collective-permute-done.7.rest_7_
  55.1 1.2 %shard_map.58 = f32[128,4,128]{2,1,0:T(4,128)} custom-call(f32[4,2,128,256]{3,2,1,0:T(8,128)S(1)} %shard_map.55.raw_ref, f32[1,16,256]{2,1,0:T(8,128)S(1)} %get-tuple-element.13.rest_0_, f32[1,16,256]{2,1,0:T(8,128)S(1)} %collective-permute-done.1.rest_1_, f32[1,16,256]{2,1,0:T(8,128)S(1)} %collective-permute-done.2.rest_2_, ...), custom_call_target="tpu_custom_call" | custom-call | tf_op jit(solution)/shard_map/pallas_call | solution.py:274
Async XLA Ops:
  3.0 6.5 %copy-start = (s32[256,512]{1,0:T(8,128)S(1)}, s32[256,512]{1,0:T(8,128)}, u32[]{:S(2)}) copy-start(s32[256,512]{1,0:T(8,128)} %phase_ref.3) | copy-start | bytes 1572868
  3.0 32.2 %all-to-all-start = ((bf16[4,128,1024]{2,1,0:T(8,128)(2,1)}), bf16[4,128,1024]{2,1,0:T(8,128)(2,1)S(1)}, u32[]{:S(2)}, u32[]{:S(2)}) async-start(bf16[4,128,1024]{2,1,0:T(8,128)(2,1)} %copy.7.mine_ref), calls=%async_computation | async-start | bytes 2097152 | tf_op jit(solution)/shard_map/all_to_all | solution.py:210
  9.5 25.7 %copy-start.1 = (f32[1,4,2,8,512]{4,3,2,1,0:T(8,128)S(1)}, f32[1,4,2,8,512]{4,3,2,1,0:T(8,128)}, u32[]{:S(2)}) copy-start(f32[1,4,2,8,512]{4,3,2,1,0:T(8,128)} %start_ref.1) | copy-start | bytes 393220
  9.5 36.7 %collective-permute-start = (bf16[4,128,1024]{2,1,0:T(8,128)(2,1)}, bf16[4,128,1024]{2,1,0:T(8,128)(2,1)S(1)}, u32[]{:S(2)}, u32[]{:S(2)}) collective-permute-start(bf16[4,128,1024]{2,1,0:T(8,128)(2,1)} %copy.7.mine_ref), channel_id=1, source_target_pairs={{0,1},{1,0},{2,3},{3,2},{4,5},{5,4},{6,7},{7,6},{8,9},{9,8},{10,11... | collective-permute-start | bytes 3145736 | tf_op jit(solution)/shard_map/ppermute | solution.py:211
  10.6 24.6 %copy-start.2 = (s32[4]{0:T(128)S(1)}, s32[4]{0:T(128)}, u32[]{:S(2)}) copy-start(s32[4]{0:T(128)} %flags_ref.1) | copy-start | bytes 52
  10.6 24.6 %copy-start.3 = (s32[4]{0:T(128)S(1)}, s32[4]{0:T(128)}, u32[]{:S(2)}) copy-start(s32[4]{0:T(128)} %ranks_ref.1) | copy-start | bytes 52
  41.9 4.3 %collective-permute-start.1 = (f32[1,16,256]{2,1,0:T(8,128)S(1)}, f32[1,16,256]{2,1,0:T(8,128)S(1)}, u32[]{:S(2)}, u32[]{:S(2)}) collective-permute-start(f32[1,16,256]{2,1,0:T(8,128)S(1)} %get-tuple-element.14), channel_id=1, source_target_pairs={{0,1},{1,0},{4,5},{5,4},{8,9},{9,8},{12,13},{13,12},{2,3},{3,2},{6... | collective-permute-start | bytes 49160 | tf_op jit(solution)/shard_map/ppermute | solution.py:271
  41.9 6.4 %collective-permute-start.2 = (f32[1,16,256]{2,1,0:T(8,128)S(1)}, f32[1,16,256]{2,1,0:T(8,128)S(1)}, u32[]{:S(2)}, u32[]{:S(2)}) collective-permute-start(f32[1,16,256]{2,1,0:T(8,128)S(1)} %get-tuple-element.15), channel_id=1, source_target_pairs={{0,4},{1,5},{4,8},{5,9},{8,12},{9,13},{12,0},{13,1},{2,6},{3,7},{6... | collective-permute-start | bytes 49160 | tf_op jit(solution)/shard_map/ppermute | solution.py:271
  42.0 13.1 %collective-permute-start.3 = (f32[1,16,256]{2,1,0:T(8,128)S(1)}, f32[1,16,256]{2,1,0:T(8,128)S(1)}, u32[]{:S(2)}, u32[]{:S(2)}) collective-permute-start(f32[1,16,256]{2,1,0:T(8,128)S(1)} %get-tuple-element.16), channel_id=1, source_target_pairs={{0,5},{1,4},{4,9},{5,8},{8,13},{9,12},{12,1},{13,0},{2,7},{3,6},{6... | collective-permute-start | bytes 49160 | tf_op jit(solution)/shard_map/ppermute | solution.py:271
  42.1 13.0 %collective-permute-start.4 = (f32[1,16,256]{2,1,0:T(8,128)S(1)}, f32[1,16,256]{2,1,0:T(8,128)S(1)}, u32[]{:S(2)}, u32[]{:S(2)}) collective-permute-start(f32[1,16,256]{2,1,0:T(8,128)S(1)} %get-tuple-element.17), channel_id=1, source_target_pairs={{0,8},{1,9},{4,12},{5,13},{8,0},{9,1},{12,4},{13,5},{2,10},{3,11},... | collective-permute-start | bytes 49160 | tf_op jit(solution)/shard_map/ppermute | solution.py:271
  46.2 8.9 %collective-permute-start.5 = (f32[1,16,256]{2,1,0:T(8,128)S(1)}, f32[1,16,256]{2,1,0:T(8,128)S(1)}, u32[]{:S(2)}, u32[]{:S(2)}) collective-permute-start(f32[1,16,256]{2,1,0:T(8,128)S(1)} %get-tuple-element.18), channel_id=1, source_target_pairs={{0,9},{1,8},{4,13},{5,12},{8,1},{9,0},{12,5},{13,4},{2,11},{3,10},... | collective-permute-start | bytes 49160 | tf_op jit(solution)/shard_map/ppermute | solution.py:271
  46.2 8.9 %collective-permute-start.6 = (f32[1,16,256]{2,1,0:T(8,128)S(1)}, f32[1,16,256]{2,1,0:T(8,128)S(1)}, u32[]{:S(2)}, u32[]{:S(2)}) collective-permute-start(f32[1,16,256]{2,1,0:T(8,128)S(1)} %get-tuple-element.19), channel_id=1, source_target_pairs={{0,12},{1,13},{4,0},{5,1},{8,4},{9,5},{12,8},{13,9},{2,14},{3,15},... | collective-permute-start | bytes 49160 | tf_op jit(solution)/shard_map/ppermute | solution.py:271
  48.3 6.8 %collective-permute-start.7 = (f32[1,16,256]{2,1,0:T(8,128)S(1)}, f32[1,16,256]{2,1,0:T(8,128)S(1)}, u32[]{:S(2)}, u32[]{:S(2)}) collective-permute-start(f32[1,16,256]{2,1,0:T(8,128)S(1)} %get-tuple-element.20), channel_id=1, source_target_pairs={{0,13},{1,12},{4,1},{5,0},{8,5},{9,4},{12,9},{13,8},{2,15},{3,14},... | collective-permute-start | bytes 49160 | tf_op jit(solution)/shard_map/ppermute | solution.py:271

commit v2 on v1

v2 whole, which is shorter than its diff:
```python
import functools

import jax
import jax.numpy as jnp
from jax import lax
from jax.experimental import pallas as pl
from jax.experimental.pallas import tpu as pltpu
from jax.sharding import PartitionSpec as P

ITERS = 4
PHASES = 1024
QUARTER = PHASES // 4
EPS = 1e-06
F32 = jnp.float32
BF16 = jnp.bfloat16
NT = (((1,), (1,)), ((), ()))
NN = (((1,), (0,)), ((), ()))
TN = (((0,), (0,)), ((), ()))
VMEM_LIMIT = 48 * 1024 * 1024


def dot(left, right, dims):
    return lax.dot_general(left, right, dims, preferred_element_type=F32)


def split(values):
    high = values.astype(BF16)
    low = (values - high.astype(F32)).astype(BF16)
    return high, low


def steer(phase, step, norm):
    turn = (phase * step) & (PHASES - 1)
    quadrant = (turn + QUARTER // 2) // QUARTER
    angle = (turn - quadrant * QUARTER).astype(F32) * (2.0 * jnp.pi / PHASES)
    sq = angle * angle
    sine = angle * (1.0 + sq * (-1.0 / 6 + sq * (1.0 / 120 + sq * (-1.0 / 5040 + sq / 362880))))
    cosine = 1.0 + sq * (-0.5 + sq * (1.0 / 24 + sq * (-1.0 / 720 + sq / 40320)))
    odd = (quadrant & 1) == 1
    real = jnp.where(odd, sine, cosine) * norm
    imag = jnp.where(odd, cosine, sine) * norm
    real = jnp.where(((quadrant + 1) & 2) == 2, -real, real)
    imag = jnp.where((quadrant & 2) == 2, -imag, imag)
    return real.astype(BF16), imag.astype(BF16)


def fill_weights(phase_ref, first, rows, step, out):
    norm = 1.0 / (phase_ref.shape[1] ** 0.5)
    chunk = 32

    def body(i, carry):
        at = pl.multiple_of(i * chunk, chunk)
        real, imag = steer(phase_ref[pl.ds(first + at, chunk), :], step, norm)
        out[pl.ds(at, chunk), :] = real
        out[pl.ds(rows + at, chunk), :] = imag
        return carry

    lax.fori_loop(0, rows // chunk, body, 0)


def own_weights_kernel(own, chan_dev, phase_ref, out_ref):
    beams = phase_ref.shape[0]
    first = lax.axis_index("chan") * chan_dev + lax.axis_index("tm") * own
    for o in range(own):
        fill_weights(phase_ref, 0, beams, first + o + 1, out_ref.at[o])


def turned(values, axis):
    size = values.shape[axis]
    at = lax.broadcasted_iota(jnp.int32, values.shape, axis)
    after = pltpu.roll(values, size - 1, axis)
    before = pltpu.roll(values, 1, axis)
    return jnp.where((at & 1) == 0, after, -before)


def raw_beams_kernel(chan_dev, phase_ref, series_ref, mine_ref, other_ref, weights):
    half = phase_ref.shape[0] // 2
    rows = series_ref.shape[1]
    chan_id = lax.axis_index("chan") * chan_dev + pl.program_id(0)
    for swap, out_ref in enumerate((mine_ref, other_ref)):
        first = pl.multiple_of((lax.axis_index("pol") ^ swap) * half, half)
        fill_weights(phase_ref, first, half, chan_id + 1, weights)
        product = dot(series_ref[0], weights[...], NT)
        by_imag = turned(product[:, half:].reshape(rows // 8, 8, half), 1).reshape(rows, half)
        out_ref[0] = product[:, :half] - by_imag


def correlate(real, imag, x):
    vectors = real.shape[0]
    rows = jnp.concatenate([real, imag], axis=0)
    product = dot(jnp.concatenate(split(rows), axis=0), x, NT)
    product = product[: 2 * vectors] + product[2 * vectors :]
    other = turned(product, 1)
    return product[:vectors] + other[vectors:], product[vectors:] - other[:vectors]


def cov_times(real, imag, blocks, factor):
    vectors = real.shape[0]
    total = None
    for x in blocks:
        pair = jnp.concatenate(correlate(real, imag, x), axis=0)
        term = dot(jnp.concatenate(split(pair), axis=0), x, NN)
        total = term if total is None else total + term
    total = (total[: 2 * vectors] + total[2 * vectors :]) * factor
    return total[:vectors], total[vectors:]


def orthonormalize(real_z, imag_z):
    vectors = real_z.shape[0]
    row = lax.broadcasted_iota(jnp.int32, real_z.shape, 0)
    real_v, imag_v = real_z, imag_z
    scale = jnp.zeros((vectors, 1), F32)
    for n in range(vectors):
        here = row == n
        real_a, imag_a = real_v[n : n + 1], imag_v[n : n + 1]
        real_z = jnp.where(here, real_v, real_z)
        imag_z = jnp.where(here, imag_v, imag_z)
        real_d = jnp.sum(real_a * real_z + imag_a * imag_z, axis=1, keepdims=True)
        norm = real_d[n : n + 1] + EPS
        scale = jnp.where(row[:, :1] == n, norm, scale)
        if n + 1 < vectors:
            imag_d = jnp.sum(real_a * imag_z - imag_a * real_z, axis=1, keepdims=True)
            inverse = 1.0 / norm
            later = row[:, :1] > n
            real_c = jnp.where(later, real_d * inverse, 0.0)
            imag_c = jnp.where(later, imag_d * inverse, 0.0)
            real_v = real_v - (real_c * real_a - imag_c * imag_a)
            imag_v = imag_v - (real_c * imag_a + imag_c * real_a)
    factor = 1.0 / jnp.sqrt(scale)
    return real_v * factor, imag_v * factor


def subspace_kernel(tm, own, factor, start_ref, flags_ref, ranks_ref, weights_ref, beams_ref, *rest):
    blocks_ref, outs = rest[:tm], rest[tm + 1 :]
    vectors, width = start_ref.shape[3], start_ref.shape[4]
    rows = blocks_ref[0].shape[1]
    tm_index = lax.axis_index("tm")
    beams = weights_ref.shape[1] // 2
    for o in range(own):
        chan = tm_index * own + o
        real_q = start_ref[0, chan, 0]
        imag_q = start_ref[0, chan, 1]
        blocks = [ref[o] for ref in blocks_ref]
        for sweep in range(ITERS):
            real_z, imag_z = cov_times(real_q, imag_q, blocks, factor)
            real_q, imag_q = orthonormalize(real_z, imag_z)
        rank = flags_ref[chan] * ranks_ref[chan]
        keep = lax.broadcasted_iota(jnp.int32, (vectors, width), 0) < rank
        real_u = jnp.where(keep, real_q, 0.0)
        imag_u = jnp.where(keep, imag_q, 0.0)
        both = jnp.concatenate([real_u, imag_u], axis=0)
        product = dot(jnp.concatenate(split(both), axis=0), weights_ref[o], NT)
        product = product[: 2 * vectors] + product[2 * vectors :]
        real_w = product[:vectors, :beams] - product[vectors:, beams:]
        imag_w = product[:vectors, beams:] + product[vectors:, :beams]
        for x in range(tm):
            outs[x][o, :, :rows] = correlate(real_u, imag_u, blocks[x])[0]
            outs[x][o, :, rows : rows + beams] = real_w
            outs[x][o, :, rows + beams :] = imag_w


def finish_kernel(tm, own, mine_ref, theirs_ref, *rest):
    arrived, out_ref, squares, powers = rest[:-3], rest[-3], rest[-2], rest[-1]
    rows, half = mine_ref.shape[1], mine_ref.shape[2]
    samples = rows // 2
    tm_index = lax.axis_index("tm")
    real_at = pl.multiple_of(rows + lax.axis_index("pol") * half, half)
    imag_at = pl.multiple_of(real_at + 2 * half, half)
    for x in range(tm):
        for o in range(own):
            chan = (tm_index ^ x) * own + o
            total = None
            for raw_ref, ref in ((mine_ref, arrived[x]), (theirs_ref, arrived[tm + x])):
                series = ref[o, :, :rows]
                left = jnp.concatenate([series, -turned(series, 1)], axis=0)
                right = jnp.concatenate(
                    [ref[o, :, pl.ds(real_at, half)], ref[o, :, pl.ds(imag_at, half)]], axis=0
                )
                high_s, low_s = split(left)
                high_w, low_w = split(right)
                left = jnp.concatenate([high_s, high_s, low_s], axis=0)
                right = jnp.concatenate([high_w, low_w, high_w], axis=0)
                beam = raw_ref[chan] - dot(left, right, TN)
                total = beam * beam if total is None else total + beam * beam
            squares[...] = total
            powers[chan] = squares[pl.ds(0, samples, 2), :] + squares[pl.ds(1, samples, 2), :]
    for chan in range(powers.shape[0]):
        out_ref[:, chan, :] = powers[chan]


def local(voltages, start_block, flags, ranks, phase_index):
    tm = lax.axis_size("tm")
    tm_index = lax.axis_index("tm")
    samples, chan_dev, width = voltages.shape[0], voltages.shape[2], voltages.shape[4]
    own = chan_dev // tm
    vectors = start_block.shape[3]
    beams = phase_index.shape[0]
    half = beams // 2
    rows = 2 * samples
    factor = 1.0 / (samples * tm)
    params = pltpu.CompilerParams(vmem_limit_bytes=VMEM_LIMIT)
    whole = pl.BlockSpec(memory_space=pltpu.VMEM)
    scalars = pl.BlockSpec(memory_space=pltpu.SMEM)
    unread = pl.BlockSpec(memory_space=pl.ANY)

    series = voltages[:, 0].transpose(1, 0, 2, 3).reshape(chan_dev, rows, width)

    blocks = [None] * tm
    for x in [*range(2, tm), 1, 0]:
        piece = lax.dynamic_slice_in_dim(series, (tm_index ^ x) * own, own, 0)
        blocks[x] = lax.ppermute(piece, "tm", [(z, z ^ x) for z in range(tm)]) if x else piece

    own_weights = pl.pallas_call(
        functools.partial(own_weights_kernel, own, chan_dev),
        out_shape=jax.ShapeDtypeStruct((own, 2 * beams, width), BF16),
        in_specs=[whole],
        out_specs=whole,
        compiler_params=params,
        cost_estimate=pl.CostEstimate(
            flops=40 * own * beams * width, bytes_accessed=8 * own * beams * width, transcendentals=0
        ),
    )(phase_index)

    raw = jax.ShapeDtypeStruct((chan_dev, rows, half), F32)
    mine, other = pl.pallas_call(
        functools.partial(raw_beams_kernel, chan_dev),
        grid=(chan_dev,),
        out_shape=[raw] * 2,
        in_specs=[
            pl.BlockSpec((beams, width), lambda c: (0, 0)),
            pl.BlockSpec((1, rows, width), lambda c: (c, 0, 0)),
        ],
        out_specs=[pl.BlockSpec((1, rows, half), lambda c: (c, 0, 0))] * 2,
        scratch_shapes=[pltpu.VMEM((beams, width), BF16)],
        compiler_params=params,
        cost_estimate=pl.CostEstimate(
            flops=8 * chan_dev * samples * width * beams,
            bytes_accessed=8 * chan_dev * samples * width,
            transcendentals=0,
        ),
    )(phase_index, series)
    cores = [(0, 1), (1, 0)]

    packet = jax.ShapeDtypeStruct((own, vectors, rows + 2 * beams), F32)
    other, *packets = pl.pallas_call(
        functools.partial(subspace_kernel, tm, own, factor),
        out_shape=[raw] + [packet] * tm,
        in_specs=[whole, scalars, scalars, whole, unread] + [whole] * tm,
        out_specs=[unread] + [whole] * tm,
        input_output_aliases={4: 0},
        compiler_params=params,
        cost_estimate=pl.CostEstimate(
            flops=64 * own * vectors * tm * samples * width * ITERS,
            bytes_accessed=4 * own * tm * samples * width,
            transcendentals=0,
        ),
    )(start_block, flags, ranks, own_weights, other, *blocks)

    theirs = lax.ppermute(other, "pol", cores)
    arrived = list(packets)
    for x in range(1, tm):
        arrived[x] = lax.ppermute(packets[x], "tm", [(z, z ^ x) for z in range(tm)])
    arrived += [lax.ppermute(packet, "pol", cores) for packet in arrived]

    return pl.pallas_call(
        functools.partial(finish_kernel, tm, own),
        out_shape=jax.ShapeDtypeStruct((samples, chan_dev, half), F32),
        in_specs=[whole] * (2 + 2 * tm),
        out_specs=whole,
        scratch_shapes=[
            pltpu.VMEM((rows, half), F32),
            pltpu.VMEM((chan_dev, samples, half), F32),
        ],
        compiler_params=params,
    )(mine, theirs, *arrived)


def solution(mesh):
    placed = (
        P(("groups", "tm"), "pol", "chan", None, None),
        P("pol", "chan", None, None, None),
        P(("groups", "chan")),
        P(("groups", "chan")),
        P(),
    )
    return jax.shard_map(
        local,
        mesh=mesh,
        in_specs=placed,
        out_specs=P(("groups", "tm"), "chan", "pol"),
        check_vma=False,
    )
```

time: 56.6 us -> 50.4 us (0.89)
  waiting for transfers between devices: 24.6 us -> 16.2 us
  Pallas kernels: 13.9 us -> 18.1 us
  starting transfers between devices: 14.6 us -> 12.7 us
    all_to_all x1 -> x0, waiting for transfers between devices: 24.6 us -> none  [local(): lax.all_to_all(series, 'tm', split_axis=0, concat_axis=0, tiled=True)]
    ppermute x8 -> x11, waiting for transfers between devices: 0.02 us -> 16.2 us  [the longest x3 10.8 us: local(): lax.ppermute(piece, 'tm', [(z, z ^ x) for z in range(tm)])]
    all_to_all x1 -> x0, starting transfers between devices: 6.45 us -> none  [local(): lax.all_to_all(series, 'tm', split_axis=0, concat_axis=0, tiled=True)]
    ppermute x8 -> x11, starting transfers between devices: 8.14 us -> 12.7 us  [the longest x3 6.4 us: local(): arrived[x] = lax.ppermute(packets[x], 'tm', [(z, z ^ x) for z in range(tm)])]
    reshape x2 -> x1, local copies, waits for them, and re-layouts: 3.03 us -> 0.44 us  [local(): series = voltages[:, 0].transpose(1, 0, 2, 3).reshape(chan_dev, rows, width)]
    pallas_call x1, Pallas kernels: 6.63 us -> 8.8 us  [local(): pl.pallas_call(functools.partial(subspace_kernel, tm, own, factor), out_s...]
    transpose x0 -> x1, local copies, waits for them, and re-layouts: none -> 1.94 us  [local(): series = voltages[:, 0].transpose(1, 0, 2, 3).reshape(chan_dev, rows, width)]
    pallas_call x1, Pallas kernels: 5.03 us -> 6.93 us  [local(): pl.pallas_call(functools.partial(raw_beams_kernel, chan_dev), grid=(chan_...]
  transfers between devices with their start and end apart: 9 -> 11, of which waited for: 1 -> 5; matrix products, arithmetic and copies ran while one was open for 0% -> 0% of each run, Pallas kernels for 23% -> 16%
where the time goes in v2:
time: 50.4 us; the launch traced here: 50.2 us
  Pallas kernels  18.1 us (36%)
  waiting for transfers between devices  16.2 us (32%)
  starting transfers between devices  12.7 us (25%)
  local copies, waits for them, and re-layouts  3.17 us (6%)
    ppermute x3, waiting for transfers between devices, local(): lax.ppermute(piece, 'tm', [(z, z ^ x) for z in range(tm)])  10.8 us
    pallas_call x1, Pallas kernels, local(): pl.pallas_call(functools.partial(subspace_kernel, tm, own, factor), out_s...  8.8 us
    pallas_call x1, Pallas kernels, local(): pl.pallas_call(functools.partial(raw_beams_kernel, chan_dev), grid=(chan_...  6.93 us
    ppermute x3, starting transfers between devices, local(): arrived[x] = lax.ppermute(packets[x], 'tm', [(z, z ^ x) for z in range(tm)])  6.4 us
    ppermute x3, starting transfers between devices, local(): lax.ppermute(piece, 'tm', [(z, z ^ x) for z in range(tm)])  5.68 us
    ppermute x3, waiting for transfers between devices, local(): arrived[x] = lax.ppermute(packets[x], 'tm', [(z, z ^ x) for z in range(tm)])  4.21 us
    transpose x1, local copies, waits for them, and re-layouts, local(): series = voltages[:, 0].transpose(1, 0, 2, 3).reshape(chan_dev, rows, width)  1.94 us
    pallas_call x1, Pallas kernels, local(): pl.pallas_call(functools.partial(finish_kernel, tm, own), out_shape=jax.S...  1.35 us
  transfers between devices with their start and end apart: 11, of which 5 were waited for; matrix products, arithmetic and copies ran while one was open for 0% of the time, Pallas kernels for 16%

profile of v2, /device:TPU:0, one launch (start us, length us, event | category | flops | bytes accessed | tf_op | source)
XLA Modules:
  0.0 50.2 jit_solution(16134728786096014657)
XLA Ops:
  0.0 1.9 %copy.7 = bf16[4,128,2,512]{3,2,1,0:T(2,128)(2,1)S(1)} copy(bf16[4,128,2,512]{3,2,0,1:T(2,128)(2,1)} %bitcast.3) | data formatting | bytes 2097152 | tf_op jit(solution)/shard_map/transpose | solution.py:206
  1.9 0.4 reshape.3.series_ref
  2.4 0.0 copy-start
  2.4 0.1 constant_dynamic-slice_fusion
  2.5 3.1 %collective-permute-start = (bf16[1,256,512]{2,1,0:T(8,128)(2,1)S(1)}, bf16[1,256,512]{2,1,0:T(8,128)(2,1)S(1)}, u32[]{:S(2)}, u32[]{:S(2)}) collective-permute-start(bf16[1,256,512]{2,1,0:T(8,128)(2,1)S(1)} %get-tuple-element.21), channel_id=1, source_target_pairs={{0,4},{4,0},{8,12},{12,8},{1,5},{5,1},{9,13},{13,9},{2,6},{6,2},{1... | collective-permute-start | bytes 786440 | tf_op jit(solution)/shard_map/ppermute | solution.py:211
  5.6 2.6 %collective-permute-start.1 = (bf16[1,256,512]{2,1,0:T(8,128)(2,1)S(1)}, bf16[1,256,512]{2,1,0:T(8,128)(2,1)S(1)}, u32[]{:S(2)}, u32[]{:S(2)}) collective-permute-start(bf16[1,256,512]{2,1,0:T(8,128)(2,1)S(1)} %get-tuple-element.20), channel_id=1, source_target_pairs={{0,8},{4,12},{8,0},{12,4},{1,9},{5,13},{9,1},{13,5},{2,10},{6,14},... | collective-permute-start | bytes 786440 | tf_op jit(solution)/shard_map/ppermute | solution.py:211
  8.2 0.0 collective-permute-start.2
  8.2 0.0 copy-done
  8.2 1.1 %shard_map.56.weights_ref = bf16[1,512,512]{2,1,0:T(8,128)(2,1)S(1)} custom-call(s32[256,512]{1,0:T(8,128)S(1)} %copy-done), custom_call_target="tpu_custom_call" | custom-call | flops 5242880 | bytes 1048576 | tf_op jit(solution)/shard_map/pallas_call | solution.py:213
  9.3 0.0 copy-start.1
  9.3 6.9 %shard_map.55 = (f32[4,256,128]{2,1,0:T(8,128)S(1)}, f32[4,256,128]{2,1,0:T(8,128)S(1)}) custom-call(s32[256,512]{1,0:T(8,128)S(1)} %copy-done, bf16[4,256,512]{2,1,0:T(8,128)(2,1)S(1)} %reshape.3.series_ref), custom_call_target="tpu_custom_call" | custom-call | flops 536870912 | bytes 2097152 | tf_op jit(solution)/shard_map/pallas_call | solution.py:225
  16.2 0.5 %collective-permute-done.rest_1_ = bf16[1,256,512]{2,1,0:T(8,128)(2,1)S(1)} collective-permute-done((bf16[1,256,512]{2,1,0:T(8,128)(2,1)S(1)}, bf16[1,256,512]{2,1,0:T(8,128)(2,1)S(1)}, u32[]{:S(2)}, u32[]{:S(2)}) %collective-permute-start) | collective-permute-done | bytes 262176 | tf_op jit(solution)/shard_map/ppermute | solution.py:211
  16.8 10.2 %collective-permute-done.1.rest_2_ = bf16[1,256,512]{2,1,0:T(8,128)(2,1)S(1)} collective-permute-done((bf16[1,256,512]{2,1,0:T(8,128)(2,1)S(1)}, bf16[1,256,512]{2,1,0:T(8,128)(2,1)S(1)}, u32[]{:S(2)}, u32[]{:S(2)}) %collective-permute-start.1) | collective-permute-done | bytes 262176 | tf_op jit(solution)/shard_map/ppermute | solution.py:211
  27.0 0.0 collective-permute-done.2.rest_3_
  27.0 0.0 copy-start.2
  27.0 0.0 copy-start.3
  27.0 0.0 copy-done.1
  27.0 0.6 %copy-done.2 = s32[4]{0:T(128)S(1)} copy-done((s32[4]{0:T(128)S(1)}, s32[4]{0:T(128)}, u32[]{:S(2)}) %copy-start.2) | copy-done | bytes 40
  27.7 0.0 copy-done.3
  27.7 8.8 %shard_map.57 = (f32[4,256,128]{2,1,0:T(8,128)S(1)}, f32[1,8,768]{2,1,0:T(8,128)S(1)}, f32[1,8,768]{2,1,0:T(8,128)S(1)}, f32[1,8,768]{2,1,0:T(8,128)S(1)}, f32[1,8,768]{2,1,0:T(8,128)S(1)}) custom-call(f32[1,4,2,8,512]{4,3,2,1,0:T(8,128)S(1)} %copy-done.1, s32[4]{0:T(128)S(1)} %copy-done.2, s32[4]{0:T(128)S(1)} %copy-done.3, ...), custom_call_target="tpu_custom_call", output_to_operand_aliasing={{0}: (4, {})} | custom-call | flops 536870912 | bytes 1048576 | tf_op jit(solution)/shard_map/pallas_call | solution.py:245
  36.5 0.1 collective-permute-start.3
  36.6 2.5 %collective-permute-start.6 = (f32[1,8,768]{2,1,0:T(8,128)S(1)}, f32[1,8,768]{2,1,0:T(8,128)S(1)}, u32[]{:S(2)}, u32[]{:S(2)}) collective-permute-start(f32[1,8,768]{2,1,0:T(8,128)S(1)} %get-tuple-element.18), channel_id=1, source_target_pairs={{0,12},{4,8},{8,4},{12,0},{1,13},{5,9},{9,5},{13,1},{2,14},{6,10},... | collective-permute-start | bytes 73736 | tf_op jit(solution)/shard_map/ppermute | solution.py:262
  39.1 3.9 %collective-permute-start.4 = (f32[1,8,768]{2,1,0:T(8,128)S(1)}, f32[1,8,768]{2,1,0:T(8,128)S(1)}, u32[]{:S(2)}, u32[]{:S(2)}) collective-permute-start(f32[1,8,768]{2,1,0:T(8,128)S(1)} %get-tuple-element.16), channel_id=1, source_target_pairs={{0,4},{4,0},{8,12},{12,8},{1,5},{5,1},{9,13},{13,9},{2,6},{6,2},{1... | collective-permute-start | bytes 73736 | tf_op jit(solution)/shard_map/ppermute | solution.py:262
  43.0 0.0 collective-permute-start.5
  43.0 0.0 collective-permute-start.7
  43.0 0.0 collective-permute-done.6.rest_3_
  43.0 0.5 %collective-permute-start.10 = (f32[1,8,768]{2,1,0:T(8,128)S(1)}, f32[1,8,768]{2,1,0:T(8,128)S(1)}, u32[]{:S(2)}, u32[]{:S(2)}) collective-permute-start(f32[1,8,768]{2,1,0:T(8,128)S(1)} %collective-permute-done.6.rest_3_), channel_id=1, source_target_pairs={{0,1},{1,0},{2,3},{3,2},{4,5},{5,4},{6,7},{7,6},{8,9},{9,8},{10,11... | collective-permute-start | bytes 73736 | tf_op jit(solution)/shard_map/ppermute | solution.py:263
  43.5 1.3 %collective-permute-done.4.rest_1_ = f32[1,8,768]{2,1,0:T(8,128)S(1)} collective-permute-done((f32[1,8,768]{2,1,0:T(8,128)S(1)}, f32[1,8,768]{2,1,0:T(8,128)S(1)}, u32[]{:S(2)}, u32[]{:S(2)}) %collective-permute-start.4) | collective-permute-done | bytes 24608 | tf_op jit(solution)/shard_map/ppermute | solution.py:262
  44.8 0.0 collective-permute-start.8
  44.8 2.9 %collective-permute-done.5.rest_2_ = f32[1,8,768]{2,1,0:T(8,128)S(1)} collective-permute-done((f32[1,8,768]{2,1,0:T(8,128)S(1)}, f32[1,8,768]{2,1,0:T(8,128)S(1)}, u32[]{:S(2)}, u32[]{:S(2)}) %collective-permute-start.5) | collective-permute-done | bytes 24608 | tf_op jit(solution)/shard_map/ppermute | solution.py:262
  47.7 0.0 collective-permute-start.9
  47.7 0.0 collective-permute-done.7.rest_4_
  47.7 0.0 collective-permute-done.10.rest_7_
  47.7 0.0 collective-permute-done.8.rest_5_
  47.7 1.2 %collective-permute-done.9.rest_6_ = f32[1,8,768]{2,1,0:T(8,128)S(1)} collective-permute-done((f32[1,8,768]{2,1,0:T(8,128)S(1)}, f32[1,8,768]{2,1,0:T(8,128)S(1)}, u32[]{:S(2)}, u32[]{:S(2)}) %collective-permute-start.9) | collective-permute-done | bytes 24608 | tf_op jit(solution)/shard_map/ppermute | solution.py:263
  48.9 0.0 collective-permute-done.3.theirs_ref
  48.9 1.4 %shard_map.58 = f32[128,4,128]{2,1,0:T(4,128)} custom-call(f32[4,256,128]{2,1,0:T(8,128)S(1)} %get-tuple-element.12.mine_ref, f32[4,256,128]{2,1,0:T(8,128)S(1)} %collective-permute-done.3.theirs_ref, f32[1,8,768]{2,1,0:T(8,128)S(1)} %get-tuple-element.15.rest_0_, f32[1,8,768]{2,1,0:T(8,128)S(1)} %collective-permute-done.4.rest_1_, ...), custom_call_target="tpu_custom_call" | custom-call | tf_op jit(solution)/shard_map/pallas_call | solution.py:265
Async XLA Ops:
  2.4 5.8 %copy-start = (s32[256,512]{1,0:T(8,128)S(1)}, s32[256,512]{1,0:T(8,128)}, u32[]{:S(2)}) copy-start(s32[256,512]{1,0:T(8,128)} %phase_ref.3) | copy-start | bytes 1572868
  2.5 14.2 %collective-permute-start = (bf16[1,256,512]{2,1,0:T(8,128)(2,1)S(1)}, bf16[1,256,512]{2,1,0:T(8,128)(2,1)S(1)}, u32[]{:S(2)}, u32[]{:S(2)}) collective-permute-start(bf16[1,256,512]{2,1,0:T(8,128)(2,1)S(1)} %get-tuple-element.21), channel_id=1, source_target_pairs={{0,4},{4,0},{8,12},{12,8},{1,5},{5,1},{9,13},{13,9},{2,6},{6,2},{1... | collective-permute-start | bytes 786440 | tf_op jit(solution)/shard_map/ppermute | solution.py:211
  5.6 21.4 %collective-permute-start.1 = (bf16[1,256,512]{2,1,0:T(8,128)(2,1)S(1)}, bf16[1,256,512]{2,1,0:T(8,128)(2,1)S(1)}, u32[]{:S(2)}, u32[]{:S(2)}) collective-permute-start(bf16[1,256,512]{2,1,0:T(8,128)(2,1)S(1)} %get-tuple-element.20), channel_id=1, source_target_pairs={{0,8},{4,12},{8,0},{12,4},{1,9},{5,13},{9,1},{13,5},{2,10},{6,14},... | collective-permute-start | bytes 786440 | tf_op jit(solution)/shard_map/ppermute | solution.py:211
  8.2 18.8 %collective-permute-start.2 = (bf16[1,256,512]{2,1,0:T(8,128)(2,1)S(1)}, bf16[1,256,512]{2,1,0:T(8,128)(2,1)S(1)}, u32[]{:S(2)}, u32[]{:S(2)}) collective-permute-start(bf16[1,256,512]{2,1,0:T(8,128)(2,1)S(1)} %get-tuple-element.19), channel_id=1, source_target_pairs={{0,12},{4,8},{8,4},{12,0},{1,13},{5,9},{9,5},{13,1},{2,14},{6,10},... | collective-permute-start | bytes 786440 | tf_op jit(solution)/shard_map/ppermute | solution.py:211
  9.3 17.7 %copy-start.1 = (f32[1,4,2,8,512]{4,3,2,1,0:T(8,128)S(1)}, f32[1,4,2,8,512]{4,3,2,1,0:T(8,128)}, u32[]{:S(2)}) copy-start(f32[1,4,2,8,512]{4,3,2,1,0:T(8,128)} %start_ref.1) | copy-start | bytes 393220
  27.0 0.7 %copy-start.2 = (s32[4]{0:T(128)S(1)}, s32[4]{0:T(128)}, u32[]{:S(2)}) copy-start(s32[4]{0:T(128)} %flags_ref.1) | copy-start | bytes 52
  27.0 0.7 %copy-start.3 = (s32[4]{0:T(128)S(1)}, s32[4]{0:T(128)}, u32[]{:S(2)}) copy-start(s32[4]{0:T(128)} %ranks_ref.1) | copy-start | bytes 52
  36.5 12.4 %collective-permute-start.3 = (f32[4,256,128]{2,1,0:T(8,128)S(1)}, f32[4,256,128]{2,1,0:T(8,128)S(1)}, u32[]{:S(2)}, u32[]{:S(2)}) collective-permute-start(f32[4,256,128]{2,1,0:T(8,128)S(1)} %get-tuple-element.14), channel_id=1, source_target_pairs={{0,1},{1,0},{2,3},{3,2},{4,5},{5,4},{6,7},{7,6},{8,9},{9,8},{10,11... | collective-permute-start | bytes 1572872 | tf_op jit(solution)/shard_map/ppermute | solution.py:259
  36.6 6.4 %collective-permute-start.6 = (f32[1,8,768]{2,1,0:T(8,128)S(1)}, f32[1,8,768]{2,1,0:T(8,128)S(1)}, u32[]{:S(2)}, u32[]{:S(2)}) collective-permute-start(f32[1,8,768]{2,1,0:T(8,128)S(1)} %get-tuple-element.18), channel_id=1, source_target_pairs={{0,12},{4,8},{8,4},{12,0},{1,13},{5,9},{9,5},{13,1},{2,14},{6,10},... | collective-permute-start | bytes 73736 | tf_op jit(solution)/shard_map/ppermute | solution.py:262
  39.1 5.7 %collective-permute-start.4 = (f32[1,8,768]{2,1,0:T(8,128)S(1)}, f32[1,8,768]{2,1,0:T(8,128)S(1)}, u32[]{:S(2)}, u32[]{:S(2)}) collective-permute-start(f32[1,8,768]{2,1,0:T(8,128)S(1)} %get-tuple-element.16), channel_id=1, source_target_pairs={{0,4},{4,0},{8,12},{12,8},{1,5},{5,1},{9,13},{13,9},{2,6},{6,2},{1... | collective-permute-start | bytes 73736 | tf_op jit(solution)/shard_map/ppermute | solution.py:262
  43.0 4.7 %collective-permute-start.5 = (f32[1,8,768]{2,1,0:T(8,128)S(1)}, f32[1,8,768]{2,1,0:T(8,128)S(1)}, u32[]{:S(2)}, u32[]{:S(2)}) collective-permute-start(f32[1,8,768]{2,1,0:T(8,128)S(1)} %get-tuple-element.17), channel_id=1, source_target_pairs={{0,8},{4,12},{8,0},{12,4},{1,9},{5,13},{9,1},{13,5},{2,10},{6,14},... | collective-permute-start | bytes 73736 | tf_op jit(solution)/shard_map/ppermute | solution.py:262
  43.0 4.7 %collective-permute-start.7 = (f32[1,8,768]{2,1,0:T(8,128)S(1)}, f32[1,8,768]{2,1,0:T(8,128)S(1)}, u32[]{:S(2)}, u32[]{:S(2)}) collective-permute-start(f32[1,8,768]{2,1,0:T(8,128)S(1)} %get-tuple-element.15.rest_0_), channel_id=1, source_target_pairs={{0,1},{1,0},{2,3},{3,2},{4,5},{5,4},{6,7},{7,6},{8,9},{9,8},{10,11... | collective-permute-start | bytes 73736 | tf_op jit(solution)/shard_map/ppermute | solution.py:263
  43.0 4.7 %collective-permute-start.10 = (f32[1,8,768]{2,1,0:T(8,128)S(1)}, f32[1,8,768]{2,1,0:T(8,128)S(1)}, u32[]{:S(2)}, u32[]{:S(2)}) collective-permute-start(f32[1,8,768]{2,1,0:T(8,128)S(1)} %collective-permute-done.6.rest_3_), channel_id=1, source_target_pairs={{0,1},{1,0},{2,3},{3,2},{4,5},{5,4},{6,7},{7,6},{8,9},{9,8},{10,11... | collective-permute-start | bytes 73736 | tf_op jit(solution)/shard_map/ppermute | solution.py:263
  44.8 2.9 %collective-permute-start.8 = (f32[1,8,768]{2,1,0:T(8,128)S(1)}, f32[1,8,768]{2,1,0:T(8,128)S(1)}, u32[]{:S(2)}, u32[]{:S(2)}) collective-permute-start(f32[1,8,768]{2,1,0:T(8,128)S(1)} %collective-permute-done.4.rest_1_), channel_id=1, source_target_pairs={{0,1},{1,0},{2,3},{3,2},{4,5},{5,4},{6,7},{7,6},{8,9},{9,8},{10,11... | collective-permute-start | bytes 73736 | tf_op jit(solution)/shard_map/ppermute | solution.py:263
  47.7 1.2 %collective-permute-start.9 = (f32[1,8,768]{2,1,0:T(8,128)S(1)}, f32[1,8,768]{2,1,0:T(8,128)S(1)}, u32[]{:S(2)}, u32[]{:S(2)}) collective-permute-start(f32[1,8,768]{2,1,0:T(8,128)S(1)} %collective-permute-done.5.rest_2_), channel_id=1, source_target_pairs={{0,1},{1,0},{2,3},{3,2},{4,5},{5,4},{6,7},{7,6},{8,9},{9,8},{10,11... | collective-permute-start | bytes 73736 | tf_op jit(solution)/shard_map/ppermute | solution.py:263

commit v3 on v2

v3 whole, which is shorter than its diff:
```python
import functools

import jax
import jax.numpy as jnp
from jax import lax
from jax.experimental import pallas as pl
from jax.experimental.pallas import tpu as pltpu
from jax.sharding import PartitionSpec as P

ITERS = 4
PHASES = 1024
QUARTER = PHASES // 4
EPS = 1e-06
F32 = jnp.float32
BF16 = jnp.bfloat16
NT = (((1,), (1,)), ((), ()))
NN = (((1,), (0,)), ((), ()))
TN = (((0,), (0,)), ((), ()))
VMEM_LIMIT = 48 * 1024 * 1024


def dot(left, right, dims):
    return lax.dot_general(left, right, dims, preferred_element_type=F32)


def split(values):
    high = values.astype(BF16)
    low = (values - high.astype(F32)).astype(BF16)
    return high, low


def steer(phase, step, norm):
    turn = (phase * step) & (PHASES - 1)
    quadrant = (turn + QUARTER // 2) // QUARTER
    angle = (turn - quadrant * QUARTER).astype(F32) * (2.0 * jnp.pi / PHASES)
    sq = angle * angle
    sine = angle * (1.0 + sq * (-1.0 / 6 + sq * (1.0 / 120 + sq * (-1.0 / 5040 + sq / 362880))))
    cosine = 1.0 + sq * (-0.5 + sq * (1.0 / 24 + sq * (-1.0 / 720 + sq / 40320)))
    odd = (quadrant & 1) == 1
    real = jnp.where(odd, sine, cosine) * norm
    imag = jnp.where(odd, cosine, sine) * norm
    real = jnp.where(((quadrant + 1) & 2) == 2, -real, real)
    imag = jnp.where((quadrant & 2) == 2, -imag, imag)
    return real.astype(BF16), imag.astype(BF16)


def fill_weights(phase_ref, first, rows, step, out):
    norm = 1.0 / (phase_ref.shape[1] ** 0.5)
    chunk = 32

    def body(i, carry):
        at = pl.multiple_of(i * chunk, chunk)
        real, imag = steer(phase_ref[pl.ds(first + at, chunk), :], step, norm)
        out[pl.ds(at, chunk), :] = real
        out[pl.ds(rows + at, chunk), :] = imag
        return carry

    lax.fori_loop(0, rows // chunk, body, 0)


def shifts(tm, pol):
    first = [*range(2, tm), 1]
    second = [1, *range(2, tm)]
    return [0] + [jnp.where(pol == 0, a, b) for a, b in zip(first, second)]


def routes(tm):
    first = [*range(2, tm), 1]
    second = [1, *range(2, tm)]
    return [
        [(2 * z + p, 2 * (z ^ x[p]) + p) for z in range(tm) for p in range(2)]
        for x in zip(first, second)
    ]


def own_weights_kernel(own, chan_dev, phase_ref, beams_ref, out_ref, beams_out_ref):
    beams = phase_ref.shape[0]
    first = lax.axis_index("chan") * chan_dev + lax.axis_index("tm") * own
    for o in range(own):
        fill_weights(phase_ref, 0, beams, first + o + 1, out_ref.at[o])


def turned(values, axis):
    size = values.shape[axis]
    at = lax.broadcasted_iota(jnp.int32, values.shape, axis)
    after = pltpu.roll(values, size - 1, axis)
    before = pltpu.roll(values, 1, axis)
    return jnp.where((at & 1) == 0, after, -before)


def raw_beams_kernel(tm, own, phase_ref, *rest):
    pieces, (mine_ref, other_ref, weights) = rest[:tm], rest[tm:]
    half = phase_ref.shape[0] // 2
    rows = pieces[0].shape[1]
    pol = lax.axis_index("pol")
    start = lax.axis_index("chan") * tm * own
    for x, piece in zip(shifts(tm, pol), pieces):
        for o in range(own):
            chan = (lax.axis_index("tm") ^ x) * own + o
            for swap, out_ref in enumerate((mine_ref, other_ref)):
                first = pl.multiple_of((pol ^ swap) * half, half)
                fill_weights(phase_ref, first, half, start + chan + 1, weights)
                product = dot(piece[o], weights[...], NT)
                by_imag = turned(product[:, half:].reshape(rows // 8, 8, half), 1).reshape(rows, half)
                out_ref[chan] = product[:, :half] - by_imag


def cov_terms(x):
    rotated = -turned(x.astype(F32), 0)
    return dot(x, x, TN), dot(x, rotated.astype(BF16), TN)


def cov_kernel(*refs):
    blocks, out_ref = refs[:-1], refs[-1]
    for o in range(out_ref.shape[0]):
        for i, ref in enumerate(blocks):
            real, imag = cov_terms(ref[o])
            out_ref[o, 0] = real if i == 0 else out_ref[o, 0] + real
            out_ref[o, 1] = imag if i == 0 else out_ref[o, 1] + imag


def correlate(real, imag, x):
    vectors = real.shape[0]
    rows = jnp.concatenate([real, imag], axis=0)
    product = dot(jnp.concatenate(split(rows), axis=0), x, NT)
    product = product[: 2 * vectors] + product[2 * vectors :]
    return product[:vectors] + turned(product[vectors:], 1)


def cov_times(real, imag, high_ref, low_ref):
    vectors = real.shape[0]
    rows = jnp.concatenate(
        [jnp.concatenate([real, imag], axis=1), jnp.concatenate([imag, -real], axis=1)], axis=0
    )
    high, low = split(rows)
    product = dot(jnp.concatenate([high, low], axis=0), high_ref[...], NN)
    product = product[: 2 * vectors] + product[2 * vectors :] + dot(high, low_ref[...], NN)
    return product[:vectors], product[vectors:]


def orthonormalize(real_z, imag_z):
    vectors = real_z.shape[0]
    row = lax.broadcasted_iota(jnp.int32, real_z.shape, 0)
    real_v, imag_v = real_z, imag_z
    scale = jnp.zeros((vectors, 1), F32)
    for n in range(vectors):
        here = row == n
        real_a, imag_a = real_v[n : n + 1], imag_v[n : n + 1]
        real_z = jnp.where(here, real_v, real_z)
        imag_z = jnp.where(here, imag_v, imag_z)
        real_d = jnp.sum(real_a * real_z + imag_a * imag_z, axis=1, keepdims=True)
        norm = real_d[n : n + 1] + EPS
        scale = jnp.where(row[:, :1] == n, norm, scale)
        if n + 1 < vectors:
            imag_d = jnp.sum(real_a * imag_z - imag_a * real_z, axis=1, keepdims=True)
            inverse = 1.0 / norm
            later = row[:, :1] > n
            real_c = jnp.where(later, real_d * inverse, 0.0)
            imag_c = jnp.where(later, imag_d * inverse, 0.0)
            real_v = real_v - (real_c * real_a - imag_c * imag_a)
            imag_v = imag_v - (real_c * imag_a + imag_c * real_a)
    factor = 1.0 / jnp.sqrt(scale)
    return real_v * factor, imag_v * factor


def subspace_kernel(tm, own, factor, start_ref, flags_ref, ranks_ref, weights_ref, cov_ref, *rest):
    blocks, (out_ref, high_ref, low_ref) = rest[:tm], rest[tm:]
    vectors, width = start_ref.shape[3], start_ref.shape[4]
    rows = blocks[0].shape[1]
    tm_index = lax.axis_index("tm")
    beams = weights_ref.shape[1] // 2
    half = beams // 2
    for o in range(own):
        chan = tm_index * own + o
        for part, term in enumerate(cov_terms(blocks[-1][o])):
            high, low = split((cov_ref[o, part] + term) * factor)
            high_ref[part * width : (part + 1) * width] = high
            low_ref[part * width : (part + 1) * width] = low
        real_q = start_ref[0, chan, 0]
        imag_q = start_ref[0, chan, 1]
        for sweep in range(ITERS):
            real_z, imag_z = cov_times(real_q, imag_q, high_ref, low_ref)
            real_q, imag_q = orthonormalize(real_z, imag_z)
        rank = flags_ref[chan] * ranks_ref[chan]
        keep = lax.broadcasted_iota(jnp.int32, (vectors, width), 0) < rank
        real_u = jnp.where(keep, real_q, 0.0)
        imag_u = jnp.where(keep, imag_q, 0.0)
        both = jnp.concatenate([real_u, imag_u], axis=0)
        product = dot(jnp.concatenate(split(both), axis=0), weights_ref[o], NT)
        product = product[: 2 * vectors] + product[2 * vectors :]
        real_w = product[:vectors, :beams] - product[vectors:, beams:]
        imag_w = product[:vectors, beams:] + product[vectors:, :beams]
        for x, block in zip(shifts(tm, lax.axis_index("pol")), blocks):
            series = correlate(real_u, imag_u, block[o])
            for core in range(2):
                to = (tm_index ^ x) * 2 + core
                out_ref[to, o, :, :rows] = series
                out_ref[to, o, :, rows : rows + half] = real_w[:, core * half : (core + 1) * half]
                out_ref[to, o, :, rows + half :] = imag_w[:, core * half : (core + 1) * half]


def finish_kernel(tm, own, mine_ref, theirs_ref, arrived_ref, out_ref, squares, powers):
    rows, half = mine_ref.shape[1], mine_ref.shape[2]
    samples = rows // 2
    pol = lax.axis_index("pol")
    for chan in range(tm * own):
        total = None
        for swap, raw_ref in enumerate((mine_ref, theirs_ref)):
            packet = arrived_ref[chan // own * 2 + (pol ^ swap), chan % own]
            series = packet[:, :rows]
            left = jnp.concatenate([series, -turned(series, 1)], axis=0)
            right = jnp.concatenate([packet[:, rows : rows + half], packet[:, rows + half :]], axis=0)
            high_s, low_s = split(left)
            high_w, low_w = split(right)
            left = jnp.concatenate([high_s, high_s, low_s], axis=0)
            right = jnp.concatenate([high_w, low_w, high_w], axis=0)
            beam = raw_ref[chan] - dot(left, right, TN)
            total = beam * beam if total is None else total + beam * beam
        squares[...] = total
        powers[chan] = squares[pl.ds(0, samples, 2), :] + squares[pl.ds(1, samples, 2), :]
    for chan in range(powers.shape[0]):
        out_ref[:, chan, :] = powers[chan]


def local(voltages, start_block, flags, ranks, phase_index):
    tm = lax.axis_size("tm")
    tm_index = lax.axis_index("tm")
    samples, chan_dev, width = voltages.shape[0], voltages.shape[2], voltages.shape[4]
    own = chan_dev // tm
    vectors = start_block.shape[3]
    beams = phase_index.shape[0]
    half = beams // 2
    rows = 2 * samples
    factor = 1.0 / (samples * tm)
    params = pltpu.CompilerParams(vmem_limit_bytes=VMEM_LIMIT)
    whole = pl.BlockSpec(memory_space=pltpu.VMEM)
    scalars = pl.BlockSpec(memory_space=pltpu.SMEM)
    unread = pl.BlockSpec(memory_space=pl.ANY)

    def cost(multiplies, moved):
        return pl.CostEstimate(flops=2 * multiplies, bytes_accessed=moved, transcendentals=0)

    pieces = [
        lax.dynamic_slice_in_dim(voltages[:, 0], (tm_index ^ x) * own, own, 1)
        .transpose(1, 0, 2, 3)
        .reshape(own, rows, width)
        for x in shifts(tm, lax.axis_index("pol"))
    ]
    blocks = pieces[:1] + [
        lax.ppermute(piece, ("tm", "pol"), route) for piece, route in zip(pieces[1:], routes(tm))
    ]

    raw = jax.ShapeDtypeStruct((chan_dev, rows, half), F32)
    mine, other = pl.pallas_call(
        functools.partial(raw_beams_kernel, tm, own),
        out_shape=[raw] * 2,
        in_specs=[whole] * (1 + tm),
        out_specs=[whole] * 2,
        scratch_shapes=[pltpu.VMEM((beams, width), BF16)],
        compiler_params=params,
        cost_estimate=cost(4 * chan_dev * samples * width * beams, 8 * chan_dev * samples * width),
    )(phase_index, *pieces)

    own_weights, other = pl.pallas_call(
        functools.partial(own_weights_kernel, own, chan_dev),
        out_shape=[jax.ShapeDtypeStruct((own, 2 * beams, width), BF16), raw],
        in_specs=[whole, unread],
        out_specs=[whole, unread],
        input_output_aliases={1: 1},
        compiler_params=params,
        cost_estimate=cost(20 * own * beams * width, 8 * own * beams * width),
    )(phase_index, other)
    theirs = lax.ppermute(other, "pol", [(0, 1), (1, 0)])

    cov = pl.pallas_call(
        cov_kernel,
        out_shape=jax.ShapeDtypeStruct((own, 2, width, width), F32),
        in_specs=[whole] * (tm - 1),
        out_specs=whole,
        compiler_params=params,
        cost_estimate=cost(4 * (tm - 1) * own * samples * width * width, 8 * own * width * width),
    )(*blocks[:-1])

    packets = pl.pallas_call(
        functools.partial(subspace_kernel, tm, own, factor),
        out_shape=jax.ShapeDtypeStruct((2 * tm, own, vectors, rows + beams), F32),
        in_specs=[whole, scalars, scalars, whole, whole] + [whole] * tm,
        out_specs=whole,
        scratch_shapes=[pltpu.VMEM((2 * width, width), BF16)] * 2,
        compiler_params=params,
        cost_estimate=cost(32 * own * vectors * tm * samples * width, 8 * own * width * width),
    )(start_block, flags, ranks, own_weights, cov, *blocks)
    arrived = lax.all_to_all(packets, ("tm", "pol"), split_axis=0, concat_axis=0, tiled=True)

    return pl.pallas_call(
        functools.partial(finish_kernel, tm, own),
        out_shape=jax.ShapeDtypeStruct((samples, chan_dev, half), F32),
        in_specs=[whole] * 3,
        out_specs=whole,
        scratch_shapes=[
            pltpu.VMEM((rows, half), F32),
            pltpu.VMEM((chan_dev, samples, half), F32),
        ],
        compiler_params=params,
    )(mine, theirs, arrived)


def solution(mesh):
    placed = (
        P(("groups", "tm"), "pol", "chan", None, None),
        P("pol", "chan", None, None, None),
        P(("groups", "chan")),
        P(("groups", "chan")),
        P(),
    )
    return jax.shard_map(
        local,
        mesh=mesh,
        in_specs=placed,
        out_specs=P(("groups", "tm"), "chan", "pol"),
        check_vma=False,
    )
```

time: 50.4 us -> 49.6 us (0.984)
  blocking collectives: 0 us -> 11.4 us
  starting transfers between devices: 12.7 us -> 5.89 us
  waiting for transfers between devices: 16.2 us -> 13.1 us
  Pallas kernels: 18.1 us -> 16.5 us
  local copies, waits for them, and re-layouts: 3.17 us -> 2.43 us
    all_to_all x0 -> x1, blocking collectives: none -> 11.4 us  [local(): lax.all_to_all(packets, ('tm', 'pol'), split_axis=0, concat_axis=0, tiled...]
    ppermute x11 -> x4, starting transfers between devices: 12.7 us -> 5.89 us  [the longest x3 5.81 us: local(): lax.ppermute(piece, ('tm', 'pol'), route)]
    ppermute x11 -> x4, waiting for transfers between devices: 16.2 us -> 13.1 us  [the longest x3 13.1 us: local(): lax.ppermute(piece, ('tm', 'pol'), route)]
    pallas_call x1, Pallas kernels: 8.8 us -> 6.29 us  [local(): pl.pallas_call(functools.partial(subspace_kernel, tm, own, factor), out_s...]
    transpose x1 -> x0, local copies, waits for them, and re-layouts: 1.94 us -> none  [local(): series = voltages[:, 0].transpose(1, 0, 2, 3).reshape(chan_dev, rows, width)]
    dynamic_slice x1, local copies, waits for them, and re-layouts: 0.1 us -> 1.99 us  [local(): lax.dynamic_slice_in_dim(voltages[:, 0], (tm_index ^ x) * own, own, 1)]
    pallas_call x1 -> x2, Pallas kernels: 6.93 us -> 7.89 us  [the longest x1 6.84 us: local(): pl.pallas_call(functools.partial(raw_beams_kernel, tm, own), out_shape=[r...]
    unnamed x8, local copies, waits for them, and re-layouts: 0.68 us -> 0.02 us
  transfers between devices with their start and end apart: 11 -> 4, of which waited for: 5 -> 1; matrix products, arithmetic and copies ran while one was open for 0% -> 1% of each run, Pallas kernels for 16% -> 31%
where the time goes in v3:
time: 49.6 us; the launch traced here: 49.4 us
  Pallas kernels  16.5 us (33%)
  waiting for transfers between devices  13.1 us (26%)
  blocking collectives  11.4 us (23%)
  starting transfers between devices  5.89 us (12%)
  local copies, waits for them, and re-layouts  2.43 us (5%)
    ppermute x3, waiting for transfers between devices, local(): lax.ppermute(piece, ('tm', 'pol'), route)  13.1 us
    all_to_all x1, blocking collectives, local(): lax.all_to_all(packets, ('tm', 'pol'), split_axis=0, concat_axis=0, tiled...  11.4 us
    pallas_call x1, Pallas kernels, local(): pl.pallas_call(functools.partial(raw_beams_kernel, tm, own), out_shape=[r...  6.84 us
    pallas_call x1, Pallas kernels, local(): pl.pallas_call(functools.partial(subspace_kernel, tm, own, factor), out_s...  6.29 us
    ppermute x3, starting transfers between devices, local(): lax.ppermute(piece, ('tm', 'pol'), route)  5.81 us
    dynamic_slice x1, local copies, waits for them, and re-layouts, local(): lax.dynamic_slice_in_dim(voltages[:, 0], (tm_index ^ x) * own, own, 1)  1.99 us
    pallas_call x1, Pallas kernels, local(): pl.pallas_call(functools.partial(finish_kernel, tm, own), out_shape=jax.S...  1.27 us
    pallas_call x1, Pallas kernels, local(): pl.pallas_call(functools.partial(own_weights_kernel, own, chan_dev), out_...  1.08 us
  transfers between devices with their start and end apart: 4, of which 1 were waited for; matrix products, arithmetic and copies ran while one was open for 1% of the time, Pallas kernels for 31%

profile of v3, /device:TPU:0, one launch (start us, length us, event | category | flops | bytes accessed | tf_op | source)
XLA Modules:
  0.0 49.4 jit_solution(10472035815881821002)
XLA Ops:
  0.0 0.0 copy-start
  0.0 2.0 %constant_dynamic-slice_fusion = (bf16[128,1,1,2,512]{4,3,2,1,0:T(2,128)(2,1)S(1)}, bf16[128,1,1,2,512]{4,3,2,1,0:T(2,128)(2,1)S(1)}, bf16[128,1,1,2,512]{4,3,2,...) fusion(bf16[128,1,4,2,512]{4,3,2,1,0:T(2,128)(2,1)} %param.5, s32[]{:T(128)S(6)} %select_n.28, s32[]{:T(128)S(6)} %select_n.24, ...), kind=kLoop, calls=%fused_computation | loop fusion | bytes 2097168 | tf_op jit(solution)/shard_map/dynamic_slice | solution.py:244
  2.0 0.1 reshape_transpose.14.rest_2_
  2.1 5.1 %collective-permute-start.2 = (bf16[1,256,512]{2,1,0:T(8,128)(2,1)S(1)}, bf16[1,256,512]{2,1,0:T(8,128)(2,1)S(1)}, u32[]{:S(2)}, u32[]{:S(2)}) collective-permute-start(bf16[1,256,512]{2,1,0:T(8,128)(2,1)S(1)} %reshape_transpose.14.rest_2_), channel_id=1, source_target_pairs={{0,12},{1,9},{4,8},{5,13},{8,4},{9,1},{12,0},{13,5},{2,14},{3,11},... | collective-permute-start | bytes 786440 | tf_op jit(solution)/shard_map/ppermute | solution.py:250
  7.2 0.1 reshape_transpose.13.rest_1_
  7.3 0.1 collective-permute-start.1
  7.4 0.1 reshape_transpose.15.rest_3_
  7.5 0.1 reshape_transpose.12.rest_0_.refs_0_
  7.6 0.0 copy-done
  7.6 6.8 %shard_map.55 = (f32[4,256,128]{2,1,0:T(8,128)S(1)}, f32[4,256,128]{2,1,0:T(8,128)S(1)}) custom-call(s32[256,512]{1,0:T(8,128)S(1)} %copy-done, bf16[1,256,512]{2,1,0:T(8,128)(2,1)S(1)} %reshape_transpose.12.rest_0_.refs_0_, bf16[1,256,512]{2,1,0:T(8,128)(2,1)S(1)} %reshape_transpose.13.rest_1_, bf16[1,256,512]{2,1,0:T(8,128)(2,1)S(1)} %reshape_transpose.14.rest_2_, ...), custom_call_target="tpu_custom_call" | custom-call | flops 536870912 | bytes 2097152 | tf_op jit(solution)/shard_map/pallas_call | solution.py:254
  14.5 0.0 copy-start.1
  14.5 0.0 copy-start.2
  14.5 0.0 copy-start.3
  14.5 1.1 %shard_map.56 = (bf16[1,512,512]{2,1,0:T(8,128)(2,1)S(1)}, f32[4,256,128]{2,1,0:T(8,128)S(1)}) custom-call(s32[256,512]{1,0:T(8,128)S(1)} %copy-done, f32[4,256,128]{2,1,0:T(8,128)S(1)} %get-tuple-element.10.beams_ref), custom_call_target="tpu_custom_call", output_to_operand_aliasing={{1}: (1, {})} | custom-call | flops 5242880 | bytes 1048576 | tf_op jit(solution)/shard_map/pallas_call | solution.py:264
  15.6 0.1 collective-permute-start
  15.7 0.6 %collective-permute-start.3 = (bf16[1,256,512]{2,1,0:T(8,128)(2,1)S(1)}, bf16[1,256,512]{2,1,0:T(8,128)(2,1)S(1)}, u32[]{:S(2)}, u32[]{:S(2)}) collective-permute-start(bf16[1,256,512]{2,1,0:T(8,128)(2,1)S(1)} %reshape_transpose.15.rest_3_), channel_id=1, source_target_pairs={{0,4},{1,13},{4,0},{5,9},{8,12},{9,5},{12,8},{13,1},{2,6},{3,15},{... | collective-permute-start | bytes 786440 | tf_op jit(solution)/shard_map/ppermute | solution.py:250
  16.3 0.0 collective-permute-done.2.refs_2_.rest_2_
  16.3 13.1 %collective-permute-done.1.refs_1_.rest_1_ = bf16[1,256,512]{2,1,0:T(8,128)(2,1)S(1)} collective-permute-done((bf16[1,256,512]{2,1,0:T(8,128)(2,1)S(1)}, bf16[1,256,512]{2,1,0:T(8,128)(2,1)S(1)}, u32[]{:S(2)}, u32[]{:S(2)}) %collective-permute-start.1) | collective-permute-done | bytes 262176 | tf_op jit(solution)/shard_map/ppermute | solution.py:250
  29.4 1.0 %shard_map.57.cov_ref = f32[1,2,512,512]{3,2,1,0:T(8,128)S(1)} custom-call(bf16[1,256,512]{2,1,0:T(8,128)(2,1)S(1)} %reshape_transpose.12.rest_0_.refs_0_, bf16[1,256,512]{2,1,0:T(8,128)(2,1)S(1)} %collective-permute-done.1.refs_1_.rest_1_, bf16[1,256,512]{2,1,0:T(8,128)(2,1)S(1)} %collective-permute-done.2.refs_2_.rest_2_), custom_call_target="tpu_custom_call" | custom-call | flops 805306368 | bytes 2097152 | tf_op jit(solution)/shard_map/pallas_call | solution.py:275
  30.4 0.0 collective-permute-done.3.rest_3_
  30.4 0.0 copy-done.1
  30.4 0.0 copy-done.2
  30.4 0.0 copy-done.3
  30.5 6.3 %shard_map.58 = f32[8,1,8,512]{3,2,1,0:T(8,128)S(1)} custom-call(f32[1,4,2,8,512]{4,3,2,1,0:T(8,128)S(1)} %copy-done.1, s32[4]{0:T(128)S(1)} %copy-done.2, s32[4]{0:T(128)S(1)} %copy-done.3, bf16[1,512,512]{2,1,0:T(8,128)(2,1)S(1)} %get-tuple-element.12.weights_ref, f32[1,2,512,512]{3,2,1,0:T(8,128)S(1)} %shard_map.57.cov_ref, ...), custom_call_target="tpu_custom_call" | custom-call | flops 134217728 | bytes 2097152 | tf_op jit(solution)/shard_map/pallas_call | solution.py:284
  36.8 11.4 %all_to_all.5.arrived_ref = f32[8,1,8,512]{3,2,1,0:T(8,128)S(1)} all-to-all(f32[8,1,8,512]{3,2,1,0:T(8,128)S(1)} %shard_map.58), channel_id=1, replica_groups=mesh['groups'=2,'tm'=4,'chan'=2,'pol'=2] {'tm','pol'}, dimensions={0} | all-to-all | bytes 262144 | tf_op jit(solution)/shard_map/all_to_all | solution.py:293
  48.1 0.0 collective-permute-done.theirs_ref
  48.1 1.3 %shard_map.59 = f32[128,4,128]{2,1,0:T(4,128)} custom-call(f32[4,256,128]{2,1,0:T(8,128)S(1)} %get-tuple-element.9.mine_ref, f32[4,256,128]{2,1,0:T(8,128)S(1)} %collective-permute-done.theirs_ref, f32[8,1,8,512]{3,2,1,0:T(8,128)S(1)} %all_to_all.5.arrived_ref), custom_call_target="tpu_custom_call" | custom-call | tf_op jit(solution)/shard_map/pallas_call | solution.py:295
Async XLA Ops:
  0.0 7.6 %copy-start = (s32[256,512]{1,0:T(8,128)S(1)}, s32[256,512]{1,0:T(8,128)}, u32[]{:S(2)}) copy-start(s32[256,512]{1,0:T(8,128)} %phase_ref.3) | copy-start | bytes 1572868
  2.1 14.2 %collective-permute-start.2 = (bf16[1,256,512]{2,1,0:T(8,128)(2,1)S(1)}, bf16[1,256,512]{2,1,0:T(8,128)(2,1)S(1)}, u32[]{:S(2)}, u32[]{:S(2)}) collective-permute-start(bf16[1,256,512]{2,1,0:T(8,128)(2,1)S(1)} %reshape_transpose.14.rest_2_), channel_id=1, source_target_pairs={{0,12},{1,9},{4,8},{5,13},{8,4},{9,1},{12,0},{13,5},{2,14},{3,11},... | collective-permute-start | bytes 786440 | tf_op jit(solution)/shard_map/ppermute | solution.py:250
  7.3 22.0 %collective-permute-start.1 = (bf16[1,256,512]{2,1,0:T(8,128)(2,1)S(1)}, bf16[1,256,512]{2,1,0:T(8,128)(2,1)S(1)}, u32[]{:S(2)}, u32[]{:S(2)}) collective-permute-start(bf16[1,256,512]{2,1,0:T(8,128)(2,1)S(1)} %reshape_transpose.13.rest_1_), channel_id=1, source_target_pairs={{0,8},{1,5},{4,12},{5,1},{8,0},{9,13},{12,4},{13,9},{2,10},{3,7},{... | collective-permute-start | bytes 786440 | tf_op jit(solution)/shard_map/ppermute | solution.py:250
  14.5 15.9 %copy-start.1 = (f32[1,4,2,8,512]{4,3,2,1,0:T(8,128)S(1)}, f32[1,4,2,8,512]{4,3,2,1,0:T(8,128)}, u32[]{:S(2)}) copy-start(f32[1,4,2,8,512]{4,3,2,1,0:T(8,128)} %start_ref.1) | copy-start | bytes 393220
  14.5 15.9 %copy-start.2 = (s32[4]{0:T(128)S(1)}, s32[4]{0:T(128)}, u32[]{:S(2)}) copy-start(s32[4]{0:T(128)} %flags_ref.1) | copy-start | bytes 52
  14.5 15.9 %copy-start.3 = (s32[4]{0:T(128)S(1)}, s32[4]{0:T(128)}, u32[]{:S(2)}) copy-start(s32[4]{0:T(128)} %ranks_ref.1) | copy-start | bytes 52
  15.6 32.5 %collective-permute-start = (f32[4,256,128]{2,1,0:T(8,128)S(1)}, f32[4,256,128]{2,1,0:T(8,128)S(1)}, u32[]{:S(2)}, u32[]{:S(2)}) collective-permute-start(f32[4,256,128]{2,1,0:T(8,128)S(1)} %get-tuple-element.11), channel_id=1, source_target_pairs={{0,1},{1,0},{2,3},{3,2},{4,5},{5,4},{6,7},{7,6},{8,9},{9,8},{10,11... | collective-permute-start | bytes 1572872 | tf_op jit(solution)/shard_map/ppermute | solution.py:273
  15.7 14.7 %collective-permute-start.3 = (bf16[1,256,512]{2,1,0:T(8,128)(2,1)S(1)}, bf16[1,256,512]{2,1,0:T(8,128)(2,1)S(1)}, u32[]{:S(2)}, u32[]{:S(2)}) collective-permute-start(bf16[1,256,512]{2,1,0:T(8,128)(2,1)S(1)} %reshape_transpose.15.rest_3_), channel_id=1, source_target_pairs={{0,4},{1,13},{4,0},{5,9},{8,12},{9,5},{12,8},{13,1},{2,6},{3,15},{... | collective-permute-start | bytes 786440 | tf_op jit(solution)/shard_map/ppermute | solution.py:250

commit v4 on v3

--- a/solution.py
+++ b/solution.py
@@ -58,26 +58,32 @@
     lax.fori_loop(0, rows // chunk, body, 0)
 
 
+def orders(tm):
+    far = [*range(2, tm)]
+    return [0, *far[:1], 1, *far[1:]], [0, *far, 1]
+
+
 def shifts(tm, pol):
-    first = [*range(2, tm), 1]
-    second = [1, *range(2, tm)]
-    return [0] + [jnp.where(pol == 0, a, b) for a, b in zip(first, second)]
+    return [jnp.where(pol == 0, a, b) for a, b in zip(*orders(tm))]
 
 
 def routes(tm):
-    first = [*range(2, tm), 1]
-    second = [1, *range(2, tm)]
     return [
         [(2 * z + p, 2 * (z ^ x[p]) + p) for z in range(tm) for p in range(2)]
-        for x in zip(first, second)
+        for x in zip(*orders(tm))
     ]
 
 
-def own_weights_kernel(own, chan_dev, phase_ref, beams_ref, out_ref, beams_out_ref):
-    beams = phase_ref.shape[0]
-    first = lax.axis_index("chan") * chan_dev + lax.axis_index("tm") * own
-    for o in range(own):
-        fill_weights(phase_ref, 0, beams, first + o + 1, out_ref.at[o])
+def cut_kernel(tm, own, voltages_ref, *rest):
+    pieces, done = rest[:tm], rest[tm]
+    copies = []
+    for i, x in enumerate(shifts(tm, lax.axis_index("pol"))):
+        first = (lax.axis_index("tm") ^ x) * own
+        copy = pltpu.make_async_copy(voltages_ref.at[:, 0, pl.ds(first, own)], pieces[i], done.at[i])
+        copy.start()
+        copies.append(copy)
+    for copy in copies:
+        copy.wait()
 
 
 def turned(values, axis):
@@ -110,13 +116,25 @@
     return dot(x, x, TN), dot(x, rotated.astype(BF16), TN)
 
 
-def cov_kernel(*refs):
-    blocks, out_ref = refs[:-1], refs[-1]
-    for o in range(out_ref.shape[0]):
-        for i, ref in enumerate(blocks):
-            real, imag = cov_terms(ref[o])
-            out_ref[o, 0] = real if i == 0 else out_ref[o, 0] + real
-            out_ref[o, 1] = imag if i == 0 else out_ref[o, 1] + imag
+def own_kernel(own, chan_dev, phase_ref, block_ref, weights_ref, cov_ref):
+    beams = phase_ref.shape[0]
+    first = lax.axis_index("chan") * chan_dev + lax.axis_index("tm") * own
+    for o in range(own):
+        fill_weights(phase_ref, 0, beams, first + o + 1, weights_ref.at[o])
+        cov_ref[o, 0], cov_ref[o, 1] = cov_terms(block_ref[o])
+
+
+def cov_kernel(factor, cov_ref, *rest):
+    blocks, (high_ref, low_ref) = rest[:-2], rest[-2:]
+    width = cov_ref.shape[2]
+    for o in range(cov_ref.shape[0]):
+        sums = cov_ref[o, 0], cov_ref[o, 1]
+        for block in blocks:
+            sums = [total + term for total, term in zip(sums, cov_terms(block[o]))]
+        for part, total in enumerate(sums):
+            high, low = split(total * factor)
+            high_ref[o, part * width : (part + 1) * width] = high
+            low_ref[o, part * width : (part + 1) * width] = low
 
 
 def correlate(real, imag, x):
@@ -163,23 +181,18 @@
     return real_v * factor, imag_v * factor
 
 
-def subspace_kernel(tm, own, factor, start_ref, flags_ref, ranks_ref, weights_ref, cov_ref, *rest):
-    blocks, (out_ref, high_ref, low_ref) = rest[:tm], rest[tm:]
+def subspace_kernel(tm, own, beams_ref, start_ref, flags_ref, ranks_ref, weights_ref, high_ref, low_ref, *rest):
+    blocks, outs = rest[:tm], rest[tm + 1 :]
     vectors, width = start_ref.shape[3], start_ref.shape[4]
     rows = blocks[0].shape[1]
     tm_index = lax.axis_index("tm")
     beams = weights_ref.shape[1] // 2
-    half = beams // 2
     for o in range(own):
         chan = tm_index * own + o
-        for part, term in enumerate(cov_terms(blocks[-1][o])):
-            high, low = split((cov_ref[o, part] + term) * factor)
-            high_ref[part * width : (part + 1) * width] = high
-            low_ref[part * width : (part + 1) * width] = low
         real_q = start_ref[0, chan, 0]
         imag_q = start_ref[0, chan, 1]
         for sweep in range(ITERS):
-            real_z, imag_z = cov_times(real_q, imag_q, high_ref, low_ref)
+            real_z, imag_z = cov_times(real_q, imag_q, high_ref.at[o], low_ref.at[o])
             real_q, imag_q = orthonormalize(real_z, imag_z)
         rank = flags_ref[chan] * ranks_ref[chan]
         keep = lax.broadcasted_iota(jnp.int32, (vectors, width), 0) < rank
@@ -190,34 +203,48 @@
         product = product[: 2 * vectors] + product[2 * vectors :]
         real_w = product[:vectors, :beams] - product[vectors:, beams:]
         imag_w = product[:vectors, beams:] + product[vectors:, :beams]
-        for x, block in zip(shifts(tm, lax.axis_index("pol")), blocks):
-            series = correlate(real_u, imag_u, block[o])
-            for core in range(2):
-                to = (tm_index ^ x) * 2 + core
-                out_ref[to, o, :, :rows] = series
-                out_ref[to, o, :, rows : rows + half] = real_w[:, core * half : (core + 1) * half]
-                out_ref[to, o, :, rows + half :] = imag_w[:, core * half : (core + 1) * half]
-
-
-def finish_kernel(tm, own, mine_ref, theirs_ref, arrived_ref, out_ref, squares, powers):
-    rows, half = mine_ref.shape[1], mine_ref.shape[2]
-    samples = rows // 2
-    pol = lax.axis_index("pol")
-    for chan in range(tm * own):
-        total = None
-        for swap, raw_ref in enumerate((mine_ref, theirs_ref)):
-            packet = arrived_ref[chan // own * 2 + (pol ^ swap), chan % own]
-            series = packet[:, :rows]
-            left = jnp.concatenate([series, -turned(series, 1)], axis=0)
-            right = jnp.concatenate([packet[:, rows : rows + half], packet[:, rows + half :]], axis=0)
-            high_s, low_s = split(left)
-            high_w, low_w = split(right)
-            left = jnp.concatenate([high_s, high_s, low_s], axis=0)
-            right = jnp.concatenate([high_w, low_w, high_w], axis=0)
-            beam = raw_ref[chan] - dot(left, right, TN)
-            total = beam * beam if total is None else total + beam * beam
-        squares[...] = total
-        powers[chan] = squares[pl.ds(0, samples, 2), :] + squares[pl.ds(1, samples, 2), :]
+        series = [correlate(real_u, imag_u, block[o]) for block in blocks]
+        first, second = orders(tm)
+        for x, out in enumerate(outs):
+            a, b = first.index(x), second.index(x)
+            out[o, :, :rows] = jnp.where(lax.axis_index("pol") == 0, series[a], series[b])
+            out[o, :, rows : rows + beams] = real_w
+            out[o, :, rows + beams :] = imag_w
+
+
+def nulled_squares(raw, packet_ref):
+    rows, half = raw.shape
+    at = pl.multiple_of(rows + lax.axis_index("pol") * half, half)
+    series = packet_ref[:, :rows]
+    left = jnp.concatenate([series, -turned(series, 1)], axis=0)
+    right = jnp.concatenate(
+        [packet_ref[:, pl.ds(at, half)], packet_ref[:, pl.ds(pl.multiple_of(at + 2 * half, half), half)]],
+        axis=0,
+    )
+    high_s, low_s = split(left)
+    high_w, low_w = split(right)
+    left = jnp.concatenate([high_s, high_s, low_s], axis=0)
+    right = jnp.concatenate([high_w, low_w, high_w], axis=0)
+    beam = raw - dot(left, right, TN)
+    return beam * beam
+
+
+def first_kernel(own, raw_ref, *rest):
+    packets, out_ref = rest[:-1], rest[-1]
+    for x, ref in enumerate(packets):
+        for o in range(own):
+            chan = (lax.axis_index("tm") ^ x) * own + o
+            out_ref[chan] = nulled_squares(raw_ref[chan], ref.at[o])
+
+
+def second_kernel(own, first_ref, raw_ref, *rest):
+    packets, (out_ref, squares, powers) = rest[:-3], rest[-3:]
+    samples = out_ref.shape[0]
+    for x, ref in enumerate(packets):
+        for o in range(own):
+            chan = (lax.axis_index("tm") ^ x) * own + o
+            squares[...] = first_ref[chan] + nulled_squares(raw_ref[chan], ref.at[o])
+            powers[chan] = squares[pl.ds(0, samples, 2), :] + squares[pl.ds(1, samples, 2), :]
     for chan in range(powers.shape[0]):
         out_ref[:, chan, :] = powers[chan]
 
@@ -240,14 +267,17 @@
     def cost(multiplies, moved):
         return pl.CostEstimate(flops=2 * multiplies, bytes_accessed=moved, transcendentals=0)
 
-    pieces = [
-        lax.dynamic_slice_in_dim(voltages[:, 0], (tm_index ^ x) * own, own, 1)
-        .transpose(1, 0, 2, 3)
-        .reshape(own, rows, width)
-        for x in shifts(tm, lax.axis_index("pol"))
-    ]
+    cut = pl.pallas_call(
+        functools.partial(cut_kernel, tm, own),
+        out_shape=[jax.ShapeDtypeStruct((samples, own, 2, width), BF16)] * tm,
+        in_specs=[unread],
+        out_specs=[whole] * tm,
+        scratch_shapes=[pltpu.SemaphoreType.DMA((tm,))],
+        compiler_params=params,
+    )(voltages)
+    pieces = [piece.transpose(1, 0, 2, 3).reshape(own, rows, width) for piece in cut]
     blocks = pieces[:1] + [
-        lax.ppermute(piece, ("tm", "pol"), route) for piece, route in zip(pieces[1:], routes(tm))
+        lax.ppermute(piece, ("tm", "pol"), route) for piece, route in zip(pieces[1:], routes(tm)[1:])
     ]
 
     raw = jax.ShapeDtypeStruct((chan_dev, rows, half), F32)
@@ -261,48 +291,63 @@
         cost_estimate=cost(4 * chan_dev * samples * width * beams, 8 * chan_dev * samples * width),
     )(phase_index, *pieces)
 
-    own_weights, other = pl.pallas_call(
-        functools.partial(own_weights_kernel, own, chan_dev),
-        out_shape=[jax.ShapeDtypeStruct((own, 2 * beams, width), BF16), raw],
-        in_specs=[whole, unread],
-        out_specs=[whole, unread],
-        input_output_aliases={1: 1},
-        compiler_params=params,
-        cost_estimate=cost(20 * own * beams * width, 8 * own * beams * width),
-    )(phase_index, other)
-    theirs = lax.ppermute(other, "pol", [(0, 1), (1, 0)])
-
-    cov = pl.pallas_call(
-        cov_kernel,
-        out_shape=jax.ShapeDtypeStruct((own, 2, width, width), F32),
-        in_specs=[whole] * (tm - 1),
+    cov = jax.ShapeDtypeStruct((own, 2, width, width), F32)
+    own_weights, cov = pl.pallas_call(
+        functools.partial(own_kernel, own, chan_dev),
+        out_shape=[jax.ShapeDtypeStruct((own, 2 * beams, width), BF16), cov],
+        in_specs=[whole] * 2,
+        out_specs=[whole] * 2,
+        compiler_params=params,
+        cost_estimate=cost(
+            own * width * (20 * beams + 4 * samples * width), 8 * own * width * (beams + width)
+        ),
+    )(phase_index, pieces[0])
+    high, low = pl.pallas_call(
+        functools.partial(cov_kernel, factor),
+        out_shape=[jax.ShapeDtypeStruct((own, 2 * width, width), BF16)] * 2,
+        in_specs=[whole] * tm,
+        out_specs=[whole] * 2,
+        compiler_params=params,
+        cost_estimate=cost(4 * (tm - 1) * own * samples * width * width, 16 * own * width * width),
+    )(cov, *blocks[1:])
+
+    other, *packets = pl.pallas_call(
+        functools.partial(subspace_kernel, tm, own),
+        out_shape=[raw] + [jax.ShapeDtypeStruct((own, vectors, rows + 2 * beams), F32)] * tm,
+        in_specs=[unread, whole, scalars, scalars] + [whole] * (3 + tm),
+        out_specs=[unread] + [whole] * tm,
+        input_output_aliases={0: 0},
+        compiler_params=params,
+        cost_estimate=cost(32 * own * vectors * tm * samples * width, 8 * own * width * width),
+    )(other, start_block, flags, ranks, own_weights, high, low, *blocks)
+    cores = [(0, 1), (1, 0)]
+    theirs = lax.ppermute(other, "pol", cores)
+    arrived = list(packets)
+    for x in reversed(range(1, tm)):
+        arrived[x] = lax.ppermute(packets[x], "tm", [(z, z ^ x) for z in range(tm)])
+    swapped = [lax.ppermute(packet, "pol", cores) for packet in arrived]
+
+    finish = cost(2 * chan_dev * rows * 6 * vectors * half, 8 * chan_dev * rows * half)
+    part = pl.pallas_call(
+        functools.partial(first_kernel, own),
+        out_shape=raw,
+        in_specs=[whole] * (1 + tm),
         out_specs=whole,
         compiler_params=params,
-        cost_estimate=cost(4 * (tm - 1) * own * samples * width * width, 8 * own * width * width),
-    )(*blocks[:-1])
-
-    packets = pl.pallas_call(
-        functools.partial(subspace_kernel, tm, own, factor),
-        out_shape=jax.ShapeDtypeStruct((2 * tm, own, vectors, rows + beams), F32),
-        in_specs=[whole, scalars, scalars, whole, whole] + [whole] * tm,
-        out_specs=whole,
-        scratch_shapes=[pltpu.VMEM((2 * width, width), BF16)] * 2,
-        compiler_params=params,
-        cost_estimate=cost(32 * own * vectors * tm * samples * width, 8 * own * width * width),
-    )(start_block, flags, ranks, own_weights, cov, *blocks)
-    arrived = lax.all_to_all(packets, ("tm", "pol"), split_axis=0, concat_axis=0, tiled=True)
-
+        cost_estimate=finish,
+    )(mine, *arrived)
     return pl.pallas_call(
-        functools.partial(finish_kernel, tm, own),
+        functools.partial(second_kernel, own),
         out_shape=jax.ShapeDtypeStruct((samples, chan_dev, half), F32),
-        in_specs=[whole] * 3,
+        in_specs=[whole] * (2 + tm),
         out_specs=whole,
         scratch_shapes=[
             pltpu.VMEM((rows, half), F32),
             pltpu.VMEM((chan_dev, samples, half), F32),
         ],
         compiler_params=params,
-    )(mine, theirs, arrived)
+        cost_estimate=finish,
+    )(part, theirs, *swapped)
 
 
 def solution(mesh):

time: 49.6 us -> 46.6 us (0.940)
  blocking collectives: 11.4 us -> 0 us
  starting transfers between devices: 5.89 us -> 13.6 us
  local copies, waits for them, and re-layouts: 2.43 us -> 1.66 us
  waiting for transfers between devices: 13.1 us -> 13.8 us
  Pallas kernels: 16.5 us -> 17.2 us
    all_to_all x1 -> x0, blocking collectives: 11.4 us -> none  [local(): lax.all_to_all(packets, ('tm', 'pol'), split_axis=0, concat_axis=0, tiled...]
    ppermute x1 -> x8, starting transfers between devices: 0.07 us -> 7.8 us  [the longest x3 7.21 us: local(): arrived[x] = lax.ppermute(packets[x], 'tm', [(z, z ^ x) for z in range(tm)])]
    ppermute x1 -> x8, waiting for transfers between devices: 0.01 us -> 5.03 us  [the longest x3 4.21 us: local(): arrived[x] = lax.ppermute(packets[x], 'tm', [(z, z ^ x) for z in range(tm)])]
    ppermute x3, waiting for transfers between devices: 13.1 us -> 8.75 us  [local(): lax.ppermute(piece, ('tm', 'pol'), route)]
    dynamic_slice x1 -> x0, local copies, waits for them, and re-layouts: 1.99 us -> none  [local(): lax.dynamic_slice_in_dim(voltages[:, 0], (tm_index ^ x) * own, own, 1)]
    unnamed x8 -> x10, local copies, waits for them, and re-layouts: 0.02 us -> 1.25 us
    pallas_call x4 -> x6, Pallas kernels: 9.68 us -> 10.4 us  [the longest x1 5.82 us: local(): pl.pallas_call(functools.partial(subspace_kernel, tm, own), out_shape=[ra...]
  transfers between devices with their start and end apart: 4 -> 11, of which waited for: 1 -> 5; matrix products, arithmetic and copies ran while one was open for 1% -> 1% of each run, Pallas kernels for 31% -> 19%
where the time goes in v4:
time: 46.6 us; the launch traced here: 46.4 us
  Pallas kernels  17.2 us (37%)
  waiting for transfers between devices  13.8 us (30%)
  starting transfers between devices  13.6 us (29%)
  local copies, waits for them, and re-layouts  1.66 us (4%)
    ppermute x3, waiting for transfers between devices, local(): lax.ppermute(piece, ('tm', 'pol'), route)  8.75 us
    ppermute x3, starting transfers between devices, local(): arrived[x] = lax.ppermute(packets[x], 'tm', [(z, z ^ x) for z in range(tm)])  7.21 us
    pallas_call x1, Pallas kernels, local(): pl.pallas_call(functools.partial(raw_beams_kernel, tm, own), out_shape=[r...  6.84 us
    pallas_call x1, Pallas kernels, local(): pl.pallas_call(functools.partial(subspace_kernel, tm, own), out_shape=[ra...  5.82 us
    ppermute x3, starting transfers between devices, local(): lax.ppermute(piece, ('tm', 'pol'), route)  5.81 us
    ppermute x3, waiting for transfers between devices, local(): arrived[x] = lax.ppermute(packets[x], 'tm', [(z, z ^ x) for z in range(tm)])  4.21 us
    pallas_call x1, Pallas kernels, local(): pl.pallas_call(functools.partial(own_kernel, own, chan_dev), out_shape=[j...  1.56 us
    unnamed x10, local copies, waits for them, and re-layouts  1.25 us
  transfers between devices with their start and end apart: 11, of which 5 were waited for; matrix products, arithmetic and copies ran while one was open for 1% of the time, Pallas kernels for 19%

profile of v4, /device:TPU:0, one launch (start us, length us, event | category | flops | bytes accessed | tf_op | source)
XLA Modules:
  0.0 46.4 jit_solution(11652192354119227726)
XLA Ops:
  0.0 0.0 copy-start
  0.0 1.2 %copy-done = bf16[128,1,4,2,512]{4,3,2,1,0:T(2,128)(2,1)S(1)} copy-done((bf16[128,1,4,2,512]{4,3,2,1,0:T(2,128)(2,1)S(1)}, bf16[128,1,4,2,512]{4,3,2,1,0:T(2,128)(2,1)}, u32[]{:S(2)}) %copy-start) | copy-done | bytes 1048600
  1.2 0.0 copy-start.4
  1.2 0.2 shard_map.55
  1.5 0.1 reshape_transpose.13.rest_1_
  1.6 4.1 %collective-permute-start = (bf16[1,256,512]{2,1,0:T(8,128)(2,1)S(1)}, bf16[1,256,512]{2,1,0:T(8,128)(2,1)S(1)}, u32[]{:S(2)}, u32[]{:S(2)}) collective-permute-start(bf16[1,256,512]{2,1,0:T(8,128)(2,1)S(1)} %reshape_transpose.13.rest_1_), channel_id=1, source_target_pairs={{0,8},{1,9},{4,12},{5,13},{8,0},{9,1},{12,4},{13,5},{2,10},{3,11},... | collective-permute-start | bytes 786440 | tf_op jit(solution)/shard_map/ppermute | solution.py:280
  5.7 0.1 reshape_transpose.14.rest_2_
  5.8 1.6 %collective-permute-start.1 = (bf16[1,256,512]{2,1,0:T(8,128)(2,1)S(1)}, bf16[1,256,512]{2,1,0:T(8,128)(2,1)S(1)}, u32[]{:S(2)}, u32[]{:S(2)}) collective-permute-start(bf16[1,256,512]{2,1,0:T(8,128)(2,1)S(1)} %reshape_transpose.14.rest_2_), channel_id=1, source_target_pairs={{0,4},{1,13},{4,0},{5,9},{8,12},{9,5},{12,8},{13,1},{2,6},{3,15},{... | collective-permute-start | bytes 786440 | tf_op jit(solution)/shard_map/ppermute | solution.py:280
  7.4 0.1 reshape_transpose.15.rest_3_
  7.5 0.1 collective-permute-start.2
  7.6 0.1 reshape_transpose.12.rest_0_.block_ref
  7.7 0.0 copy-done.4
  7.7 1.6 %shard_map.57 = (bf16[1,512,512]{2,1,0:T(8,128)(2,1)S(1)}, f32[1,2,512,512]{3,2,1,0:T(8,128)S(1)}) custom-call(s32[256,512]{1,0:T(8,128)S(1)} %copy-done.4, bf16[1,256,512]{2,1,0:T(8,128)(2,1)S(1)} %reshape_transpose.12.rest_0_.block_ref), custom_call_target="tpu_custom_call" | custom-call | flops 273678336 | bytes 3145728 | tf_op jit(solution)/shard_map/pallas_call | solution.py:295
  9.3 0.0 copy-start.1
  9.3 0.0 copy-start.2
  9.3 0.0 copy-start.3
  9.3 6.8 %shard_map.56 = (f32[4,256,128]{2,1,0:T(8,128)S(1)}, f32[4,256,128]{2,1,0:T(8,128)S(1)}) custom-call(s32[256,512]{1,0:T(8,128)S(1)} %copy-done.4, bf16[1,256,512]{2,1,0:T(8,128)(2,1)S(1)} %reshape_transpose.12.rest_0_.block_ref, bf16[1,256,512]{2,1,0:T(8,128)(2,1)S(1)} %reshape_transpose.13.rest_1_, bf16[1,256,512]{2,1,0:T(8,128)(2,1)S(1)} %reshape_transpose.14.rest_2_, ...), custom_call_target="tpu_custom_call" | custom-call | flops 536870912 | bytes 2097152 | tf_op jit(solution)/shard_map/pallas_call | solution.py:284
  16.2 6.6 %collective-permute-done.rest_0_.rest_1_ = bf16[1,256,512]{2,1,0:T(8,128)(2,1)S(1)} collective-permute-done((bf16[1,256,512]{2,1,0:T(8,128)(2,1)S(1)}, bf16[1,256,512]{2,1,0:T(8,128)(2,1)S(1)}, u32[]{:S(2)}, u32[]{:S(2)}) %collective-permute-start) | collective-permute-done | bytes 262176 | tf_op jit(solution)/shard_map/ppermute | solution.py:280
  22.7 2.2 %collective-permute-done.1.rest_1_.rest_2_ = bf16[1,256,512]{2,1,0:T(8,128)(2,1)S(1)} collective-permute-done((bf16[1,256,512]{2,1,0:T(8,128)(2,1)S(1)}, bf16[1,256,512]{2,1,0:T(8,128)(2,1)S(1)}, u32[]{:S(2)}, u32[]{:S(2)}) %collective-permute-start.1) | collective-permute-done | bytes 262176 | tf_op jit(solution)/shard_map/ppermute | solution.py:280
  24.9 0.0 collective-permute-done.2.rest_2_.rest_3_
  24.9 1.2 %shard_map.58 = (bf16[1,1024,512]{2,1,0:T(8,128)(2,1)S(1)}, bf16[1,1024,512]{2,1,0:T(8,128)(2,1)S(1)}) custom-call(f32[1,2,512,512]{3,2,1,0:T(8,128)S(1)} %get-tuple-element.27.cov_ref, bf16[1,256,512]{2,1,0:T(8,128)(2,1)S(1)} %collective-permute-done.rest_0_.rest_1_, bf16[1,256,512]{2,1,0:T(8,128)(2,1)S(1)} %collective-permute-done.1.rest_1_.rest_2_, ...), custom_call_target="tpu_custom_call" | custom-call | flops 805306368 | bytes 4194304 | tf_op jit(solution)/shard_map/pallas_call | solution.py:305
  26.1 0.0 copy-done.1
  26.1 0.0 copy-done.2
  26.2 0.0 copy-done.3
  26.2 5.8 %shard_map.59 = (f32[4,256,128]{2,1,0:T(8,128)S(1)}, f32[1,8,768]{2,1,0:T(8,128)S(1)}, f32[1,8,768]{2,1,0:T(8,128)S(1)}, f32[1,8,768]{2,1,0:T(8,128)S(1)}, f32[1,8,768]{2,1,0:T(8,128)S(1)}) custom-call(f32[4,256,128]{2,1,0:T(8,128)S(1)} %get-tuple-element.25.beams_ref, f32[1,4,2,8,512]{4,3,2,1,0:T(8,128)S(1)} %copy-done.1, ...), custom_call_target="tpu_custom_call", output_to_operand_aliasing={{0}: (0, {})} | custom-call | flops 134217728 | bytes 2097152 | tf_op jit(solution)/shard_map/pallas_call | solution.py:314
  32.0 0.1 collective-permute-start.6
  32.1 2.4 %collective-permute-start.5 = (f32[1,8,768]{2,1,0:T(8,128)S(1)}, f32[1,8,768]{2,1,0:T(8,128)S(1)}, u32[]{:S(2)}, u32[]{:S(2)}) collective-permute-start(f32[1,8,768]{2,1,0:T(8,128)S(1)} %get-tuple-element.33), channel_id=1, source_target_pairs={{0,12},{4,8},{8,4},{12,0},{1,13},{5,9},{9,5},{13,1},{2,14},{6,10},... | collective-permute-start | bytes 73736 | tf_op jit(solution)/shard_map/ppermute | solution.py:327
  34.5 4.8 %collective-permute-start.3 = (f32[1,8,768]{2,1,0:T(8,128)S(1)}, f32[1,8,768]{2,1,0:T(8,128)S(1)}, u32[]{:S(2)}, u32[]{:S(2)}) collective-permute-start(f32[1,8,768]{2,1,0:T(8,128)S(1)} %get-tuple-element.31), channel_id=1, source_target_pairs={{0,4},{4,0},{8,12},{12,8},{1,5},{5,1},{9,13},{13,9},{2,6},{6,2},{1... | collective-permute-start | bytes 73736 | tf_op jit(solution)/shard_map/ppermute | solution.py:327
  39.3 0.0 collective-permute-start.4
  39.3 0.0 collective-permute-start.7
  39.3 0.0 collective-permute-done.5.rest_3_
  39.3 0.5 %collective-permute-start.10 = (f32[1,8,768]{2,1,0:T(8,128)S(1)}, f32[1,8,768]{2,1,0:T(8,128)S(1)}, u32[]{:S(2)}, u32[]{:S(2)}) collective-permute-start(f32[1,8,768]{2,1,0:T(8,128)S(1)} %collective-permute-done.5.rest_3_), channel_id=1, source_target_pairs={{0,1},{1,0},{2,3},{3,2},{4,5},{5,4},{6,7},{7,6},{8,9},{9,8},{10,11... | collective-permute-start | bytes 73736 | tf_op jit(solution)/shard_map/ppermute | solution.py:328
  39.8 1.3 %collective-permute-done.3.rest_1_ = f32[1,8,768]{2,1,0:T(8,128)S(1)} collective-permute-done((f32[1,8,768]{2,1,0:T(8,128)S(1)}, f32[1,8,768]{2,1,0:T(8,128)S(1)}, u32[]{:S(2)}, u32[]{:S(2)}) %collective-permute-start.3) | collective-permute-done | bytes 24608 | tf_op jit(solution)/shard_map/ppermute | solution.py:327
  41.1 0.0 collective-permute-start.8
  41.1 2.9 %collective-permute-done.4.rest_2_ = f32[1,8,768]{2,1,0:T(8,128)S(1)} collective-permute-done((f32[1,8,768]{2,1,0:T(8,128)S(1)}, f32[1,8,768]{2,1,0:T(8,128)S(1)}, u32[]{:S(2)}, u32[]{:S(2)}) %collective-permute-start.4) | collective-permute-done | bytes 24608 | tf_op jit(solution)/shard_map/ppermute | solution.py:327
  44.0 0.0 collective-permute-start.9
  44.0 0.3 shard_map.60.first_ref
  44.4 0.0 collective-permute-done.7.rest_0_
  44.4 0.0 collective-permute-done.10.rest_3_
  44.4 0.0 collective-permute-done.8.rest_1_
  44.4 0.8 %collective-permute-done.9.rest_2_ = f32[1,8,768]{2,1,0:T(8,128)S(1)} collective-permute-done((f32[1,8,768]{2,1,0:T(8,128)S(1)}, f32[1,8,768]{2,1,0:T(8,128)S(1)}, u32[]{:S(2)}, u32[]{:S(2)}) %collective-permute-start.9) | collective-permute-done | bytes 24608 | tf_op jit(solution)/shard_map/ppermute | solution.py:328
  45.2 0.0 collective-permute-done.6.raw_ref
  45.2 1.2 %shard_map.61 = f32[128,4,128]{2,1,0:T(4,128)} custom-call(f32[4,256,128]{2,1,0:T(8,128)S(1)} %shard_map.60.first_ref, f32[4,256,128]{2,1,0:T(8,128)S(1)} %collective-permute-done.6.raw_ref, f32[1,8,768]{2,1,0:T(8,128)S(1)} %collective-permute-done.7.rest_0_, f32[1,8,768]{2,1,0:T(8,128)S(1)} %collective-permute-done.8.rest_1_, ...), custom_call_target="tpu_custom_call" | custom-call | flops 25165824 | bytes 1048576 | tf_op jit(solution)/shard_map/pallas_call | solution.py:339
Async XLA Ops:
  0.0 1.2 %copy-start = (bf16[128,1,4,2,512]{4,3,2,1,0:T(2,128)(2,1)S(1)}, bf16[128,1,4,2,512]{4,3,2,1,0:T(2,128)(2,1)}, u32[]{:S(2)}) copy-start(bf16[128,1,4,2,512]{4,3,2,1,0:T(2,128)(2,1)} %voltages_ref.1) | copy-start | bytes 3145732
  1.2 6.5 %copy-start.4 = (s32[256,512]{1,0:T(8,128)S(1)}, s32[256,512]{1,0:T(8,128)}, u32[]{:S(2)}) copy-start(s32[256,512]{1,0:T(8,128)} %phase_ref.3) | copy-start | bytes 1572868
  1.6 21.2 %collective-permute-start = (bf16[1,256,512]{2,1,0:T(8,128)(2,1)S(1)}, bf16[1,256,512]{2,1,0:T(8,128)(2,1)S(1)}, u32[]{:S(2)}, u32[]{:S(2)}) collective-permute-start(bf16[1,256,512]{2,1,0:T(8,128)(2,1)S(1)} %reshape_transpose.13.rest_1_), channel_id=1, source_target_pairs={{0,8},{1,9},{4,12},{5,13},{8,0},{9,1},{12,4},{13,5},{2,10},{3,11},... | collective-permute-start | bytes 786440 | tf_op jit(solution)/shard_map/ppermute | solution.py:280
  5.8 19.1 %collective-permute-start.1 = (bf16[1,256,512]{2,1,0:T(8,128)(2,1)S(1)}, bf16[1,256,512]{2,1,0:T(8,128)(2,1)S(1)}, u32[]{:S(2)}, u32[]{:S(2)}) collective-permute-start(bf16[1,256,512]{2,1,0:T(8,128)(2,1)S(1)} %reshape_transpose.14.rest_2_), channel_id=1, source_target_pairs={{0,4},{1,13},{4,0},{5,9},{8,12},{9,5},{12,8},{13,1},{2,6},{3,15},{... | collective-permute-start | bytes 786440 | tf_op jit(solution)/shard_map/ppermute | solution.py:280
  7.5 17.4 %collective-permute-start.2 = (bf16[1,256,512]{2,1,0:T(8,128)(2,1)S(1)}, bf16[1,256,512]{2,1,0:T(8,128)(2,1)S(1)}, u32[]{:S(2)}, u32[]{:S(2)}) collective-permute-start(bf16[1,256,512]{2,1,0:T(8,128)(2,1)S(1)} %reshape_transpose.15.rest_3_), channel_id=1, source_target_pairs={{0,12},{1,5},{4,8},{5,1},{8,4},{9,13},{12,0},{13,9},{2,14},{3,7},{... | collective-permute-start | bytes 786440 | tf_op jit(solution)/shard_map/ppermute | solution.py:280
  9.3 16.9 %copy-start.1 = (f32[1,4,2,8,512]{4,3,2,1,0:T(8,128)S(1)}, f32[1,4,2,8,512]{4,3,2,1,0:T(8,128)}, u32[]{:S(2)}) copy-start(f32[1,4,2,8,512]{4,3,2,1,0:T(8,128)} %start_ref.1) | copy-start | bytes 393220
  9.3 16.9 %copy-start.2 = (s32[4]{0:T(128)S(1)}, s32[4]{0:T(128)}, u32[]{:S(2)}) copy-start(s32[4]{0:T(128)} %flags_ref.1) | copy-start | bytes 52
  9.3 16.9 %copy-start.3 = (s32[4]{0:T(128)S(1)}, s32[4]{0:T(128)}, u32[]{:S(2)}) copy-start(s32[4]{0:T(128)} %ranks_ref.1) | copy-start | bytes 52
  32.0 13.2 %collective-permute-start.6 = (f32[4,256,128]{2,1,0:T(8,128)S(1)}, f32[4,256,128]{2,1,0:T(8,128)S(1)}, u32[]{:S(2)}, u32[]{:S(2)}) collective-permute-start(f32[4,256,128]{2,1,0:T(8,128)S(1)} %get-tuple-element.34), channel_id=1, source_target_pairs={{0,1},{1,0},{2,3},{3,2},{4,5},{5,4},{6,7},{7,6},{8,9},{9,8},{10,11... | collective-permute-start | bytes 1572872 | tf_op jit(solution)/shard_map/ppermute | solution.py:324
  32.1 7.2 %collective-permute-start.5 = (f32[1,8,768]{2,1,0:T(8,128)S(1)}, f32[1,8,768]{2,1,0:T(8,128)S(1)}, u32[]{:S(2)}, u32[]{:S(2)}) collective-permute-start(f32[1,8,768]{2,1,0:T(8,128)S(1)} %get-tuple-element.33), channel_id=1, source_target_pairs={{0,12},{4,8},{8,4},{12,0},{1,13},{5,9},{9,5},{13,1},{2,14},{6,10},... | collective-permute-start | bytes 73736 | tf_op jit(solution)/shard_map/ppermute | solution.py:327
  34.5 6.6 %collective-permute-start.3 = (f32[1,8,768]{2,1,0:T(8,128)S(1)}, f32[1,8,768]{2,1,0:T(8,128)S(1)}, u32[]{:S(2)}, u32[]{:S(2)}) collective-permute-start(f32[1,8,768]{2,1,0:T(8,128)S(1)} %get-tuple-element.31), channel_id=1, source_target_pairs={{0,4},{4,0},{8,12},{12,8},{1,5},{5,1},{9,13},{13,9},{2,6},{6,2},{1... | collective-permute-start | bytes 73736 | tf_op jit(solution)/shard_map/ppermute | solution.py:327
  39.3 4.7 %collective-permute-start.4 = (f32[1,8,768]{2,1,0:T(8,128)S(1)}, f32[1,8,768]{2,1,0:T(8,128)S(1)}, u32[]{:S(2)}, u32[]{:S(2)}) collective-permute-start(f32[1,8,768]{2,1,0:T(8,128)S(1)} %get-tuple-element.32), channel_id=1, source_target_pairs={{0,8},{4,12},{8,0},{12,4},{1,9},{5,13},{9,1},{13,5},{2,10},{6,14},... | collective-permute-start | bytes 73736 | tf_op jit(solution)/shard_map/ppermute | solution.py:327
  39.3 5.1 %collective-permute-start.7 = (f32[1,8,768]{2,1,0:T(8,128)S(1)}, f32[1,8,768]{2,1,0:T(8,128)S(1)}, u32[]{:S(2)}, u32[]{:S(2)}) collective-permute-start(f32[1,8,768]{2,1,0:T(8,128)S(1)} %get-tuple-element.30.rest_0_), channel_id=1, source_target_pairs={{0,1},{1,0},{2,3},{3,2},{4,5},{5,4},{6,7},{7,6},{8,9},{9,8},{10,11... | collective-permute-start | bytes 73736 | tf_op jit(solution)/shard_map/ppermute | solution.py:328
  39.3 5.1 %collective-permute-start.10 = (f32[1,8,768]{2,1,0:T(8,128)S(1)}, f32[1,8,768]{2,1,0:T(8,128)S(1)}, u32[]{:S(2)}, u32[]{:S(2)}) collective-permute-start(f32[1,8,768]{2,1,0:T(8,128)S(1)} %collective-permute-done.5.rest_3_), channel_id=1, source_target_pairs={{0,1},{1,0},{2,3},{3,2},{4,5},{5,4},{6,7},{7,6},{8,9},{9,8},{10,11... | collective-permute-start | bytes 73736 | tf_op jit(solution)/shard_map/ppermute | solution.py:328
  41.1 3.3 %collective-permute-start.8 = (f32[1,8,768]{2,1,0:T(8,128)S(1)}, f32[1,8,768]{2,1,0:T(8,128)S(1)}, u32[]{:S(2)}, u32[]{:S(2)}) collective-permute-start(f32[1,8,768]{2,1,0:T(8,128)S(1)} %collective-permute-done.3.rest_1_), channel_id=1, source_target_pairs={{0,1},{1,0},{2,3},{3,2},{4,5},{5,4},{6,7},{7,6},{8,9},{9,8},{10,11... | collective-permute-start | bytes 73736 | tf_op jit(solution)/shard_map/ppermute | solution.py:328
  44.0 1.2 %collective-permute-start.9 = (f32[1,8,768]{2,1,0:T(8,128)S(1)}, f32[1,8,768]{2,1,0:T(8,128)S(1)}, u32[]{:S(2)}, u32[]{:S(2)}) collective-permute-start(f32[1,8,768]{2,1,0:T(8,128)S(1)} %collective-permute-done.4.rest_2_), channel_id=1, source_target_pairs={{0,1},{1,0},{2,3},{3,2},{4,5},{5,4},{6,7},{7,6},{8,9},{9,8},{10,11... | collective-permute-start | bytes 73736 | tf_op jit(solution)/shard_map/ppermute | solution.py:328

commit v5 on v4

--- a/solution.py
+++ b/solution.py
@@ -111,38 +111,27 @@
                 out_ref[chan] = product[:, :half] - by_imag
 
 
-def cov_terms(x):
-    rotated = -turned(x.astype(F32), 0)
-    return dot(x, x, TN), dot(x, rotated.astype(BF16), TN)
-
-
-def own_kernel(own, chan_dev, phase_ref, block_ref, weights_ref, cov_ref):
+def own_weights_kernel(own, chan_dev, phase_ref, out_ref):
     beams = phase_ref.shape[0]
     first = lax.axis_index("chan") * chan_dev + lax.axis_index("tm") * own
     for o in range(own):
-        fill_weights(phase_ref, 0, beams, first + o + 1, weights_ref.at[o])
-        cov_ref[o, 0], cov_ref[o, 1] = cov_terms(block_ref[o])
-
-
-def cov_kernel(factor, cov_ref, *rest):
-    blocks, (high_ref, low_ref) = rest[:-2], rest[-2:]
-    width = cov_ref.shape[2]
-    for o in range(cov_ref.shape[0]):
-        sums = cov_ref[o, 0], cov_ref[o, 1]
-        for block in blocks:
-            sums = [total + term for total, term in zip(sums, cov_terms(block[o]))]
-        for part, total in enumerate(sums):
-            high, low = split(total * factor)
-            high_ref[o, part * width : (part + 1) * width] = high
-            low_ref[o, part * width : (part + 1) * width] = low
-
-
-def correlate(real, imag, x):
-    vectors = real.shape[0]
-    rows = jnp.concatenate([real, imag], axis=0)
-    product = dot(jnp.concatenate(split(rows), axis=0), x, NT)
-    product = product[: 2 * vectors] + product[2 * vectors :]
-    return product[:vectors] + turned(product[vectors:], 1)
+        fill_weights(phase_ref, 0, beams, first + o + 1, out_ref.at[o])
+
+
+def fill_cov(factor, blocks, own_at, across_ref, along_ref, rotated_ref, high_ref, low_ref):
+    rows, width = blocks[0].shape[1:]
+    for i, block in enumerate(blocks):
+        x = block[own_at]
+        at = slice(i * rows, (i + 1) * rows)
+        along_ref[at] = x
+        rotated_ref[at] = -turned(x.astype(F32), 0).astype(BF16)
+        across_ref[:, at] = x.T
+    step = width // 2
+    for part, right in enumerate((along_ref, rotated_ref)):
+        for first in range(0, width, step):
+            total = dot(across_ref[first : first + step], right[...], NN) * factor
+            at = slice(part * width + first, part * width + first + step)
+            high_ref[at], low_ref[at] = split(total)
 
 
 def cov_times(real, imag, high_ref, low_ref):
@@ -157,53 +146,58 @@
 
 
 def orthonormalize(real_z, imag_z):
-    vectors = real_z.shape[0]
-    row = lax.broadcasted_iota(jnp.int32, real_z.shape, 0)
+    vectors, width = real_z.shape
+    row = lax.broadcasted_iota(jnp.int32, (vectors, 1), 0)
     real_v, imag_v = real_z, imag_z
     scale = jnp.zeros((vectors, 1), F32)
     for n in range(vectors):
-        here = row == n
-        real_a, imag_a = real_v[n : n + 1], imag_v[n : n + 1]
-        real_z = jnp.where(here, real_v, real_z)
-        imag_z = jnp.where(here, imag_v, imag_z)
-        real_d = jnp.sum(real_a * real_z + imag_a * imag_z, axis=1, keepdims=True)
-        norm = real_d[n : n + 1] + EPS
-        scale = jnp.where(row[:, :1] == n, norm, scale)
+        real_a = jnp.broadcast_to(real_v[n : n + 1], real_z.shape)
+        imag_a = jnp.broadcast_to(imag_v[n : n + 1], real_z.shape)
+        norm = jnp.sum(real_a * real_a + imag_a * imag_a, axis=1, keepdims=True) + EPS
+        scale = jnp.where(row == n, norm, scale)
         if n + 1 < vectors:
+            real_d = jnp.sum(real_a * real_z + imag_a * imag_z, axis=1, keepdims=True)
             imag_d = jnp.sum(real_a * imag_z - imag_a * real_z, axis=1, keepdims=True)
-            inverse = 1.0 / norm
-            later = row[:, :1] > n
-            real_c = jnp.where(later, real_d * inverse, 0.0)
-            imag_c = jnp.where(later, imag_d * inverse, 0.0)
+            inverse = jnp.where(row > n, 1.0 / norm, 0.0)
+            real_c = real_d * inverse
+            imag_c = imag_d * inverse
             real_v = real_v - (real_c * real_a - imag_c * imag_a)
             imag_v = imag_v - (real_c * imag_a + imag_c * real_a)
     factor = 1.0 / jnp.sqrt(scale)
     return real_v * factor, imag_v * factor
 
 
-def subspace_kernel(tm, own, beams_ref, start_ref, flags_ref, ranks_ref, weights_ref, high_ref, low_ref, *rest):
-    blocks, outs = rest[:tm], rest[tm + 1 :]
+def subspace_kernel(tm, own, factor, beams_ref, start_ref, flags_ref, ranks_ref, weights_ref, *rest):
+    blocks, outs, scratch = rest[:tm], rest[tm + 1 : 2 * tm + 1], rest[2 * tm + 1 :]
+    across_ref, along_ref, rotated_ref, high_ref, low_ref = scratch
     vectors, width = start_ref.shape[3], start_ref.shape[4]
     rows = blocks[0].shape[1]
     tm_index = lax.axis_index("tm")
     beams = weights_ref.shape[1] // 2
     for o in range(own):
         chan = tm_index * own + o
+        fill_cov(factor, blocks, o, *scratch)
         real_q = start_ref[0, chan, 0]
         imag_q = start_ref[0, chan, 1]
         for sweep in range(ITERS):
-            real_z, imag_z = cov_times(real_q, imag_q, high_ref.at[o], low_ref.at[o])
+            real_z, imag_z = cov_times(real_q, imag_q, high_ref, low_ref)
             real_q, imag_q = orthonormalize(real_z, imag_z)
         rank = flags_ref[chan] * ranks_ref[chan]
         keep = lax.broadcasted_iota(jnp.int32, (vectors, width), 0) < rank
         real_u = jnp.where(keep, real_q, 0.0)
         imag_u = jnp.where(keep, imag_q, 0.0)
-        both = jnp.concatenate([real_u, imag_u], axis=0)
-        product = dot(jnp.concatenate(split(both), axis=0), weights_ref[o], NT)
+        both = jnp.concatenate(split(jnp.concatenate([real_u, imag_u], axis=0)), axis=0)
+        product = dot(both, weights_ref[o], NT)
         product = product[: 2 * vectors] + product[2 * vectors :]
         real_w = product[:vectors, :beams] - product[vectors:, beams:]
         imag_w = product[:vectors, beams:] + product[vectors:, :beams]
-        series = [correlate(real_u, imag_u, block[o]) for block in blocks]
+        product = dot(both, across_ref[...], NN)
+        product = product[: 2 * vectors] + product[2 * vectors :]
+        series = [
+            product[:vectors, i * rows : (i + 1) * rows]
+            + turned(product[vectors:, i * rows : (i + 1) * rows], 1)
+            for i in range(tm)
+        ]
         first, second = orders(tm)
         for x, out in enumerate(outs):
             a, b = first.index(x), second.index(x)
@@ -229,22 +223,27 @@
     return beam * beam
 
 
+def pair_sums(squares):
+    samples = squares.shape[0] // 2
+    return squares[pl.ds(0, samples, 2), :] + squares[pl.ds(1, samples, 2), :]
+
+
 def first_kernel(own, raw_ref, *rest):
-    packets, out_ref = rest[:-1], rest[-1]
+    packets, (out_ref, squares) = rest[:-2], rest[-2:]
     for x, ref in enumerate(packets):
         for o in range(own):
             chan = (lax.axis_index("tm") ^ x) * own + o
-            out_ref[chan] = nulled_squares(raw_ref[chan], ref.at[o])
+            squares[...] = nulled_squares(raw_ref[chan], ref.at[o])
+            out_ref[chan] = pair_sums(squares)
 
 
 def second_kernel(own, first_ref, raw_ref, *rest):
     packets, (out_ref, squares, powers) = rest[:-3], rest[-3:]
-    samples = out_ref.shape[0]
     for x, ref in enumerate(packets):
         for o in range(own):
             chan = (lax.axis_index("tm") ^ x) * own + o
-            squares[...] = first_ref[chan] + nulled_squares(raw_ref[chan], ref.at[o])
-            powers[chan] = squares[pl.ds(0, samples, 2), :] + squares[pl.ds(1, samples, 2), :]
+            squares[...] = nulled_squares(raw_ref[chan], ref.at[o])
+            powers[chan] = first_ref[chan] + pair_sums(squares)
     for chan in range(powers.shape[0]):
         out_ref[:, chan, :] = powers[chan]
 
@@ -270,7 +269,7 @@
     cut = pl.pallas_call(
         functools.partial(cut_kernel, tm, own),
         out_shape=[jax.ShapeDtypeStruct((samples, own, 2, width), BF16)] * tm,
-        in_specs=[unread],
+        in_specs=[pl.BlockSpec(memory_space=pltpu.HBM)],
         out_specs=[whole] * tm,
         scratch_shapes=[pltpu.SemaphoreType.DMA((tm,))],
         compiler_params=params,
@@ -291,35 +290,31 @@
         cost_estimate=cost(4 * chan_dev * samples * width * beams, 8 * chan_dev * samples * width),
     )(phase_index, *pieces)
 
-    cov = jax.ShapeDtypeStruct((own, 2, width, width), F32)
-    own_weights, cov = pl.pallas_call(
-        functools.partial(own_kernel, own, chan_dev),
-        out_shape=[jax.ShapeDtypeStruct((own, 2 * beams, width), BF16), cov],
-        in_specs=[whole] * 2,
-        out_specs=[whole] * 2,
-        compiler_params=params,
-        cost_estimate=cost(
-            own * width * (20 * beams + 4 * samples * width), 8 * own * width * (beams + width)
-        ),
-    )(phase_index, pieces[0])
-    high, low = pl.pallas_call(
-        functools.partial(cov_kernel, factor),
-        out_shape=[jax.ShapeDtypeStruct((own, 2 * width, width), BF16)] * 2,
-        in_specs=[whole] * tm,
-        out_specs=[whole] * 2,
-        compiler_params=params,
-        cost_estimate=cost(4 * (tm - 1) * own * samples * width * width, 16 * own * width * width),
-    )(cov, *blocks[1:])
+    own_weights = pl.pallas_call(
+        functools.partial(own_weights_kernel, own, chan_dev),
+        out_shape=jax.ShapeDtypeStruct((own, 2 * beams, width), BF16),
+        in_specs=[whole],
+        out_specs=whole,
+        compiler_params=params,
+        cost_estimate=cost(20 * own * beams * width, 8 * own * beams * width),
+    )(phase_index)
 
     other, *packets = pl.pallas_call(
-        functools.partial(subspace_kernel, tm, own),
+        functools.partial(subspace_kernel, tm, own, factor),
         out_shape=[raw] + [jax.ShapeDtypeStruct((own, vectors, rows + 2 * beams), F32)] * tm,
-        in_specs=[unread, whole, scalars, scalars] + [whole] * (3 + tm),
+        in_specs=[unread, whole, scalars, scalars] + [whole] * (1 + tm),
         out_specs=[unread] + [whole] * tm,
         input_output_aliases={0: 0},
+        scratch_shapes=[
+            pltpu.VMEM((width, tm * rows), BF16),
+            pltpu.VMEM((tm * rows, width), BF16),
+            pltpu.VMEM((tm * rows, width), BF16),
+            pltpu.VMEM((2 * width, width), BF16),
+            pltpu.VMEM((2 * width, width), BF16),
+        ],
         compiler_params=params,
         cost_estimate=cost(32 * own * vectors * tm * samples * width, 8 * own * width * width),
-    )(other, start_block, flags, ranks, own_weights, high, low, *blocks)
+    )(other, start_block, flags, ranks, own_weights, *blocks)
     cores = [(0, 1), (1, 0)]
     theirs = lax.ppermute(other, "pol", cores)
     arrived = list(packets)
@@ -330,9 +325,10 @@
     finish = cost(2 * chan_dev * rows * 6 * vectors * half, 8 * chan_dev * rows * half)
     part = pl.pallas_call(
         functools.partial(first_kernel, own),
-        out_shape=raw,
+        out_shape=jax.ShapeDtypeStruct((chan_dev, samples, half), F32),
         in_specs=[whole] * (1 + tm),
         out_specs=whole,
+        scratch_shapes=[pltpu.VMEM((rows, half), F32)],
         compiler_params=params,
         cost_estimate=finish,
     )(mine, *arrived)

time: 46.6 us -> 47.2 us (1.013)
  starting transfers between devices: 13.6 us -> 14.5 us
  waiting for transfers between devices: 13.8 us -> 13 us
  local copies, waits for them, and re-layouts: 1.66 us -> 2.4 us
    ppermute x3, starting transfers between devices: 7.21 us -> 8.11 us  [local(): arrived[x] = lax.ppermute(packets[x], 'tm', [(z, z ^ x) for z in range(tm)])]
    unnamed x10, local copies, waits for them, and re-layouts: 1.25 us -> 1.99 us
    ppermute x3, waiting for transfers between devices: 4.21 us -> 3.72 us  [local(): arrived[x] = lax.ppermute(packets[x], 'tm', [(z, z ^ x) for z in range(tm)])]
    pallas_call x4 -> x3, Pallas kernels: 8.93 us -> 8.61 us  [the longest x1 7.2 us: local(): pl.pallas_call(functools.partial(subspace_kernel, tm, own, factor), out_s...]
  transfers between devices with their start and end apart: 11 -> 11, of which waited for: 5 -> 5; matrix products, arithmetic and copies ran while one was open for 1% -> 1% of each run, Pallas kernels for 19% -> 18%
where the time goes in v5:
time: 47.2 us; the launch traced here: 47 us
  Pallas kernels  16.9 us (36%)
  starting transfers between devices  14.5 us (31%)
  waiting for transfers between devices  13 us (28%)
  local copies, waits for them, and re-layouts  2.4 us (5%)
    ppermute x3, waiting for transfers between devices, local(): lax.ppermute(piece, ('tm', 'pol'), route)  8.51 us
    ppermute x3, starting transfers between devices, local(): arrived[x] = lax.ppermute(packets[x], 'tm', [(z, z ^ x) for z in range(tm)])  8.11 us
    pallas_call x1, Pallas kernels, local(): pl.pallas_call(functools.partial(subspace_kernel, tm, own, factor), out_s...  7.2 us
    pallas_call x1, Pallas kernels, local(): pl.pallas_call(functools.partial(raw_beams_kernel, tm, own), out_shape=[r...  6.84 us
    ppermute x3, starting transfers between devices, local(): lax.ppermute(piece, ('tm', 'pol'), route)  5.81 us
    ppermute x3, waiting for transfers between devices, local(): arrived[x] = lax.ppermute(packets[x], 'tm', [(z, z ^ x) for z in range(tm)])  3.72 us
    unnamed x10, local copies, waits for them, and re-layouts  1.99 us
    pallas_call x1, Pallas kernels, local(): pl.pallas_call(functools.partial(second_kernel, own), out_shape=jax.Shape...  1.21 us
  transfers between devices with their start and end apart: 11, of which 5 were waited for; matrix products, arithmetic and copies ran while one was open for 1% of the time, Pallas kernels for 18%

profile of v5, /device:TPU:0, one launch (start us, length us, event | category | flops | bytes accessed | tf_op | source)
XLA Modules:
  0.0 47.0 jit_solution(11295552839783786574)
XLA Ops:
  0.0 0.0 copy-start
  0.0 1.2 %copy-done = bf16[128,1,4,2,512]{4,3,2,1,0:T(2,128)(2,1)S(1)} copy-done((bf16[128,1,4,2,512]{4,3,2,1,0:T(2,128)(2,1)S(1)}, bf16[128,1,4,2,512]{4,3,2,1,0:T(2,128)(2,1)}, u32[]{:S(2)}) %copy-start) | copy-done | bytes 1048600
  1.2 0.2 shard_map.55
  1.5 0.1 reshape_transpose.13.rest_1_
  1.6 4.1 %collective-permute-start = (bf16[1,256,512]{2,1,0:T(8,128)(2,1)S(1)}, bf16[1,256,512]{2,1,0:T(8,128)(2,1)S(1)}, u32[]{:S(2)}, u32[]{:S(2)}) collective-permute-start(bf16[1,256,512]{2,1,0:T(8,128)(2,1)S(1)} %reshape_transpose.13.rest_1_), channel_id=1, source_target_pairs={{0,8},{1,9},{4,12},{5,13},{8,0},{9,1},{12,4},{13,5},{2,10},{3,11},... | collective-permute-start | bytes 786440 | tf_op jit(solution)/shard_map/ppermute | solution.py:279
  5.7 0.1 reshape_transpose.14.rest_2_
  5.8 1.6 %collective-permute-start.1 = (bf16[1,256,512]{2,1,0:T(8,128)(2,1)S(1)}, bf16[1,256,512]{2,1,0:T(8,128)(2,1)S(1)}, u32[]{:S(2)}, u32[]{:S(2)}) collective-permute-start(bf16[1,256,512]{2,1,0:T(8,128)(2,1)S(1)} %reshape_transpose.14.rest_2_), channel_id=1, source_target_pairs={{0,4},{1,13},{4,0},{5,9},{8,12},{9,5},{12,8},{13,1},{2,6},{3,15},{... | collective-permute-start | bytes 786440 | tf_op jit(solution)/shard_map/ppermute | solution.py:279
  7.4 0.0 copy-start.1
  7.4 0.1 reshape_transpose.15.rest_3_
  7.5 0.1 collective-permute-start.2
  7.6 0.1 reshape_transpose.12.rest_0_
  7.7 0.7 %copy-done.1 = s32[256,512]{1,0:T(8,128)S(1)} copy-done((s32[256,512]{1,0:T(8,128)S(1)}, s32[256,512]{1,0:T(8,128)}, u32[]{:S(2)}) %copy-start.1) | copy-done | bytes 524312
  8.5 1.1 %shard_map.57.weights_ref = bf16[1,512,512]{2,1,0:T(8,128)(2,1)S(1)} custom-call(s32[256,512]{1,0:T(8,128)S(1)} %copy-done.1), custom_call_target="tpu_custom_call" | custom-call | flops 5242880 | bytes 1048576 | tf_op jit(solution)/shard_map/pallas_call | solution.py:293
  9.5 0.0 copy-start.2
  9.5 6.8 %shard_map.56 = (f32[4,256,128]{2,1,0:T(8,128)S(1)}, f32[4,256,128]{2,1,0:T(8,128)S(1)}) custom-call(s32[256,512]{1,0:T(8,128)S(1)} %copy-done.1, bf16[1,256,512]{2,1,0:T(8,128)(2,1)S(1)} %reshape_transpose.12.rest_0_, bf16[1,256,512]{2,1,0:T(8,128)(2,1)S(1)} %reshape_transpose.13.rest_1_, bf16[1,256,512]{2,1,0:T(8,128)(2,1)S(1)} %reshape_transpose.14.rest_2_, ...), custom_call_target="tpu_custom_call" | custom-call | flops 536870912 | bytes 2097152 | tf_op jit(solution)/shard_map/pallas_call | solution.py:283
  16.4 0.0 copy-start.3
  16.4 0.0 copy-start.4
  16.4 6.3 %collective-permute-done.rest_1_ = bf16[1,256,512]{2,1,0:T(8,128)(2,1)S(1)} collective-permute-done((bf16[1,256,512]{2,1,0:T(8,128)(2,1)S(1)}, bf16[1,256,512]{2,1,0:T(8,128)(2,1)S(1)}, u32[]{:S(2)}, u32[]{:S(2)}) %collective-permute-start) | collective-permute-done | bytes 262176 | tf_op jit(solution)/shard_map/ppermute | solution.py:279
  22.7 2.2 %collective-permute-done.1.rest_2_ = bf16[1,256,512]{2,1,0:T(8,128)(2,1)S(1)} collective-permute-done((bf16[1,256,512]{2,1,0:T(8,128)(2,1)S(1)}, bf16[1,256,512]{2,1,0:T(8,128)(2,1)S(1)}, u32[]{:S(2)}, u32[]{:S(2)}) %collective-permute-start.1) | collective-permute-done | bytes 262176 | tf_op jit(solution)/shard_map/ppermute | solution.py:279
  24.9 0.0 collective-permute-done.2.rest_3_
  24.9 0.0 copy-done.2
  24.9 0.0 copy-done.3
  24.9 0.0 copy-done.4
  24.9 7.2 %shard_map.58 = (f32[4,256,128]{2,1,0:T(8,128)S(1)}, f32[1,8,768]{2,1,0:T(8,128)S(1)}, f32[1,8,768]{2,1,0:T(8,128)S(1)}, f32[1,8,768]{2,1,0:T(8,128)S(1)}, f32[1,8,768]{2,1,0:T(8,128)S(1)}) custom-call(f32[4,256,128]{2,1,0:T(8,128)S(1)} %get-tuple-element.21.beams_ref, f32[1,4,2,8,512]{4,3,2,1,0:T(8,128)S(1)} %copy-done.2, ...), custom_call_target="tpu_custom_call", output_to_operand_aliasing={{0}: (0, {})} | custom-call | flops 134217728 | bytes 2097152 | tf_op jit(solution)/shard_map/pallas_call | solution.py:302
  32.2 0.1 collective-permute-start.6
  32.2 4.7 %collective-permute-start.3 = (f32[1,8,768]{2,1,0:T(8,128)S(1)}, f32[1,8,768]{2,1,0:T(8,128)S(1)}, u32[]{:S(2)}, u32[]{:S(2)}) collective-permute-start(f32[1,8,768]{2,1,0:T(8,128)S(1)} %get-tuple-element.23), channel_id=1, source_target_pairs={{0,4},{4,0},{8,12},{12,8},{1,5},{5,1},{9,13},{13,9},{2,6},{6,2},{1... | collective-permute-start | bytes 73736 | tf_op jit(solution)/shard_map/ppermute | solution.py:322
  37.0 2.0 %collective-permute-start.4 = (f32[1,8,768]{2,1,0:T(8,128)S(1)}, f32[1,8,768]{2,1,0:T(8,128)S(1)}, u32[]{:S(2)}, u32[]{:S(2)}) collective-permute-start(f32[1,8,768]{2,1,0:T(8,128)S(1)} %get-tuple-element.24), channel_id=1, source_target_pairs={{0,8},{4,12},{8,0},{12,4},{1,9},{5,13},{9,1},{13,5},{2,10},{6,14},... | collective-permute-start | bytes 73736 | tf_op jit(solution)/shard_map/ppermute | solution.py:322
  39.0 1.4 %collective-permute-start.5 = (f32[1,8,768]{2,1,0:T(8,128)S(1)}, f32[1,8,768]{2,1,0:T(8,128)S(1)}, u32[]{:S(2)}, u32[]{:S(2)}) collective-permute-start(f32[1,8,768]{2,1,0:T(8,128)S(1)} %get-tuple-element.25), channel_id=1, source_target_pairs={{0,12},{4,8},{8,4},{12,0},{1,13},{5,9},{9,5},{13,1},{2,14},{6,10},... | collective-permute-start | bytes 73736 | tf_op jit(solution)/shard_map/ppermute | solution.py:322
  40.3 0.0 collective-permute-start.7
  40.3 0.0 collective-permute-done.3.rest_1_
  40.4 0.5 %collective-permute-start.8 = (f32[1,8,768]{2,1,0:T(8,128)S(1)}, f32[1,8,768]{2,1,0:T(8,128)S(1)}, u32[]{:S(2)}, u32[]{:S(2)}) collective-permute-start(f32[1,8,768]{2,1,0:T(8,128)S(1)} %collective-permute-done.3.rest_1_), channel_id=1, source_target_pairs={{0,1},{1,0},{2,3},{3,2},{4,5},{5,4},{6,7},{7,6},{8,9},{9,8},{10,11... | collective-permute-start | bytes 73736 | tf_op jit(solution)/shard_map/ppermute | solution.py:323
  40.9 0.8 %collective-permute-done.4.rest_2_ = f32[1,8,768]{2,1,0:T(8,128)S(1)} collective-permute-done((f32[1,8,768]{2,1,0:T(8,128)S(1)}, f32[1,8,768]{2,1,0:T(8,128)S(1)}, u32[]{:S(2)}, u32[]{:S(2)}) %collective-permute-start.4) | collective-permute-done | bytes 24608 | tf_op jit(solution)/shard_map/ppermute | solution.py:322
  41.7 0.0 collective-permute-start.9
  41.7 2.9 %collective-permute-done.5.rest_3_ = f32[1,8,768]{2,1,0:T(8,128)S(1)} collective-permute-done((f32[1,8,768]{2,1,0:T(8,128)S(1)}, f32[1,8,768]{2,1,0:T(8,128)S(1)}, u32[]{:S(2)}, u32[]{:S(2)}) %collective-permute-start.5) | collective-permute-done | bytes 24608 | tf_op jit(solution)/shard_map/ppermute | solution.py:322
  44.6 0.0 collective-permute-start.10
  44.6 0.4 shard_map.59.first_ref
  44.9 0.0 collective-permute-done.7.rest_0_
  45.0 0.0 collective-permute-done.8.rest_1_
  45.0 0.0 collective-permute-done.9.rest_2_
  45.0 0.8 %collective-permute-done.10.rest_3_ = f32[1,8,768]{2,1,0:T(8,128)S(1)} collective-permute-done((f32[1,8,768]{2,1,0:T(8,128)S(1)}, f32[1,8,768]{2,1,0:T(8,128)S(1)}, u32[]{:S(2)}, u32[]{:S(2)}) %collective-permute-start.10) | collective-permute-done | bytes 24608 | tf_op jit(solution)/shard_map/ppermute | solution.py:323
  45.8 0.0 collective-permute-done.6.raw_ref
  45.8 1.2 %shard_map.60 = f32[128,4,128]{2,1,0:T(4,128)} custom-call(f32[4,128,128]{2,1,0:T(8,128)S(1)} %shard_map.59.first_ref, f32[4,256,128]{2,1,0:T(8,128)S(1)} %collective-permute-done.6.raw_ref, f32[1,8,768]{2,1,0:T(8,128)S(1)} %collective-permute-done.7.rest_0_, f32[1,8,768]{2,1,0:T(8,128)S(1)} %collective-permute-done.8.rest_1_, ...), custom_call_target="tpu_custom_call" | custom-call | flops 25165824 | bytes 1048576 | tf_op jit(solution)/shard_map/pallas_call | solution.py:335
Async XLA Ops:
  0.0 1.2 %copy-start = (bf16[128,1,4,2,512]{4,3,2,1,0:T(2,128)(2,1)S(1)}, bf16[128,1,4,2,512]{4,3,2,1,0:T(2,128)(2,1)}, u32[]{:S(2)}) copy-start(bf16[128,1,4,2,512]{4,3,2,1,0:T(2,128)(2,1)} %voltages_ref.1) | copy-start | bytes 3145732
  1.6 21.2 %collective-permute-start = (bf16[1,256,512]{2,1,0:T(8,128)(2,1)S(1)}, bf16[1,256,512]{2,1,0:T(8,128)(2,1)S(1)}, u32[]{:S(2)}, u32[]{:S(2)}) collective-permute-start(bf16[1,256,512]{2,1,0:T(8,128)(2,1)S(1)} %reshape_transpose.13.rest_1_), channel_id=1, source_target_pairs={{0,8},{1,9},{4,12},{5,13},{8,0},{9,1},{12,4},{13,5},{2,10},{3,11},... | collective-permute-start | bytes 786440 | tf_op jit(solution)/shard_map/ppermute | solution.py:279
  5.8 19.1 %collective-permute-start.1 = (bf16[1,256,512]{2,1,0:T(8,128)(2,1)S(1)}, bf16[1,256,512]{2,1,0:T(8,128)(2,1)S(1)}, u32[]{:S(2)}, u32[]{:S(2)}) collective-permute-start(bf16[1,256,512]{2,1,0:T(8,128)(2,1)S(1)} %reshape_transpose.14.rest_2_), channel_id=1, source_target_pairs={{0,4},{1,13},{4,0},{5,9},{8,12},{9,5},{12,8},{13,1},{2,6},{3,15},{... | collective-permute-start | bytes 786440 | tf_op jit(solution)/shard_map/ppermute | solution.py:279
  7.4 1.0 %copy-start.1 = (s32[256,512]{1,0:T(8,128)S(1)}, s32[256,512]{1,0:T(8,128)}, u32[]{:S(2)}) copy-start(s32[256,512]{1,0:T(8,128)} %phase_ref.3) | copy-start | bytes 1572868
  7.5 17.4 %collective-permute-start.2 = (bf16[1,256,512]{2,1,0:T(8,128)(2,1)S(1)}, bf16[1,256,512]{2,1,0:T(8,128)(2,1)S(1)}, u32[]{:S(2)}, u32[]{:S(2)}) collective-permute-start(bf16[1,256,512]{2,1,0:T(8,128)(2,1)S(1)} %reshape_transpose.15.rest_3_), channel_id=1, source_target_pairs={{0,12},{1,5},{4,8},{5,1},{8,4},{9,13},{12,0},{13,9},{2,14},{3,7},{... | collective-permute-start | bytes 786440 | tf_op jit(solution)/shard_map/ppermute | solution.py:279
  9.5 15.4 %copy-start.2 = (f32[1,4,2,8,512]{4,3,2,1,0:T(8,128)S(1)}, f32[1,4,2,8,512]{4,3,2,1,0:T(8,128)}, u32[]{:S(2)}) copy-start(f32[1,4,2,8,512]{4,3,2,1,0:T(8,128)} %start_ref.1) | copy-start | bytes 393220
  16.4 8.5 %copy-start.3 = (s32[4]{0:T(128)S(1)}, s32[4]{0:T(128)}, u32[]{:S(2)}) copy-start(s32[4]{0:T(128)} %flags_ref.1) | copy-start | bytes 52
  16.4 8.5 %copy-start.4 = (s32[4]{0:T(128)S(1)}, s32[4]{0:T(128)}, u32[]{:S(2)}) copy-start(s32[4]{0:T(128)} %ranks_ref.1) | copy-start | bytes 52
  32.2 13.6 %collective-permute-start.6 = (f32[4,256,128]{2,1,0:T(8,128)S(1)}, f32[4,256,128]{2,1,0:T(8,128)S(1)}, u32[]{:S(2)}, u32[]{:S(2)}) collective-permute-start(f32[4,256,128]{2,1,0:T(8,128)S(1)} %get-tuple-element.26), channel_id=1, source_target_pairs={{0,1},{1,0},{2,3},{3,2},{4,5},{5,4},{6,7},{7,6},{8,9},{9,8},{10,11... | collective-permute-start | bytes 1572872 | tf_op jit(solution)/shard_map/ppermute | solution.py:319
  32.2 8.1 %collective-permute-start.3 = (f32[1,8,768]{2,1,0:T(8,128)S(1)}, f32[1,8,768]{2,1,0:T(8,128)S(1)}, u32[]{:S(2)}, u32[]{:S(2)}) collective-permute-start(f32[1,8,768]{2,1,0:T(8,128)S(1)} %get-tuple-element.23), channel_id=1, source_target_pairs={{0,4},{4,0},{8,12},{12,8},{1,5},{5,1},{9,13},{13,9},{2,6},{6,2},{1... | collective-permute-start | bytes 73736 | tf_op jit(solution)/shard_map/ppermute | solution.py:322
  37.0 4.7 %collective-permute-start.4 = (f32[1,8,768]{2,1,0:T(8,128)S(1)}, f32[1,8,768]{2,1,0:T(8,128)S(1)}, u32[]{:S(2)}, u32[]{:S(2)}) collective-permute-start(f32[1,8,768]{2,1,0:T(8,128)S(1)} %get-tuple-element.24), channel_id=1, source_target_pairs={{0,8},{4,12},{8,0},{12,4},{1,9},{5,13},{9,1},{13,5},{2,10},{6,14},... | collective-permute-start | bytes 73736 | tf_op jit(solution)/shard_map/ppermute | solution.py:322
  39.0 5.6 %collective-permute-start.5 = (f32[1,8,768]{2,1,0:T(8,128)S(1)}, f32[1,8,768]{2,1,0:T(8,128)S(1)}, u32[]{:S(2)}, u32[]{:S(2)}) collective-permute-start(f32[1,8,768]{2,1,0:T(8,128)S(1)} %get-tuple-element.25), channel_id=1, source_target_pairs={{0,12},{4,8},{8,4},{12,0},{1,13},{5,9},{9,5},{13,1},{2,14},{6,10},... | collective-permute-start | bytes 73736 | tf_op jit(solution)/shard_map/ppermute | solution.py:322
  40.3 4.6 %collective-permute-start.7 = (f32[1,8,768]{2,1,0:T(8,128)S(1)}, f32[1,8,768]{2,1,0:T(8,128)S(1)}, u32[]{:S(2)}, u32[]{:S(2)}) collective-permute-start(f32[1,8,768]{2,1,0:T(8,128)S(1)} %get-tuple-element.22.rest_0_), channel_id=1, source_target_pairs={{0,1},{1,0},{2,3},{3,2},{4,5},{5,4},{6,7},{7,6},{8,9},{9,8},{10,11... | collective-permute-start | bytes 73736 | tf_op jit(solution)/shard_map/ppermute | solution.py:323
  40.4 4.6 %collective-permute-start.8 = (f32[1,8,768]{2,1,0:T(8,128)S(1)}, f32[1,8,768]{2,1,0:T(8,128)S(1)}, u32[]{:S(2)}, u32[]{:S(2)}) collective-permute-start(f32[1,8,768]{2,1,0:T(8,128)S(1)} %collective-permute-done.3.rest_1_), channel_id=1, source_target_pairs={{0,1},{1,0},{2,3},{3,2},{4,5},{5,4},{6,7},{7,6},{8,9},{9,8},{10,11... | collective-permute-start | bytes 73736 | tf_op jit(solution)/shard_map/ppermute | solution.py:323
  41.7 3.3 %collective-permute-start.9 = (f32[1,8,768]{2,1,0:T(8,128)S(1)}, f32[1,8,768]{2,1,0:T(8,128)S(1)}, u32[]{:S(2)}, u32[]{:S(2)}) collective-permute-start(f32[1,8,768]{2,1,0:T(8,128)S(1)} %collective-permute-done.4.rest_2_), channel_id=1, source_target_pairs={{0,1},{1,0},{2,3},{3,2},{4,5},{5,4},{6,7},{7,6},{8,9},{9,8},{10,11... | collective-permute-start | bytes 73736 | tf_op jit(solution)/shard_map/ppermute | solution.py:323
  44.6 1.2 %collective-permute-start.10 = (f32[1,8,768]{2,1,0:T(8,128)S(1)}, f32[1,8,768]{2,1,0:T(8,128)S(1)}, u32[]{:S(2)}, u32[]{:S(2)}) collective-permute-start(f32[1,8,768]{2,1,0:T(8,128)S(1)} %collective-permute-done.5.rest_3_), channel_id=1, source_target_pairs={{0,1},{1,0},{2,3},{3,2},{4,5},{5,4},{6,7},{7,6},{8,9},{9,8},{10,11... | collective-permute-start | bytes 73736 | tf_op jit(solution)/shard_map/ppermute | solution.py:323

commit v6 on v5

--- a/solution.py
+++ b/solution.py
@@ -17,6 +17,7 @@
 NN = (((1,), (0,)), ((), ()))
 TN = (((0,), (0,)), ((), ()))
 VMEM_LIMIT = 48 * 1024 * 1024
+CUT_LIMIT = (64 * 1024 - 768) * 1024
 
 
 def dot(left, right, dims):
@@ -118,20 +119,23 @@
         fill_weights(phase_ref, 0, beams, first + o + 1, out_ref.at[o])
 
 
-def fill_cov(factor, blocks, own_at, across_ref, along_ref, rotated_ref, high_ref, low_ref):
+def cov_terms(x, across):
+    rotated = -turned(x.astype(F32), 0)
+    return dot(across, x, NN), dot(across, rotated.astype(BF16), NN)
+
+
+def early_cov_kernel(*refs):
+    blocks, (cov_ref, across_ref, along_ref, rotated_ref) = refs[:-4], refs[-4:]
     rows, width = blocks[0].shape[1:]
-    for i, block in enumerate(blocks):
-        x = block[own_at]
-        at = slice(i * rows, (i + 1) * rows)
-        along_ref[at] = x
-        rotated_ref[at] = -turned(x.astype(F32), 0).astype(BF16)
-        across_ref[:, at] = x.T
-    step = width // 2
-    for part, right in enumerate((along_ref, rotated_ref)):
-        for first in range(0, width, step):
-            total = dot(across_ref[first : first + step], right[...], NN) * factor
-            at = slice(part * width + first, part * width + first + step)
-            high_ref[at], low_ref[at] = split(total)
+    for o in range(cov_ref.shape[0]):
+        for i, block in enumerate(blocks):
+            x = block[o]
+            at = slice(i * rows, (i + 1) * rows)
+            along_ref[at] = x
+            rotated_ref[at] = -turned(x.astype(F32), 0).astype(BF16)
+            across_ref[o, :, at] = x.T
+        cov_ref[o, 0] = dot(across_ref[o], along_ref[...], NN)
+        cov_ref[o, 1] = dot(across_ref[o], rotated_ref[...], NN)
 
 
 def cov_times(real, imag, high_ref, low_ref):
@@ -167,16 +171,20 @@
     return real_v * factor, imag_v * factor
 
 
-def subspace_kernel(tm, own, factor, beams_ref, start_ref, flags_ref, ranks_ref, weights_ref, *rest):
-    blocks, outs, scratch = rest[:tm], rest[tm + 1 : 2 * tm + 1], rest[2 * tm + 1 :]
-    across_ref, along_ref, rotated_ref, high_ref, low_ref = scratch
+def subspace_kernel(
+    tm, own, factor, beams_ref, start_ref, flags_ref, ranks_ref, weights_ref, cov_ref, across_ref, last_ref, *rest
+):
+    outs, (high_ref, low_ref) = rest[1 : tm + 1], rest[tm + 1 :]
     vectors, width = start_ref.shape[3], start_ref.shape[4]
-    rows = blocks[0].shape[1]
+    rows = last_ref.shape[1]
     tm_index = lax.axis_index("tm")
     beams = weights_ref.shape[1] // 2
     for o in range(own):
         chan = tm_index * own + o
-        fill_cov(factor, blocks, o, *scratch)
+        across = last_ref[o].T
+        for part, term in enumerate(cov_terms(last_ref[o], across)):
+            at = slice(part * width, (part + 1) * width)
+            high_ref[at], low_ref[at] = split((cov_ref[o, part] + term) * factor)
         real_q = start_ref[0, chan, 0]
         imag_q = start_ref[0, chan, 1]
         for sweep in range(ITERS):
@@ -191,13 +199,12 @@
         product = product[: 2 * vectors] + product[2 * vectors :]
         real_w = product[:vectors, :beams] - product[vectors:, beams:]
         imag_w = product[:vectors, beams:] + product[vectors:, :beams]
-        product = dot(both, across_ref[...], NN)
-        product = product[: 2 * vectors] + product[2 * vectors :]
-        series = [
-            product[:vectors, i * rows : (i + 1) * rows]
-            + turned(product[vectors:, i * rows : (i + 1) * rows], 1)
-            for i in range(tm)
-        ]
+        series = []
+        for i in range(tm):
+            block = across_ref[o, :, i * rows : (i + 1) * rows] if i < tm - 1 else across
+            product = dot(both, block, NN)
+            product = product[: 2 * vectors] + product[2 * vectors :]
+            series.append(product[:vectors] + turned(product[vectors:], 1))
         first, second = orders(tm)
         for x, out in enumerate(outs):
             a, b = first.index(x), second.index(x)
@@ -228,22 +235,21 @@
     return squares[pl.ds(0, samples, 2), :] + squares[pl.ds(1, samples, 2), :]
 
 
-def first_kernel(own, raw_ref, *rest):
-    packets, (out_ref, squares) = rest[:-2], rest[-2:]
-    for x, ref in enumerate(packets):
+def first_kernel(own, xs, raw_ref, *rest):
+    packets, outs, squares = rest[: len(xs)], rest[-1 - len(xs) : -1], rest[-1]
+    for x, ref, out_ref in zip(xs, packets, outs):
+        for o in range(own):
+            squares[...] = nulled_squares(raw_ref[(lax.axis_index("tm") ^ x) * own + o], ref.at[o])
+            out_ref[o] = pair_sums(squares)
+
+
+def second_kernel(tm, own, raw_ref, *rest):
+    firsts, packets, (out_ref, squares, powers) = rest[:tm], rest[tm : 2 * tm], rest[2 * tm :]
+    for x, (first_ref, ref) in enumerate(zip(firsts, packets)):
         for o in range(own):
             chan = (lax.axis_index("tm") ^ x) * own + o
             squares[...] = nulled_squares(raw_ref[chan], ref.at[o])
-            out_ref[chan] = pair_sums(squares)
-
-
-def second_kernel(own, first_ref, raw_ref, *rest):
-    packets, (out_ref, squares, powers) = rest[:-3], rest[-3:]
-    for x, ref in enumerate(packets):
-        for o in range(own):
-            chan = (lax.axis_index("tm") ^ x) * own + o
-            squares[...] = nulled_squares(raw_ref[chan], ref.at[o])
-            powers[chan] = first_ref[chan] + pair_sums(squares)
+            powers[chan] = first_ref[o] + pair_sums(squares)
     for chan in range(powers.shape[0]):
         out_ref[:, chan, :] = powers[chan]
 
@@ -272,7 +278,7 @@
         in_specs=[pl.BlockSpec(memory_space=pltpu.HBM)],
         out_specs=[whole] * tm,
         scratch_shapes=[pltpu.SemaphoreType.DMA((tm,))],
-        compiler_params=params,
+        compiler_params=pltpu.CompilerParams(vmem_limit_bytes=CUT_LIMIT),
     )(voltages)
     pieces = [piece.transpose(1, 0, 2, 3).reshape(own, rows, width) for piece in cut]
     blocks = pieces[:1] + [
@@ -299,51 +305,65 @@
         cost_estimate=cost(20 * own * beams * width, 8 * own * beams * width),
     )(phase_index)
 
+    early = (tm - 1) * rows
+    cov, across = pl.pallas_call(
+        early_cov_kernel,
+        out_shape=[
+            jax.ShapeDtypeStruct((own, 2, width, width), F32),
+            jax.ShapeDtypeStruct((own, width, early), BF16),
+        ],
+        in_specs=[whole] * (tm - 1),
+        out_specs=[whole] * 2,
+        scratch_shapes=[pltpu.VMEM((early, width), BF16)] * 2,
+        compiler_params=params,
+        cost_estimate=cost(2 * own * early * width * width, 8 * own * width * width),
+    )(*blocks[:-1])
+
     other, *packets = pl.pallas_call(
         functools.partial(subspace_kernel, tm, own, factor),
         out_shape=[raw] + [jax.ShapeDtypeStruct((own, vectors, rows + 2 * beams), F32)] * tm,
-        in_specs=[unread, whole, scalars, scalars] + [whole] * (1 + tm),
+        in_specs=[unread, whole, scalars, scalars] + [whole] * 4,
         out_specs=[unread] + [whole] * tm,
         input_output_aliases={0: 0},
-        scratch_shapes=[
-            pltpu.VMEM((width, tm * rows), BF16),
-            pltpu.VMEM((tm * rows, width), BF16),
-            pltpu.VMEM((tm * rows, width), BF16),
-            pltpu.VMEM((2 * width, width), BF16),
-            pltpu.VMEM((2 * width, width), BF16),
-        ],
+        scratch_shapes=[pltpu.VMEM((2 * width, width), BF16)] * 2,
         compiler_params=params,
         cost_estimate=cost(32 * own * vectors * tm * samples * width, 8 * own * width * width),
-    )(other, start_block, flags, ranks, own_weights, *blocks)
+    )(other, start_block, flags, ranks, own_weights, cov, across, blocks[-1])
     cores = [(0, 1), (1, 0)]
     theirs = lax.ppermute(other, "pol", cores)
+
+    def first(xs, *before):
+        return pl.pallas_call(
+            functools.partial(first_kernel, own, xs),
+            out_shape=[jax.ShapeDtypeStruct((own, samples, half), F32)] * len(xs),
+            in_specs=[whole] * (1 + len(xs)) + [unread] * len(before),
+            out_specs=[whole] * len(xs),
+            scratch_shapes=[pltpu.VMEM((rows, half), F32)],
+            compiler_params=params,
+            cost_estimate=cost(len(xs) * own * rows * 6 * vectors * half, 8 * own * rows * half),
+        )(mine, *[arrived[x] for x in xs], *before)
+
     arrived = list(packets)
     for x in reversed(range(1, tm)):
         arrived[x] = lax.ppermute(packets[x], "tm", [(z, z ^ x) for z in range(tm)])
     swapped = [lax.ppermute(packet, "pol", cores) for packet in arrived]
-
-    finish = cost(2 * chan_dev * rows * 6 * vectors * half, 8 * chan_dev * rows * half)
-    part = pl.pallas_call(
-        functools.partial(first_kernel, own),
-        out_shape=jax.ShapeDtypeStruct((chan_dev, samples, half), F32),
-        in_specs=[whole] * (1 + tm),
-        out_specs=whole,
-        scratch_shapes=[pltpu.VMEM((rows, half), F32)],
-        compiler_params=params,
-        cost_estimate=finish,
-    )(mine, *arrived)
+    firsts = [None] * tm
+    firsts[0], firsts[-1] = first([0, tm - 1])
+    for x in reversed(range(1, tm - 1)):
+        (firsts[x],) = first([x], firsts[x + 1])
+
     return pl.pallas_call(
-        functools.partial(second_kernel, own),
+        functools.partial(second_kernel, tm, own),
         out_shape=jax.ShapeDtypeStruct((samples, chan_dev, half), F32),
-        in_specs=[whole] * (2 + tm),
+        in_specs=[whole] * (1 + 2 * tm),
         out_specs=whole,
         scratch_shapes=[
             pltpu.VMEM((rows, half), F32),
             pltpu.VMEM((chan_dev, samples, half), F32),
         ],
         compiler_params=params,
-        cost_estimate=finish,
-    )(part, theirs, *swapped)
+        cost_estimate=cost(2 * chan_dev * rows * 6 * vectors * half, 8 * chan_dev * rows * half),
+    )(theirs, *firsts, *swapped)
 
 
 def solution(mesh):

time: 47.2 us -> 48.5 us (1.028)
  Pallas kernels: 16.9 us -> 19.4 us
  local copies, waits for them, and re-layouts: 2.4 us -> 4.23 us
  waiting for transfers between devices: 13 us -> 11.3 us
  starting transfers between devices: 14.5 us -> 13.2 us
    another operation x4, local copies, waits for them, and re-layouts: 0.41 us -> 4.21 us  [local(): piece.transpose(1, 0, 2, 3).reshape(own, rows, width)]
    pallas_call x1, Pallas kernels: 0.23 us -> 2.26 us  [local(): pl.pallas_call(functools.partial(cut_kernel, tm, own), out_shape=[jax.Sha...]
    unnamed x10 -> x8, local copies, waits for them, and re-layouts: 1.99 us -> 0.02 us
    ppermute x3, waiting for transfers between devices: 8.51 us -> 6.77 us  [local(): lax.ppermute(piece, ('tm', 'pol'), route)]
    pallas_call x2 -> x5, Pallas kernels: 1.56 us -> 3.1 us  [the longest x1 1.21 us: local(): pl.pallas_call(functools.partial(second_kernel, tm, own), out_shape=jax.S...]
    ppermute x3, starting transfers between devices: 8.11 us -> 6.78 us  [local(): arrived[x] = lax.ppermute(packets[x], 'tm', [(z, z ^ x) for z in range(tm)])]
    pallas_call x1, Pallas kernels: 7.2 us -> 6.12 us  [local(): pl.pallas_call(functools.partial(subspace_kernel, tm, own, factor), out_s...]
    ppermute x4, waiting for transfers between devices: 0.81 us -> 0.3 us  [local(): swapped = [lax.ppermute(packet, 'pol', cores) for packet in arrived]]
  transfers between devices with their start and end apart: 11 -> 11, of which waited for: 5 -> 5; matrix products, arithmetic and copies ran while one was open for 1% -> 7% of each run, Pallas kernels for 18% -> 20%
where the time goes in v6:
time: 48.5 us; the launch traced here: 48.3 us
  Pallas kernels  19.4 us (40%)
  starting transfers between devices  13.2 us (27%)
  waiting for transfers between devices  11.3 us (23%)
  local copies, waits for them, and re-layouts  4.23 us (9%)
    pallas_call x1, Pallas kernels, local(): pl.pallas_call(functools.partial(raw_beams_kernel, tm, own), out_shape=[r...  6.84 us
    ppermute x3, starting transfers between devices, local(): arrived[x] = lax.ppermute(packets[x], 'tm', [(z, z ^ x) for z in range(tm)])  6.78 us
    ppermute x3, waiting for transfers between devices, local(): lax.ppermute(piece, ('tm', 'pol'), route)  6.77 us
    pallas_call x1, Pallas kernels, local(): pl.pallas_call(functools.partial(subspace_kernel, tm, own, factor), out_s...  6.12 us
    ppermute x3, starting transfers between devices, local(): lax.ppermute(piece, ('tm', 'pol'), route)  5.81 us
    ppermute x3, waiting for transfers between devices, local(): arrived[x] = lax.ppermute(packets[x], 'tm', [(z, z ^ x) for z in range(tm)])  4.21 us
    another operation x4, local copies, waits for them, and re-layouts, local(): piece.transpose(1, 0, 2, 3).reshape(own, rows, width)  4.21 us
    pallas_call x1, Pallas kernels, local(): pl.pallas_call(functools.partial(cut_kernel, tm, own), out_shape=[jax.Sha...  2.26 us
  transfers between devices with their start and end apart: 11, of which 5 were waited for; matrix products, arithmetic and copies ran while one was open for 7% of the time, Pallas kernels for 20%

profile of v6, /device:TPU:0, one launch (start us, length us, event | category | flops | bytes accessed | tf_op | source)
XLA Modules:
  0.0 48.3 jit_solution(6495341543976371564)
XLA Ops:
  0.0 0.0 copy-start
  0.0 2.3 %shard_map.55 = (bf16[128,1,2,512]{3,2,1,0:T(2,128)(2,1)}, bf16[128,1,2,512]{3,2,1,0:T(2,128)(2,1)}, bf16[128,1,2,512]{3,2,1,0:T(2,128)(2,1)}, bf16[128,1,2,512]{3,2,1,0:T(2,128)(2,1)}) custom-call(bf16[128,1,4,2,512]{4,3,2,1,0:T(2,128)(2,1)} %voltages_ref.1), custom_call_target="tpu_custom_call" | custom-call | tf_op jit(solution)/shard_map/pallas_call | solution.py:275
  2.3 1.1 %reshape_transpose.13.rest_1_ = bf16[1,256,512]{2,1,0:T(8,128)(2,1)S(1)} reshape(bf16[128,1,2,512]{3,2,1,0:T(2,128)(2,1)} %get-tuple-element.21) | data formatting | bytes 524288 | tf_op jit(solution)/shard_map/reshape;transpose | solution.py:283
  3.3 4.1 %collective-permute-start = (bf16[1,256,512]{2,1,0:T(8,128)(2,1)S(1)}, bf16[1,256,512]{2,1,0:T(8,128)(2,1)S(1)}, u32[]{:S(2)}, u32[]{:S(2)}) collective-permute-start(bf16[1,256,512]{2,1,0:T(8,128)(2,1)S(1)} %reshape_transpose.13.rest_1_), channel_id=1, source_target_pairs={{0,8},{1,9},{4,12},{5,13},{8,0},{9,1},{12,4},{13,5},{2,10},{3,11},... | collective-permute-start | bytes 786440 | tf_op jit(solution)/shard_map/ppermute | solution.py:285
  7.4 1.1 %reshape_transpose.14.rest_2_ = bf16[1,256,512]{2,1,0:T(8,128)(2,1)S(1)} reshape(bf16[128,1,2,512]{3,2,1,0:T(2,128)(2,1)} %get-tuple-element.22) | data formatting | bytes 524288 | tf_op jit(solution)/shard_map/reshape;transpose | solution.py:283
  8.5 1.6 %collective-permute-start.1 = (bf16[1,256,512]{2,1,0:T(8,128)(2,1)S(1)}, bf16[1,256,512]{2,1,0:T(8,128)(2,1)S(1)}, u32[]{:S(2)}, u32[]{:S(2)}) collective-permute-start(bf16[1,256,512]{2,1,0:T(8,128)(2,1)S(1)} %reshape_transpose.14.rest_2_), channel_id=1, source_target_pairs={{0,4},{1,13},{4,0},{5,9},{8,12},{9,5},{12,8},{13,1},{2,6},{3,15},{... | collective-permute-start | bytes 786440 | tf_op jit(solution)/shard_map/ppermute | solution.py:285
  10.1 1.1 %reshape_transpose.15.rest_3_ = bf16[1,256,512]{2,1,0:T(8,128)(2,1)S(1)} reshape(bf16[128,1,2,512]{3,2,1,0:T(2,128)(2,1)} %get-tuple-element.23) | data formatting | bytes 524288 | tf_op jit(solution)/shard_map/reshape;transpose | solution.py:283
  11.2 0.1 collective-permute-start.2
  11.3 1.1 %reshape_transpose.12.rest_0_.refs_0_ = bf16[1,256,512]{2,1,0:T(8,128)(2,1)S(1)} reshape(bf16[128,1,2,512]{3,2,1,0:T(2,128)(2,1)} %get-tuple-element.20) | data formatting | bytes 524288 | tf_op jit(solution)/shard_map/reshape;transpose | solution.py:283
  12.3 0.0 copy-done
  12.3 1.1 %shard_map.57.weights_ref = bf16[1,512,512]{2,1,0:T(8,128)(2,1)S(1)} custom-call(s32[256,512]{1,0:T(8,128)S(1)} %copy-done), custom_call_target="tpu_custom_call" | custom-call | flops 5242880 | bytes 1048576 | tf_op jit(solution)/shard_map/pallas_call | solution.py:299
  13.4 0.0 copy-start.1
  13.4 0.0 copy-start.2
  13.4 0.0 copy-start.3
  13.4 6.8 %shard_map.56 = (f32[4,256,128]{2,1,0:T(8,128)S(1)}, f32[4,256,128]{2,1,0:T(8,128)S(1)}) custom-call(s32[256,512]{1,0:T(8,128)S(1)} %copy-done, bf16[1,256,512]{2,1,0:T(8,128)(2,1)S(1)} %reshape_transpose.12.rest_0_.refs_0_, bf16[1,256,512]{2,1,0:T(8,128)(2,1)S(1)} %reshape_transpose.13.rest_1_, bf16[1,256,512]{2,1,0:T(8,128)(2,1)S(1)} %reshape_transpose.14.rest_2_, ...), custom_call_target="tpu_custom_call" | custom-call | flops 536870912 | bytes 2097152 | tf_op jit(solution)/shard_map/pallas_call | solution.py:289
  20.3 4.2 %collective-permute-done.refs_1_ = bf16[1,256,512]{2,1,0:T(8,128)(2,1)S(1)} collective-permute-done((bf16[1,256,512]{2,1,0:T(8,128)(2,1)S(1)}, bf16[1,256,512]{2,1,0:T(8,128)(2,1)S(1)}, u32[]{:S(2)}, u32[]{:S(2)}) %collective-permute-start) | collective-permute-done | bytes 262176 | tf_op jit(solution)/shard_map/ppermute | solution.py:285
  24.5 2.6 %collective-permute-done.1.refs_2_ = bf16[1,256,512]{2,1,0:T(8,128)(2,1)S(1)} collective-permute-done((bf16[1,256,512]{2,1,0:T(8,128)(2,1)S(1)}, bf16[1,256,512]{2,1,0:T(8,128)(2,1)S(1)}, u32[]{:S(2)}, u32[]{:S(2)}) %collective-permute-start.1) | collective-permute-done | bytes 262176 | tf_op jit(solution)/shard_map/ppermute | solution.py:285
  27.1 1.0 %shard_map.58 = (f32[1,2,512,512]{3,2,1,0:T(8,128)S(1)}, bf16[1,512,768]{2,1,0:T(8,128)(2,1)S(1)}) custom-call(bf16[1,256,512]{2,1,0:T(8,128)(2,1)S(1)} %reshape_transpose.12.rest_0_.refs_0_, bf16[1,256,512]{2,1,0:T(8,128)(2,1)S(1)} %collective-permute-done.refs_1_, bf16[1,256,512]{2,1,0:T(8,128)(2,1)S(1)} %collective-permute-done.1.refs_2_), custom_call_target="tpu_custom_call" | custom-call | flops 805306368 | bytes 2097152 | tf_op jit(solution)/shard_map/pallas_call | solution.py:309
  28.1 0.0 collective-permute-done.2.last_ref
  28.1 0.0 copy-done.1
  28.1 0.0 copy-done.2
  28.1 0.0 copy-done.3
  28.1 6.1 %shard_map.59 = (f32[4,256,128]{2,1,0:T(8,128)S(1)}, f32[1,8,768]{2,1,0:T(8,128)S(1)}, f32[1,8,768]{2,1,0:T(8,128)S(1)}, f32[1,8,768]{2,1,0:T(8,128)S(1)}, f32[1,8,768]{2,1,0:T(8,128)S(1)}) custom-call(f32[4,256,128]{2,1,0:T(8,128)S(1)} %get-tuple-element.24.beams_ref, f32[1,4,2,8,512]{4,3,2,1,0:T(8,128)S(1)} %copy-done.1, ...), custom_call_target="tpu_custom_call", output_to_operand_aliasing={{0}: (0, {})} | custom-call | flops 134217728 | bytes 2097152 | tf_op jit(solution)/shard_map/pallas_call | solution.py:322
  34.3 0.1 collective-permute-start.3
  34.4 1.9 %collective-permute-start.4 = (f32[1,8,768]{2,1,0:T(8,128)S(1)}, f32[1,8,768]{2,1,0:T(8,128)S(1)}, u32[]{:S(2)}, u32[]{:S(2)}) collective-permute-start(f32[1,8,768]{2,1,0:T(8,128)S(1)} %get-tuple-element.30), channel_id=1, source_target_pairs={{0,12},{4,8},{8,4},{12,0},{1,13},{5,9},{9,5},{13,1},{2,14},{6,10},... | collective-permute-start | bytes 73736 | tf_op jit(solution)/shard_map/ppermute | solution.py:348
  36.2 4.9 %collective-permute-start.5 = (f32[1,8,768]{2,1,0:T(8,128)S(1)}, f32[1,8,768]{2,1,0:T(8,128)S(1)}, u32[]{:S(2)}, u32[]{:S(2)}) collective-permute-start(f32[1,8,768]{2,1,0:T(8,128)S(1)} %get-tuple-element.32), channel_id=1, source_target_pairs={{0,4},{4,0},{8,12},{12,8},{1,5},{5,1},{9,13},{13,9},{2,6},{6,2},{1... | collective-permute-start | bytes 73736 | tf_op jit(solution)/shard_map/ppermute | solution.py:348
  41.1 0.0 collective-permute-start.6
  41.1 0.0 collective-permute-start.7
  41.1 0.0 collective-permute-done.4.rest_1_
  41.1 0.5 %collective-permute-start.10 = (f32[1,8,768]{2,1,0:T(8,128)S(1)}, f32[1,8,768]{2,1,0:T(8,128)S(1)}, u32[]{:S(2)}, u32[]{:S(2)}) collective-permute-start(f32[1,8,768]{2,1,0:T(8,128)S(1)} %collective-permute-done.4.rest_1_), channel_id=1, source_target_pairs={{0,1},{1,0},{2,3},{3,2},{4,5},{5,4},{6,7},{7,6},{8,9},{9,8},{10,11... | collective-permute-start | bytes 73736 | tf_op jit(solution)/shard_map/ppermute | solution.py:349
  41.6 1.3 %collective-permute-done.5.rest_0_ = f32[1,8,768]{2,1,0:T(8,128)S(1)} collective-permute-done((f32[1,8,768]{2,1,0:T(8,128)S(1)}, f32[1,8,768]{2,1,0:T(8,128)S(1)}, u32[]{:S(2)}, u32[]{:S(2)}) %collective-permute-start.5) | collective-permute-done | bytes 24608 | tf_op jit(solution)/shard_map/ppermute | solution.py:348
  42.9 0.0 collective-permute-start.8
  42.9 2.9 %collective-permute-done.6.rest_0_ = f32[1,8,768]{2,1,0:T(8,128)S(1)} collective-permute-done((f32[1,8,768]{2,1,0:T(8,128)S(1)}, f32[1,8,768]{2,1,0:T(8,128)S(1)}, u32[]{:S(2)}, u32[]{:S(2)}) %collective-permute-start.6) | collective-permute-done | bytes 24608 | tf_op jit(solution)/shard_map/ppermute | solution.py:348
  45.9 0.0 collective-permute-start.9
  45.9 0.3 shard_map.60
  46.2 0.3 shard_map.61.rest_1_.rest_2_
  46.5 0.3 shard_map.62.rest_1_
  46.7 0.0 collective-permute-done.7.rest_4_
  46.7 0.0 collective-permute-done.10.rest_7_
  46.8 0.0 collective-permute-done.8.rest_5_
  46.8 0.3 collective-permute-done.9.rest_6_
  47.1 0.0 collective-permute-done.3.raw_ref
  47.1 1.2 %shard_map.63 = f32[128,4,128]{2,1,0:T(4,128)} custom-call(f32[4,256,128]{2,1,0:T(8,128)S(1)} %collective-permute-done.3.raw_ref, f32[1,128,128]{2,1,0:T(8,128)S(1)} %get-tuple-element.31.rest_0_, f32[1,128,128]{2,1,0:T(8,128)S(1)} %shard_map.62.rest_1_, f32[1,128,128]{2,1,0:T(8,128)S(1)} %shard_map.61.rest_1_.rest_2_, ...), custom_call_target="tpu_custom_call" | custom-call | flops 25165824 | bytes 1048576 | tf_op jit(solution)/shard_map/pallas_call | solution.py:355
Async XLA Ops:
  0.0 12.3 %copy-start = (s32[256,512]{1,0:T(8,128)S(1)}, s32[256,512]{1,0:T(8,128)}, u32[]{:S(2)}) copy-start(s32[256,512]{1,0:T(8,128)} %phase_ref.3) | copy-start | bytes 1572868
  3.3 21.2 %collective-permute-start = (bf16[1,256,512]{2,1,0:T(8,128)(2,1)S(1)}, bf16[1,256,512]{2,1,0:T(8,128)(2,1)S(1)}, u32[]{:S(2)}, u32[]{:S(2)}) collective-permute-start(bf16[1,256,512]{2,1,0:T(8,128)(2,1)S(1)} %reshape_transpose.13.rest_1_), channel_id=1, source_target_pairs={{0,8},{1,9},{4,12},{5,13},{8,0},{9,1},{12,4},{13,5},{2,10},{3,11},... | collective-permute-start | bytes 786440 | tf_op jit(solution)/shard_map/ppermute | solution.py:285
  8.5 18.6 %collective-permute-start.1 = (bf16[1,256,512]{2,1,0:T(8,128)(2,1)S(1)}, bf16[1,256,512]{2,1,0:T(8,128)(2,1)S(1)}, u32[]{:S(2)}, u32[]{:S(2)}) collective-permute-start(bf16[1,256,512]{2,1,0:T(8,128)(2,1)S(1)} %reshape_transpose.14.rest_2_), channel_id=1, source_target_pairs={{0,4},{1,13},{4,0},{5,9},{8,12},{9,5},{12,8},{13,1},{2,6},{3,15},{... | collective-permute-start | bytes 786440 | tf_op jit(solution)/shard_map/ppermute | solution.py:285
  11.2 16.9 %collective-permute-start.2 = (bf16[1,256,512]{2,1,0:T(8,128)(2,1)S(1)}, bf16[1,256,512]{2,1,0:T(8,128)(2,1)S(1)}, u32[]{:S(2)}, u32[]{:S(2)}) collective-permute-start(bf16[1,256,512]{2,1,0:T(8,128)(2,1)S(1)} %reshape_transpose.15.rest_3_), channel_id=1, source_target_pairs={{0,12},{1,5},{4,8},{5,1},{8,4},{9,13},{12,0},{13,9},{2,14},{3,7},{... | collective-permute-start | bytes 786440 | tf_op jit(solution)/shard_map/ppermute | solution.py:285
  13.4 14.7 %copy-start.1 = (f32[1,4,2,8,512]{4,3,2,1,0:T(8,128)S(1)}, f32[1,4,2,8,512]{4,3,2,1,0:T(8,128)}, u32[]{:S(2)}) copy-start(f32[1,4,2,8,512]{4,3,2,1,0:T(8,128)} %start_ref.1) | copy-start | bytes 393220
  13.4 14.7 %copy-start.2 = (s32[4]{0:T(128)S(1)}, s32[4]{0:T(128)}, u32[]{:S(2)}) copy-start(s32[4]{0:T(128)} %flags_ref.1) | copy-start | bytes 52
  13.4 14.7 %copy-start.3 = (s32[4]{0:T(128)S(1)}, s32[4]{0:T(128)}, u32[]{:S(2)}) copy-start(s32[4]{0:T(128)} %ranks_ref.1) | copy-start | bytes 52
  34.3 12.8 %collective-permute-start.3 = (f32[4,256,128]{2,1,0:T(8,128)S(1)}, f32[4,256,128]{2,1,0:T(8,128)S(1)}, u32[]{:S(2)}, u32[]{:S(2)}) collective-permute-start(f32[4,256,128]{2,1,0:T(8,128)S(1)} %get-tuple-element.27), channel_id=1, source_target_pairs={{0,1},{1,0},{2,3},{3,2},{4,5},{5,4},{6,7},{7,6},{8,9},{9,8},{10,11... | collective-permute-start | bytes 1572872 | tf_op jit(solution)/shard_map/ppermute | solution.py:333
  34.4 6.8 %collective-permute-start.4 = (f32[1,8,768]{2,1,0:T(8,128)S(1)}, f32[1,8,768]{2,1,0:T(8,128)S(1)}, u32[]{:S(2)}, u32[]{:S(2)}) collective-permute-start(f32[1,8,768]{2,1,0:T(8,128)S(1)} %get-tuple-element.30), channel_id=1, source_target_pairs={{0,12},{4,8},{8,4},{12,0},{1,13},{5,9},{9,5},{13,1},{2,14},{6,10},... | collective-permute-start | bytes 73736 | tf_op jit(solution)/shard_map/ppermute | solution.py:348
  36.2 6.7 %collective-permute-start.5 = (f32[1,8,768]{2,1,0:T(8,128)S(1)}, f32[1,8,768]{2,1,0:T(8,128)S(1)}, u32[]{:S(2)}, u32[]{:S(2)}) collective-permute-start(f32[1,8,768]{2,1,0:T(8,128)S(1)} %get-tuple-element.32), channel_id=1, source_target_pairs={{0,4},{4,0},{8,12},{12,8},{1,5},{5,1},{9,13},{13,9},{2,6},{6,2},{1... | collective-permute-start | bytes 73736 | tf_op jit(solution)/shard_map/ppermute | solution.py:348
  41.1 4.7 %collective-permute-start.6 = (f32[1,8,768]{2,1,0:T(8,128)S(1)}, f32[1,8,768]{2,1,0:T(8,128)S(1)}, u32[]{:S(2)}, u32[]{:S(2)}) collective-permute-start(f32[1,8,768]{2,1,0:T(8,128)S(1)} %get-tuple-element.33), channel_id=1, source_target_pairs={{0,8},{4,12},{8,0},{12,4},{1,9},{5,13},{9,1},{13,5},{2,10},{6,14},... | collective-permute-start | bytes 73736 | tf_op jit(solution)/shard_map/ppermute | solution.py:348
  41.1 5.6 %collective-permute-start.7 = (f32[1,8,768]{2,1,0:T(8,128)S(1)}, f32[1,8,768]{2,1,0:T(8,128)S(1)}, u32[]{:S(2)}, u32[]{:S(2)}) collective-permute-start(f32[1,8,768]{2,1,0:T(8,128)S(1)} %get-tuple-element.29.rest_0_), channel_id=1, source_target_pairs={{0,1},{1,0},{2,3},{3,2},{4,5},{5,4},{6,7},{7,6},{8,9},{9,8},{10,11... | collective-permute-start | bytes 73736 | tf_op jit(solution)/shard_map/ppermute | solution.py:349
  41.1 5.6 %collective-permute-start.10 = (f32[1,8,768]{2,1,0:T(8,128)S(1)}, f32[1,8,768]{2,1,0:T(8,128)S(1)}, u32[]{:S(2)}, u32[]{:S(2)}) collective-permute-start(f32[1,8,768]{2,1,0:T(8,128)S(1)} %collective-permute-done.4.rest_1_), channel_id=1, source_target_pairs={{0,1},{1,0},{2,3},{3,2},{4,5},{5,4},{6,7},{7,6},{8,9},{9,8},{10,11... | collective-permute-start | bytes 73736 | tf_op jit(solution)/shard_map/ppermute | solution.py:349
  42.9 3.8 %collective-permute-start.8 = (f32[1,8,768]{2,1,0:T(8,128)S(1)}, f32[1,8,768]{2,1,0:T(8,128)S(1)}, u32[]{:S(2)}, u32[]{:S(2)}) collective-permute-start(f32[1,8,768]{2,1,0:T(8,128)S(1)} %collective-permute-done.5.rest_0_), channel_id=1, source_target_pairs={{0,1},{1,0},{2,3},{3,2},{4,5},{5,4},{6,7},{7,6},{8,9},{9,8},{10,11... | collective-permute-start | bytes 73736 | tf_op jit(solution)/shard_map/ppermute | solution.py:349
  45.9 1.2 %collective-permute-start.9 = (f32[1,8,768]{2,1,0:T(8,128)S(1)}, f32[1,8,768]{2,1,0:T(8,128)S(1)}, u32[]{:S(2)}, u32[]{:S(2)}) collective-permute-start(f32[1,8,768]{2,1,0:T(8,128)S(1)} %collective-permute-done.6.rest_0_), channel_id=1, source_target_pairs={{0,1},{1,0},{2,3},{3,2},{4,5},{5,4},{6,7},{7,6},{8,9},{9,8},{10,11... | collective-permute-start | bytes 73736 | tf_op jit(solution)/shard_map/ppermute | solution.py:349

commit v7 on v6

--- a/solution.py
+++ b/solution.py
@@ -17,7 +17,6 @@
 NN = (((1,), (0,)), ((), ()))
 TN = (((0,), (0,)), ((), ()))
 VMEM_LIMIT = 48 * 1024 * 1024
-CUT_LIMIT = (64 * 1024 - 768) * 1024
 
 
 def dot(left, right, dims):
@@ -59,28 +58,17 @@
     lax.fori_loop(0, rows // chunk, body, 0)
 
 
-def orders(tm):
-    far = [*range(2, tm)]
-    return [0, *far[:1], 1, *far[1:]], [0, *far, 1]
-
-
-def shifts(tm, pol):
-    return [jnp.where(pol == 0, a, b) for a, b in zip(*orders(tm))]
-
-
-def routes(tm):
-    return [
-        [(2 * z + p, 2 * (z ^ x[p]) + p) for z in range(tm) for p in range(2)]
-        for x in zip(*orders(tm))
-    ]
+def shifted(by):
+    tm = lax.axis_size("tm")
+    return lax.rem(lax.axis_index("tm") + tm + by, tm)
 
 
 def cut_kernel(tm, own, voltages_ref, *rest):
     pieces, done = rest[:tm], rest[tm]
     copies = []
-    for i, x in enumerate(shifts(tm, lax.axis_index("pol"))):
-        first = (lax.axis_index("tm") ^ x) * own
-        copy = pltpu.make_async_copy(voltages_ref.at[:, 0, pl.ds(first, own)], pieces[i], done.at[i])
+    for i, piece in enumerate(pieces):
+        channels = pl.ds(shifted(i) * own, own)
+        copy = pltpu.make_async_copy(voltages_ref.at[:, 0, channels], piece, done.at[i])
         copy.start()
         copies.append(copy)
     for copy in copies:
@@ -101,9 +89,9 @@
     rows = pieces[0].shape[1]
     pol = lax.axis_index("pol")
     start = lax.axis_index("chan") * tm * own
-    for x, piece in zip(shifts(tm, pol), pieces):
+    for i, piece in enumerate(pieces):
         for o in range(own):
-            chan = (lax.axis_index("tm") ^ x) * own + o
+            chan = shifted(i) * own + o
             for swap, out_ref in enumerate((mine_ref, other_ref)):
                 first = pl.multiple_of((pol ^ swap) * half, half)
                 fill_weights(phase_ref, first, half, start + chan + 1, weights)
@@ -174,7 +162,7 @@
 def subspace_kernel(
     tm, own, factor, beams_ref, start_ref, flags_ref, ranks_ref, weights_ref, cov_ref, across_ref, last_ref, *rest
 ):
-    outs, (high_ref, low_ref) = rest[1 : tm + 1], rest[tm + 1 :]
+    outs, (high_ref, low_ref, series_ref) = rest[1 : tm + 1], rest[tm + 1 :]
     vectors, width = start_ref.shape[3], start_ref.shape[4]
     rows = last_ref.shape[1]
     tm_index = lax.axis_index("tm")
@@ -199,16 +187,14 @@
         product = product[: 2 * vectors] + product[2 * vectors :]
         real_w = product[:vectors, :beams] - product[vectors:, beams:]
         imag_w = product[:vectors, beams:] + product[vectors:, :beams]
-        series = []
         for i in range(tm):
             block = across_ref[o, :, i * rows : (i + 1) * rows] if i < tm - 1 else across
             product = dot(both, block, NN)
             product = product[: 2 * vectors] + product[2 * vectors :]
-            series.append(product[:vectors] + turned(product[vectors:], 1))
-        first, second = orders(tm)
+            series = product[:vectors] + turned(product[vectors:], 1)
+            series_ref[tm_index ^ shifted(-i)] = series
         for x, out in enumerate(outs):
-            a, b = first.index(x), second.index(x)
-            out[o, :, :rows] = jnp.where(lax.axis_index("pol") == 0, series[a], series[b])
+            out[o, :, :rows] = series_ref[x]
             out[o, :, rows : rows + beams] = real_w
             out[o, :, rows + beams :] = imag_w
 
@@ -278,11 +264,11 @@
         in_specs=[pl.BlockSpec(memory_space=pltpu.HBM)],
         out_specs=[whole] * tm,
         scratch_shapes=[pltpu.SemaphoreType.DMA((tm,))],
-        compiler_params=pltpu.CompilerParams(vmem_limit_bytes=CUT_LIMIT),
+        compiler_params=params,
     )(voltages)
     pieces = [piece.transpose(1, 0, 2, 3).reshape(own, rows, width) for piece in cut]
     blocks = pieces[:1] + [
-        lax.ppermute(piece, ("tm", "pol"), route) for piece, route in zip(pieces[1:], routes(tm)[1:])
+        lax.ppermute(pieces[i], "tm", [(z, (z + i) % tm) for z in range(tm)]) for i in range(1, tm)
     ]
 
     raw = jax.ShapeDtypeStruct((chan_dev, rows, half), F32)
@@ -325,7 +311,8 @@
         in_specs=[unread, whole, scalars, scalars] + [whole] * 4,
         out_specs=[unread] + [whole] * tm,
         input_output_aliases={0: 0},
-        scratch_shapes=[pltpu.VMEM((2 * width, width), BF16)] * 2,
+        scratch_shapes=[pltpu.VMEM((2 * width, width), BF16)] * 2
+        + [pltpu.VMEM((tm, vectors, rows), F32)],
         compiler_params=params,
         cost_estimate=cost(32 * own * vectors * tm * samples * width, 8 * own * width * width),
     )(other, start_block, flags, ranks, own_weights, cov, across, blocks[-1])

time: 48.5 us -> 46.1 us (0.951)
  local copies, waits for them, and re-layouts: 4.23 us -> 1.66 us
  Pallas kernels: 19.4 us -> 17.4 us
  starting transfers between devices: 13.2 us -> 15 us
    another operation x4, local copies, waits for them, and re-layouts: 4.21 us -> 0.41 us  [local(): piece.transpose(1, 0, 2, 3).reshape(own, rows, width)]
    pallas_call x1, Pallas kernels: 2.26 us -> 0.23 us  [local(): pl.pallas_call(functools.partial(cut_kernel, tm, own), out_shape=[jax.Sha...]
    ppermute x3, starting transfers between devices: 5.81 us -> 7.13 us  [local(): lax.ppermute(pieces[i], 'tm', [(z, (z + i) % tm) for z in range(tm)])]
    unnamed x8 -> x10, local copies, waits for them, and re-layouts: 0.02 us -> 1.25 us
    ppermute x3, starting transfers between devices: 6.78 us -> 7.82 us  [local(): arrived[x] = lax.ppermute(packets[x], 'tm', [(z, z ^ x) for z in range(tm)])]
    ppermute x3, waiting for transfers between devices: 6.77 us -> 7.34 us  [local(): lax.ppermute(pieces[i], 'tm', [(z, (z + i) % tm) for z in range(tm)])]
    ppermute x4, starting transfers between devices: 0.51 us -> 0.01 us  [local(): swapped = [lax.ppermute(packet, 'pol', cores) for packet in arrived]]
  transfers between devices with their start and end apart: 11 -> 11, of which waited for: 5 -> 5; matrix products, arithmetic and copies ran while one was open for 7% -> 1% of each run, Pallas kernels for 20% -> 21%
where the time goes in v7:
time: 46.1 us; the launch traced here: 46 us
  Pallas kernels  17.4 us (38%)
  starting transfers between devices  15 us (33%)
  waiting for transfers between devices  11.7 us (25%)
  local copies, waits for them, and re-layouts  1.66 us (4%)
    ppermute x3, starting transfers between devices, local(): arrived[x] = lax.ppermute(packets[x], 'tm', [(z, z ^ x) for z in range(tm)])  7.82 us
    ppermute x3, waiting for transfers between devices, local(): lax.ppermute(pieces[i], 'tm', [(z, (z + i) % tm) for z in range(tm)])  7.34 us
    ppermute x3, starting transfers between devices, local(): lax.ppermute(pieces[i], 'tm', [(z, (z + i) % tm) for z in range(tm)])  7.13 us
    pallas_call x1, Pallas kernels, local(): pl.pallas_call(functools.partial(raw_beams_kernel, tm, own), out_shape=[r...  6.85 us
    pallas_call x1, Pallas kernels, local(): pl.pallas_call(functools.partial(subspace_kernel, tm, own, factor), out_s...  6.15 us
    ppermute x3, waiting for transfers between devices, local(): arrived[x] = lax.ppermute(packets[x], 'tm', [(z, z ^ x) for z in range(tm)])  4.08 us
    unnamed x10, local copies, waits for them, and re-layouts  1.25 us
    pallas_call x1, Pallas kernels, local(): pl.pallas_call(functools.partial(second_kernel, tm, own), out_shape=jax.S...  1.21 us
  transfers between devices with their start and end apart: 11, of which 5 were waited for; matrix products, arithmetic and copies ran while one was open for 1% of the time, Pallas kernels for 21%

profile of v7, /device:TPU:0, one launch (start us, length us, event | category | flops | bytes accessed | tf_op | source)
XLA Modules:
  0.0 46.0 jit_solution(4286875977876409492)
XLA Ops:
  0.0 0.0 copy-start
  0.0 1.2 %copy-done = bf16[128,1,4,2,512]{4,3,2,1,0:T(2,128)(2,1)S(1)} copy-done((bf16[128,1,4,2,512]{4,3,2,1,0:T(2,128)(2,1)S(1)}, bf16[128,1,4,2,512]{4,3,2,1,0:T(2,128)(2,1)}, u32[]{:S(2)}) %copy-start) | copy-done | bytes 1048600
  1.2 0.0 copy-start.1
  1.2 0.2 shard_map.55
  1.5 0.1 reshape_transpose.13.rest_1_
  1.6 3.1 %collective-permute-start = (bf16[1,256,512]{2,1,0:T(8,128)(2,1)S(1)}, bf16[1,256,512]{2,1,0:T(8,128)(2,1)S(1)}, u32[]{:S(2)}, u32[]{:S(2)}) collective-permute-start(bf16[1,256,512]{2,1,0:T(8,128)(2,1)S(1)} %reshape_transpose.13.rest_1_), channel_id=1, source_target_pairs={{0,4},{4,8},{8,12},{12,0},{1,5},{5,9},{9,13},{13,1},{2,6},{6,10},{... | collective-permute-start | bytes 786440 | tf_op jit(solution)/shard_map/ppermute | solution.py:271
  4.7 0.1 reshape_transpose.14.rest_2_
  4.8 2.7 %collective-permute-start.1 = (bf16[1,256,512]{2,1,0:T(8,128)(2,1)S(1)}, bf16[1,256,512]{2,1,0:T(8,128)(2,1)S(1)}, u32[]{:S(2)}, u32[]{:S(2)}) collective-permute-start(bf16[1,256,512]{2,1,0:T(8,128)(2,1)S(1)} %reshape_transpose.14.rest_2_), channel_id=1, source_target_pairs={{0,8},{4,12},{8,0},{12,4},{1,9},{5,13},{9,1},{13,5},{2,10},{6,14},... | collective-permute-start | bytes 786440 | tf_op jit(solution)/shard_map/ppermute | solution.py:271
  7.4 0.1 reshape_transpose.15.rest_3_
  7.5 1.4 %collective-permute-start.2 = (bf16[1,256,512]{2,1,0:T(8,128)(2,1)S(1)}, bf16[1,256,512]{2,1,0:T(8,128)(2,1)S(1)}, u32[]{:S(2)}, u32[]{:S(2)}) collective-permute-start(bf16[1,256,512]{2,1,0:T(8,128)(2,1)S(1)} %reshape_transpose.15.rest_3_), channel_id=1, source_target_pairs={{0,12},{4,0},{8,4},{12,8},{1,13},{5,1},{9,5},{13,9},{2,14},{6,2},{... | collective-permute-start | bytes 786440 | tf_op jit(solution)/shard_map/ppermute | solution.py:271
  8.9 0.1 reshape_transpose.12.rest_0_.refs_0_
  9.0 0.0 copy-done.1
  9.0 1.1 %shard_map.57.weights_ref = bf16[1,512,512]{2,1,0:T(8,128)(2,1)S(1)} custom-call(s32[256,512]{1,0:T(8,128)S(1)} %copy-done.1), custom_call_target="tpu_custom_call" | custom-call | flops 5242880 | bytes 1048576 | tf_op jit(solution)/shard_map/pallas_call | solution.py:285
  10.1 0.0 copy-start.2
  10.1 0.0 copy-start.3
  10.1 0.0 copy-start.4
  10.2 6.8 %shard_map.56 = (f32[4,256,128]{2,1,0:T(8,128)S(1)}, f32[4,256,128]{2,1,0:T(8,128)S(1)}) custom-call(s32[256,512]{1,0:T(8,128)S(1)} %copy-done.1, bf16[1,256,512]{2,1,0:T(8,128)(2,1)S(1)} %reshape_transpose.12.rest_0_.refs_0_, bf16[1,256,512]{2,1,0:T(8,128)(2,1)S(1)} %reshape_transpose.13.rest_1_, bf16[1,256,512]{2,1,0:T(8,128)(2,1)S(1)} %reshape_transpose.14.rest_2_, ...), custom_call_target="tpu_custom_call" | custom-call | flops 536870912 | bytes 2097152 | tf_op jit(solution)/shard_map/pallas_call | solution.py:275
  17.0 0.0 collective-permute-done.refs_1_
  17.0 7.3 %collective-permute-done.1.refs_2_ = bf16[1,256,512]{2,1,0:T(8,128)(2,1)S(1)} collective-permute-done((bf16[1,256,512]{2,1,0:T(8,128)(2,1)S(1)}, bf16[1,256,512]{2,1,0:T(8,128)(2,1)S(1)}, u32[]{:S(2)}, u32[]{:S(2)}) %collective-permute-start.1) | collective-permute-done | bytes 262176 | tf_op jit(solution)/shard_map/ppermute | solution.py:271
  24.4 1.0 %shard_map.58 = (f32[1,2,512,512]{3,2,1,0:T(8,128)S(1)}, bf16[1,512,768]{2,1,0:T(8,128)(2,1)S(1)}) custom-call(bf16[1,256,512]{2,1,0:T(8,128)(2,1)S(1)} %reshape_transpose.12.rest_0_.refs_0_, bf16[1,256,512]{2,1,0:T(8,128)(2,1)S(1)} %collective-permute-done.refs_1_, bf16[1,256,512]{2,1,0:T(8,128)(2,1)S(1)} %collective-permute-done.1.refs_2_), custom_call_target="tpu_custom_call" | custom-call | flops 805306368 | bytes 2097152 | tf_op jit(solution)/shard_map/pallas_call | solution.py:295
  25.4 0.0 collective-permute-done.2.last_ref
  25.4 0.0 copy-done.2
  25.4 0.0 copy-done.3
  25.4 0.0 copy-done.4
  25.4 6.1 %shard_map.59 = (f32[4,256,128]{2,1,0:T(8,128)S(1)}, f32[1,8,768]{2,1,0:T(8,128)S(1)}, f32[1,8,768]{2,1,0:T(8,128)S(1)}, f32[1,8,768]{2,1,0:T(8,128)S(1)}, f32[1,8,768]{2,1,0:T(8,128)S(1)}) custom-call(f32[4,256,128]{2,1,0:T(8,128)S(1)} %get-tuple-element.24.beams_ref, f32[1,4,2,8,512]{4,3,2,1,0:T(8,128)S(1)} %copy-done.2, ...), custom_call_target="tpu_custom_call", output_to_operand_aliasing={{0}: (0, {})} | custom-call | flops 134217728 | bytes 2097152 | tf_op jit(solution)/shard_map/pallas_call | solution.py:308
  31.6 0.1 collective-permute-start.3
  31.7 7.2 %collective-permute-start.4 = (f32[1,8,768]{2,1,0:T(8,128)S(1)}, f32[1,8,768]{2,1,0:T(8,128)S(1)}, u32[]{:S(2)}, u32[]{:S(2)}) collective-permute-start(f32[1,8,768]{2,1,0:T(8,128)S(1)} %get-tuple-element.30), channel_id=1, source_target_pairs={{0,12},{4,8},{8,4},{12,0},{1,13},{5,9},{9,5},{13,1},{2,14},{6,10},... | collective-permute-start | bytes 73736 | tf_op jit(solution)/shard_map/ppermute | solution.py:335
  38.8 0.0 collective-permute-start.5
  38.8 0.6 %collective-permute-start.6 = (f32[1,8,768]{2,1,0:T(8,128)S(1)}, f32[1,8,768]{2,1,0:T(8,128)S(1)}, u32[]{:S(2)}, u32[]{:S(2)}) collective-permute-start(f32[1,8,768]{2,1,0:T(8,128)S(1)} %get-tuple-element.33), channel_id=1, source_target_pairs={{0,8},{4,12},{8,0},{12,4},{1,9},{5,13},{9,1},{13,5},{2,10},{6,14},... | collective-permute-start | bytes 73736 | tf_op jit(solution)/shard_map/ppermute | solution.py:335
  39.5 0.0 collective-permute-start.7
  39.5 1.4 %collective-permute-done.4.rest_1_ = f32[1,8,768]{2,1,0:T(8,128)S(1)} collective-permute-done((f32[1,8,768]{2,1,0:T(8,128)S(1)}, f32[1,8,768]{2,1,0:T(8,128)S(1)}, u32[]{:S(2)}, u32[]{:S(2)}) %collective-permute-start.4) | collective-permute-done | bytes 24608 | tf_op jit(solution)/shard_map/ppermute | solution.py:335
  40.9 0.0 collective-permute-start.10
  40.9 2.0 %collective-permute-done.5.rest_0_ = f32[1,8,768]{2,1,0:T(8,128)S(1)} collective-permute-done((f32[1,8,768]{2,1,0:T(8,128)S(1)}, f32[1,8,768]{2,1,0:T(8,128)S(1)}, u32[]{:S(2)}, u32[]{:S(2)}) %collective-permute-start.5) | collective-permute-done | bytes 24608 | tf_op jit(solution)/shard_map/ppermute | solution.py:335
  42.9 0.0 collective-permute-start.8
  42.9 0.6 %collective-permute-done.6.rest_0_ = f32[1,8,768]{2,1,0:T(8,128)S(1)} collective-permute-done((f32[1,8,768]{2,1,0:T(8,128)S(1)}, f32[1,8,768]{2,1,0:T(8,128)S(1)}, u32[]{:S(2)}, u32[]{:S(2)}) %collective-permute-start.6) | collective-permute-done | bytes 24608 | tf_op jit(solution)/shard_map/ppermute | solution.py:335
  43.6 0.0 collective-permute-start.9
  43.6 0.3 shard_map.60
  43.9 0.3 shard_map.61.rest_1_.rest_2_
  44.2 0.3 shard_map.62.rest_1_
  44.5 0.0 collective-permute-done.7.rest_4_
  44.5 0.0 collective-permute-done.10.rest_7_
  44.5 0.0 collective-permute-done.8.rest_5_
  44.5 0.3 collective-permute-done.9.rest_6_
  44.8 0.0 collective-permute-done.3.raw_ref
  44.8 1.2 %shard_map.63 = f32[128,4,128]{2,1,0:T(4,128)} custom-call(f32[4,256,128]{2,1,0:T(8,128)S(1)} %collective-permute-done.3.raw_ref, f32[1,128,128]{2,1,0:T(8,128)S(1)} %get-tuple-element.31.rest_0_, f32[1,128,128]{2,1,0:T(8,128)S(1)} %shard_map.62.rest_1_, f32[1,128,128]{2,1,0:T(8,128)S(1)} %shard_map.61.rest_1_.rest_2_, ...), custom_call_target="tpu_custom_call" | custom-call | flops 25165824 | bytes 1048576 | tf_op jit(solution)/shard_map/pallas_call | solution.py:342
Async XLA Ops:
  0.0 1.2 %copy-start = (bf16[128,1,4,2,512]{4,3,2,1,0:T(2,128)(2,1)S(1)}, bf16[128,1,4,2,512]{4,3,2,1,0:T(2,128)(2,1)}, u32[]{:S(2)}) copy-start(bf16[128,1,4,2,512]{4,3,2,1,0:T(2,128)(2,1)} %voltages_ref.1) | copy-start | bytes 3145732
  1.2 7.8 %copy-start.1 = (s32[256,512]{1,0:T(8,128)S(1)}, s32[256,512]{1,0:T(8,128)}, u32[]{:S(2)}) copy-start(s32[256,512]{1,0:T(8,128)} %phase_ref.3) | copy-start | bytes 1572868
  1.6 15.4 %collective-permute-start = (bf16[1,256,512]{2,1,0:T(8,128)(2,1)S(1)}, bf16[1,256,512]{2,1,0:T(8,128)(2,1)S(1)}, u32[]{:S(2)}, u32[]{:S(2)}) collective-permute-start(bf16[1,256,512]{2,1,0:T(8,128)(2,1)S(1)} %reshape_transpose.13.rest_1_), channel_id=1, source_target_pairs={{0,4},{4,8},{8,12},{12,0},{1,5},{5,9},{9,13},{13,1},{2,6},{6,10},{... | collective-permute-start | bytes 786440 | tf_op jit(solution)/shard_map/ppermute | solution.py:271
  4.8 19.6 %collective-permute-start.1 = (bf16[1,256,512]{2,1,0:T(8,128)(2,1)S(1)}, bf16[1,256,512]{2,1,0:T(8,128)(2,1)S(1)}, u32[]{:S(2)}, u32[]{:S(2)}) collective-permute-start(bf16[1,256,512]{2,1,0:T(8,128)(2,1)S(1)} %reshape_transpose.14.rest_2_), channel_id=1, source_target_pairs={{0,8},{4,12},{8,0},{12,4},{1,9},{5,13},{9,1},{13,5},{2,10},{6,14},... | collective-permute-start | bytes 786440 | tf_op jit(solution)/shard_map/ppermute | solution.py:271
  7.5 17.9 %collective-permute-start.2 = (bf16[1,256,512]{2,1,0:T(8,128)(2,1)S(1)}, bf16[1,256,512]{2,1,0:T(8,128)(2,1)S(1)}, u32[]{:S(2)}, u32[]{:S(2)}) collective-permute-start(bf16[1,256,512]{2,1,0:T(8,128)(2,1)S(1)} %reshape_transpose.15.rest_3_), channel_id=1, source_target_pairs={{0,12},{4,0},{8,4},{12,8},{1,13},{5,1},{9,5},{13,9},{2,14},{6,2},{... | collective-permute-start | bytes 786440 | tf_op jit(solution)/shard_map/ppermute | solution.py:271
  10.1 15.3 %copy-start.2 = (f32[1,4,2,8,512]{4,3,2,1,0:T(8,128)S(1)}, f32[1,4,2,8,512]{4,3,2,1,0:T(8,128)}, u32[]{:S(2)}) copy-start(f32[1,4,2,8,512]{4,3,2,1,0:T(8,128)} %start_ref.1) | copy-start | bytes 393220
  10.1 15.3 %copy-start.3 = (s32[4]{0:T(128)S(1)}, s32[4]{0:T(128)}, u32[]{:S(2)}) copy-start(s32[4]{0:T(128)} %flags_ref.1) | copy-start | bytes 52
  10.1 15.3 %copy-start.4 = (s32[4]{0:T(128)S(1)}, s32[4]{0:T(128)}, u32[]{:S(2)}) copy-start(s32[4]{0:T(128)} %ranks_ref.1) | copy-start | bytes 52
  31.6 13.2 %collective-permute-start.3 = (f32[4,256,128]{2,1,0:T(8,128)S(1)}, f32[4,256,128]{2,1,0:T(8,128)S(1)}, u32[]{:S(2)}, u32[]{:S(2)}) collective-permute-start(f32[4,256,128]{2,1,0:T(8,128)S(1)} %get-tuple-element.27), channel_id=1, source_target_pairs={{0,1},{1,0},{2,3},{3,2},{4,5},{5,4},{6,7},{7,6},{8,9},{9,8},{10,11... | collective-permute-start | bytes 1572872 | tf_op jit(solution)/shard_map/ppermute | solution.py:320
  31.7 9.2 %collective-permute-start.4 = (f32[1,8,768]{2,1,0:T(8,128)S(1)}, f32[1,8,768]{2,1,0:T(8,128)S(1)}, u32[]{:S(2)}, u32[]{:S(2)}) collective-permute-start(f32[1,8,768]{2,1,0:T(8,128)S(1)} %get-tuple-element.30), channel_id=1, source_target_pairs={{0,12},{4,8},{8,4},{12,0},{1,13},{5,9},{9,5},{13,1},{2,14},{6,10},... | collective-permute-start | bytes 73736 | tf_op jit(solution)/shard_map/ppermute | solution.py:335
  38.8 4.1 %collective-permute-start.5 = (f32[1,8,768]{2,1,0:T(8,128)S(1)}, f32[1,8,768]{2,1,0:T(8,128)S(1)}, u32[]{:S(2)}, u32[]{:S(2)}) collective-permute-start(f32[1,8,768]{2,1,0:T(8,128)S(1)} %get-tuple-element.32), channel_id=1, source_target_pairs={{0,4},{4,0},{8,12},{12,8},{1,5},{5,1},{9,13},{13,9},{2,6},{6,2},{1... | collective-permute-start | bytes 73736 | tf_op jit(solution)/shard_map/ppermute | solution.py:335
  38.8 4.7 %collective-permute-start.6 = (f32[1,8,768]{2,1,0:T(8,128)S(1)}, f32[1,8,768]{2,1,0:T(8,128)S(1)}, u32[]{:S(2)}, u32[]{:S(2)}) collective-permute-start(f32[1,8,768]{2,1,0:T(8,128)S(1)} %get-tuple-element.33), channel_id=1, source_target_pairs={{0,8},{4,12},{8,0},{12,4},{1,9},{5,13},{9,1},{13,5},{2,10},{6,14},... | collective-permute-start | bytes 73736 | tf_op jit(solution)/shard_map/ppermute | solution.py:335
  39.5 5.0 %collective-permute-start.7 = (f32[1,8,768]{2,1,0:T(8,128)S(1)}, f32[1,8,768]{2,1,0:T(8,128)S(1)}, u32[]{:S(2)}, u32[]{:S(2)}) collective-permute-start(f32[1,8,768]{2,1,0:T(8,128)S(1)} %get-tuple-element.29.rest_0_), channel_id=1, source_target_pairs={{0,1},{1,0},{2,3},{3,2},{4,5},{5,4},{6,7},{7,6},{8,9},{9,8},{10,11... | collective-permute-start | bytes 73736 | tf_op jit(solution)/shard_map/ppermute | solution.py:336
  40.9 3.6 %collective-permute-start.10 = (f32[1,8,768]{2,1,0:T(8,128)S(1)}, f32[1,8,768]{2,1,0:T(8,128)S(1)}, u32[]{:S(2)}, u32[]{:S(2)}) collective-permute-start(f32[1,8,768]{2,1,0:T(8,128)S(1)} %collective-permute-done.4.rest_1_), channel_id=1, source_target_pairs={{0,1},{1,0},{2,3},{3,2},{4,5},{5,4},{6,7},{7,6},{8,9},{9,8},{10,11... | collective-permute-start | bytes 73736 | tf_op jit(solution)/shard_map/ppermute | solution.py:336
  42.9 1.5 %collective-permute-start.8 = (f32[1,8,768]{2,1,0:T(8,128)S(1)}, f32[1,8,768]{2,1,0:T(8,128)S(1)}, u32[]{:S(2)}, u32[]{:S(2)}) collective-permute-start(f32[1,8,768]{2,1,0:T(8,128)S(1)} %collective-permute-done.5.rest_0_), channel_id=1, source_target_pairs={{0,1},{1,0},{2,3},{3,2},{4,5},{5,4},{6,7},{7,6},{8,9},{9,8},{10,11... | collective-permute-start | bytes 73736 | tf_op jit(solution)/shard_map/ppermute | solution.py:336
  43.6 1.2 %collective-permute-start.9 = (f32[1,8,768]{2,1,0:T(8,128)S(1)}, f32[1,8,768]{2,1,0:T(8,128)S(1)}, u32[]{:S(2)}, u32[]{:S(2)}) collective-permute-start(f32[1,8,768]{2,1,0:T(8,128)S(1)} %collective-permute-done.6.rest_0_), channel_id=1, source_target_pairs={{0,1},{1,0},{2,3},{3,2},{4,5},{5,4},{6,7},{7,6},{8,9},{9,8},{10,11... | collective-permute-start | bytes 73736 | tf_op jit(solution)/shard_map/ppermute | solution.py:336

commit v8 on v7

--- a/solution.py
+++ b/solution.py
@@ -58,6 +58,10 @@
     lax.fori_loop(0, rows // chunk, body, 0)
 
 
+def steps(tm):
+    return [0, *[by for by in range(1, tm) if by != tm // 2], tm // 2]
+
+
 def shifted(by):
     tm = lax.axis_size("tm")
     return lax.rem(lax.axis_index("tm") + tm + by, tm)
@@ -66,8 +70,8 @@
 def cut_kernel(tm, own, voltages_ref, *rest):
     pieces, done = rest[:tm], rest[tm]
     copies = []
-    for i, piece in enumerate(pieces):
-        channels = pl.ds(shifted(i) * own, own)
+    for i, (by, piece) in enumerate(zip(steps(tm), pieces)):
+        channels = pl.ds(shifted(by) * own, own)
         copy = pltpu.make_async_copy(voltages_ref.at[:, 0, channels], piece, done.at[i])
         copy.start()
         copies.append(copy)
@@ -89,9 +93,9 @@
     rows = pieces[0].shape[1]
     pol = lax.axis_index("pol")
     start = lax.axis_index("chan") * tm * own
-    for i, piece in enumerate(pieces):
+    for by, piece in zip(steps(tm), pieces):
         for o in range(own):
-            chan = shifted(i) * own + o
+            chan = shifted(by) * own + o
             for swap, out_ref in enumerate((mine_ref, other_ref)):
                 first = pl.multiple_of((pol ^ swap) * half, half)
                 fill_weights(phase_ref, first, half, start + chan + 1, weights)
@@ -162,7 +166,7 @@
 def subspace_kernel(
     tm, own, factor, beams_ref, start_ref, flags_ref, ranks_ref, weights_ref, cov_ref, across_ref, last_ref, *rest
 ):
-    outs, (high_ref, low_ref, series_ref) = rest[1 : tm + 1], rest[tm + 1 :]
+    outs, (high_ref, low_ref, series_ref) = rest[:tm], rest[tm:]
     vectors, width = start_ref.shape[3], start_ref.shape[4]
     rows = last_ref.shape[1]
     tm_index = lax.axis_index("tm")
@@ -187,57 +191,44 @@
         product = product[: 2 * vectors] + product[2 * vectors :]
         real_w = product[:vectors, :beams] - product[vectors:, beams:]
         imag_w = product[:vectors, beams:] + product[vectors:, :beams]
-        for i in range(tm):
+        for i, by in enumerate(steps(tm)):
             block = across_ref[o, :, i * rows : (i + 1) * rows] if i < tm - 1 else across
             product = dot(both, block, NN)
             product = product[: 2 * vectors] + product[2 * vectors :]
             series = product[:vectors] + turned(product[vectors:], 1)
-            series_ref[tm_index ^ shifted(-i)] = series
+            series_ref[tm_index ^ shifted(-by)] = series
         for x, out in enumerate(outs):
             out[o, :, :rows] = series_ref[x]
             out[o, :, rows : rows + beams] = real_w
             out[o, :, rows + beams :] = imag_w
 
 
-def nulled_squares(raw, packet_ref):
-    rows, half = raw.shape
-    at = pl.multiple_of(rows + lax.axis_index("pol") * half, half)
-    series = packet_ref[:, :rows]
-    left = jnp.concatenate([series, -turned(series, 1)], axis=0)
-    right = jnp.concatenate(
-        [packet_ref[:, pl.ds(at, half)], packet_ref[:, pl.ds(pl.multiple_of(at + 2 * half, half), half)]],
-        axis=0,
-    )
-    high_s, low_s = split(left)
-    high_w, low_w = split(right)
-    left = jnp.concatenate([high_s, high_s, low_s], axis=0)
-    right = jnp.concatenate([high_w, low_w, high_w], axis=0)
-    beam = raw - dot(left, right, TN)
-    return beam * beam
-
-
-def pair_sums(squares):
-    samples = squares.shape[0] // 2
-    return squares[pl.ds(0, samples, 2), :] + squares[pl.ds(1, samples, 2), :]
-
-
-def first_kernel(own, xs, raw_ref, *rest):
-    packets, outs, squares = rest[: len(xs)], rest[-1 - len(xs) : -1], rest[-1]
-    for x, ref, out_ref in zip(xs, packets, outs):
-        for o in range(own):
-            squares[...] = nulled_squares(raw_ref[(lax.axis_index("tm") ^ x) * own + o], ref.at[o])
-            out_ref[o] = pair_sums(squares)
-
-
-def second_kernel(tm, own, raw_ref, *rest):
-    firsts, packets, (out_ref, squares, powers) = rest[:tm], rest[tm : 2 * tm], rest[2 * tm :]
-    for x, (first_ref, ref) in enumerate(zip(firsts, packets)):
+def first_kernel(own, xs, mine_ref, other_ref, *rest):
+    packets, (mine_out, other_out, squares) = rest[: len(xs)], rest[-3:]
+    rows, half = mine_ref.shape[1:]
+    samples = rows // 2
+    for x, ref in zip(xs, packets):
         for o in range(own):
             chan = (lax.axis_index("tm") ^ x) * own + o
-            squares[...] = nulled_squares(raw_ref[chan], ref.at[o])
-            powers[chan] = first_ref[o] + pair_sums(squares)
-    for chan in range(powers.shape[0]):
-        out_ref[:, chan, :] = powers[chan]
+            series = ref[o, :, :rows]
+            left = jnp.concatenate([series, -turned(series, 1)], axis=0)
+            high_s, low_s = split(left)
+            left = jnp.concatenate([high_s, high_s, low_s], axis=0)
+            for swap, (raw_ref, out_ref) in enumerate(((mine_ref, mine_out), (other_ref, other_out))):
+                at = rows + (lax.axis_index("pol") ^ swap) * half
+                real_at = pl.ds(pl.multiple_of(at, half), half)
+                imag_at = pl.ds(pl.multiple_of(at + 2 * half, half), half)
+                right = jnp.concatenate([ref[o, :, real_at], ref[o, :, imag_at]], axis=0)
+                high_w, low_w = split(right)
+                right = jnp.concatenate([high_w, low_w, high_w], axis=0)
+                beam = raw_ref[chan] - dot(left, right, TN)
+                squares[...] = beam * beam
+                out_ref[chan] = squares[pl.ds(0, samples, 2), :] + squares[pl.ds(1, samples, 2), :]
+
+
+def second_kernel(mine_ref, theirs_ref, out_ref):
+    for chan in range(out_ref.shape[1]):
+        out_ref[:, chan, :] = mine_ref[chan] + theirs_ref[chan]
 
 
 def local(voltages, start_block, flags, ranks, phase_index):
@@ -268,7 +259,8 @@
     )(voltages)
     pieces = [piece.transpose(1, 0, 2, 3).reshape(own, rows, width) for piece in cut]
     blocks = pieces[:1] + [
-        lax.ppermute(pieces[i], "tm", [(z, (z + i) % tm) for z in range(tm)]) for i in range(1, tm)
+        lax.ppermute(piece, "tm", [(z, (z + by) % tm) for z in range(tm)])
+        for by, piece in zip(steps(tm)[1:], pieces[1:])
     ]
 
     raw = jax.ShapeDtypeStruct((chan_dev, rows, half), F32)
@@ -305,52 +297,44 @@
         cost_estimate=cost(2 * own * early * width * width, 8 * own * width * width),
     )(*blocks[:-1])
 
-    other, *packets = pl.pallas_call(
+    packets = pl.pallas_call(
         functools.partial(subspace_kernel, tm, own, factor),
-        out_shape=[raw] + [jax.ShapeDtypeStruct((own, vectors, rows + 2 * beams), F32)] * tm,
+        out_shape=[jax.ShapeDtypeStruct((own, vectors, rows + 2 * beams), F32)] * tm,
         in_specs=[unread, whole, scalars, scalars] + [whole] * 4,
-        out_specs=[unread] + [whole] * tm,
-        input_output_aliases={0: 0},
+        out_specs=[whole] * tm,
         scratch_shapes=[pltpu.VMEM((2 * width, width), BF16)] * 2
         + [pltpu.VMEM((tm, vectors, rows), F32)],
         compiler_params=params,
         cost_estimate=cost(32 * own * vectors * tm * samples * width, 8 * own * width * width),
-    )(other, start_block, flags, ranks, own_weights, cov, across, blocks[-1])
-    cores = [(0, 1), (1, 0)]
-    theirs = lax.ppermute(other, "pol", cores)
-
-    def first(xs, *before):
-        return pl.pallas_call(
-            functools.partial(first_kernel, own, xs),
-            out_shape=[jax.ShapeDtypeStruct((own, samples, half), F32)] * len(xs),
-            in_specs=[whole] * (1 + len(xs)) + [unread] * len(before),
-            out_specs=[whole] * len(xs),
-            scratch_shapes=[pltpu.VMEM((rows, half), F32)],
-            compiler_params=params,
-            cost_estimate=cost(len(xs) * own * rows * 6 * vectors * half, 8 * own * rows * half),
-        )(mine, *[arrived[x] for x in xs], *before)
+    )(mine, start_block, flags, ranks, own_weights, cov, across, blocks[-1])
 
     arrived = list(packets)
     for x in reversed(range(1, tm)):
         arrived[x] = lax.ppermute(packets[x], "tm", [(z, z ^ x) for z in range(tm)])
-    swapped = [lax.ppermute(packet, "pol", cores) for packet in arrived]
-    firsts = [None] * tm
-    firsts[0], firsts[-1] = first([0, tm - 1])
-    for x in reversed(range(1, tm - 1)):
-        (firsts[x],) = first([x], firsts[x + 1])
+    groups = [[0, tm - 1], *[[x] for x in reversed(range(1, tm - 1))]]
+    shape = jax.ShapeDtypeStruct((chan_dev, samples, half), F32)
+    powers = []
+    for xs in groups:
+        powers = pl.pallas_call(
+            functools.partial(first_kernel, own, xs),
+            out_shape=[shape] * 2,
+            in_specs=[whole] * (2 + len(xs) + len(powers)),
+            out_specs=[whole] * 2,
+            input_output_aliases={2 + len(xs) + i: i for i in range(len(powers))},
+            scratch_shapes=[pltpu.VMEM((rows, half), F32)],
+            compiler_params=params,
+            cost_estimate=cost(len(xs) * own * rows * 6 * vectors * beams, 8 * own * rows * beams),
+        )(mine, other, *[arrived[x] for x in xs], *powers)
+    theirs = lax.ppermute(powers[1], "pol", [(0, 1), (1, 0)])
 
     return pl.pallas_call(
-        functools.partial(second_kernel, tm, own),
+        second_kernel,
         out_shape=jax.ShapeDtypeStruct((samples, chan_dev, half), F32),
-        in_specs=[whole] * (1 + 2 * tm),
+        in_specs=[whole] * 2,
         out_specs=whole,
-        scratch_shapes=[
-            pltpu.VMEM((rows, half), F32),
-            pltpu.VMEM((chan_dev, samples, half), F32),
-        ],
-        compiler_params=params,
-        cost_estimate=cost(2 * chan_dev * rows * 6 * vectors * half, 8 * chan_dev * rows * half),
-    )(theirs, *firsts, *swapped)
+        compiler_params=params,
+        cost_estimate=cost(chan_dev * samples * half, 12 * chan_dev * samples * half),
+    )(powers[0], theirs)
 
 
 def solution(mesh):

time: 46.1 us -> 45.7 us (level)
  waiting for transfers between devices: 11.7 us -> 15.9 us
  starting transfers between devices: 15 us -> 10.8 us
    ppermute x8 -> x4, waiting for transfers between devices: 7.64 us -> 14.2 us  [the longest x3 12.7 us: local(): lax.ppermute(piece, 'tm', [(z, (z + by) % tm) for z in range(tm)])]
    ppermute x3, starting transfers between devices: 7.82 us -> 4.45 us  [local(): arrived[x] = lax.ppermute(packets[x], 'tm', [(z, z ^ x) for z in range(tm)])]
    ppermute x3, waiting for transfers between devices: 4.08 us -> 1.71 us  [local(): arrived[x] = lax.ppermute(packets[x], 'tm', [(z, z ^ x) for z in range(tm)])]
    ppermute x8 -> x4, starting transfers between devices: 7.21 us -> 6.3 us  [the longest x3 6.23 us: local(): lax.ppermute(piece, 'tm', [(z, (z + by) % tm) for z in range(tm)])]
  transfers between devices with their start and end apart: 11 -> 7, of which waited for: 5 -> 5; matrix products, arithmetic and copies ran while one was open for 1% -> 1% of each run, Pallas kernels for 21% -> 21%
where the time goes in v8:
time: 45.7 us; the launch traced here: 45.6 us
  Pallas kernels  17.1 us (37%)
  waiting for transfers between devices  15.9 us (35%)
  starting transfers between devices  10.8 us (24%)
  local copies, waits for them, and re-layouts  1.66 us (4%)
    ppermute x3, waiting for transfers between devices, local(): lax.ppermute(piece, 'tm', [(z, (z + by) % tm) for z in range(tm)])  12.7 us
    pallas_call x1, Pallas kernels, local(): pl.pallas_call(functools.partial(raw_beams_kernel, tm, own), out_shape=[r...  6.85 us
    ppermute x3, starting transfers between devices, local(): lax.ppermute(piece, 'tm', [(z, (z + by) % tm) for z in range(tm)])  6.23 us
    pallas_call x1, Pallas kernels, local(): pl.pallas_call(functools.partial(subspace_kernel, tm, own, factor), out_s...  6.13 us
    ppermute x3, starting transfers between devices, local(): arrived[x] = lax.ppermute(packets[x], 'tm', [(z, z ^ x) for z in range(tm)])  4.45 us
    ppermute x3, waiting for transfers between devices, local(): arrived[x] = lax.ppermute(packets[x], 'tm', [(z, z ^ x) for z in range(tm)])  1.71 us
    ppermute x1, waiting for transfers between devices, local(): theirs = lax.ppermute(powers[1], 'pol', [(0, 1), (1, 0)])  1.52 us
    unnamed x10, local copies, waits for them, and re-layouts  1.25 us
  transfers between devices with their start and end apart: 7, of which 5 were waited for; matrix products, arithmetic and copies ran while one was open for 1% of the time, Pallas kernels for 21%

profile of v8, /device:TPU:0, one launch (start us, length us, event | category | flops | bytes accessed | tf_op | source)
XLA Modules:
  0.0 45.6 jit_solution(6963585475139659502)
XLA Ops:
  0.0 0.0 copy-start
  0.0 1.2 %copy-done = bf16[128,1,4,2,512]{4,3,2,1,0:T(2,128)(2,1)S(1)} copy-done((bf16[128,1,4,2,512]{4,3,2,1,0:T(2,128)(2,1)S(1)}, bf16[128,1,4,2,512]{4,3,2,1,0:T(2,128)(2,1)}, u32[]{:S(2)}) %copy-start) | copy-done | bytes 1048600
  1.2 0.0 copy-start.1
  1.2 0.2 shard_map.55
  1.5 0.1 reshape_transpose.13.rest_1_
  1.6 3.1 %collective-permute-start = (bf16[1,256,512]{2,1,0:T(8,128)(2,1)S(1)}, bf16[1,256,512]{2,1,0:T(8,128)(2,1)S(1)}, u32[]{:S(2)}, u32[]{:S(2)}) collective-permute-start(bf16[1,256,512]{2,1,0:T(8,128)(2,1)S(1)} %reshape_transpose.13.rest_1_), channel_id=1, source_target_pairs={{0,4},{4,8},{8,12},{12,0},{1,5},{5,9},{9,13},{13,1},{2,6},{6,10},{... | collective-permute-start | bytes 786440 | tf_op jit(solution)/shard_map/ppermute | solution.py:262
  4.7 0.1 reshape_transpose.14.rest_2_
  4.8 2.1 %collective-permute-start.1 = (bf16[1,256,512]{2,1,0:T(8,128)(2,1)S(1)}, bf16[1,256,512]{2,1,0:T(8,128)(2,1)S(1)}, u32[]{:S(2)}, u32[]{:S(2)}) collective-permute-start(bf16[1,256,512]{2,1,0:T(8,128)(2,1)S(1)} %reshape_transpose.14.rest_2_), channel_id=1, source_target_pairs={{0,12},{4,0},{8,4},{12,8},{1,13},{5,1},{9,5},{13,9},{2,14},{6,2},{... | collective-permute-start | bytes 786440 | tf_op jit(solution)/shard_map/ppermute | solution.py:262
  6.9 0.1 reshape_transpose.15.rest_3_
  7.0 1.1 %collective-permute-start.2 = (bf16[1,256,512]{2,1,0:T(8,128)(2,1)S(1)}, bf16[1,256,512]{2,1,0:T(8,128)(2,1)S(1)}, u32[]{:S(2)}, u32[]{:S(2)}) collective-permute-start(bf16[1,256,512]{2,1,0:T(8,128)(2,1)S(1)} %reshape_transpose.15.rest_3_), channel_id=1, source_target_pairs={{0,8},{4,12},{8,0},{12,4},{1,9},{5,13},{9,1},{13,5},{2,10},{6,14},... | collective-permute-start | bytes 786440 | tf_op jit(solution)/shard_map/ppermute | solution.py:262
  8.0 0.1 reshape_transpose.12.rest_0_.refs_0_
  8.1 0.0 copy-done.1
  8.1 1.1 %shard_map.57.weights_ref = bf16[1,512,512]{2,1,0:T(8,128)(2,1)S(1)} custom-call(s32[256,512]{1,0:T(8,128)S(1)} %copy-done.1), custom_call_target="tpu_custom_call" | custom-call | flops 5242880 | bytes 1048576 | tf_op jit(solution)/shard_map/pallas_call | solution.py:277
  9.2 0.0 copy-start.2
  9.2 0.0 copy-start.3
  9.2 0.0 copy-start.4
  9.3 6.8 %shard_map.56 = (f32[4,256,128]{2,1,0:T(8,128)S(1)}, f32[4,256,128]{2,1,0:T(8,128)S(1)}) custom-call(s32[256,512]{1,0:T(8,128)S(1)} %copy-done.1, bf16[1,256,512]{2,1,0:T(8,128)(2,1)S(1)} %reshape_transpose.12.rest_0_.refs_0_, bf16[1,256,512]{2,1,0:T(8,128)(2,1)S(1)} %reshape_transpose.13.rest_1_, bf16[1,256,512]{2,1,0:T(8,128)(2,1)S(1)} %reshape_transpose.14.rest_2_, ...), custom_call_target="tpu_custom_call" | custom-call | flops 536870912 | bytes 2097152 | tf_op jit(solution)/shard_map/pallas_call | solution.py:267
  16.1 0.0 collective-permute-done.refs_1_
  16.1 2.1 %collective-permute-done.1.refs_2_ = bf16[1,256,512]{2,1,0:T(8,128)(2,1)S(1)} collective-permute-done((bf16[1,256,512]{2,1,0:T(8,128)(2,1)S(1)}, bf16[1,256,512]{2,1,0:T(8,128)(2,1)S(1)}, u32[]{:S(2)}, u32[]{:S(2)}) %collective-permute-start.1) | collective-permute-done | bytes 262176 | tf_op jit(solution)/shard_map/ppermute | solution.py:262
  18.2 1.0 %shard_map.58 = (f32[1,2,512,512]{3,2,1,0:T(8,128)S(1)}, bf16[1,512,768]{2,1,0:T(8,128)(2,1)S(1)}) custom-call(bf16[1,256,512]{2,1,0:T(8,128)(2,1)S(1)} %reshape_transpose.12.rest_0_.refs_0_, bf16[1,256,512]{2,1,0:T(8,128)(2,1)S(1)} %collective-permute-done.refs_1_, bf16[1,256,512]{2,1,0:T(8,128)(2,1)S(1)} %collective-permute-done.1.refs_2_), custom_call_target="tpu_custom_call" | custom-call | flops 805306368 | bytes 2097152 | tf_op jit(solution)/shard_map/pallas_call | solution.py:287
  19.2 10.6 %collective-permute-done.2.last_ref = bf16[1,256,512]{2,1,0:T(8,128)(2,1)S(1)} collective-permute-done((bf16[1,256,512]{2,1,0:T(8,128)(2,1)S(1)}, bf16[1,256,512]{2,1,0:T(8,128)(2,1)S(1)}, u32[]{:S(2)}, u32[]{:S(2)}) %collective-permute-start.2) | collective-permute-done | bytes 262176 | tf_op jit(solution)/shard_map/ppermute | solution.py:262
  29.8 0.0 copy-done.2
  29.8 0.0 copy-done.3
  29.8 0.0 copy-done.4
  29.8 6.1 %shard_map.59 = (f32[1,8,768]{2,1,0:T(8,128)S(1)}, f32[1,8,768]{2,1,0:T(8,128)S(1)}, f32[1,8,768]{2,1,0:T(8,128)S(1)}, f32[1,8,768]{2,1,0:T(8,128)S(1)}) custom-call(f32[4,256,128]{2,1,0:T(8,128)S(1)} %get-tuple-element.27.beams_ref.mine_ref, f32[1,4,2,8,512]{4,3,2,1,0:T(8,128)S(1)} %copy-done.2, s32[4]{0:T(128)S(1)} %copy-done.3, s32[4]{0:T(128)S(1)} %copy-done.4, ...), custom_call_target="tpu_custom_call" | custom-call | flops 134217728 | bytes 2097152 | tf_op jit(solution)/shard_map/pallas_call | solution.py:300
  36.0 1.7 %collective-permute-start.5 = (f32[1,8,768]{2,1,0:T(8,128)S(1)}, f32[1,8,768]{2,1,0:T(8,128)S(1)}, u32[]{:S(2)}, u32[]{:S(2)}) collective-permute-start(f32[1,8,768]{2,1,0:T(8,128)S(1)} %get-tuple-element.34), channel_id=1, source_target_pairs={{0,12},{4,8},{8,4},{12,0},{1,13},{5,9},{9,5},{13,1},{2,14},{6,10},... | collective-permute-start | bytes 73736 | tf_op jit(solution)/shard_map/ppermute | solution.py:313
  37.7 0.0 collective-permute-start.4
  37.7 2.8 %collective-permute-start.3 = (f32[1,8,768]{2,1,0:T(8,128)S(1)}, f32[1,8,768]{2,1,0:T(8,128)S(1)}, u32[]{:S(2)}, u32[]{:S(2)}) collective-permute-start(f32[1,8,768]{2,1,0:T(8,128)S(1)} %get-tuple-element.31), channel_id=1, source_target_pairs={{0,4},{4,0},{8,12},{12,8},{1,5},{5,1},{9,13},{13,9},{2,6},{6,2},{1... | collective-permute-start | bytes 73736 | tf_op jit(solution)/shard_map/ppermute | solution.py:313
  40.4 1.2 %collective-permute-done.5.rest_1_ = f32[1,8,768]{2,1,0:T(8,128)S(1)} collective-permute-done((f32[1,8,768]{2,1,0:T(8,128)S(1)}, f32[1,8,768]{2,1,0:T(8,128)S(1)}, u32[]{:S(2)}, u32[]{:S(2)}) %collective-permute-start.5) | collective-permute-done | bytes 24608 | tf_op jit(solution)/shard_map/ppermute | solution.py:313
  41.7 0.4 shard_map.60
  42.0 0.5 %collective-permute-done.4.rest_0_ = f32[1,8,768]{2,1,0:T(8,128)S(1)} collective-permute-done((f32[1,8,768]{2,1,0:T(8,128)S(1)}, f32[1,8,768]{2,1,0:T(8,128)S(1)}, u32[]{:S(2)}, u32[]{:S(2)}) %collective-permute-start.4) | collective-permute-done | bytes 24608 | tf_op jit(solution)/shard_map/ppermute | solution.py:313
  42.5 0.3 shard_map.61
  42.8 0.0 collective-permute-done.3.rest_0_
  42.8 0.3 shard_map.62
  43.1 0.1 collective-permute-start.6
  43.2 1.5 %collective-permute-done.6.theirs_ref = f32[4,128,128]{2,1,0:T(8,128)S(1)} collective-permute-done((f32[4,128,128]{2,1,0:T(8,128)S(1)}, f32[4,128,128]{2,1,0:T(8,128)S(1)}, u32[]{:S(2)}, u32[]{:S(2)}) %collective-permute-start.6) | collective-permute-done | bytes 262176 | tf_op jit(solution)/shard_map/ppermute | solution.py:328
  44.7 0.9 %shard_map.63 = f32[128,4,128]{2,1,0:T(4,128)} custom-call(f32[4,128,128]{2,1,0:T(8,128)S(1)} %get-tuple-element.39.mine_ref, f32[4,128,128]{2,1,0:T(8,128)S(1)} %collective-permute-done.6.theirs_ref), custom_call_target="tpu_custom_call" | custom-call | flops 131072 | bytes 786432 | tf_op jit(solution)/shard_map/pallas_call | solution.py:330
Async XLA Ops:
  0.0 1.2 %copy-start = (bf16[128,1,4,2,512]{4,3,2,1,0:T(2,128)(2,1)S(1)}, bf16[128,1,4,2,512]{4,3,2,1,0:T(2,128)(2,1)}, u32[]{:S(2)}) copy-start(bf16[128,1,4,2,512]{4,3,2,1,0:T(2,128)(2,1)} %voltages_ref.1) | copy-start | bytes 3145732
  1.2 6.9 %copy-start.1 = (s32[256,512]{1,0:T(8,128)S(1)}, s32[256,512]{1,0:T(8,128)}, u32[]{:S(2)}) copy-start(s32[256,512]{1,0:T(8,128)} %phase_ref.3) | copy-start | bytes 1572868
  1.6 14.5 %collective-permute-start = (bf16[1,256,512]{2,1,0:T(8,128)(2,1)S(1)}, bf16[1,256,512]{2,1,0:T(8,128)(2,1)S(1)}, u32[]{:S(2)}, u32[]{:S(2)}) collective-permute-start(bf16[1,256,512]{2,1,0:T(8,128)(2,1)S(1)} %reshape_transpose.13.rest_1_), channel_id=1, source_target_pairs={{0,4},{4,8},{8,12},{12,0},{1,5},{5,9},{9,13},{13,1},{2,6},{6,10},{... | collective-permute-start | bytes 786440 | tf_op jit(solution)/shard_map/ppermute | solution.py:262
  4.8 13.4 %collective-permute-start.1 = (bf16[1,256,512]{2,1,0:T(8,128)(2,1)S(1)}, bf16[1,256,512]{2,1,0:T(8,128)(2,1)S(1)}, u32[]{:S(2)}, u32[]{:S(2)}) collective-permute-start(bf16[1,256,512]{2,1,0:T(8,128)(2,1)S(1)} %reshape_transpose.14.rest_2_), channel_id=1, source_target_pairs={{0,12},{4,0},{8,4},{12,8},{1,13},{5,1},{9,5},{13,9},{2,14},{6,2},{... | collective-permute-start | bytes 786440 | tf_op jit(solution)/shard_map/ppermute | solution.py:262
  7.0 22.9 %collective-permute-start.2 = (bf16[1,256,512]{2,1,0:T(8,128)(2,1)S(1)}, bf16[1,256,512]{2,1,0:T(8,128)(2,1)S(1)}, u32[]{:S(2)}, u32[]{:S(2)}) collective-permute-start(bf16[1,256,512]{2,1,0:T(8,128)(2,1)S(1)} %reshape_transpose.15.rest_3_), channel_id=1, source_target_pairs={{0,8},{4,12},{8,0},{12,4},{1,9},{5,13},{9,1},{13,5},{2,10},{6,14},... | collective-permute-start | bytes 786440 | tf_op jit(solution)/shard_map/ppermute | solution.py:262
  9.2 20.6 %copy-start.2 = (f32[1,4,2,8,512]{4,3,2,1,0:T(8,128)S(1)}, f32[1,4,2,8,512]{4,3,2,1,0:T(8,128)}, u32[]{:S(2)}) copy-start(f32[1,4,2,8,512]{4,3,2,1,0:T(8,128)} %start_ref.1) | copy-start | bytes 393220
  9.2 20.6 %copy-start.3 = (s32[4]{0:T(128)S(1)}, s32[4]{0:T(128)}, u32[]{:S(2)}) copy-start(s32[4]{0:T(128)} %flags_ref.1) | copy-start | bytes 52
  9.2 20.6 %copy-start.4 = (s32[4]{0:T(128)S(1)}, s32[4]{0:T(128)}, u32[]{:S(2)}) copy-start(s32[4]{0:T(128)} %ranks_ref.1) | copy-start | bytes 52
  36.0 5.7 %collective-permute-start.5 = (f32[1,8,768]{2,1,0:T(8,128)S(1)}, f32[1,8,768]{2,1,0:T(8,128)S(1)}, u32[]{:S(2)}, u32[]{:S(2)}) collective-permute-start(f32[1,8,768]{2,1,0:T(8,128)S(1)} %get-tuple-element.34), channel_id=1, source_target_pairs={{0,12},{4,8},{8,4},{12,0},{1,13},{5,9},{9,5},{13,1},{2,14},{6,10},... | collective-permute-start | bytes 73736 | tf_op jit(solution)/shard_map/ppermute | solution.py:313
  37.7 4.8 %collective-permute-start.4 = (f32[1,8,768]{2,1,0:T(8,128)S(1)}, f32[1,8,768]{2,1,0:T(8,128)S(1)}, u32[]{:S(2)}, u32[]{:S(2)}) collective-permute-start(f32[1,8,768]{2,1,0:T(8,128)S(1)} %get-tuple-element.32), channel_id=1, source_target_pairs={{0,8},{4,12},{8,0},{12,4},{1,9},{5,13},{9,1},{13,5},{2,10},{6,14},... | collective-permute-start | bytes 73736 | tf_op jit(solution)/shard_map/ppermute | solution.py:313
  37.7 5.1 %collective-permute-start.3 = (f32[1,8,768]{2,1,0:T(8,128)S(1)}, f32[1,8,768]{2,1,0:T(8,128)S(1)}, u32[]{:S(2)}, u32[]{:S(2)}) collective-permute-start(f32[1,8,768]{2,1,0:T(8,128)S(1)} %get-tuple-element.31), channel_id=1, source_target_pairs={{0,4},{4,0},{8,12},{12,8},{1,5},{5,1},{9,13},{13,9},{2,6},{6,2},{1... | collective-permute-start | bytes 73736 | tf_op jit(solution)/shard_map/ppermute | solution.py:313
  43.1 1.6 %collective-permute-start.6 = (f32[4,128,128]{2,1,0:T(8,128)S(1)}, f32[4,128,128]{2,1,0:T(8,128)S(1)}, u32[]{:S(2)}, u32[]{:S(2)}) collective-permute-start(f32[4,128,128]{2,1,0:T(8,128)S(1)} %get-tuple-element.40), channel_id=1, source_target_pairs={{0,1},{1,0},{2,3},{3,2},{4,5},{5,4},{6,7},{7,6},{8,9},{9,8},{10,11... | collective-permute-start | bytes 786440 | tf_op jit(solution)/shard_map/ppermute | solution.py:328

commit v9 on v8

--- a/solution.py
+++ b/solution.py
@@ -17,6 +17,7 @@
 NN = (((1,), (0,)), ((), ()))
 TN = (((0,), (0,)), ((), ()))
 VMEM_LIMIT = 48 * 1024 * 1024
+CHUNK = 128
 
 
 def dot(left, right, dims):
@@ -67,10 +68,10 @@
     return lax.rem(lax.axis_index("tm") + tm + by, tm)
 
 
-def cut_kernel(tm, own, voltages_ref, *rest):
-    pieces, done = rest[:tm], rest[tm]
+def cut_kernel(own, bys, voltages_ref, *rest):
+    pieces, done = rest[:-1], rest[-1]
     copies = []
-    for i, (by, piece) in enumerate(zip(steps(tm), pieces)):
+    for i, (by, piece) in enumerate(zip(bys, pieces)):
         channels = pl.ds(shifted(by) * own, own)
         copy = pltpu.make_async_copy(voltages_ref.at[:, 0, channels], piece, done.at[i])
         copy.start()
@@ -111,23 +112,40 @@
         fill_weights(phase_ref, 0, beams, first + o + 1, out_ref.at[o])
 
 
-def cov_terms(x, across):
-    rotated = -turned(x.astype(F32), 0)
-    return dot(across, x, NN), dot(across, rotated.astype(BF16), NN)
-
-
-def early_cov_kernel(*refs):
-    blocks, (cov_ref, across_ref, along_ref, rotated_ref) = refs[:-4], refs[-4:]
+def rotate(x):
+    return (-turned(x.astype(F32), 0)).astype(BF16)
+
+
+def early_kernel(start_ref, *refs):
+    blocks, (cov_ref, first_ref, across_ref, along_ref, rotated_ref) = refs[:-5], refs[-5:]
     rows, width = blocks[0].shape[1:]
-    for o in range(cov_ref.shape[0]):
+    own = cov_ref.shape[0]
+    for o in range(own):
         for i, block in enumerate(blocks):
             x = block[o]
             at = slice(i * rows, (i + 1) * rows)
             along_ref[at] = x
-            rotated_ref[at] = -turned(x.astype(F32), 0).astype(BF16)
+            rotated_ref[at] = rotate(x)
             across_ref[o, :, at] = x.T
         cov_ref[o, 0] = dot(across_ref[o], along_ref[...], NN)
         cov_ref[o, 1] = dot(across_ref[o], rotated_ref[...], NN)
+        chan = lax.axis_index("tm") * own + o
+        first_ref[o] = block_times(start_ref[0, chan, 0], start_ref[0, chan, 1], across_ref[o], along_ref[...])
+
+
+def project(real, imag, across):
+    vectors = real.shape[0]
+    both = jnp.concatenate(split(jnp.concatenate([real, imag], axis=0)), axis=0)
+    product = dot(both, across, NN)
+    product = product[: 2 * vectors] + product[2 * vectors :]
+    other = turned(product, 1)
+    return product[:vectors] + other[vectors:], product[vectors:] - other[:vectors]
+
+
+def block_times(real, imag, across, along):
+    pair = jnp.concatenate(project(real, imag, across), axis=0)
+    product = dot(jnp.concatenate(split(pair), axis=0), along, NN)
+    return product[: pair.shape[0]] + product[pair.shape[0] :]
 
 
 def cov_times(real, imag, high_ref, low_ref):
@@ -141,7 +159,8 @@
     return product[:vectors], product[vectors:]
 
 
-def orthonormalize(real_z, imag_z):
+def orthonormalize(real_z, imag_z, beside=()):
+    beside = list(beside)
     vectors, width = real_z.shape
     row = lax.broadcasted_iota(jnp.int32, (vectors, 1), 0)
     real_v, imag_v = real_z, imag_z
@@ -159,12 +178,14 @@
             imag_c = imag_d * inverse
             real_v = real_v - (real_c * real_a - imag_c * imag_a)
             imag_v = imag_v - (real_c * imag_a + imag_c * real_a)
+        for work in beside[n::vectors]:
+            work()
     factor = 1.0 / jnp.sqrt(scale)
     return real_v * factor, imag_v * factor
 
 
 def subspace_kernel(
-    tm, own, factor, beams_ref, start_ref, flags_ref, ranks_ref, weights_ref, cov_ref, across_ref, last_ref, *rest
+    tm, own, factor, beams_ref, start_ref, flags_ref, ranks_ref, weights_ref, cov_ref, first_ref, across_ref, last_ref, *rest
 ):
     outs, (high_ref, low_ref, series_ref) = rest[:tm], rest[tm:]
     vectors, width = start_ref.shape[3], start_ref.shape[4]
@@ -174,12 +195,21 @@
     for o in range(own):
         chan = tm_index * own + o
         across = last_ref[o].T
-        for part, term in enumerate(cov_terms(last_ref[o], across)):
-            at = slice(part * width, (part + 1) * width)
-            high_ref[at], low_ref[at] = split((cov_ref[o, part] + term) * factor)
-        real_q = start_ref[0, chan, 0]
-        imag_q = start_ref[0, chan, 1]
-        for sweep in range(ITERS):
+        rotated = rotate(last_ref[o])
+
+        def add_last(part, first):
+            right = last_ref[o] if part == 0 else rotated
+            term = dot(across[first : first + CHUNK], right, NN)
+            at = slice(part * width + first, part * width + first + CHUNK)
+            high_ref[at], low_ref[at] = split((cov_ref[o, part, first : first + CHUNK] + term) * factor)
+
+        chunks = [
+            functools.partial(add_last, part, first) for part in range(2) for first in range(0, width, CHUNK)
+        ]
+        last = block_times(start_ref[0, chan, 0], start_ref[0, chan, 1], across, last_ref[o])
+        both = (first_ref[o] + last) * factor
+        real_q, imag_q = orthonormalize(both[:vectors], both[vectors:], chunks)
+        for sweep in range(1, ITERS):
             real_z, imag_z = cov_times(real_q, imag_q, high_ref, low_ref)
             real_q, imag_q = orthonormalize(real_z, imag_z)
         rank = flags_ref[chan] * ranks_ref[chan]
@@ -193,9 +223,7 @@
         imag_w = product[:vectors, beams:] + product[vectors:, :beams]
         for i, by in enumerate(steps(tm)):
             block = across_ref[o, :, i * rows : (i + 1) * rows] if i < tm - 1 else across
-            product = dot(both, block, NN)
-            product = product[: 2 * vectors] + product[2 * vectors :]
-            series = product[:vectors] + turned(product[vectors:], 1)
+            series = project(real_u, imag_u, block)[0]
             series_ref[tm_index ^ shifted(-by)] = series
         for x, out in enumerate(outs):
             out[o, :, :rows] = series_ref[x]
@@ -249,14 +277,17 @@
     def cost(multiplies, moved):
         return pl.CostEstimate(flops=2 * multiplies, bytes_accessed=moved, transcendentals=0)
 
-    cut = pl.pallas_call(
-        functools.partial(cut_kernel, tm, own),
-        out_shape=[jax.ShapeDtypeStruct((samples, own, 2, width), BF16)] * tm,
+    by = steps(tm)
+    later = pl.pallas_call(
+        functools.partial(cut_kernel, own, [by[0], *by[2:]]),
+        out_shape=[jax.ShapeDtypeStruct((samples, own, 2, width), BF16)] * (tm - 1),
         in_specs=[pl.BlockSpec(memory_space=pltpu.HBM)],
-        out_specs=[whole] * tm,
-        scratch_shapes=[pltpu.SemaphoreType.DMA((tm,))],
+        out_specs=[whole] * (tm - 1),
+        scratch_shapes=[pltpu.SemaphoreType.DMA((tm - 1,))],
         compiler_params=params,
     )(voltages)
+    urgent = lax.dynamic_slice_in_dim(voltages[:, 0], shifted(by[1]) * own, own, 1)
+    cut = [later[0], urgent, *later[1:]]
     pieces = [piece.transpose(1, 0, 2, 3).reshape(own, rows, width) for piece in cut]
     blocks = pieces[:1] + [
         lax.ppermute(piece, "tm", [(z, (z + by) % tm) for z in range(tm)])
@@ -284,29 +315,30 @@
     )(phase_index)
 
     early = (tm - 1) * rows
-    cov, across = pl.pallas_call(
-        early_cov_kernel,
+    cov, first, across = pl.pallas_call(
+        early_kernel,
         out_shape=[
             jax.ShapeDtypeStruct((own, 2, width, width), F32),
+            jax.ShapeDtypeStruct((own, 2 * vectors, width), F32),
             jax.ShapeDtypeStruct((own, width, early), BF16),
         ],
-        in_specs=[whole] * (tm - 1),
-        out_specs=[whole] * 2,
+        in_specs=[whole] * tm,
+        out_specs=[whole] * 3,
         scratch_shapes=[pltpu.VMEM((early, width), BF16)] * 2,
         compiler_params=params,
         cost_estimate=cost(2 * own * early * width * width, 8 * own * width * width),
-    )(*blocks[:-1])
+    )(start_block, *blocks[:-1])
 
     packets = pl.pallas_call(
         functools.partial(subspace_kernel, tm, own, factor),
         out_shape=[jax.ShapeDtypeStruct((own, vectors, rows + 2 * beams), F32)] * tm,
-        in_specs=[unread, whole, scalars, scalars] + [whole] * 4,
+        in_specs=[unread, whole, scalars, scalars] + [whole] * 5,
         out_specs=[whole] * tm,
         scratch_shapes=[pltpu.VMEM((2 * width, width), BF16)] * 2
         + [pltpu.VMEM((tm, vectors, rows), F32)],
         compiler_params=params,
         cost_estimate=cost(32 * own * vectors * tm * samples * width, 8 * own * width * width),
-    )(mine, start_block, flags, ranks, own_weights, cov, across, blocks[-1])
+    )(mine, start_block, flags, ranks, own_weights, cov, first, across, blocks[-1])
 
     arrived = list(packets)
     for x in reversed(range(1, tm)):

time: 45.7 us -> 45.1 us (0.987)
  waiting for transfers between devices: 15.9 us -> 14 us
  local copies, waits for them, and re-layouts: 1.66 us -> 2.85 us
    ppermute x3, waiting for transfers between devices: 12.7 us -> 10.8 us  [local(): lax.ppermute(piece, 'tm', [(z, (z + by) % tm) for z in range(tm)])]
    dynamic_slice x0 -> x1, local copies, waits for them, and re-layouts: none -> 1.19 us  [local(): lax.dynamic_slice_in_dim(voltages[:, 0], shifted(by[1]) * own, own, 1)]
  transfers between devices with their start and end apart: 7 -> 7, of which waited for: 5 -> 5; matrix products, arithmetic and copies ran while one was open for 1% -> 1% of each run, Pallas kernels for 21% -> 23%
where the time goes in v9:
time: 45.1 us; the launch traced here: 45 us
  Pallas kernels  17.2 us (38%)
  waiting for transfers between devices  14 us (31%)
  starting transfers between devices  10.8 us (24%)
  local copies, waits for them, and re-layouts  2.85 us (6%)
    ppermute x3, waiting for transfers between devices, local(): lax.ppermute(piece, 'tm', [(z, (z + by) % tm) for z in range(tm)])  10.8 us
    pallas_call x1, Pallas kernels, local(): pl.pallas_call(functools.partial(raw_beams_kernel, tm, own), out_shape=[r...  6.85 us
    ppermute x3, starting transfers between devices, local(): lax.ppermute(piece, 'tm', [(z, (z + by) % tm) for z in range(tm)])  6.23 us
    pallas_call x1, Pallas kernels, local(): pl.pallas_call(functools.partial(subspace_kernel, tm, own, factor), out_s...  5.79 us
    ppermute x3, starting transfers between devices, local(): arrived[x] = lax.ppermute(packets[x], 'tm', [(z, z ^ x) for z in range(tm)])  4.45 us
    ppermute x3, waiting for transfers between devices, local(): arrived[x] = lax.ppermute(packets[x], 'tm', [(z, z ^ x) for z in range(tm)])  1.71 us
    ppermute x1, waiting for transfers between devices, local(): theirs = lax.ppermute(powers[1], 'pol', [(0, 1), (1, 0)])  1.52 us
    pallas_call x1, Pallas kernels, local(): pl.pallas_call(early_kernel, out_shape=[jax.ShapeDtypeStruct((own, 2, wid...  1.51 us
  transfers between devices with their start and end apart: 7, of which 5 were waited for; matrix products, arithmetic and copies ran while one was open for 1% of the time, Pallas kernels for 23%

profile of v9, /device:TPU:0, one launch (start us, length us, event | category | flops | bytes accessed | tf_op | source)
XLA Modules:
  0.0 45.0 jit_solution(12599377652973505476)
XLA Ops:
  0.0 0.0 copy-start.1
  0.0 1.2 %constant_dynamic-slice_fusion = bf16[128,1,1,2,512]{4,3,2,1,0:T(2,128)(2,1)S(1)} fusion(bf16[128,1,4,2,512]{4,3,2,1,0:T(2,128)(2,1)} %voltages_ref.1, s32[]{:T(128)S(6)} %select_n.3), kind=kLoop, calls=%fused_computation | loop fusion | bytes 524292 | tf_op jit(solution)/shard_map/dynamic_slice | solution.py:289
  1.2 0.1 reshape_transpose.13.rest_1_
  1.3 3.1 %collective-permute-start = (bf16[1,256,512]{2,1,0:T(8,128)(2,1)S(1)}, bf16[1,256,512]{2,1,0:T(8,128)(2,1)S(1)}, u32[]{:S(2)}, u32[]{:S(2)}) collective-permute-start(bf16[1,256,512]{2,1,0:T(8,128)(2,1)S(1)} %reshape_transpose.13.rest_1_), channel_id=1, source_target_pairs={{0,4},{4,8},{8,12},{12,0},{1,5},{5,9},{9,13},{13,1},{2,6},{6,10},{... | collective-permute-start | bytes 786440 | tf_op jit(solution)/shard_map/ppermute | solution.py:293
  4.4 0.0 copy-start
  4.4 1.2 %copy-done = bf16[128,1,4,2,512]{4,3,2,1,0:T(2,128)(2,1)S(1)} copy-done((bf16[128,1,4,2,512]{4,3,2,1,0:T(2,128)(2,1)S(1)}, bf16[128,1,4,2,512]{4,3,2,1,0:T(2,128)(2,1)}, u32[]{:S(2)}) %copy-start) | copy-done | bytes 1048600
  5.6 0.2 shard_map.55
  5.8 0.1 reshape_transpose.14.rest_2_
  5.9 0.0 copy-start.2
  5.9 2.1 %collective-permute-start.1 = (bf16[1,256,512]{2,1,0:T(8,128)(2,1)S(1)}, bf16[1,256,512]{2,1,0:T(8,128)(2,1)S(1)}, u32[]{:S(2)}, u32[]{:S(2)}) collective-permute-start(bf16[1,256,512]{2,1,0:T(8,128)(2,1)S(1)} %reshape_transpose.14.rest_2_), channel_id=1, source_target_pairs={{0,12},{4,0},{8,4},{12,8},{1,13},{5,1},{9,5},{13,9},{2,14},{6,2},{... | collective-permute-start | bytes 786440 | tf_op jit(solution)/shard_map/ppermute | solution.py:293
  8.0 0.1 reshape_transpose.15.rest_3_
  8.1 1.1 %collective-permute-start.2 = (bf16[1,256,512]{2,1,0:T(8,128)(2,1)S(1)}, bf16[1,256,512]{2,1,0:T(8,128)(2,1)S(1)}, u32[]{:S(2)}, u32[]{:S(2)}) collective-permute-start(bf16[1,256,512]{2,1,0:T(8,128)(2,1)S(1)} %reshape_transpose.15.rest_3_), channel_id=1, source_target_pairs={{0,8},{4,12},{8,0},{12,4},{1,9},{5,13},{9,1},{13,5},{2,10},{6,14},... | collective-permute-start | bytes 786440 | tf_op jit(solution)/shard_map/ppermute | solution.py:293
  9.2 0.1 reshape_transpose.12.rest_0_.refs_0_
  9.3 0.0 copy-done.1
  9.3 1.1 %shard_map.57.weights_ref = bf16[1,512,512]{2,1,0:T(8,128)(2,1)S(1)} custom-call(s32[256,512]{1,0:T(8,128)S(1)} %copy-done.1), custom_call_target="tpu_custom_call" | custom-call | flops 5242880 | bytes 1048576 | tf_op jit(solution)/shard_map/pallas_call | solution.py:308
  10.4 0.0 copy-start.3
  10.4 0.0 copy-start.4
  10.4 6.8 %shard_map.56 = (f32[4,256,128]{2,1,0:T(8,128)S(1)}, f32[4,256,128]{2,1,0:T(8,128)S(1)}) custom-call(s32[256,512]{1,0:T(8,128)S(1)} %copy-done.1, bf16[1,256,512]{2,1,0:T(8,128)(2,1)S(1)} %reshape_transpose.12.rest_0_.refs_0_, bf16[1,256,512]{2,1,0:T(8,128)(2,1)S(1)} %reshape_transpose.13.rest_1_, bf16[1,256,512]{2,1,0:T(8,128)(2,1)S(1)} %reshape_transpose.14.rest_2_, ...), custom_call_target="tpu_custom_call" | custom-call | flops 536870912 | bytes 2097152 | tf_op jit(solution)/shard_map/pallas_call | solution.py:298
  17.2 0.0 collective-permute-done.refs_1_
  17.3 1.1 %collective-permute-done.1.refs_2_ = bf16[1,256,512]{2,1,0:T(8,128)(2,1)S(1)} collective-permute-done((bf16[1,256,512]{2,1,0:T(8,128)(2,1)S(1)}, bf16[1,256,512]{2,1,0:T(8,128)(2,1)S(1)}, u32[]{:S(2)}, u32[]{:S(2)}) %collective-permute-start.1) | collective-permute-done | bytes 262176 | tf_op jit(solution)/shard_map/ppermute | solution.py:293
  18.3 0.0 copy-done.2
  18.3 1.5 %shard_map.58 = (f32[1,2,512,512]{3,2,1,0:T(8,128)S(1)}, f32[1,16,512]{2,1,0:T(8,128)S(1)}, bf16[1,512,768]{2,1,0:T(8,128)(2,1)S(1)}) custom-call(f32[1,4,2,8,512]{4,3,2,1,0:T(8,128)S(1)} %copy-done.2, bf16[1,256,512]{2,1,0:T(8,128)(2,1)S(1)} %reshape_transpose.12.rest_0_.refs_0_, bf16[1,256,512]{2,1,0:T(8,128)(2,1)S(1)} %collective-permute-done.refs_1_, ...), custom_call_target="tpu_custom_call" | custom-call | flops 805306368 | bytes 2097152 | tf_op jit(solution)/shard_map/pallas_call | solution.py:318
  19.8 9.7 %collective-permute-done.2.last_ref = bf16[1,256,512]{2,1,0:T(8,128)(2,1)S(1)} collective-permute-done((bf16[1,256,512]{2,1,0:T(8,128)(2,1)S(1)}, bf16[1,256,512]{2,1,0:T(8,128)(2,1)S(1)}, u32[]{:S(2)}, u32[]{:S(2)}) %collective-permute-start.2) | collective-permute-done | bytes 262176 | tf_op jit(solution)/shard_map/ppermute | solution.py:293
  29.6 0.0 copy-done.3
  29.6 0.0 copy-done.4
  29.6 5.8 %shard_map.59 = (f32[1,8,768]{2,1,0:T(8,128)S(1)}, f32[1,8,768]{2,1,0:T(8,128)S(1)}, f32[1,8,768]{2,1,0:T(8,128)S(1)}, f32[1,8,768]{2,1,0:T(8,128)S(1)}) custom-call(f32[4,256,128]{2,1,0:T(8,128)S(1)} %get-tuple-element.26.beams_ref.mine_ref, f32[1,4,2,8,512]{4,3,2,1,0:T(8,128)S(1)} %copy-done.2, s32[4]{0:T(128)S(1)} %copy-done.3, s32[4]{0:T(128)S(1)} %copy-done.4, ...), custom_call_target="tpu_custom_call" | custom-call | flops 134217728 | bytes 2097152 | tf_op jit(solution)/shard_map/pallas_call | solution.py:332
  35.4 1.7 %collective-permute-start.5 = (f32[1,8,768]{2,1,0:T(8,128)S(1)}, f32[1,8,768]{2,1,0:T(8,128)S(1)}, u32[]{:S(2)}, u32[]{:S(2)}) collective-permute-start(f32[1,8,768]{2,1,0:T(8,128)S(1)} %get-tuple-element.34), channel_id=1, source_target_pairs={{0,12},{4,8},{8,4},{12,0},{1,13},{5,9},{9,5},{13,1},{2,14},{6,10},... | collective-permute-start | bytes 73736 | tf_op jit(solution)/shard_map/ppermute | solution.py:345
  37.1 0.0 collective-permute-start.4
  37.1 2.8 %collective-permute-start.3 = (f32[1,8,768]{2,1,0:T(8,128)S(1)}, f32[1,8,768]{2,1,0:T(8,128)S(1)}, u32[]{:S(2)}, u32[]{:S(2)}) collective-permute-start(f32[1,8,768]{2,1,0:T(8,128)S(1)} %get-tuple-element.31), channel_id=1, source_target_pairs={{0,4},{4,0},{8,12},{12,8},{1,5},{5,1},{9,13},{13,9},{2,6},{6,2},{1... | collective-permute-start | bytes 73736 | tf_op jit(solution)/shard_map/ppermute | solution.py:345
  39.8 1.2 %collective-permute-done.5.rest_1_ = f32[1,8,768]{2,1,0:T(8,128)S(1)} collective-permute-done((f32[1,8,768]{2,1,0:T(8,128)S(1)}, f32[1,8,768]{2,1,0:T(8,128)S(1)}, u32[]{:S(2)}, u32[]{:S(2)}) %collective-permute-start.5) | collective-permute-done | bytes 24608 | tf_op jit(solution)/shard_map/ppermute | solution.py:345
  41.1 0.4 shard_map.60
  41.4 0.5 %collective-permute-done.4.rest_0_ = f32[1,8,768]{2,1,0:T(8,128)S(1)} collective-permute-done((f32[1,8,768]{2,1,0:T(8,128)S(1)}, f32[1,8,768]{2,1,0:T(8,128)S(1)}, u32[]{:S(2)}, u32[]{:S(2)}) %collective-permute-start.4) | collective-permute-done | bytes 24608 | tf_op jit(solution)/shard_map/ppermute | solution.py:345
  41.9 0.3 shard_map.61
  42.2 0.0 collective-permute-done.3.rest_0_
  42.2 0.3 shard_map.62
  42.5 0.1 collective-permute-start.6
  42.6 1.5 %collective-permute-done.6.theirs_ref = f32[4,128,128]{2,1,0:T(8,128)S(1)} collective-permute-done((f32[4,128,128]{2,1,0:T(8,128)S(1)}, f32[4,128,128]{2,1,0:T(8,128)S(1)}, u32[]{:S(2)}, u32[]{:S(2)}) %collective-permute-start.6) | collective-permute-done | bytes 262176 | tf_op jit(solution)/shard_map/ppermute | solution.py:360
  44.1 0.9 %shard_map.63 = f32[128,4,128]{2,1,0:T(4,128)} custom-call(f32[4,128,128]{2,1,0:T(8,128)S(1)} %get-tuple-element.39.mine_ref, f32[4,128,128]{2,1,0:T(8,128)S(1)} %collective-permute-done.6.theirs_ref), custom_call_target="tpu_custom_call" | custom-call | flops 131072 | bytes 786432 | tf_op jit(solution)/shard_map/pallas_call | solution.py:362
Async XLA Ops:
  0.0 9.3 %copy-start.1 = (s32[256,512]{1,0:T(8,128)S(1)}, s32[256,512]{1,0:T(8,128)}, u32[]{:S(2)}) copy-start(s32[256,512]{1,0:T(8,128)} %phase_ref.3) | copy-start | bytes 1572868
  1.3 15.9 %collective-permute-start = (bf16[1,256,512]{2,1,0:T(8,128)(2,1)S(1)}, bf16[1,256,512]{2,1,0:T(8,128)(2,1)S(1)}, u32[]{:S(2)}, u32[]{:S(2)}) collective-permute-start(bf16[1,256,512]{2,1,0:T(8,128)(2,1)S(1)} %reshape_transpose.13.rest_1_), channel_id=1, source_target_pairs={{0,4},{4,8},{8,12},{12,0},{1,5},{5,9},{9,13},{13,1},{2,6},{6,10},{... | collective-permute-start | bytes 786440 | tf_op jit(solution)/shard_map/ppermute | solution.py:293
  4.4 1.2 %copy-start = (bf16[128,1,4,2,512]{4,3,2,1,0:T(2,128)(2,1)S(1)}, bf16[128,1,4,2,512]{4,3,2,1,0:T(2,128)(2,1)}, u32[]{:S(2)}) copy-start(bf16[128,1,4,2,512]{4,3,2,1,0:T(2,128)(2,1)} %voltages_ref.1) | copy-start | bytes 3145732
  5.9 12.4 %copy-start.2 = (f32[1,4,2,8,512]{4,3,2,1,0:T(8,128)S(1)}, f32[1,4,2,8,512]{4,3,2,1,0:T(8,128)}, u32[]{:S(2)}) copy-start(f32[1,4,2,8,512]{4,3,2,1,0:T(8,128)} %start_ref.3) | copy-start | bytes 393220
  5.9 12.4 %collective-permute-start.1 = (bf16[1,256,512]{2,1,0:T(8,128)(2,1)S(1)}, bf16[1,256,512]{2,1,0:T(8,128)(2,1)S(1)}, u32[]{:S(2)}, u32[]{:S(2)}) collective-permute-start(bf16[1,256,512]{2,1,0:T(8,128)(2,1)S(1)} %reshape_transpose.14.rest_2_), channel_id=1, source_target_pairs={{0,12},{4,0},{8,4},{12,8},{1,13},{5,1},{9,5},{13,9},{2,14},{6,2},{... | collective-permute-start | bytes 786440 | tf_op jit(solution)/shard_map/ppermute | solution.py:293
  8.1 21.5 %collective-permute-start.2 = (bf16[1,256,512]{2,1,0:T(8,128)(2,1)S(1)}, bf16[1,256,512]{2,1,0:T(8,128)(2,1)S(1)}, u32[]{:S(2)}, u32[]{:S(2)}) collective-permute-start(bf16[1,256,512]{2,1,0:T(8,128)(2,1)S(1)} %reshape_transpose.15.rest_3_), channel_id=1, source_target_pairs={{0,8},{4,12},{8,0},{12,4},{1,9},{5,13},{9,1},{13,5},{2,10},{6,14},... | collective-permute-start | bytes 786440 | tf_op jit(solution)/shard_map/ppermute | solution.py:293
  10.4 19.2 %copy-start.3 = (s32[4]{0:T(128)S(1)}, s32[4]{0:T(128)}, u32[]{:S(2)}) copy-start(s32[4]{0:T(128)} %flags_ref.1) | copy-start | bytes 52
  10.4 19.2 %copy-start.4 = (s32[4]{0:T(128)S(1)}, s32[4]{0:T(128)}, u32[]{:S(2)}) copy-start(s32[4]{0:T(128)} %ranks_ref.1) | copy-start | bytes 52
  35.4 5.7 %collective-permute-start.5 = (f32[1,8,768]{2,1,0:T(8,128)S(1)}, f32[1,8,768]{2,1,0:T(8,128)S(1)}, u32[]{:S(2)}, u32[]{:S(2)}) collective-permute-start(f32[1,8,768]{2,1,0:T(8,128)S(1)} %get-tuple-element.34), channel_id=1, source_target_pairs={{0,12},{4,8},{8,4},{12,0},{1,13},{5,9},{9,5},{13,1},{2,14},{6,10},... | collective-permute-start | bytes 73736 | tf_op jit(solution)/shard_map/ppermute | solution.py:345
  37.1 4.8 %collective-permute-start.4 = (f32[1,8,768]{2,1,0:T(8,128)S(1)}, f32[1,8,768]{2,1,0:T(8,128)S(1)}, u32[]{:S(2)}, u32[]{:S(2)}) collective-permute-start(f32[1,8,768]{2,1,0:T(8,128)S(1)} %get-tuple-element.32), channel_id=1, source_target_pairs={{0,8},{4,12},{8,0},{12,4},{1,9},{5,13},{9,1},{13,5},{2,10},{6,14},... | collective-permute-start | bytes 73736 | tf_op jit(solution)/shard_map/ppermute | solution.py:345
  37.1 5.1 %collective-permute-start.3 = (f32[1,8,768]{2,1,0:T(8,128)S(1)}, f32[1,8,768]{2,1,0:T(8,128)S(1)}, u32[]{:S(2)}, u32[]{:S(2)}) collective-permute-start(f32[1,8,768]{2,1,0:T(8,128)S(1)} %get-tuple-element.31), channel_id=1, source_target_pairs={{0,4},{4,0},{8,12},{12,8},{1,5},{5,1},{9,13},{13,9},{2,6},{6,2},{1... | collective-permute-start | bytes 73736 | tf_op jit(solution)/shard_map/ppermute | solution.py:345
  42.5 1.6 %collective-permute-start.6 = (f32[4,128,128]{2,1,0:T(8,128)S(1)}, f32[4,128,128]{2,1,0:T(8,128)S(1)}, u32[]{:S(2)}, u32[]{:S(2)}) collective-permute-start(f32[4,128,128]{2,1,0:T(8,128)S(1)} %get-tuple-element.40), channel_id=1, source_target_pairs={{0,1},{1,0},{2,3},{3,2},{4,5},{5,4},{6,7},{7,6},{8,9},{9,8},{10,11... | collective-permute-start | bytes 786440 | tf_op jit(solution)/shard_map/ppermute | solution.py:360

commit v10 on v9

--- a/solution.py
+++ b/solution.py
@@ -184,6 +184,47 @@
     return real_v * factor, imag_v * factor
 
 
+def orthonormalize_by_gram(real_z, imag_z):
+    vectors = real_z.shape[0]
+    row = lax.broadcasted_iota(jnp.int32, (vectors, 1), 0)
+    by_z = []
+    for n in range(vectors):
+        real_a = jnp.broadcast_to(real_z[n : n + 1], real_z.shape)
+        imag_a = jnp.broadcast_to(imag_z[n : n + 1], real_z.shape)
+        by_z.append(
+            (
+                jnp.sum(real_a * real_z + imag_a * imag_z, axis=1, keepdims=True),
+                jnp.sum(real_a * imag_z - imag_a * real_z, axis=1, keepdims=True),
+            )
+        )
+    by_v = list(by_z)
+    real_v, imag_v = real_z, imag_z
+    for n in range(vectors - 1):
+        (real_d, imag_d), (real_p, imag_p) = by_z[n], by_v[n]
+        square = jnp.maximum(real_p[n : n + 1], 0.0)
+        inverse = jnp.where(row > n, 1.0 / (square + EPS), 0.0)
+        real_c, imag_c = real_d * inverse, imag_d * inverse
+        real_b, imag_b = real_p - real_c * square, imag_p - imag_c * square
+        for j in range(n + 1, vectors):
+            real_s, imag_s = real_c[j : j + 1], imag_c[j : j + 1]
+            real_q, imag_q = real_p[j : j + 1], -imag_p[j : j + 1]
+            real, imag = by_v[j]
+            by_v[j] = (
+                real - (real_c * real_q - imag_c * imag_q) - (real_s * real_b + imag_s * imag_b),
+                imag - (real_c * imag_q + imag_c * real_q) - (real_s * imag_b - imag_s * real_b),
+            )
+            real, imag = by_z[j]
+            by_z[j] = (
+                real - (real_s * real_d + imag_s * imag_d),
+                imag - (real_s * imag_d - imag_s * real_d),
+            )
+        real_a, imag_a = real_v[n : n + 1], imag_v[n : n + 1]
+        real_v = real_v - (real_c * real_a - imag_c * imag_a)
+        imag_v = imag_v - (real_c * imag_a + imag_c * real_a)
+    factor = 1.0 / jnp.sqrt(jnp.sum(real_v * real_v + imag_v * imag_v, axis=1, keepdims=True) + EPS)
+    return real_v * factor, imag_v * factor
+
+
 def subspace_kernel(
     tm, own, factor, beams_ref, start_ref, flags_ref, ranks_ref, weights_ref, cov_ref, first_ref, across_ref, last_ref, *rest
 ):
@@ -211,7 +252,7 @@
         real_q, imag_q = orthonormalize(both[:vectors], both[vectors:], chunks)
         for sweep in range(1, ITERS):
             real_z, imag_z = cov_times(real_q, imag_q, high_ref, low_ref)
-            real_q, imag_q = orthonormalize(real_z, imag_z)
+            real_q, imag_q = orthonormalize_by_gram(real_z, imag_z)
         rank = flags_ref[chan] * ranks_ref[chan]
         keep = lax.broadcasted_iota(jnp.int32, (vectors, width), 0) < rank
         real_u = jnp.where(keep, real_q, 0.0)

time: 45.1 us -> 43.8 us (0.971)
  Pallas kernels: 17.2 us -> 15.8 us
    pallas_call x1, Pallas kernels: 5.79 us -> 4.43 us  [local(): pl.pallas_call(functools.partial(subspace_kernel, tm, own, factor), out_s...]
  transfers between devices with their start and end apart: 7 -> 7, of which waited for: 5 -> 5; matrix products, arithmetic and copies ran while one was open for 1% -> 1% of each run, Pallas kernels for 23% -> 24%
where the time goes in v10:
time: 43.8 us; the launch traced here: 43.6 us
  Pallas kernels  15.8 us (36%)
  waiting for transfers between devices  14 us (32%)
  starting transfers between devices  10.8 us (25%)
  local copies, waits for them, and re-layouts  2.85 us (7%)
    ppermute x3, waiting for transfers between devices, local(): lax.ppermute(piece, 'tm', [(z, (z + by) % tm) for z in range(tm)])  10.8 us
    pallas_call x1, Pallas kernels, local(): pl.pallas_call(functools.partial(raw_beams_kernel, tm, own), out_shape=[r...  6.85 us
    ppermute x3, starting transfers between devices, local(): lax.ppermute(piece, 'tm', [(z, (z + by) % tm) for z in range(tm)])  6.23 us
    ppermute x3, starting transfers between devices, local(): arrived[x] = lax.ppermute(packets[x], 'tm', [(z, z ^ x) for z in range(tm)])  4.45 us
    pallas_call x1, Pallas kernels, local(): pl.pallas_call(functools.partial(subspace_kernel, tm, own, factor), out_s...  4.43 us
    ppermute x3, waiting for transfers between devices, local(): arrived[x] = lax.ppermute(packets[x], 'tm', [(z, z ^ x) for z in range(tm)])  1.71 us
    ppermute x1, waiting for transfers between devices, local(): theirs = lax.ppermute(powers[1], 'pol', [(0, 1), (1, 0)])  1.52 us
    pallas_call x1, Pallas kernels, local(): pl.pallas_call(early_kernel, out_shape=[jax.ShapeDtypeStruct((own, 2, wid...  1.51 us
  transfers between devices with their start and end apart: 7, of which 5 were waited for; matrix products, arithmetic and copies ran while one was open for 1% of the time, Pallas kernels for 24%

profile of v10, /device:TPU:0, one launch (start us, length us, event | category | flops | bytes accessed | tf_op | source)
XLA Modules:
  0.0 43.6 jit_solution(5630918428922578268)
XLA Ops:
  0.0 0.0 copy-start.1
  0.0 1.2 %constant_dynamic-slice_fusion = bf16[128,1,1,2,512]{4,3,2,1,0:T(2,128)(2,1)S(1)} fusion(bf16[128,1,4,2,512]{4,3,2,1,0:T(2,128)(2,1)} %voltages_ref.1, s32[]{:T(128)S(6)} %select_n.3), kind=kLoop, calls=%fused_computation | loop fusion | bytes 524292 | tf_op jit(solution)/shard_map/dynamic_slice | solution.py:330
  1.2 0.1 reshape_transpose.13.rest_1_
  1.3 3.1 %collective-permute-start = (bf16[1,256,512]{2,1,0:T(8,128)(2,1)S(1)}, bf16[1,256,512]{2,1,0:T(8,128)(2,1)S(1)}, u32[]{:S(2)}, u32[]{:S(2)}) collective-permute-start(bf16[1,256,512]{2,1,0:T(8,128)(2,1)S(1)} %reshape_transpose.13.rest_1_), channel_id=1, source_target_pairs={{0,4},{4,8},{8,12},{12,0},{1,5},{5,9},{9,13},{13,1},{2,6},{6,10},{... | collective-permute-start | bytes 786440 | tf_op jit(solution)/shard_map/ppermute | solution.py:334
  4.4 0.0 copy-start
  4.4 1.2 %copy-done = bf16[128,1,4,2,512]{4,3,2,1,0:T(2,128)(2,1)S(1)} copy-done((bf16[128,1,4,2,512]{4,3,2,1,0:T(2,128)(2,1)S(1)}, bf16[128,1,4,2,512]{4,3,2,1,0:T(2,128)(2,1)}, u32[]{:S(2)}) %copy-start) | copy-done | bytes 1048600
  5.6 0.2 shard_map.55
  5.8 0.1 reshape_transpose.14.rest_2_
  5.9 0.0 copy-start.2
  5.9 2.1 %collective-permute-start.1 = (bf16[1,256,512]{2,1,0:T(8,128)(2,1)S(1)}, bf16[1,256,512]{2,1,0:T(8,128)(2,1)S(1)}, u32[]{:S(2)}, u32[]{:S(2)}) collective-permute-start(bf16[1,256,512]{2,1,0:T(8,128)(2,1)S(1)} %reshape_transpose.14.rest_2_), channel_id=1, source_target_pairs={{0,12},{4,0},{8,4},{12,8},{1,13},{5,1},{9,5},{13,9},{2,14},{6,2},{... | collective-permute-start | bytes 786440 | tf_op jit(solution)/shard_map/ppermute | solution.py:334
  8.0 0.1 reshape_transpose.15.rest_3_
  8.1 1.1 %collective-permute-start.2 = (bf16[1,256,512]{2,1,0:T(8,128)(2,1)S(1)}, bf16[1,256,512]{2,1,0:T(8,128)(2,1)S(1)}, u32[]{:S(2)}, u32[]{:S(2)}) collective-permute-start(bf16[1,256,512]{2,1,0:T(8,128)(2,1)S(1)} %reshape_transpose.15.rest_3_), channel_id=1, source_target_pairs={{0,8},{4,12},{8,0},{12,4},{1,9},{5,13},{9,1},{13,5},{2,10},{6,14},... | collective-permute-start | bytes 786440 | tf_op jit(solution)/shard_map/ppermute | solution.py:334
  9.2 0.1 reshape_transpose.12.rest_0_.refs_0_
  9.3 0.0 copy-done.1
  9.3 1.1 %shard_map.57.weights_ref = bf16[1,512,512]{2,1,0:T(8,128)(2,1)S(1)} custom-call(s32[256,512]{1,0:T(8,128)S(1)} %copy-done.1), custom_call_target="tpu_custom_call" | custom-call | flops 5242880 | bytes 1048576 | tf_op jit(solution)/shard_map/pallas_call | solution.py:349
  10.4 0.0 copy-start.3
  10.4 0.0 copy-start.4
  10.4 6.8 %shard_map.56 = (f32[4,256,128]{2,1,0:T(8,128)S(1)}, f32[4,256,128]{2,1,0:T(8,128)S(1)}) custom-call(s32[256,512]{1,0:T(8,128)S(1)} %copy-done.1, bf16[1,256,512]{2,1,0:T(8,128)(2,1)S(1)} %reshape_transpose.12.rest_0_.refs_0_, bf16[1,256,512]{2,1,0:T(8,128)(2,1)S(1)} %reshape_transpose.13.rest_1_, bf16[1,256,512]{2,1,0:T(8,128)(2,1)S(1)} %reshape_transpose.14.rest_2_, ...), custom_call_target="tpu_custom_call" | custom-call | flops 536870912 | bytes 2097152 | tf_op jit(solution)/shard_map/pallas_call | solution.py:339
  17.2 0.0 collective-permute-done.refs_1_
  17.3 1.1 %collective-permute-done.1.refs_2_ = bf16[1,256,512]{2,1,0:T(8,128)(2,1)S(1)} collective-permute-done((bf16[1,256,512]{2,1,0:T(8,128)(2,1)S(1)}, bf16[1,256,512]{2,1,0:T(8,128)(2,1)S(1)}, u32[]{:S(2)}, u32[]{:S(2)}) %collective-permute-start.1) | collective-permute-done | bytes 262176 | tf_op jit(solution)/shard_map/ppermute | solution.py:334
  18.3 0.0 copy-done.2
  18.3 1.5 %shard_map.58 = (f32[1,2,512,512]{3,2,1,0:T(8,128)S(1)}, f32[1,16,512]{2,1,0:T(8,128)S(1)}, bf16[1,512,768]{2,1,0:T(8,128)(2,1)S(1)}) custom-call(f32[1,4,2,8,512]{4,3,2,1,0:T(8,128)S(1)} %copy-done.2, bf16[1,256,512]{2,1,0:T(8,128)(2,1)S(1)} %reshape_transpose.12.rest_0_.refs_0_, bf16[1,256,512]{2,1,0:T(8,128)(2,1)S(1)} %collective-permute-done.refs_1_, ...), custom_call_target="tpu_custom_call" | custom-call | flops 805306368 | bytes 2097152 | tf_op jit(solution)/shard_map/pallas_call | solution.py:359
  19.8 9.7 %collective-permute-done.2.last_ref = bf16[1,256,512]{2,1,0:T(8,128)(2,1)S(1)} collective-permute-done((bf16[1,256,512]{2,1,0:T(8,128)(2,1)S(1)}, bf16[1,256,512]{2,1,0:T(8,128)(2,1)S(1)}, u32[]{:S(2)}, u32[]{:S(2)}) %collective-permute-start.2) | collective-permute-done | bytes 262176 | tf_op jit(solution)/shard_map/ppermute | solution.py:334
  29.6 0.0 copy-done.3
  29.6 0.0 copy-done.4
  29.6 4.4 %shard_map.59 = (f32[1,8,768]{2,1,0:T(8,128)S(1)}, f32[1,8,768]{2,1,0:T(8,128)S(1)}, f32[1,8,768]{2,1,0:T(8,128)S(1)}, f32[1,8,768]{2,1,0:T(8,128)S(1)}) custom-call(f32[4,256,128]{2,1,0:T(8,128)S(1)} %get-tuple-element.26.beams_ref.mine_ref, f32[1,4,2,8,512]{4,3,2,1,0:T(8,128)S(1)} %copy-done.2, s32[4]{0:T(128)S(1)} %copy-done.3, s32[4]{0:T(128)S(1)} %copy-done.4, ...), custom_call_target="tpu_custom_call" | custom-call | flops 134217728 | bytes 2097152 | tf_op jit(solution)/shard_map/pallas_call | solution.py:373
  34.0 1.7 %collective-permute-start.5 = (f32[1,8,768]{2,1,0:T(8,128)S(1)}, f32[1,8,768]{2,1,0:T(8,128)S(1)}, u32[]{:S(2)}, u32[]{:S(2)}) collective-permute-start(f32[1,8,768]{2,1,0:T(8,128)S(1)} %get-tuple-element.34), channel_id=1, source_target_pairs={{0,12},{4,8},{8,4},{12,0},{1,13},{5,9},{9,5},{13,1},{2,14},{6,10},... | collective-permute-start | bytes 73736 | tf_op jit(solution)/shard_map/ppermute | solution.py:386
  35.7 0.0 collective-permute-start.4
  35.7 2.8 %collective-permute-start.3 = (f32[1,8,768]{2,1,0:T(8,128)S(1)}, f32[1,8,768]{2,1,0:T(8,128)S(1)}, u32[]{:S(2)}, u32[]{:S(2)}) collective-permute-start(f32[1,8,768]{2,1,0:T(8,128)S(1)} %get-tuple-element.31), channel_id=1, source_target_pairs={{0,4},{4,0},{8,12},{12,8},{1,5},{5,1},{9,13},{13,9},{2,6},{6,2},{1... | collective-permute-start | bytes 73736 | tf_op jit(solution)/shard_map/ppermute | solution.py:386
  38.5 1.2 %collective-permute-done.5.rest_1_ = f32[1,8,768]{2,1,0:T(8,128)S(1)} collective-permute-done((f32[1,8,768]{2,1,0:T(8,128)S(1)}, f32[1,8,768]{2,1,0:T(8,128)S(1)}, u32[]{:S(2)}, u32[]{:S(2)}) %collective-permute-start.5) | collective-permute-done | bytes 24608 | tf_op jit(solution)/shard_map/ppermute | solution.py:386
  39.7 0.4 shard_map.60
  40.1 0.5 %collective-permute-done.4.rest_0_ = f32[1,8,768]{2,1,0:T(8,128)S(1)} collective-permute-done((f32[1,8,768]{2,1,0:T(8,128)S(1)}, f32[1,8,768]{2,1,0:T(8,128)S(1)}, u32[]{:S(2)}, u32[]{:S(2)}) %collective-permute-start.4) | collective-permute-done | bytes 24608 | tf_op jit(solution)/shard_map/ppermute | solution.py:386
  40.5 0.3 shard_map.61
  40.8 0.0 collective-permute-done.3.rest_0_
  40.9 0.3 shard_map.62
  41.2 0.1 collective-permute-start.6
  41.2 1.5 %collective-permute-done.6.theirs_ref = f32[4,128,128]{2,1,0:T(8,128)S(1)} collective-permute-done((f32[4,128,128]{2,1,0:T(8,128)S(1)}, f32[4,128,128]{2,1,0:T(8,128)S(1)}, u32[]{:S(2)}, u32[]{:S(2)}) %collective-permute-start.6) | collective-permute-done | bytes 262176 | tf_op jit(solution)/shard_map/ppermute | solution.py:401
  42.8 0.9 %shard_map.63 = f32[128,4,128]{2,1,0:T(4,128)} custom-call(f32[4,128,128]{2,1,0:T(8,128)S(1)} %get-tuple-element.39.mine_ref, f32[4,128,128]{2,1,0:T(8,128)S(1)} %collective-permute-done.6.theirs_ref), custom_call_target="tpu_custom_call" | custom-call | flops 131072 | bytes 786432 | tf_op jit(solution)/shard_map/pallas_call | solution.py:403
Async XLA Ops:
  0.0 9.3 %copy-start.1 = (s32[256,512]{1,0:T(8,128)S(1)}, s32[256,512]{1,0:T(8,128)}, u32[]{:S(2)}) copy-start(s32[256,512]{1,0:T(8,128)} %phase_ref.3) | copy-start | bytes 1572868
  1.3 15.9 %collective-permute-start = (bf16[1,256,512]{2,1,0:T(8,128)(2,1)S(1)}, bf16[1,256,512]{2,1,0:T(8,128)(2,1)S(1)}, u32[]{:S(2)}, u32[]{:S(2)}) collective-permute-start(bf16[1,256,512]{2,1,0:T(8,128)(2,1)S(1)} %reshape_transpose.13.rest_1_), channel_id=1, source_target_pairs={{0,4},{4,8},{8,12},{12,0},{1,5},{5,9},{9,13},{13,1},{2,6},{6,10},{... | collective-permute-start | bytes 786440 | tf_op jit(solution)/shard_map/ppermute | solution.py:334
  4.4 1.2 %copy-start = (bf16[128,1,4,2,512]{4,3,2,1,0:T(2,128)(2,1)S(1)}, bf16[128,1,4,2,512]{4,3,2,1,0:T(2,128)(2,1)}, u32[]{:S(2)}) copy-start(bf16[128,1,4,2,512]{4,3,2,1,0:T(2,128)(2,1)} %voltages_ref.1) | copy-start | bytes 3145732
  5.9 12.4 %copy-start.2 = (f32[1,4,2,8,512]{4,3,2,1,0:T(8,128)S(1)}, f32[1,4,2,8,512]{4,3,2,1,0:T(8,128)}, u32[]{:S(2)}) copy-start(f32[1,4,2,8,512]{4,3,2,1,0:T(8,128)} %start_ref.3) | copy-start | bytes 393220
  5.9 12.4 %collective-permute-start.1 = (bf16[1,256,512]{2,1,0:T(8,128)(2,1)S(1)}, bf16[1,256,512]{2,1,0:T(8,128)(2,1)S(1)}, u32[]{:S(2)}, u32[]{:S(2)}) collective-permute-start(bf16[1,256,512]{2,1,0:T(8,128)(2,1)S(1)} %reshape_transpose.14.rest_2_), channel_id=1, source_target_pairs={{0,12},{4,0},{8,4},{12,8},{1,13},{5,1},{9,5},{13,9},{2,14},{6,2},{... | collective-permute-start | bytes 786440 | tf_op jit(solution)/shard_map/ppermute | solution.py:334
  8.1 21.5 %collective-permute-start.2 = (bf16[1,256,512]{2,1,0:T(8,128)(2,1)S(1)}, bf16[1,256,512]{2,1,0:T(8,128)(2,1)S(1)}, u32[]{:S(2)}, u32[]{:S(2)}) collective-permute-start(bf16[1,256,512]{2,1,0:T(8,128)(2,1)S(1)} %reshape_transpose.15.rest_3_), channel_id=1, source_target_pairs={{0,8},{4,12},{8,0},{12,4},{1,9},{5,13},{9,1},{13,5},{2,10},{6,14},... | collective-permute-start | bytes 786440 | tf_op jit(solution)/shard_map/ppermute | solution.py:334
  10.4 19.2 %copy-start.3 = (s32[4]{0:T(128)S(1)}, s32[4]{0:T(128)}, u32[]{:S(2)}) copy-start(s32[4]{0:T(128)} %flags_ref.1) | copy-start | bytes 52
  10.4 19.2 %copy-start.4 = (s32[4]{0:T(128)S(1)}, s32[4]{0:T(128)}, u32[]{:S(2)}) copy-start(s32[4]{0:T(128)} %ranks_ref.1) | copy-start | bytes 52
  34.0 5.7 %collective-permute-start.5 = (f32[1,8,768]{2,1,0:T(8,128)S(1)}, f32[1,8,768]{2,1,0:T(8,128)S(1)}, u32[]{:S(2)}, u32[]{:S(2)}) collective-permute-start(f32[1,8,768]{2,1,0:T(8,128)S(1)} %get-tuple-element.34), channel_id=1, source_target_pairs={{0,12},{4,8},{8,4},{12,0},{1,13},{5,9},{9,5},{13,1},{2,14},{6,10},... | collective-permute-start | bytes 73736 | tf_op jit(solution)/shard_map/ppermute | solution.py:386
  35.7 4.8 %collective-permute-start.4 = (f32[1,8,768]{2,1,0:T(8,128)S(1)}, f32[1,8,768]{2,1,0:T(8,128)S(1)}, u32[]{:S(2)}, u32[]{:S(2)}) collective-permute-start(f32[1,8,768]{2,1,0:T(8,128)S(1)} %get-tuple-element.32), channel_id=1, source_target_pairs={{0,8},{4,12},{8,0},{12,4},{1,9},{5,13},{9,1},{13,5},{2,10},{6,14},... | collective-permute-start | bytes 73736 | tf_op jit(solution)/shard_map/ppermute | solution.py:386
  35.7 5.1 %collective-permute-start.3 = (f32[1,8,768]{2,1,0:T(8,128)S(1)}, f32[1,8,768]{2,1,0:T(8,128)S(1)}, u32[]{:S(2)}, u32[]{:S(2)}) collective-permute-start(f32[1,8,768]{2,1,0:T(8,128)S(1)} %get-tuple-element.31), channel_id=1, source_target_pairs={{0,4},{4,0},{8,12},{12,8},{1,5},{5,1},{9,13},{13,9},{2,6},{6,2},{1... | collective-permute-start | bytes 73736 | tf_op jit(solution)/shard_map/ppermute | solution.py:386
  41.2 1.6 %collective-permute-start.6 = (f32[4,128,128]{2,1,0:T(8,128)S(1)}, f32[4,128,128]{2,1,0:T(8,128)S(1)}, u32[]{:S(2)}, u32[]{:S(2)}) collective-permute-start(f32[4,128,128]{2,1,0:T(8,128)S(1)} %get-tuple-element.40), channel_id=1, source_target_pairs={{0,1},{1,0},{2,3},{3,2},{4,5},{5,4},{6,7},{7,6},{8,9},{9,8},{10,11... | collective-permute-start | bytes 786440 | tf_op jit(solution)/shard_map/ppermute | solution.py:401

commit v11 on v10

--- a/solution.py
+++ b/solution.py
@@ -105,11 +105,12 @@
                 out_ref[chan] = product[:, :half] - by_imag
 
 
-def own_weights_kernel(own, chan_dev, phase_ref, out_ref):
+def own_weights_kernel(own, chan_dev, phase_ref, out_ref, weights):
     beams = phase_ref.shape[0]
     first = lax.axis_index("chan") * chan_dev + lax.axis_index("tm") * own
     for o in range(own):
-        fill_weights(phase_ref, 0, beams, first + o + 1, out_ref.at[o])
+        fill_weights(phase_ref, 0, beams, first + o + 1, weights)
+        out_ref[o] = weights[...].T
 
 
 def rotate(x):
@@ -232,7 +233,7 @@
     vectors, width = start_ref.shape[3], start_ref.shape[4]
     rows = last_ref.shape[1]
     tm_index = lax.axis_index("tm")
-    beams = weights_ref.shape[1] // 2
+    beams = weights_ref.shape[2] // 2
     for o in range(own):
         chan = tm_index * own + o
         across = last_ref[o].T
@@ -258,7 +259,7 @@
         real_u = jnp.where(keep, real_q, 0.0)
         imag_u = jnp.where(keep, imag_q, 0.0)
         both = jnp.concatenate(split(jnp.concatenate([real_u, imag_u], axis=0)), axis=0)
-        product = dot(both, weights_ref[o], NT)
+        product = dot(both, weights_ref[o], NN)
         product = product[: 2 * vectors] + product[2 * vectors :]
         real_w = product[:vectors, :beams] - product[vectors:, beams:]
         imag_w = product[:vectors, beams:] + product[vectors:, :beams]
@@ -348,9 +349,10 @@
 
     own_weights = pl.pallas_call(
         functools.partial(own_weights_kernel, own, chan_dev),
-        out_shape=jax.ShapeDtypeStruct((own, 2 * beams, width), BF16),
+        out_shape=jax.ShapeDtypeStruct((own, width, 2 * beams), BF16),
         in_specs=[whole],
         out_specs=whole,
+        scratch_shapes=[pltpu.VMEM((2 * beams, width), BF16)],
         compiler_params=params,
         cost_estimate=cost(20 * own * beams * width, 8 * own * beams * width),
     )(phase_index)
@@ -381,10 +383,11 @@
         cost_estimate=cost(32 * own * vectors * tm * samples * width, 8 * own * width * width),
     )(mine, start_block, flags, ranks, own_weights, cov, first, across, blocks[-1])
 
+    order = [*range(2, tm), 1]
     arrived = list(packets)
-    for x in reversed(range(1, tm)):
+    for x in order:
         arrived[x] = lax.ppermute(packets[x], "tm", [(z, z ^ x) for z in range(tm)])
-    groups = [[0, tm - 1], *[[x] for x in reversed(range(1, tm - 1))]]
+    groups = [[0, order[0]], *[[x] for x in order[1:]]]
     shape = jax.ShapeDtypeStruct((chan_dev, samples, half), F32)
     powers = []
     for xs in groups:

time: 43.8 us -> 43.1 us (0.984)
  starting transfers between devices: 10.8 us -> 9.85 us
    ppermute x3, starting transfers between devices: 4.45 us -> 3.55 us  [local(): arrived[x] = lax.ppermute(packets[x], 'tm', [(z, z ^ x) for z in range(tm)])]
where the time goes in v11:
time: 43.1 us; the launch traced here: 42.9 us
  Pallas kernels  16 us (37%)
  waiting for transfers between devices  14.1 us (33%)
  starting transfers between devices  9.85 us (23%)
  local copies, waits for them, and re-layouts  2.85 us (7%)
    ppermute x3, waiting for transfers between devices, local(): lax.ppermute(piece, 'tm', [(z, (z + by) % tm) for z in range(tm)])  10.6 us
    pallas_call x1, Pallas kernels, local(): pl.pallas_call(functools.partial(raw_beams_kernel, tm, own), out_shape=[r...  6.85 us
    ppermute x3, starting transfers between devices, local(): lax.ppermute(piece, 'tm', [(z, (z + by) % tm) for z in range(tm)])  6.23 us
    pallas_call x1, Pallas kernels, local(): pl.pallas_call(functools.partial(subspace_kernel, tm, own, factor), out_s...  4.4 us
    ppermute x3, starting transfers between devices, local(): arrived[x] = lax.ppermute(packets[x], 'tm', [(z, z ^ x) for z in range(tm)])  3.55 us
    ppermute x3, waiting for transfers between devices, local(): arrived[x] = lax.ppermute(packets[x], 'tm', [(z, z ^ x) for z in range(tm)])  1.95 us
    ppermute x1, waiting for transfers between devices, local(): theirs = lax.ppermute(powers[1], 'pol', [(0, 1), (1, 0)])  1.52 us
    pallas_call x1, Pallas kernels, local(): pl.pallas_call(early_kernel, out_shape=[jax.ShapeDtypeStruct((own, 2, wid...  1.51 us
  transfers between devices with their start and end apart: 7, of which 5 were waited for; matrix products, arithmetic and copies ran while one was open for 1% of the time, Pallas kernels for 24%

profile of v11, /device:TPU:0, one launch (start us, length us, event | category | flops | bytes accessed | tf_op | source)
XLA Modules:
  0.0 42.9 jit_solution(10467329093702432057)
XLA Ops:
  0.0 0.0 copy-start.1
  0.0 1.2 %constant_dynamic-slice_fusion = bf16[128,1,1,2,512]{4,3,2,1,0:T(2,128)(2,1)S(1)} fusion(bf16[128,1,4,2,512]{4,3,2,1,0:T(2,128)(2,1)} %voltages_ref.1, s32[]{:T(128)S(6)} %select_n.3), kind=kLoop, calls=%fused_computation | loop fusion | bytes 524292 | tf_op jit(solution)/shard_map/dynamic_slice | solution.py:331
  1.2 0.1 reshape_transpose.13.rest_1_
  1.3 3.1 %collective-permute-start = (bf16[1,256,512]{2,1,0:T(8,128)(2,1)S(1)}, bf16[1,256,512]{2,1,0:T(8,128)(2,1)S(1)}, u32[]{:S(2)}, u32[]{:S(2)}) collective-permute-start(bf16[1,256,512]{2,1,0:T(8,128)(2,1)S(1)} %reshape_transpose.13.rest_1_), channel_id=1, source_target_pairs={{0,4},{4,8},{8,12},{12,0},{1,5},{5,9},{9,13},{13,1},{2,6},{6,10},{... | collective-permute-start | bytes 786440 | tf_op jit(solution)/shard_map/ppermute | solution.py:335
  4.4 0.0 copy-start
  4.4 1.2 %copy-done = bf16[128,1,4,2,512]{4,3,2,1,0:T(2,128)(2,1)S(1)} copy-done((bf16[128,1,4,2,512]{4,3,2,1,0:T(2,128)(2,1)S(1)}, bf16[128,1,4,2,512]{4,3,2,1,0:T(2,128)(2,1)}, u32[]{:S(2)}) %copy-start) | copy-done | bytes 1048600
  5.6 0.2 shard_map.55
  5.8 0.1 reshape_transpose.14.rest_2_
  5.9 0.0 copy-start.2
  5.9 2.1 %collective-permute-start.1 = (bf16[1,256,512]{2,1,0:T(8,128)(2,1)S(1)}, bf16[1,256,512]{2,1,0:T(8,128)(2,1)S(1)}, u32[]{:S(2)}, u32[]{:S(2)}) collective-permute-start(bf16[1,256,512]{2,1,0:T(8,128)(2,1)S(1)} %reshape_transpose.14.rest_2_), channel_id=1, source_target_pairs={{0,12},{4,0},{8,4},{12,8},{1,13},{5,1},{9,5},{13,9},{2,14},{6,2},{... | collective-permute-start | bytes 786440 | tf_op jit(solution)/shard_map/ppermute | solution.py:335
  8.0 0.1 reshape_transpose.15.rest_3_
  8.1 1.1 %collective-permute-start.2 = (bf16[1,256,512]{2,1,0:T(8,128)(2,1)S(1)}, bf16[1,256,512]{2,1,0:T(8,128)(2,1)S(1)}, u32[]{:S(2)}, u32[]{:S(2)}) collective-permute-start(bf16[1,256,512]{2,1,0:T(8,128)(2,1)S(1)} %reshape_transpose.15.rest_3_), channel_id=1, source_target_pairs={{0,8},{4,12},{8,0},{12,4},{1,9},{5,13},{9,1},{13,5},{2,10},{6,14},... | collective-permute-start | bytes 786440 | tf_op jit(solution)/shard_map/ppermute | solution.py:335
  9.2 0.1 reshape_transpose.12.rest_0_.refs_0_
  9.3 0.0 copy-done.1
  9.3 1.3 %shard_map.57.weights_ref = bf16[1,512,512]{2,1,0:T(8,128)(2,1)S(1)} custom-call(s32[256,512]{1,0:T(8,128)S(1)} %copy-done.1), custom_call_target="tpu_custom_call" | custom-call | flops 5242880 | bytes 1048576 | tf_op jit(solution)/shard_map/pallas_call | solution.py:350
  10.5 0.0 copy-start.3
  10.6 0.0 copy-start.4
  10.6 6.8 %shard_map.56 = (f32[4,256,128]{2,1,0:T(8,128)S(1)}, f32[4,256,128]{2,1,0:T(8,128)S(1)}) custom-call(s32[256,512]{1,0:T(8,128)S(1)} %copy-done.1, bf16[1,256,512]{2,1,0:T(8,128)(2,1)S(1)} %reshape_transpose.12.rest_0_.refs_0_, bf16[1,256,512]{2,1,0:T(8,128)(2,1)S(1)} %reshape_transpose.13.rest_1_, bf16[1,256,512]{2,1,0:T(8,128)(2,1)S(1)} %reshape_transpose.14.rest_2_, ...), custom_call_target="tpu_custom_call" | custom-call | flops 536870912 | bytes 2097152 | tf_op jit(solution)/shard_map/pallas_call | solution.py:340
  17.4 0.0 collective-permute-done.refs_1_
  17.4 0.9 %collective-permute-done.1.refs_2_ = bf16[1,256,512]{2,1,0:T(8,128)(2,1)S(1)} collective-permute-done((bf16[1,256,512]{2,1,0:T(8,128)(2,1)S(1)}, bf16[1,256,512]{2,1,0:T(8,128)(2,1)S(1)}, u32[]{:S(2)}, u32[]{:S(2)}) %collective-permute-start.1) | collective-permute-done | bytes 262176 | tf_op jit(solution)/shard_map/ppermute | solution.py:335
  18.3 0.0 copy-done.2
  18.3 1.5 %shard_map.58 = (f32[1,2,512,512]{3,2,1,0:T(8,128)S(1)}, f32[1,16,512]{2,1,0:T(8,128)S(1)}, bf16[1,512,768]{2,1,0:T(8,128)(2,1)S(1)}) custom-call(f32[1,4,2,8,512]{4,3,2,1,0:T(8,128)S(1)} %copy-done.2, bf16[1,256,512]{2,1,0:T(8,128)(2,1)S(1)} %reshape_transpose.12.rest_0_.refs_0_, bf16[1,256,512]{2,1,0:T(8,128)(2,1)S(1)} %collective-permute-done.refs_1_, ...), custom_call_target="tpu_custom_call" | custom-call | flops 805306368 | bytes 2097152 | tf_op jit(solution)/shard_map/pallas_call | solution.py:361
  19.8 9.7 %collective-permute-done.2.last_ref = bf16[1,256,512]{2,1,0:T(8,128)(2,1)S(1)} collective-permute-done((bf16[1,256,512]{2,1,0:T(8,128)(2,1)S(1)}, bf16[1,256,512]{2,1,0:T(8,128)(2,1)S(1)}, u32[]{:S(2)}, u32[]{:S(2)}) %collective-permute-start.2) | collective-permute-done | bytes 262176 | tf_op jit(solution)/shard_map/ppermute | solution.py:335
  29.6 0.0 copy-done.3
  29.6 0.0 copy-done.4
  29.6 4.4 %shard_map.59 = (f32[1,8,768]{2,1,0:T(8,128)S(1)}, f32[1,8,768]{2,1,0:T(8,128)S(1)}, f32[1,8,768]{2,1,0:T(8,128)S(1)}, f32[1,8,768]{2,1,0:T(8,128)S(1)}) custom-call(f32[4,256,128]{2,1,0:T(8,128)S(1)} %get-tuple-element.26.beams_ref.mine_ref, f32[1,4,2,8,512]{4,3,2,1,0:T(8,128)S(1)} %copy-done.2, s32[4]{0:T(128)S(1)} %copy-done.3, s32[4]{0:T(128)S(1)} %copy-done.4, ...), custom_call_target="tpu_custom_call" | custom-call | flops 134217728 | bytes 2097152 | tf_op jit(solution)/shard_map/pallas_call | solution.py:375
  34.0 0.1 collective-permute-start.5
  34.1 1.7 %collective-permute-start.4 = (f32[1,8,768]{2,1,0:T(8,128)S(1)}, f32[1,8,768]{2,1,0:T(8,128)S(1)}, u32[]{:S(2)}, u32[]{:S(2)}) collective-permute-start(f32[1,8,768]{2,1,0:T(8,128)S(1)} %get-tuple-element.32), channel_id=1, source_target_pairs={{0,12},{4,8},{8,4},{12,0},{1,13},{5,9},{9,5},{13,1},{2,14},{6,10},... | collective-permute-start | bytes 73736 | tf_op jit(solution)/shard_map/ppermute | solution.py:389
  35.7 1.8 %collective-permute-start.3 = (f32[1,8,768]{2,1,0:T(8,128)S(1)}, f32[1,8,768]{2,1,0:T(8,128)S(1)}, u32[]{:S(2)}, u32[]{:S(2)}) collective-permute-start(f32[1,8,768]{2,1,0:T(8,128)S(1)} %get-tuple-element.31), channel_id=1, source_target_pairs={{0,4},{4,0},{8,12},{12,8},{1,5},{5,1},{9,13},{13,9},{2,6},{6,2},{1... | collective-permute-start | bytes 73736 | tf_op jit(solution)/shard_map/ppermute | solution.py:389
  37.5 1.5 %collective-permute-done.5.rest_1_ = f32[1,8,768]{2,1,0:T(8,128)S(1)} collective-permute-done((f32[1,8,768]{2,1,0:T(8,128)S(1)}, f32[1,8,768]{2,1,0:T(8,128)S(1)}, u32[]{:S(2)}, u32[]{:S(2)}) %collective-permute-start.5) | collective-permute-done | bytes 24608 | tf_op jit(solution)/shard_map/ppermute | solution.py:389
  39.0 0.4 shard_map.60
  39.4 0.4 %collective-permute-done.4.rest_0_ = f32[1,8,768]{2,1,0:T(8,128)S(1)} collective-permute-done((f32[1,8,768]{2,1,0:T(8,128)S(1)}, f32[1,8,768]{2,1,0:T(8,128)S(1)}, u32[]{:S(2)}, u32[]{:S(2)}) %collective-permute-start.4) | collective-permute-done | bytes 24608 | tf_op jit(solution)/shard_map/ppermute | solution.py:389
  39.8 0.3 shard_map.61
  40.1 0.0 collective-permute-done.3.rest_0_
  40.2 0.3 shard_map.62
  40.5 0.1 collective-permute-start.6
  40.5 1.5 %collective-permute-done.6.theirs_ref = f32[4,128,128]{2,1,0:T(8,128)S(1)} collective-permute-done((f32[4,128,128]{2,1,0:T(8,128)S(1)}, f32[4,128,128]{2,1,0:T(8,128)S(1)}, u32[]{:S(2)}, u32[]{:S(2)}) %collective-permute-start.6) | collective-permute-done | bytes 262176 | tf_op jit(solution)/shard_map/ppermute | solution.py:404
  42.1 0.9 %shard_map.63 = f32[128,4,128]{2,1,0:T(4,128)} custom-call(f32[4,128,128]{2,1,0:T(8,128)S(1)} %get-tuple-element.39.mine_ref, f32[4,128,128]{2,1,0:T(8,128)S(1)} %collective-permute-done.6.theirs_ref), custom_call_target="tpu_custom_call" | custom-call | flops 131072 | bytes 786432 | tf_op jit(solution)/shard_map/pallas_call | solution.py:406
Async XLA Ops:
  0.0 9.3 %copy-start.1 = (s32[256,512]{1,0:T(8,128)S(1)}, s32[256,512]{1,0:T(8,128)}, u32[]{:S(2)}) copy-start(s32[256,512]{1,0:T(8,128)} %phase_ref.3) | copy-start | bytes 1572868
  1.3 16.1 %collective-permute-start = (bf16[1,256,512]{2,1,0:T(8,128)(2,1)S(1)}, bf16[1,256,512]{2,1,0:T(8,128)(2,1)S(1)}, u32[]{:S(2)}, u32[]{:S(2)}) collective-permute-start(bf16[1,256,512]{2,1,0:T(8,128)(2,1)S(1)} %reshape_transpose.13.rest_1_), channel_id=1, source_target_pairs={{0,4},{4,8},{8,12},{12,0},{1,5},{5,9},{9,13},{13,1},{2,6},{6,10},{... | collective-permute-start | bytes 786440 | tf_op jit(solution)/shard_map/ppermute | solution.py:335
  4.4 1.2 %copy-start = (bf16[128,1,4,2,512]{4,3,2,1,0:T(2,128)(2,1)S(1)}, bf16[128,1,4,2,512]{4,3,2,1,0:T(2,128)(2,1)}, u32[]{:S(2)}) copy-start(bf16[128,1,4,2,512]{4,3,2,1,0:T(2,128)(2,1)} %voltages_ref.1) | copy-start | bytes 3145732
  5.9 12.4 %copy-start.2 = (f32[1,4,2,8,512]{4,3,2,1,0:T(8,128)S(1)}, f32[1,4,2,8,512]{4,3,2,1,0:T(8,128)}, u32[]{:S(2)}) copy-start(f32[1,4,2,8,512]{4,3,2,1,0:T(8,128)} %start_ref.3) | copy-start | bytes 393220
  5.9 12.4 %collective-permute-start.1 = (bf16[1,256,512]{2,1,0:T(8,128)(2,1)S(1)}, bf16[1,256,512]{2,1,0:T(8,128)(2,1)S(1)}, u32[]{:S(2)}, u32[]{:S(2)}) collective-permute-start(bf16[1,256,512]{2,1,0:T(8,128)(2,1)S(1)} %reshape_transpose.14.rest_2_), channel_id=1, source_target_pairs={{0,12},{4,0},{8,4},{12,8},{1,13},{5,1},{9,5},{13,9},{2,14},{6,2},{... | collective-permute-start | bytes 786440 | tf_op jit(solution)/shard_map/ppermute | solution.py:335
  8.1 21.5 %collective-permute-start.2 = (bf16[1,256,512]{2,1,0:T(8,128)(2,1)S(1)}, bf16[1,256,512]{2,1,0:T(8,128)(2,1)S(1)}, u32[]{:S(2)}, u32[]{:S(2)}) collective-permute-start(bf16[1,256,512]{2,1,0:T(8,128)(2,1)S(1)} %reshape_transpose.15.rest_3_), channel_id=1, source_target_pairs={{0,8},{4,12},{8,0},{12,4},{1,9},{5,13},{9,1},{13,5},{2,10},{6,14},... | collective-permute-start | bytes 786440 | tf_op jit(solution)/shard_map/ppermute | solution.py:335
  10.5 19.0 %copy-start.3 = (s32[4]{0:T(128)S(1)}, s32[4]{0:T(128)}, u32[]{:S(2)}) copy-start(s32[4]{0:T(128)} %flags_ref.1) | copy-start | bytes 52
  10.6 19.0 %copy-start.4 = (s32[4]{0:T(128)S(1)}, s32[4]{0:T(128)}, u32[]{:S(2)}) copy-start(s32[4]{0:T(128)} %ranks_ref.1) | copy-start | bytes 52
  34.0 5.1 %collective-permute-start.5 = (f32[1,8,768]{2,1,0:T(8,128)S(1)}, f32[1,8,768]{2,1,0:T(8,128)S(1)}, u32[]{:S(2)}, u32[]{:S(2)}) collective-permute-start(f32[1,8,768]{2,1,0:T(8,128)S(1)} %get-tuple-element.34), channel_id=1, source_target_pairs={{0,8},{4,12},{8,0},{12,4},{1,9},{5,13},{9,1},{13,5},{2,10},{6,14},... | collective-permute-start | bytes 73736 | tf_op jit(solution)/shard_map/ppermute | solution.py:389
  34.1 5.8 %collective-permute-start.4 = (f32[1,8,768]{2,1,0:T(8,128)S(1)}, f32[1,8,768]{2,1,0:T(8,128)S(1)}, u32[]{:S(2)}, u32[]{:S(2)}) collective-permute-start(f32[1,8,768]{2,1,0:T(8,128)S(1)} %get-tuple-element.32), channel_id=1, source_target_pairs={{0,12},{4,8},{8,4},{12,0},{1,13},{5,9},{9,5},{13,1},{2,14},{6,10},... | collective-permute-start | bytes 73736 | tf_op jit(solution)/shard_map/ppermute | solution.py:389
  35.7 4.4 %collective-permute-start.3 = (f32[1,8,768]{2,1,0:T(8,128)S(1)}, f32[1,8,768]{2,1,0:T(8,128)S(1)}, u32[]{:S(2)}, u32[]{:S(2)}) collective-permute-start(f32[1,8,768]{2,1,0:T(8,128)S(1)} %get-tuple-element.31), channel_id=1, source_target_pairs={{0,4},{4,0},{8,12},{12,8},{1,5},{5,1},{9,13},{13,9},{2,6},{6,2},{1... | collective-permute-start | bytes 73736 | tf_op jit(solution)/shard_map/ppermute | solution.py:389
  40.5 1.6 %collective-permute-start.6 = (f32[4,128,128]{2,1,0:T(8,128)S(1)}, f32[4,128,128]{2,1,0:T(8,128)S(1)}, u32[]{:S(2)}, u32[]{:S(2)}) collective-permute-start(f32[4,128,128]{2,1,0:T(8,128)S(1)} %get-tuple-element.40), channel_id=1, source_target_pairs={{0,1},{1,0},{2,3},{3,2},{4,5},{5,4},{6,7},{7,6},{8,9},{9,8},{10,11... | collective-permute-start | bytes 786440 | tf_op jit(solution)/shard_map/ppermute | solution.py:404

commit v12 on v11

--- a/solution.py
+++ b/solution.py
@@ -267,10 +267,12 @@
             block = across_ref[o, :, i * rows : (i + 1) * rows] if i < tm - 1 else across
             series = project(real_u, imag_u, block)[0]
             series_ref[tm_index ^ shifted(-by)] = series
+        steered = jnp.concatenate([real_w, imag_w], axis=0).astype(BF16)
         for x, out in enumerate(outs):
-            out[o, :, :rows] = series_ref[x]
-            out[o, :, rows : rows + beams] = real_w
-            out[o, :, rows + beams :] = imag_w
+            series = series_ref[x]
+            series = jnp.concatenate([series[:, : rows // 2], series[:, rows // 2 :]], axis=0)
+            out[o, :, :beams] = steered
+            out[o, :, beams:] = series.astype(BF16)
 
 
 def first_kernel(own, xs, mine_ref, other_ref, *rest):
@@ -280,17 +282,13 @@
     for x, ref in zip(xs, packets):
         for o in range(own):
             chan = (lax.axis_index("tm") ^ x) * own + o
-            series = ref[o, :, :rows]
-            left = jnp.concatenate([series, -turned(series, 1)], axis=0)
-            high_s, low_s = split(left)
-            left = jnp.concatenate([high_s, high_s, low_s], axis=0)
+            series = ref[o, :, 2 * half :].astype(F32)
+            vectors = series.shape[0] // 2
+            series = jnp.concatenate([series[:vectors], series[vectors:]], axis=1)
+            left = jnp.concatenate([series, -turned(series, 1)], axis=0).astype(BF16)
             for swap, (raw_ref, out_ref) in enumerate(((mine_ref, mine_out), (other_ref, other_out))):
-                at = rows + (lax.axis_index("pol") ^ swap) * half
-                real_at = pl.ds(pl.multiple_of(at, half), half)
-                imag_at = pl.ds(pl.multiple_of(at + 2 * half, half), half)
-                right = jnp.concatenate([ref[o, :, real_at], ref[o, :, imag_at]], axis=0)
-                high_w, low_w = split(right)
-                right = jnp.concatenate([high_w, low_w, high_w], axis=0)
+                at = pl.multiple_of((lax.axis_index("pol") ^ swap) * half, half)
+                right = ref[o, :, pl.ds(at, half)]
                 beam = raw_ref[chan] - dot(left, right, TN)
                 squares[...] = beam * beam
                 out_ref[chan] = squares[pl.ds(0, samples, 2), :] + squares[pl.ds(1, samples, 2), :]
@@ -374,7 +372,7 @@
 
     packets = pl.pallas_call(
         functools.partial(subspace_kernel, tm, own, factor),
-        out_shape=[jax.ShapeDtypeStruct((own, vectors, rows + 2 * beams), F32)] * tm,
+        out_shape=[jax.ShapeDtypeStruct((own, 2 * vectors, beams + samples), BF16)] * tm,
         in_specs=[unread, whole, scalars, scalars] + [whole] * 5,
         out_specs=[whole] * tm,
         scratch_shapes=[pltpu.VMEM((2 * width, width), BF16)] * 2
@@ -399,7 +397,7 @@
             input_output_aliases={2 + len(xs) + i: i for i in range(len(powers))},
             scratch_shapes=[pltpu.VMEM((rows, half), F32)],
             compiler_params=params,
-            cost_estimate=cost(len(xs) * own * rows * 6 * vectors * beams, 8 * own * rows * beams),
+            cost_estimate=cost(len(xs) * own * rows * 2 * vectors * beams, 8 * own * rows * beams),
         )(mine, other, *[arrived[x] for x in xs], *powers)
     theirs = lax.ppermute(powers[1], "pol", [(0, 1), (1, 0)])
 

time: 43.1 us -> 42.9 us (level)
  no operation moved by 1% of the time
where the time goes in v12:
time: 42.9 us; the launch traced here: 42.7 us
  Pallas kernels  16 us (37%)
  waiting for transfers between devices  13.9 us (32%)
  starting transfers between devices  9.85 us (23%)
  local copies, waits for them, and re-layouts  2.85 us (7%)
    ppermute x3, waiting for transfers between devices, local(): lax.ppermute(piece, 'tm', [(z, (z + by) % tm) for z in range(tm)])  10.6 us
    pallas_call x1, Pallas kernels, local(): pl.pallas_call(functools.partial(raw_beams_kernel, tm, own), out_shape=[r...  6.85 us
    ppermute x3, starting transfers between devices, local(): lax.ppermute(piece, 'tm', [(z, (z + by) % tm) for z in range(tm)])  6.23 us
    pallas_call x1, Pallas kernels, local(): pl.pallas_call(functools.partial(subspace_kernel, tm, own, factor), out_s...  4.4 us
    ppermute x3, starting transfers between devices, local(): arrived[x] = lax.ppermute(packets[x], 'tm', [(z, z ^ x) for z in range(tm)])  3.55 us
    ppermute x3, waiting for transfers between devices, local(): arrived[x] = lax.ppermute(packets[x], 'tm', [(z, z ^ x) for z in range(tm)])  1.72 us
    ppermute x1, waiting for transfers between devices, local(): theirs = lax.ppermute(powers[1], 'pol', [(0, 1), (1, 0)])  1.52 us
    pallas_call x1, Pallas kernels, local(): pl.pallas_call(early_kernel, out_shape=[jax.ShapeDtypeStruct((own, 2, wid...  1.51 us
  transfers between devices with their start and end apart: 7, of which 5 were waited for; matrix products, arithmetic and copies ran while one was open for 1% of the time, Pallas kernels for 24%

profile of v12, /device:TPU:0, one launch (start us, length us, event | category | flops | bytes accessed | tf_op | source)
XLA Modules:
  0.0 42.7 jit_solution(4566993049697685753)
XLA Ops:
  0.0 0.0 copy-start.1
  0.0 1.2 %constant_dynamic-slice_fusion = bf16[128,1,1,2,512]{4,3,2,1,0:T(2,128)(2,1)S(1)} fusion(bf16[128,1,4,2,512]{4,3,2,1,0:T(2,128)(2,1)} %voltages_ref.1, s32[]{:T(128)S(6)} %select_n.3), kind=kLoop, calls=%fused_computation | loop fusion | bytes 524292 | tf_op jit(solution)/shard_map/dynamic_slice | solution.py:329
  1.2 0.1 reshape_transpose.13.rest_1_
  1.3 3.1 %collective-permute-start = (bf16[1,256,512]{2,1,0:T(8,128)(2,1)S(1)}, bf16[1,256,512]{2,1,0:T(8,128)(2,1)S(1)}, u32[]{:S(2)}, u32[]{:S(2)}) collective-permute-start(bf16[1,256,512]{2,1,0:T(8,128)(2,1)S(1)} %reshape_transpose.13.rest_1_), channel_id=1, source_target_pairs={{0,4},{4,8},{8,12},{12,0},{1,5},{5,9},{9,13},{13,1},{2,6},{6,10},{... | collective-permute-start | bytes 786440 | tf_op jit(solution)/shard_map/ppermute | solution.py:333
  4.4 0.0 copy-start
  4.4 1.2 %copy-done = bf16[128,1,4,2,512]{4,3,2,1,0:T(2,128)(2,1)S(1)} copy-done((bf16[128,1,4,2,512]{4,3,2,1,0:T(2,128)(2,1)S(1)}, bf16[128,1,4,2,512]{4,3,2,1,0:T(2,128)(2,1)}, u32[]{:S(2)}) %copy-start) | copy-done | bytes 1048600
  5.6 0.2 shard_map.55
  5.8 0.1 reshape_transpose.14.rest_2_
  5.9 0.0 copy-start.2
  5.9 2.1 %collective-permute-start.1 = (bf16[1,256,512]{2,1,0:T(8,128)(2,1)S(1)}, bf16[1,256,512]{2,1,0:T(8,128)(2,1)S(1)}, u32[]{:S(2)}, u32[]{:S(2)}) collective-permute-start(bf16[1,256,512]{2,1,0:T(8,128)(2,1)S(1)} %reshape_transpose.14.rest_2_), channel_id=1, source_target_pairs={{0,12},{4,0},{8,4},{12,8},{1,13},{5,1},{9,5},{13,9},{2,14},{6,2},{... | collective-permute-start | bytes 786440 | tf_op jit(solution)/shard_map/ppermute | solution.py:333
  8.0 0.1 reshape_transpose.15.rest_3_
  8.1 1.1 %collective-permute-start.2 = (bf16[1,256,512]{2,1,0:T(8,128)(2,1)S(1)}, bf16[1,256,512]{2,1,0:T(8,128)(2,1)S(1)}, u32[]{:S(2)}, u32[]{:S(2)}) collective-permute-start(bf16[1,256,512]{2,1,0:T(8,128)(2,1)S(1)} %reshape_transpose.15.rest_3_), channel_id=1, source_target_pairs={{0,8},{4,12},{8,0},{12,4},{1,9},{5,13},{9,1},{13,5},{2,10},{6,14},... | collective-permute-start | bytes 786440 | tf_op jit(solution)/shard_map/ppermute | solution.py:333
  9.2 0.1 reshape_transpose.12.rest_0_.refs_0_
  9.3 0.0 copy-done.1
  9.3 1.3 %shard_map.57.weights_ref = bf16[1,512,512]{2,1,0:T(8,128)(2,1)S(1)} custom-call(s32[256,512]{1,0:T(8,128)S(1)} %copy-done.1), custom_call_target="tpu_custom_call" | custom-call | flops 5242880 | bytes 1048576 | tf_op jit(solution)/shard_map/pallas_call | solution.py:348
  10.5 0.0 copy-start.3
  10.6 0.0 copy-start.4
  10.6 6.8 %shard_map.56 = (f32[4,256,128]{2,1,0:T(8,128)S(1)}, f32[4,256,128]{2,1,0:T(8,128)S(1)}) custom-call(s32[256,512]{1,0:T(8,128)S(1)} %copy-done.1, bf16[1,256,512]{2,1,0:T(8,128)(2,1)S(1)} %reshape_transpose.12.rest_0_.refs_0_, bf16[1,256,512]{2,1,0:T(8,128)(2,1)S(1)} %reshape_transpose.13.rest_1_, bf16[1,256,512]{2,1,0:T(8,128)(2,1)S(1)} %reshape_transpose.14.rest_2_, ...), custom_call_target="tpu_custom_call" | custom-call | flops 536870912 | bytes 2097152 | tf_op jit(solution)/shard_map/pallas_call | solution.py:338
  17.4 0.0 collective-permute-done.refs_1_
  17.4 0.9 %collective-permute-done.1.refs_2_ = bf16[1,256,512]{2,1,0:T(8,128)(2,1)S(1)} collective-permute-done((bf16[1,256,512]{2,1,0:T(8,128)(2,1)S(1)}, bf16[1,256,512]{2,1,0:T(8,128)(2,1)S(1)}, u32[]{:S(2)}, u32[]{:S(2)}) %collective-permute-start.1) | collective-permute-done | bytes 262176 | tf_op jit(solution)/shard_map/ppermute | solution.py:333
  18.3 0.0 copy-done.2
  18.3 1.5 %shard_map.58 = (f32[1,2,512,512]{3,2,1,0:T(8,128)S(1)}, f32[1,16,512]{2,1,0:T(8,128)S(1)}, bf16[1,512,768]{2,1,0:T(8,128)(2,1)S(1)}) custom-call(f32[1,4,2,8,512]{4,3,2,1,0:T(8,128)S(1)} %copy-done.2, bf16[1,256,512]{2,1,0:T(8,128)(2,1)S(1)} %reshape_transpose.12.rest_0_.refs_0_, bf16[1,256,512]{2,1,0:T(8,128)(2,1)S(1)} %collective-permute-done.refs_1_, ...), custom_call_target="tpu_custom_call" | custom-call | flops 805306368 | bytes 2097152 | tf_op jit(solution)/shard_map/pallas_call | solution.py:359
  19.8 9.7 %collective-permute-done.2.last_ref = bf16[1,256,512]{2,1,0:T(8,128)(2,1)S(1)} collective-permute-done((bf16[1,256,512]{2,1,0:T(8,128)(2,1)S(1)}, bf16[1,256,512]{2,1,0:T(8,128)(2,1)S(1)}, u32[]{:S(2)}, u32[]{:S(2)}) %collective-permute-start.2) | collective-permute-done | bytes 262176 | tf_op jit(solution)/shard_map/ppermute | solution.py:333
  29.6 0.0 copy-done.3
  29.6 0.0 copy-done.4
  29.6 4.4 %shard_map.59 = (bf16[1,16,384]{2,1,0:T(8,128)(2,1)S(1)}, bf16[1,16,384]{2,1,0:T(8,128)(2,1)S(1)}, bf16[1,16,384]{2,1,0:T(8,128)(2,1)S(1)}, bf16[1,16,384]{2,1,0:T(8,128)(2,1)S(1)}) custom-call(f32[4,256,128]{2,1,0:T(8,128)S(1)} %get-tuple-element.26.beams_ref.mine_ref, f32[1,4,2,8,512]{4,3,2,1,0:T(8,128)S(1)} %copy-done.2, s32[4]{0:T(128)S(1)} %copy-done.3, ...), custom_call_target="tpu_custom_call" | custom-call | flops 134217728 | bytes 2097152 | tf_op jit(solution)/shard_map/pallas_call | solution.py:373
  34.0 0.1 collective-permute-start.5
  34.1 1.7 %collective-permute-start.4 = (bf16[1,16,384]{2,1,0:T(8,128)(2,1)S(1)}, bf16[1,16,384]{2,1,0:T(8,128)(2,1)S(1)}, u32[]{:S(2)}, u32[]{:S(2)}) collective-permute-start(bf16[1,16,384]{2,1,0:T(8,128)(2,1)S(1)} %get-tuple-element.32), channel_id=1, source_target_pairs={{0,12},{4,8},{8,4},{12,0},{1,13},{5,9},{9,5},{13,1},{2,14},{6,10},... | collective-permute-start | bytes 36872 | tf_op jit(solution)/shard_map/ppermute | solution.py:387
  35.7 1.8 %collective-permute-start.3 = (bf16[1,16,384]{2,1,0:T(8,128)(2,1)S(1)}, bf16[1,16,384]{2,1,0:T(8,128)(2,1)S(1)}, u32[]{:S(2)}, u32[]{:S(2)}) collective-permute-start(bf16[1,16,384]{2,1,0:T(8,128)(2,1)S(1)} %get-tuple-element.31), channel_id=1, source_target_pairs={{0,4},{4,0},{8,12},{12,8},{1,5},{5,1},{9,13},{13,9},{2,6},{6,2},{1... | collective-permute-start | bytes 36872 | tf_op jit(solution)/shard_map/ppermute | solution.py:387
  37.5 1.2 %collective-permute-done.5.rest_1_ = bf16[1,16,384]{2,1,0:T(8,128)(2,1)S(1)} collective-permute-done((bf16[1,16,384]{2,1,0:T(8,128)(2,1)S(1)}, bf16[1,16,384]{2,1,0:T(8,128)(2,1)S(1)}, u32[]{:S(2)}, u32[]{:S(2)}) %collective-permute-start.5) | collective-permute-done | bytes 12320 | tf_op jit(solution)/shard_map/ppermute | solution.py:387
  38.8 0.4 shard_map.60
  39.1 0.5 %collective-permute-done.4.rest_0_ = bf16[1,16,384]{2,1,0:T(8,128)(2,1)S(1)} collective-permute-done((bf16[1,16,384]{2,1,0:T(8,128)(2,1)S(1)}, bf16[1,16,384]{2,1,0:T(8,128)(2,1)S(1)}, u32[]{:S(2)}, u32[]{:S(2)}) %collective-permute-start.4) | collective-permute-done | bytes 12320 | tf_op jit(solution)/shard_map/ppermute | solution.py:387
  39.6 0.3 shard_map.61
  39.9 0.0 collective-permute-done.3.rest_0_
  39.9 0.3 shard_map.62
  40.2 0.1 collective-permute-start.6
  40.3 1.5 %collective-permute-done.6.theirs_ref = f32[4,128,128]{2,1,0:T(8,128)S(1)} collective-permute-done((f32[4,128,128]{2,1,0:T(8,128)S(1)}, f32[4,128,128]{2,1,0:T(8,128)S(1)}, u32[]{:S(2)}, u32[]{:S(2)}) %collective-permute-start.6) | collective-permute-done | bytes 262176 | tf_op jit(solution)/shard_map/ppermute | solution.py:402
  41.9 0.9 %shard_map.63 = f32[128,4,128]{2,1,0:T(4,128)} custom-call(f32[4,128,128]{2,1,0:T(8,128)S(1)} %get-tuple-element.39.mine_ref, f32[4,128,128]{2,1,0:T(8,128)S(1)} %collective-permute-done.6.theirs_ref), custom_call_target="tpu_custom_call" | custom-call | flops 131072 | bytes 786432 | tf_op jit(solution)/shard_map/pallas_call | solution.py:404
Async XLA Ops:
  0.0 9.3 %copy-start.1 = (s32[256,512]{1,0:T(8,128)S(1)}, s32[256,512]{1,0:T(8,128)}, u32[]{:S(2)}) copy-start(s32[256,512]{1,0:T(8,128)} %phase_ref.3) | copy-start | bytes 1572868
  1.3 16.1 %collective-permute-start = (bf16[1,256,512]{2,1,0:T(8,128)(2,1)S(1)}, bf16[1,256,512]{2,1,0:T(8,128)(2,1)S(1)}, u32[]{:S(2)}, u32[]{:S(2)}) collective-permute-start(bf16[1,256,512]{2,1,0:T(8,128)(2,1)S(1)} %reshape_transpose.13.rest_1_), channel_id=1, source_target_pairs={{0,4},{4,8},{8,12},{12,0},{1,5},{5,9},{9,13},{13,1},{2,6},{6,10},{... | collective-permute-start | bytes 786440 | tf_op jit(solution)/shard_map/ppermute | solution.py:333
  4.4 1.2 %copy-start = (bf16[128,1,4,2,512]{4,3,2,1,0:T(2,128)(2,1)S(1)}, bf16[128,1,4,2,512]{4,3,2,1,0:T(2,128)(2,1)}, u32[]{:S(2)}) copy-start(bf16[128,1,4,2,512]{4,3,2,1,0:T(2,128)(2,1)} %voltages_ref.1) | copy-start | bytes 3145732
  5.9 12.4 %copy-start.2 = (f32[1,4,2,8,512]{4,3,2,1,0:T(8,128)S(1)}, f32[1,4,2,8,512]{4,3,2,1,0:T(8,128)}, u32[]{:S(2)}) copy-start(f32[1,4,2,8,512]{4,3,2,1,0:T(8,128)} %start_ref.3) | copy-start | bytes 393220
  5.9 12.4 %collective-permute-start.1 = (bf16[1,256,512]{2,1,0:T(8,128)(2,1)S(1)}, bf16[1,256,512]{2,1,0:T(8,128)(2,1)S(1)}, u32[]{:S(2)}, u32[]{:S(2)}) collective-permute-start(bf16[1,256,512]{2,1,0:T(8,128)(2,1)S(1)} %reshape_transpose.14.rest_2_), channel_id=1, source_target_pairs={{0,12},{4,0},{8,4},{12,8},{1,13},{5,1},{9,5},{13,9},{2,14},{6,2},{... | collective-permute-start | bytes 786440 | tf_op jit(solution)/shard_map/ppermute | solution.py:333
  8.1 21.5 %collective-permute-start.2 = (bf16[1,256,512]{2,1,0:T(8,128)(2,1)S(1)}, bf16[1,256,512]{2,1,0:T(8,128)(2,1)S(1)}, u32[]{:S(2)}, u32[]{:S(2)}) collective-permute-start(bf16[1,256,512]{2,1,0:T(8,128)(2,1)S(1)} %reshape_transpose.15.rest_3_), channel_id=1, source_target_pairs={{0,8},{4,12},{8,0},{12,4},{1,9},{5,13},{9,1},{13,5},{2,10},{6,14},... | collective-permute-start | bytes 786440 | tf_op jit(solution)/shard_map/ppermute | solution.py:333
  10.5 19.0 %copy-start.3 = (s32[4]{0:T(128)S(1)}, s32[4]{0:T(128)}, u32[]{:S(2)}) copy-start(s32[4]{0:T(128)} %flags_ref.1) | copy-start | bytes 52
  10.6 19.0 %copy-start.4 = (s32[4]{0:T(128)S(1)}, s32[4]{0:T(128)}, u32[]{:S(2)}) copy-start(s32[4]{0:T(128)} %ranks_ref.1) | copy-start | bytes 52
  34.0 4.8 %collective-permute-start.5 = (bf16[1,16,384]{2,1,0:T(8,128)(2,1)S(1)}, bf16[1,16,384]{2,1,0:T(8,128)(2,1)S(1)}, u32[]{:S(2)}, u32[]{:S(2)}) collective-permute-start(bf16[1,16,384]{2,1,0:T(8,128)(2,1)S(1)} %get-tuple-element.34), channel_id=1, source_target_pairs={{0,8},{4,12},{8,0},{12,4},{1,9},{5,13},{9,1},{13,5},{2,10},{6,14},... | collective-permute-start | bytes 36872 | tf_op jit(solution)/shard_map/ppermute | solution.py:387
  34.1 5.6 %collective-permute-start.4 = (bf16[1,16,384]{2,1,0:T(8,128)(2,1)S(1)}, bf16[1,16,384]{2,1,0:T(8,128)(2,1)S(1)}, u32[]{:S(2)}, u32[]{:S(2)}) collective-permute-start(bf16[1,16,384]{2,1,0:T(8,128)(2,1)S(1)} %get-tuple-element.32), channel_id=1, source_target_pairs={{0,12},{4,8},{8,4},{12,0},{1,13},{5,9},{9,5},{13,1},{2,14},{6,10},... | collective-permute-start | bytes 36872 | tf_op jit(solution)/shard_map/ppermute | solution.py:387
  35.7 4.2 %collective-permute-start.3 = (bf16[1,16,384]{2,1,0:T(8,128)(2,1)S(1)}, bf16[1,16,384]{2,1,0:T(8,128)(2,1)S(1)}, u32[]{:S(2)}, u32[]{:S(2)}) collective-permute-start(bf16[1,16,384]{2,1,0:T(8,128)(2,1)S(1)} %get-tuple-element.31), channel_id=1, source_target_pairs={{0,4},{4,0},{8,12},{12,8},{1,5},{5,1},{9,13},{13,9},{2,6},{6,2},{1... | collective-permute-start | bytes 36872 | tf_op jit(solution)/shard_map/ppermute | solution.py:387
  40.2 1.6 %collective-permute-start.6 = (f32[4,128,128]{2,1,0:T(8,128)S(1)}, f32[4,128,128]{2,1,0:T(8,128)S(1)}, u32[]{:S(2)}, u32[]{:S(2)}) collective-permute-start(f32[4,128,128]{2,1,0:T(8,128)S(1)} %get-tuple-element.40), channel_id=1, source_target_pairs={{0,1},{1,0},{2,3},{3,2},{4,5},{5,4},{6,7},{7,6},{8,9},{9,8},{10,11... | collective-permute-start | bytes 786440 | tf_op jit(solution)/shard_map/ppermute | solution.py:402

commit v13 on v12

--- a/solution.py
+++ b/solution.py
@@ -59,8 +59,13 @@
     lax.fori_loop(0, rows // chunk, body, 0)
 
 
+def orders(tm):
+    near = [by for by in range(1, tm - 1) if by != tm // 2]
+    return [0, tm // 2, *near, tm - 1], [0, *near, tm // 2, tm - 1]
+
+
 def steps(tm):
-    return [0, *[by for by in range(1, tm) if by != tm // 2], tm // 2]
+    return [jnp.where(lax.axis_index("pol") == 0, a, b) for a, b in zip(*orders(tm))]
 
 
 def shifted(by):
@@ -68,10 +73,11 @@
     return lax.rem(lax.axis_index("tm") + tm + by, tm)
 
 
-def cut_kernel(own, bys, voltages_ref, *rest):
+def cut_kernel(tm, own, voltages_ref, *rest):
     pieces, done = rest[:-1], rest[-1]
     copies = []
-    for i, (by, piece) in enumerate(zip(bys, pieces)):
+    by = steps(tm)
+    for i, (by, piece) in enumerate(zip([by[0], *by[2:]], pieces)):
         channels = pl.ds(shifted(by) * own, own)
         copy = pltpu.make_async_copy(voltages_ref.at[:, 0, channels], piece, done.at[i])
         copy.start()
@@ -319,7 +325,7 @@
 
     by = steps(tm)
     later = pl.pallas_call(
-        functools.partial(cut_kernel, own, [by[0], *by[2:]]),
+        functools.partial(cut_kernel, tm, own),
         out_shape=[jax.ShapeDtypeStruct((samples, own, 2, width), BF16)] * (tm - 1),
         in_specs=[pl.BlockSpec(memory_space=pltpu.HBM)],
         out_specs=[whole] * (tm - 1),
@@ -330,8 +336,10 @@
     cut = [later[0], urgent, *later[1:]]
     pieces = [piece.transpose(1, 0, 2, 3).reshape(own, rows, width) for piece in cut]
     blocks = pieces[:1] + [
-        lax.ppermute(piece, "tm", [(z, (z + by) % tm) for z in range(tm)])
-        for by, piece in zip(steps(tm)[1:], pieces[1:])
+        lax.ppermute(
+            piece, ("tm", "pol"), [(2 * z + p, (z + by[p]) % tm * 2 + p) for z in range(tm) for p in range(2)]
+        )
+        for by, piece in list(zip(zip(*orders(tm)), pieces))[1:]
     ]
 
     raw = jax.ShapeDtypeStruct((chan_dev, rows, half), F32)

time: 42.9 us -> 45.1 us (1.051)
  starting transfers between devices: 9.85 us -> 15.5 us
  waiting for transfers between devices: 13.9 us -> 10.4 us
    ppermute x3, waiting for transfers between devices: 10.6 us -> 4.42 us  [local(): lax.ppermute(piece, ('tm', 'pol'), [(2 * z + p, (z + by[p]) % tm * 2 + p)...]
    ppermute x3, starting transfers between devices: 3.55 us -> 7.37 us  [local(): arrived[x] = lax.ppermute(packets[x], 'tm', [(z, z ^ x) for z in range(tm)])]
    ppermute x3, waiting for transfers between devices: 1.72 us -> 4.49 us  [local(): arrived[x] = lax.ppermute(packets[x], 'tm', [(z, z ^ x) for z in range(tm)])]
    ppermute x3, starting transfers between devices: 6.23 us -> 8.02 us  [local(): lax.ppermute(piece, ('tm', 'pol'), [(2 * z + p, (z + by[p]) % tm * 2 + p)...]
  transfers between devices with their start and end apart: 7 -> 7, of which waited for: 5 -> 4; matrix products, arithmetic and copies ran while one was open for 1% -> 1% of each run, Pallas kernels for 24% -> 23%
where the time goes in v13:
time: 45.1 us; the launch traced here: 44.9 us
  Pallas kernels  16 us (35%)
  starting transfers between devices  15.5 us (34%)
  waiting for transfers between devices  10.4 us (23%)
  local copies, waits for them, and re-layouts  2.86 us (6%)
    ppermute x3, starting transfers between devices, local(): lax.ppermute(piece, ('tm', 'pol'), [(2 * z + p, (z + by[p]) % tm * 2 + p)...  8.02 us
    ppermute x3, starting transfers between devices, local(): arrived[x] = lax.ppermute(packets[x], 'tm', [(z, z ^ x) for z in range(tm)])  7.37 us
    pallas_call x1, Pallas kernels, local(): pl.pallas_call(functools.partial(raw_beams_kernel, tm, own), out_shape=[r...  6.85 us
    ppermute x3, waiting for transfers between devices, local(): arrived[x] = lax.ppermute(packets[x], 'tm', [(z, z ^ x) for z in range(tm)])  4.49 us
    ppermute x3, waiting for transfers between devices, local(): lax.ppermute(piece, ('tm', 'pol'), [(2 * z + p, (z + by[p]) % tm * 2 + p)...  4.42 us
    pallas_call x1, Pallas kernels, local(): pl.pallas_call(functools.partial(subspace_kernel, tm, own, factor), out_s...  4.4 us
    ppermute x1, waiting for transfers between devices, local(): theirs = lax.ppermute(powers[1], 'pol', [(0, 1), (1, 0)])  1.52 us
    pallas_call x1, Pallas kernels, local(): pl.pallas_call(early_kernel, out_shape=[jax.ShapeDtypeStruct((own, 2, wid...  1.51 us
  transfers between devices with their start and end apart: 7, of which 4 were waited for; matrix products, arithmetic and copies ran while one was open for 1% of the time, Pallas kernels for 23%

profile of v13, /device:TPU:0, one launch (start us, length us, event | category | flops | bytes accessed | tf_op | source)
XLA Modules:
  0.0 44.9 jit_solution(8396669757703112292)
XLA Ops:
  0.0 0.0 copy-start.1
  0.0 1.2 %constant_dynamic-slice_fusion = bf16[128,1,1,2,512]{4,3,2,1,0:T(2,128)(2,1)S(1)} fusion(bf16[128,1,4,2,512]{4,3,2,1,0:T(2,128)(2,1)} %voltages_ref.1, s32[]{:T(128)S(6)} %select_n.8), kind=kLoop, calls=%fused_computation | loop fusion | bytes 524292 | tf_op jit(solution)/shard_map/dynamic_slice | solution.py:335
  1.2 0.1 reshape_transpose.13.rest_1_
  1.3 4.1 %collective-permute-start = (bf16[1,256,512]{2,1,0:T(8,128)(2,1)S(1)}, bf16[1,256,512]{2,1,0:T(8,128)(2,1)S(1)}, u32[]{:S(2)}, u32[]{:S(2)}) collective-permute-start(bf16[1,256,512]{2,1,0:T(8,128)(2,1)S(1)} %reshape_transpose.13.rest_1_), channel_id=1, source_target_pairs={{0,8},{1,5},{4,12},{5,9},{8,0},{9,13},{12,4},{13,1},{2,10},{3,7},{... | collective-permute-start | bytes 786440 | tf_op jit(solution)/shard_map/ppermute | solution.py:339
  5.4 0.0 copy-start
  5.4 1.2 %copy-done = bf16[128,1,4,2,512]{4,3,2,1,0:T(2,128)(2,1)S(1)} copy-done((bf16[128,1,4,2,512]{4,3,2,1,0:T(2,128)(2,1)S(1)}, bf16[128,1,4,2,512]{4,3,2,1,0:T(2,128)(2,1)}, u32[]{:S(2)}) %copy-start) | copy-done | bytes 1048600
  6.6 0.2 shard_map.55
  6.8 0.1 reshape_transpose.14.rest_2_
  6.9 0.0 copy-start.2
  6.9 1.6 %collective-permute-start.1 = (bf16[1,256,512]{2,1,0:T(8,128)(2,1)S(1)}, bf16[1,256,512]{2,1,0:T(8,128)(2,1)S(1)}, u32[]{:S(2)}, u32[]{:S(2)}) collective-permute-start(bf16[1,256,512]{2,1,0:T(8,128)(2,1)S(1)} %reshape_transpose.14.rest_2_), channel_id=1, source_target_pairs={{0,4},{1,9},{4,8},{5,13},{8,12},{9,1},{12,0},{13,5},{2,6},{3,11},{... | collective-permute-start | bytes 786440 | tf_op jit(solution)/shard_map/ppermute | solution.py:339
  8.5 0.1 reshape_transpose.15.rest_3_
  8.7 2.3 %collective-permute-start.2 = (bf16[1,256,512]{2,1,0:T(8,128)(2,1)S(1)}, bf16[1,256,512]{2,1,0:T(8,128)(2,1)S(1)}, u32[]{:S(2)}, u32[]{:S(2)}) collective-permute-start(bf16[1,256,512]{2,1,0:T(8,128)(2,1)S(1)} %reshape_transpose.15.rest_3_), channel_id=1, source_target_pairs={{0,12},{1,13},{4,0},{5,1},{8,4},{9,5},{12,8},{13,9},{2,14},{3,15},... | collective-permute-start | bytes 786440 | tf_op jit(solution)/shard_map/ppermute | solution.py:339
  11.0 0.1 reshape_transpose.12.rest_0_.refs_0_
  11.1 0.0 copy-done.1
  11.1 1.3 %shard_map.57.weights_ref = bf16[1,512,512]{2,1,0:T(8,128)(2,1)S(1)} custom-call(s32[256,512]{1,0:T(8,128)S(1)} %copy-done.1), custom_call_target="tpu_custom_call" | custom-call | flops 5242880 | bytes 1048576 | tf_op jit(solution)/shard_map/pallas_call | solution.py:356
  12.3 0.0 copy-start.3
  12.3 0.0 copy-start.4
  12.4 6.8 %shard_map.56 = (f32[4,256,128]{2,1,0:T(8,128)S(1)}, f32[4,256,128]{2,1,0:T(8,128)S(1)}) custom-call(s32[256,512]{1,0:T(8,128)S(1)} %copy-done.1, bf16[1,256,512]{2,1,0:T(8,128)(2,1)S(1)} %reshape_transpose.12.rest_0_.refs_0_, bf16[1,256,512]{2,1,0:T(8,128)(2,1)S(1)} %reshape_transpose.13.rest_1_, bf16[1,256,512]{2,1,0:T(8,128)(2,1)S(1)} %reshape_transpose.14.rest_2_, ...), custom_call_target="tpu_custom_call" | custom-call | flops 536870912 | bytes 2097152 | tf_op jit(solution)/shard_map/pallas_call | solution.py:346
  19.2 4.4 %collective-permute-done.refs_1_ = bf16[1,256,512]{2,1,0:T(8,128)(2,1)S(1)} collective-permute-done((bf16[1,256,512]{2,1,0:T(8,128)(2,1)S(1)}, bf16[1,256,512]{2,1,0:T(8,128)(2,1)S(1)}, u32[]{:S(2)}, u32[]{:S(2)}) %collective-permute-start) | collective-permute-done | bytes 262176 | tf_op jit(solution)/shard_map/ppermute | solution.py:339
  23.6 0.0 collective-permute-done.1.refs_2_
  23.6 0.0 copy-done.2
  23.6 1.5 %shard_map.58 = (f32[1,2,512,512]{3,2,1,0:T(8,128)S(1)}, f32[1,16,512]{2,1,0:T(8,128)S(1)}, bf16[1,512,768]{2,1,0:T(8,128)(2,1)S(1)}) custom-call(f32[1,4,2,8,512]{4,3,2,1,0:T(8,128)S(1)} %copy-done.2, bf16[1,256,512]{2,1,0:T(8,128)(2,1)S(1)} %reshape_transpose.12.rest_0_.refs_0_, bf16[1,256,512]{2,1,0:T(8,128)(2,1)S(1)} %collective-permute-done.refs_1_, ...), custom_call_target="tpu_custom_call" | custom-call | flops 805306368 | bytes 2097152 | tf_op jit(solution)/shard_map/pallas_call | solution.py:367
  25.1 0.0 collective-permute-done.2.last_ref
  25.1 0.0 copy-done.3
  25.2 0.0 copy-done.4
  25.2 4.4 %shard_map.59 = (bf16[1,16,384]{2,1,0:T(8,128)(2,1)S(1)}, bf16[1,16,384]{2,1,0:T(8,128)(2,1)S(1)}, bf16[1,16,384]{2,1,0:T(8,128)(2,1)S(1)}, bf16[1,16,384]{2,1,0:T(8,128)(2,1)S(1)}) custom-call(f32[4,256,128]{2,1,0:T(8,128)S(1)} %get-tuple-element.26.beams_ref.mine_ref, f32[1,4,2,8,512]{4,3,2,1,0:T(8,128)S(1)} %copy-done.2, s32[4]{0:T(128)S(1)} %copy-done.3, ...), custom_call_target="tpu_custom_call" | custom-call | flops 134217728 | bytes 2097152 | tf_op jit(solution)/shard_map/pallas_call | solution.py:381
  29.6 6.7 %collective-permute-start.5 = (bf16[1,16,384]{2,1,0:T(8,128)(2,1)S(1)}, bf16[1,16,384]{2,1,0:T(8,128)(2,1)S(1)}, u32[]{:S(2)}, u32[]{:S(2)}) collective-permute-start(bf16[1,16,384]{2,1,0:T(8,128)(2,1)S(1)} %get-tuple-element.34), channel_id=1, source_target_pairs={{0,8},{4,12},{8,0},{12,4},{1,9},{5,13},{9,1},{13,5},{2,10},{6,14},... | collective-permute-start | bytes 36872 | tf_op jit(solution)/shard_map/ppermute | solution.py:395
  36.3 0.4 collective-permute-start.4
  36.8 0.2 collective-permute-start.3
  37.0 1.0 %collective-permute-done.5.rest_1_ = bf16[1,16,384]{2,1,0:T(8,128)(2,1)S(1)} collective-permute-done((bf16[1,16,384]{2,1,0:T(8,128)(2,1)S(1)}, bf16[1,16,384]{2,1,0:T(8,128)(2,1)S(1)}, u32[]{:S(2)}, u32[]{:S(2)}) %collective-permute-start.5) | collective-permute-done | bytes 12320 | tf_op jit(solution)/shard_map/ppermute | solution.py:395
  38.0 0.4 shard_map.60
  38.4 3.5 %collective-permute-done.4.rest_0_ = bf16[1,16,384]{2,1,0:T(8,128)(2,1)S(1)} collective-permute-done((bf16[1,16,384]{2,1,0:T(8,128)(2,1)S(1)}, bf16[1,16,384]{2,1,0:T(8,128)(2,1)S(1)}, u32[]{:S(2)}, u32[]{:S(2)}) %collective-permute-start.4) | collective-permute-done | bytes 12320 | tf_op jit(solution)/shard_map/ppermute | solution.py:395
  41.8 0.3 shard_map.61
  42.1 0.0 collective-permute-done.3.rest_0_
  42.1 0.3 shard_map.62
  42.4 0.1 collective-permute-start.6
  42.5 1.5 %collective-permute-done.6.theirs_ref = f32[4,128,128]{2,1,0:T(8,128)S(1)} collective-permute-done((f32[4,128,128]{2,1,0:T(8,128)S(1)}, f32[4,128,128]{2,1,0:T(8,128)S(1)}, u32[]{:S(2)}, u32[]{:S(2)}) %collective-permute-start.6) | collective-permute-done | bytes 262176 | tf_op jit(solution)/shard_map/ppermute | solution.py:410
  44.0 0.9 %shard_map.63 = f32[128,4,128]{2,1,0:T(4,128)} custom-call(f32[4,128,128]{2,1,0:T(8,128)S(1)} %get-tuple-element.39.mine_ref, f32[4,128,128]{2,1,0:T(8,128)S(1)} %collective-permute-done.6.theirs_ref), custom_call_target="tpu_custom_call" | custom-call | flops 131072 | bytes 786432 | tf_op jit(solution)/shard_map/pallas_call | solution.py:412
Async XLA Ops:
  0.0 11.1 %copy-start.1 = (s32[256,512]{1,0:T(8,128)S(1)}, s32[256,512]{1,0:T(8,128)}, u32[]{:S(2)}) copy-start(s32[256,512]{1,0:T(8,128)} %phase_ref.3) | copy-start | bytes 1572868
  1.3 22.3 %collective-permute-start = (bf16[1,256,512]{2,1,0:T(8,128)(2,1)S(1)}, bf16[1,256,512]{2,1,0:T(8,128)(2,1)S(1)}, u32[]{:S(2)}, u32[]{:S(2)}) collective-permute-start(bf16[1,256,512]{2,1,0:T(8,128)(2,1)S(1)} %reshape_transpose.13.rest_1_), channel_id=1, source_target_pairs={{0,8},{1,5},{4,12},{5,9},{8,0},{9,13},{12,4},{13,1},{2,10},{3,7},{... | collective-permute-start | bytes 786440 | tf_op jit(solution)/shard_map/ppermute | solution.py:339
  5.4 1.2 %copy-start = (bf16[128,1,4,2,512]{4,3,2,1,0:T(2,128)(2,1)S(1)}, bf16[128,1,4,2,512]{4,3,2,1,0:T(2,128)(2,1)}, u32[]{:S(2)}) copy-start(bf16[128,1,4,2,512]{4,3,2,1,0:T(2,128)(2,1)} %voltages_ref.1) | copy-start | bytes 3145732
  6.9 16.7 %copy-start.2 = (f32[1,4,2,8,512]{4,3,2,1,0:T(8,128)S(1)}, f32[1,4,2,8,512]{4,3,2,1,0:T(8,128)}, u32[]{:S(2)}) copy-start(f32[1,4,2,8,512]{4,3,2,1,0:T(8,128)} %start_ref.3) | copy-start | bytes 393220
  6.9 16.7 %collective-permute-start.1 = (bf16[1,256,512]{2,1,0:T(8,128)(2,1)S(1)}, bf16[1,256,512]{2,1,0:T(8,128)(2,1)S(1)}, u32[]{:S(2)}, u32[]{:S(2)}) collective-permute-start(bf16[1,256,512]{2,1,0:T(8,128)(2,1)S(1)} %reshape_transpose.14.rest_2_), channel_id=1, source_target_pairs={{0,4},{1,9},{4,8},{5,13},{8,12},{9,1},{12,0},{13,5},{2,6},{3,11},{... | collective-permute-start | bytes 786440 | tf_op jit(solution)/shard_map/ppermute | solution.py:339
  8.7 16.5 %collective-permute-start.2 = (bf16[1,256,512]{2,1,0:T(8,128)(2,1)S(1)}, bf16[1,256,512]{2,1,0:T(8,128)(2,1)S(1)}, u32[]{:S(2)}, u32[]{:S(2)}) collective-permute-start(bf16[1,256,512]{2,1,0:T(8,128)(2,1)S(1)} %reshape_transpose.15.rest_3_), channel_id=1, source_target_pairs={{0,12},{1,13},{4,0},{5,1},{8,4},{9,5},{12,8},{13,9},{2,14},{3,15},... | collective-permute-start | bytes 786440 | tf_op jit(solution)/shard_map/ppermute | solution.py:339
  12.3 12.8 %copy-start.3 = (s32[4]{0:T(128)S(1)}, s32[4]{0:T(128)}, u32[]{:S(2)}) copy-start(s32[4]{0:T(128)} %flags_ref.1) | copy-start | bytes 52
  12.3 12.8 %copy-start.4 = (s32[4]{0:T(128)S(1)}, s32[4]{0:T(128)}, u32[]{:S(2)}) copy-start(s32[4]{0:T(128)} %ranks_ref.1) | copy-start | bytes 52
  29.6 8.4 %collective-permute-start.5 = (bf16[1,16,384]{2,1,0:T(8,128)(2,1)S(1)}, bf16[1,16,384]{2,1,0:T(8,128)(2,1)S(1)}, u32[]{:S(2)}, u32[]{:S(2)}) collective-permute-start(bf16[1,16,384]{2,1,0:T(8,128)(2,1)S(1)} %get-tuple-element.34), channel_id=1, source_target_pairs={{0,8},{4,12},{8,0},{12,4},{1,9},{5,13},{9,1},{13,5},{2,10},{6,14},... | collective-permute-start | bytes 36872 | tf_op jit(solution)/shard_map/ppermute | solution.py:395
  36.3 5.5 %collective-permute-start.4 = (bf16[1,16,384]{2,1,0:T(8,128)(2,1)S(1)}, bf16[1,16,384]{2,1,0:T(8,128)(2,1)S(1)}, u32[]{:S(2)}, u32[]{:S(2)}) collective-permute-start(bf16[1,16,384]{2,1,0:T(8,128)(2,1)S(1)} %get-tuple-element.32), channel_id=1, source_target_pairs={{0,12},{4,8},{8,4},{12,0},{1,13},{5,9},{9,5},{13,1},{2,14},{6,10},... | collective-permute-start | bytes 36872 | tf_op jit(solution)/shard_map/ppermute | solution.py:395
  36.8 5.4 %collective-permute-start.3 = (bf16[1,16,384]{2,1,0:T(8,128)(2,1)S(1)}, bf16[1,16,384]{2,1,0:T(8,128)(2,1)S(1)}, u32[]{:S(2)}, u32[]{:S(2)}) collective-permute-start(bf16[1,16,384]{2,1,0:T(8,128)(2,1)S(1)} %get-tuple-element.31), channel_id=1, source_target_pairs={{0,4},{4,0},{8,12},{12,8},{1,5},{5,1},{9,13},{13,9},{2,6},{6,2},{1... | collective-permute-start | bytes 36872 | tf_op jit(solution)/shard_map/ppermute | solution.py:395
  42.4 1.6 %collective-permute-start.6 = (f32[4,128,128]{2,1,0:T(8,128)S(1)}, f32[4,128,128]{2,1,0:T(8,128)S(1)}, u32[]{:S(2)}, u32[]{:S(2)}) collective-permute-start(f32[4,128,128]{2,1,0:T(8,128)S(1)} %get-tuple-element.40), channel_id=1, source_target_pairs={{0,1},{1,0},{2,3},{3,2},{4,5},{5,4},{6,7},{7,6},{8,9},{9,8},{10,11... | collective-permute-start | bytes 786440 | tf_op jit(solution)/shard_map/ppermute | solution.py:410

commit v14 on v12

--- a/solution.py
+++ b/solution.py
@@ -229,7 +229,7 @@
 def subspace_kernel(
     tm, own, factor, beams_ref, start_ref, flags_ref, ranks_ref, weights_ref, cov_ref, first_ref, across_ref, last_ref, *rest
 ):
-    outs, (high_ref, low_ref, series_ref) = rest[:tm], rest[tm:]
+    outs, (high_ref, low_ref, series_ref) = rest[1 : tm + 1], rest[tm + 1 :]
     vectors, width = start_ref.shape[3], start_ref.shape[4]
     rows = last_ref.shape[1]
     tm_index = lax.axis_index("tm")
@@ -275,28 +275,39 @@
             out[o, :, beams:] = series.astype(BF16)
 
 
-def first_kernel(own, xs, mine_ref, other_ref, *rest):
-    packets, (mine_out, other_out, squares) = rest[: len(xs)], rest[-3:]
-    rows, half = mine_ref.shape[1:]
+def nulled_power(raw, packet_ref, squares):
+    rows, half = raw.shape
     samples = rows // 2
+    series = packet_ref[:, 2 * half :].astype(F32)
+    vectors = series.shape[0] // 2
+    series = jnp.concatenate([series[:vectors], series[vectors:]], axis=1)
+    left = jnp.concatenate([series, -turned(series, 1)], axis=0).astype(BF16)
+    right = packet_ref[:, pl.ds(pl.multiple_of(lax.axis_index("pol") * half, half), half)]
+    beam = raw - dot(left, right, TN)
+    squares[...] = beam * beam
+    return squares[pl.ds(0, samples, 2), :] + squares[pl.ds(1, samples, 2), :]
+
+
+def power_kernel(own, xs, later_xs, mine_ref, theirs_ref, *rest):
+    packets, later = rest[: len(xs)], rest[len(xs) : len(xs) + len(later_xs)]
+    power_ref, squares = rest[-2:]
     for x, ref in zip(xs, packets):
         for o in range(own):
             chan = (lax.axis_index("tm") ^ x) * own + o
-            series = ref[o, :, 2 * half :].astype(F32)
-            vectors = series.shape[0] // 2
-            series = jnp.concatenate([series[:vectors], series[vectors:]], axis=1)
-            left = jnp.concatenate([series, -turned(series, 1)], axis=0).astype(BF16)
-            for swap, (raw_ref, out_ref) in enumerate(((mine_ref, mine_out), (other_ref, other_out))):
-                at = pl.multiple_of((lax.axis_index("pol") ^ swap) * half, half)
-                right = ref[o, :, pl.ds(at, half)]
-                beam = raw_ref[chan] - dot(left, right, TN)
-                squares[...] = beam * beam
-                out_ref[chan] = squares[pl.ds(0, samples, 2), :] + squares[pl.ds(1, samples, 2), :]
-
-
-def second_kernel(mine_ref, theirs_ref, out_ref):
-    for chan in range(out_ref.shape[1]):
-        out_ref[:, chan, :] = mine_ref[chan] + theirs_ref[chan]
+            power_ref[chan] = nulled_power(mine_ref[chan], ref.at[o], squares)
+    for x, ref in zip(later_xs, later):
+        for o in range(own):
+            chan = (lax.axis_index("tm") ^ x) * own + o
+            power_ref[chan] = power_ref[chan] + nulled_power(theirs_ref[chan], ref.at[o], squares)
+
+
+def last_kernel(own, x, theirs_ref, packet_ref, power_ref, out_ref, powers, squares):
+    powers[...] = power_ref[...]
+    for o in range(own):
+        chan = (lax.axis_index("tm") ^ x) * own + o
+        powers[chan] = power_ref[chan] + nulled_power(theirs_ref[chan], packet_ref.at[o], squares)
+    for chan in range(powers.shape[0]):
+        out_ref[:, chan, :] = powers[chan]
 
 
 def local(voltages, start_block, flags, ranks, phase_index):
@@ -370,45 +381,53 @@
         cost_estimate=cost(2 * own * early * width * width, 8 * own * width * width),
     )(start_block, *blocks[:-1])
 
-    packets = pl.pallas_call(
+    other, *packets = pl.pallas_call(
         functools.partial(subspace_kernel, tm, own, factor),
-        out_shape=[jax.ShapeDtypeStruct((own, 2 * vectors, beams + samples), BF16)] * tm,
+        out_shape=[raw] + [jax.ShapeDtypeStruct((own, 2 * vectors, beams + samples), BF16)] * tm,
         in_specs=[unread, whole, scalars, scalars] + [whole] * 5,
-        out_specs=[whole] * tm,
+        out_specs=[unread] + [whole] * tm,
+        input_output_aliases={0: 0},
         scratch_shapes=[pltpu.VMEM((2 * width, width), BF16)] * 2
         + [pltpu.VMEM((tm, vectors, rows), F32)],
         compiler_params=params,
         cost_estimate=cost(32 * own * vectors * tm * samples * width, 8 * own * width * width),
-    )(mine, start_block, flags, ranks, own_weights, cov, first, across, blocks[-1])
-
+    )(other, start_block, flags, ranks, own_weights, cov, first, across, blocks[-1])
+
+    cores = [(0, 1), (1, 0)]
+    theirs = lax.ppermute(other, "pol", cores)
     order = [*range(2, tm), 1]
     arrived = list(packets)
     for x in order:
         arrived[x] = lax.ppermute(packets[x], "tm", [(z, z ^ x) for z in range(tm)])
-    groups = [[0, order[0]], *[[x] for x in order[1:]]]
+    swapped = [lax.ppermute(packet, "pol", cores) for packet in arrived]
+
     shape = jax.ShapeDtypeStruct((chan_dev, samples, half), F32)
-    powers = []
-    for xs in groups:
-        powers = pl.pallas_call(
-            functools.partial(first_kernel, own, xs),
-            out_shape=[shape] * 2,
-            in_specs=[whole] * (2 + len(xs) + len(powers)),
-            out_specs=[whole] * 2,
-            input_output_aliases={2 + len(xs) + i: i for i in range(len(powers))},
-            scratch_shapes=[pltpu.VMEM((rows, half), F32)],
-            compiler_params=params,
-            cost_estimate=cost(len(xs) * own * rows * 2 * vectors * beams, 8 * own * rows * beams),
-        )(mine, other, *[arrived[x] for x in xs], *powers)
-    theirs = lax.ppermute(powers[1], "pol", [(0, 1), (1, 0)])
+    groups = [([0, order[0]], [])] + [([x], []) for x in order[1:-1]] + [(order[-1:], [0, *order[-2::-1]])]
+    power = []
+    for xs, later_xs in groups:
+        used = [arrived[x] for x in xs] + [swapped[x] for x in later_xs]
+        power = [
+            pl.pallas_call(
+                functools.partial(power_kernel, own, xs, later_xs),
+                out_shape=shape,
+                in_specs=[whole, whole if later_xs else unread] + [whole] * (len(used) + len(power)),
+                out_specs=whole,
+                input_output_aliases={2 + len(used): 0} if power else {},
+                scratch_shapes=[pltpu.VMEM((rows, half), F32)],
+                compiler_params=params,
+                cost_estimate=cost(len(used) * own * rows * 2 * vectors * half, 8 * own * rows * half),
+            )(mine, theirs if later_xs else mine, *used, *power)
+        ]
 
     return pl.pallas_call(
-        second_kernel,
+        functools.partial(last_kernel, own, order[-1]),
         out_shape=jax.ShapeDtypeStruct((samples, chan_dev, half), F32),
-        in_specs=[whole] * 2,
+        in_specs=[whole] * 3,
         out_specs=whole,
+        scratch_shapes=[pltpu.VMEM((chan_dev, samples, half), F32), pltpu.VMEM((rows, half), F32)],
         compiler_params=params,
         cost_estimate=cost(chan_dev * samples * half, 12 * chan_dev * samples * half),
-    )(powers[0], theirs)
+    )(theirs, swapped[order[-1]], *power)
 
 
 def solution(mesh):

time: 42.9 us -> 42.6 us (level)
  waiting for transfers between devices: 13.9 us -> 12.7 us
  starting transfers between devices: 9.85 us -> 10.4 us
    ppermute x1 -> x5, waiting for transfers between devices: 1.52 us -> 0.04 us  [the longest x4 0.04 us: local(): swapped = [lax.ppermute(packet, 'pol', cores) for packet in arrived]]
    ppermute x1 -> x5, starting transfers between devices: 0.07 us -> 0.6 us  [the longest x4 0.52 us: local(): swapped = [lax.ppermute(packet, 'pol', cores) for packet in arrived]]
  transfers between devices with their start and end apart: 7 -> 11, of which waited for: 5 -> 4; matrix products, arithmetic and copies ran while one was open for 1% -> 1% of each run, Pallas kernels for 24% -> 25%
where the time goes in v14:
time: 42.6 us; the launch traced here: 42.4 us
  Pallas kernels  16.3 us (38%)
  waiting for transfers between devices  12.7 us (30%)
  starting transfers between devices  10.4 us (24%)
  local copies, waits for them, and re-layouts  2.85 us (7%)
    ppermute x3, waiting for transfers between devices, local(): lax.ppermute(piece, 'tm', [(z, (z + by) % tm) for z in range(tm)])  10.6 us
    pallas_call x1, Pallas kernels, local(): pl.pallas_call(functools.partial(raw_beams_kernel, tm, own), out_shape=[r...  6.85 us
    ppermute x3, starting transfers between devices, local(): lax.ppermute(piece, 'tm', [(z, (z + by) % tm) for z in range(tm)])  6.23 us
    pallas_call x1, Pallas kernels, local(): pl.pallas_call(functools.partial(subspace_kernel, tm, own, factor), out_s...  4.4 us
    ppermute x3, starting transfers between devices, local(): arrived[x] = lax.ppermute(packets[x], 'tm', [(z, z ^ x) for z in range(tm)])  3.54 us
    ppermute x3, waiting for transfers between devices, local(): arrived[x] = lax.ppermute(packets[x], 'tm', [(z, z ^ x) for z in range(tm)])  2.08 us
    pallas_call x1, Pallas kernels, local(): pl.pallas_call(early_kernel, out_shape=[jax.ShapeDtypeStruct((own, 2, wid...  1.51 us
    pallas_call x1, Pallas kernels, local(): pl.pallas_call(functools.partial(own_weights_kernel, own, chan_dev), out_...  1.26 us
  transfers between devices with their start and end apart: 11, of which 4 were waited for; matrix products, arithmetic and copies ran while one was open for 1% of the time, Pallas kernels for 25%

profile of v14, /device:TPU:0, one launch (start us, length us, event | category | flops | bytes accessed | tf_op | source)
XLA Modules:
  0.0 42.4 jit_solution(1891193940482066335)
XLA Ops:
  0.0 0.0 copy-start.1
  0.0 1.2 %constant_dynamic-slice_fusion = bf16[128,1,1,2,512]{4,3,2,1,0:T(2,128)(2,1)S(1)} fusion(bf16[128,1,4,2,512]{4,3,2,1,0:T(2,128)(2,1)} %voltages_ref.1, s32[]{:T(128)S(6)} %select_n.3), kind=kLoop, calls=%fused_computation | loop fusion | bytes 524292 | tf_op jit(solution)/shard_map/dynamic_slice | solution.py:340
  1.2 0.1 reshape_transpose.13.rest_1_
  1.3 3.1 %collective-permute-start = (bf16[1,256,512]{2,1,0:T(8,128)(2,1)S(1)}, bf16[1,256,512]{2,1,0:T(8,128)(2,1)S(1)}, u32[]{:S(2)}, u32[]{:S(2)}) collective-permute-start(bf16[1,256,512]{2,1,0:T(8,128)(2,1)S(1)} %reshape_transpose.13.rest_1_), channel_id=1, source_target_pairs={{0,4},{4,8},{8,12},{12,0},{1,5},{5,9},{9,13},{13,1},{2,6},{6,10},{... | collective-permute-start | bytes 786440 | tf_op jit(solution)/shard_map/ppermute | solution.py:344
  4.4 0.0 copy-start
  4.4 1.2 %copy-done = bf16[128,1,4,2,512]{4,3,2,1,0:T(2,128)(2,1)S(1)} copy-done((bf16[128,1,4,2,512]{4,3,2,1,0:T(2,128)(2,1)S(1)}, bf16[128,1,4,2,512]{4,3,2,1,0:T(2,128)(2,1)}, u32[]{:S(2)}) %copy-start) | copy-done | bytes 1048600
  5.6 0.2 shard_map.55
  5.8 0.1 reshape_transpose.14.rest_2_
  5.9 0.0 copy-start.2
  5.9 2.1 %collective-permute-start.1 = (bf16[1,256,512]{2,1,0:T(8,128)(2,1)S(1)}, bf16[1,256,512]{2,1,0:T(8,128)(2,1)S(1)}, u32[]{:S(2)}, u32[]{:S(2)}) collective-permute-start(bf16[1,256,512]{2,1,0:T(8,128)(2,1)S(1)} %reshape_transpose.14.rest_2_), channel_id=1, source_target_pairs={{0,12},{4,0},{8,4},{12,8},{1,13},{5,1},{9,5},{13,9},{2,14},{6,2},{... | collective-permute-start | bytes 786440 | tf_op jit(solution)/shard_map/ppermute | solution.py:344
  8.0 0.1 reshape_transpose.15.rest_3_
  8.1 1.1 %collective-permute-start.2 = (bf16[1,256,512]{2,1,0:T(8,128)(2,1)S(1)}, bf16[1,256,512]{2,1,0:T(8,128)(2,1)S(1)}, u32[]{:S(2)}, u32[]{:S(2)}) collective-permute-start(bf16[1,256,512]{2,1,0:T(8,128)(2,1)S(1)} %reshape_transpose.15.rest_3_), channel_id=1, source_target_pairs={{0,8},{4,12},{8,0},{12,4},{1,9},{5,13},{9,1},{13,5},{2,10},{6,14},... | collective-permute-start | bytes 786440 | tf_op jit(solution)/shard_map/ppermute | solution.py:344
  9.2 0.1 reshape_transpose.12.rest_0_.refs_0_
  9.3 0.0 copy-done.1
  9.3 1.3 %shard_map.57.weights_ref = bf16[1,512,512]{2,1,0:T(8,128)(2,1)S(1)} custom-call(s32[256,512]{1,0:T(8,128)S(1)} %copy-done.1), custom_call_target="tpu_custom_call" | custom-call | flops 5242880 | bytes 1048576 | tf_op jit(solution)/shard_map/pallas_call | solution.py:359
  10.5 0.0 copy-start.3
  10.6 0.0 copy-start.4
  10.6 6.8 %shard_map.56 = (f32[4,256,128]{2,1,0:T(8,128)S(1)}, f32[4,256,128]{2,1,0:T(8,128)S(1)}) custom-call(s32[256,512]{1,0:T(8,128)S(1)} %copy-done.1, bf16[1,256,512]{2,1,0:T(8,128)(2,1)S(1)} %reshape_transpose.12.rest_0_.refs_0_, bf16[1,256,512]{2,1,0:T(8,128)(2,1)S(1)} %reshape_transpose.13.rest_1_, bf16[1,256,512]{2,1,0:T(8,128)(2,1)S(1)} %reshape_transpose.14.rest_2_, ...), custom_call_target="tpu_custom_call" | custom-call | flops 536870912 | bytes 2097152 | tf_op jit(solution)/shard_map/pallas_call | solution.py:349
  17.4 0.0 collective-permute-done.refs_1_
  17.4 0.9 %collective-permute-done.1.refs_2_ = bf16[1,256,512]{2,1,0:T(8,128)(2,1)S(1)} collective-permute-done((bf16[1,256,512]{2,1,0:T(8,128)(2,1)S(1)}, bf16[1,256,512]{2,1,0:T(8,128)(2,1)S(1)}, u32[]{:S(2)}, u32[]{:S(2)}) %collective-permute-start.1) | collective-permute-done | bytes 262176 | tf_op jit(solution)/shard_map/ppermute | solution.py:344
  18.3 0.0 copy-done.2
  18.3 1.5 %shard_map.58 = (f32[1,2,512,512]{3,2,1,0:T(8,128)S(1)}, f32[1,16,512]{2,1,0:T(8,128)S(1)}, bf16[1,512,768]{2,1,0:T(8,128)(2,1)S(1)}) custom-call(f32[1,4,2,8,512]{4,3,2,1,0:T(8,128)S(1)} %copy-done.2, bf16[1,256,512]{2,1,0:T(8,128)(2,1)S(1)} %reshape_transpose.12.rest_0_.refs_0_, bf16[1,256,512]{2,1,0:T(8,128)(2,1)S(1)} %collective-permute-done.refs_1_, ...), custom_call_target="tpu_custom_call" | custom-call | flops 805306368 | bytes 2097152 | tf_op jit(solution)/shard_map/pallas_call | solution.py:370
  19.8 9.7 %collective-permute-done.2.last_ref = bf16[1,256,512]{2,1,0:T(8,128)(2,1)S(1)} collective-permute-done((bf16[1,256,512]{2,1,0:T(8,128)(2,1)S(1)}, bf16[1,256,512]{2,1,0:T(8,128)(2,1)S(1)}, u32[]{:S(2)}, u32[]{:S(2)}) %collective-permute-start.2) | collective-permute-done | bytes 262176 | tf_op jit(solution)/shard_map/ppermute | solution.py:344
  29.6 0.0 copy-done.3
  29.6 0.0 copy-done.4
  29.6 4.4 %shard_map.59 = (f32[4,256,128]{2,1,0:T(8,128)S(1)}, bf16[1,16,384]{2,1,0:T(8,128)(2,1)S(1)}, bf16[1,16,384]{2,1,0:T(8,128)(2,1)S(1)}, bf16[1,16,384]{2,1,0:T(8,128)(2,1)S(1)}, bf16[1,16,384]{2,1,0:T(8,128)(2,1)S(1)}) custom-call(f32[4,256,128]{2,1,0:T(8,128)S(1)} %get-tuple-element.21.beams_ref, ...), custom_call_target="tpu_custom_call", output_to_operand_aliasing={{0}: (0, {})} | custom-call | flops 134217728 | bytes 2097152 | tf_op jit(solution)/shard_map/pallas_call | solution.py:384
  34.0 0.1 collective-permute-start.3
  34.1 0.1 collective-permute-start.9
  34.1 1.7 %collective-permute-start.7 = (bf16[1,16,384]{2,1,0:T(8,128)(2,1)S(1)}, bf16[1,16,384]{2,1,0:T(8,128)(2,1)S(1)}, u32[]{:S(2)}, u32[]{:S(2)}) collective-permute-start(bf16[1,16,384]{2,1,0:T(8,128)(2,1)S(1)} %get-tuple-element.29), channel_id=1, source_target_pairs={{0,12},{4,8},{8,4},{12,0},{1,13},{5,9},{9,5},{13,1},{2,14},{6,10},... | collective-permute-start | bytes 36872 | tf_op jit(solution)/shard_map/ppermute | solution.py:401
  35.8 1.8 %collective-permute-start.4 = (bf16[1,16,384]{2,1,0:T(8,128)(2,1)S(1)}, bf16[1,16,384]{2,1,0:T(8,128)(2,1)S(1)}, u32[]{:S(2)}, u32[]{:S(2)}) collective-permute-start(bf16[1,16,384]{2,1,0:T(8,128)(2,1)S(1)} %get-tuple-element.26), channel_id=1, source_target_pairs={{0,4},{4,0},{8,12},{12,8},{1,5},{5,1},{9,13},{13,9},{2,6},{6,2},{1... | collective-permute-start | bytes 36872 | tf_op jit(solution)/shard_map/ppermute | solution.py:401
  37.6 0.0 collective-permute-start.6
  37.6 1.2 %collective-permute-done.9.rest_1_ = bf16[1,16,384]{2,1,0:T(8,128)(2,1)S(1)} collective-permute-done((bf16[1,16,384]{2,1,0:T(8,128)(2,1)S(1)}, bf16[1,16,384]{2,1,0:T(8,128)(2,1)S(1)}, u32[]{:S(2)}, u32[]{:S(2)}) %collective-permute-start.9) | collective-permute-done | bytes 12320 | tf_op jit(solution)/shard_map/ppermute | solution.py:401
  38.8 0.0 collective-permute-start.10
  38.8 0.9 %collective-permute-done.7.rest_0_ = bf16[1,16,384]{2,1,0:T(8,128)(2,1)S(1)} collective-permute-done((bf16[1,16,384]{2,1,0:T(8,128)(2,1)S(1)}, bf16[1,16,384]{2,1,0:T(8,128)(2,1)S(1)}, u32[]{:S(2)}, u32[]{:S(2)}) %collective-permute-start.7) | collective-permute-done | bytes 12320 | tf_op jit(solution)/shard_map/ppermute | solution.py:401
  39.7 0.0 collective-permute-start.8
  39.7 0.0 collective-permute-done.4.rest_0_
  39.7 0.5 %collective-permute-start.5 = (bf16[1,16,384]{2,1,0:T(8,128)(2,1)S(1)}, bf16[1,16,384]{2,1,0:T(8,128)(2,1)S(1)}, u32[]{:S(2)}, u32[]{:S(2)}) collective-permute-start(bf16[1,16,384]{2,1,0:T(8,128)(2,1)S(1)} %collective-permute-done.4.rest_0_), channel_id=1, source_target_pairs={{0,1},{1,0},{2,3},{3,2},{4,5},{5,4},{6,7},{7,6},{8,9},{9,8},{10,11... | collective-permute-start | bytes 36872 | tf_op jit(solution)/shard_map/ppermute | solution.py:402
  40.2 0.3 shard_map.60.rest_1_
  40.5 0.3 shard_map.61.rest_4_
  40.8 0.0 collective-permute-done.6.rest_1_
  40.8 0.0 collective-permute-done.10.rest_3_
  40.8 0.0 collective-permute-done.8.rest_2_
  40.9 0.0 collective-permute-done.3.theirs_ref
  40.9 0.4 shard_map.62.power_ref
  41.2 0.0 collective-permute-done.5.packet_ref
  41.3 1.1 %shard_map.63 = f32[128,4,128]{2,1,0:T(4,128)} custom-call(f32[4,256,128]{2,1,0:T(8,128)S(1)} %collective-permute-done.3.theirs_ref, bf16[1,16,384]{2,1,0:T(8,128)(2,1)S(1)} %collective-permute-done.5.packet_ref, f32[4,128,128]{2,1,0:T(8,128)S(1)} %shard_map.62.power_ref), custom_call_target="tpu_custom_call" | custom-call | flops 131072 | bytes 786432 | tf_op jit(solution)/shard_map/pallas_call | solution.py:422
Async XLA Ops:
  0.0 9.3 %copy-start.1 = (s32[256,512]{1,0:T(8,128)S(1)}, s32[256,512]{1,0:T(8,128)}, u32[]{:S(2)}) copy-start(s32[256,512]{1,0:T(8,128)} %phase_ref.3) | copy-start | bytes 1572868
  1.3 16.1 %collective-permute-start = (bf16[1,256,512]{2,1,0:T(8,128)(2,1)S(1)}, bf16[1,256,512]{2,1,0:T(8,128)(2,1)S(1)}, u32[]{:S(2)}, u32[]{:S(2)}) collective-permute-start(bf16[1,256,512]{2,1,0:T(8,128)(2,1)S(1)} %reshape_transpose.13.rest_1_), channel_id=1, source_target_pairs={{0,4},{4,8},{8,12},{12,0},{1,5},{5,9},{9,13},{13,1},{2,6},{6,10},{... | collective-permute-start | bytes 786440 | tf_op jit(solution)/shard_map/ppermute | solution.py:344
  4.4 1.2 %copy-start = (bf16[128,1,4,2,512]{4,3,2,1,0:T(2,128)(2,1)S(1)}, bf16[128,1,4,2,512]{4,3,2,1,0:T(2,128)(2,1)}, u32[]{:S(2)}) copy-start(bf16[128,1,4,2,512]{4,3,2,1,0:T(2,128)(2,1)} %voltages_ref.1) | copy-start | bytes 3145732
  5.9 12.4 %copy-start.2 = (f32[1,4,2,8,512]{4,3,2,1,0:T(8,128)S(1)}, f32[1,4,2,8,512]{4,3,2,1,0:T(8,128)}, u32[]{:S(2)}) copy-start(f32[1,4,2,8,512]{4,3,2,1,0:T(8,128)} %start_ref.3) | copy-start | bytes 393220
  5.9 12.4 %collective-permute-start.1 = (bf16[1,256,512]{2,1,0:T(8,128)(2,1)S(1)}, bf16[1,256,512]{2,1,0:T(8,128)(2,1)S(1)}, u32[]{:S(2)}, u32[]{:S(2)}) collective-permute-start(bf16[1,256,512]{2,1,0:T(8,128)(2,1)S(1)} %reshape_transpose.14.rest_2_), channel_id=1, source_target_pairs={{0,12},{4,0},{8,4},{12,8},{1,13},{5,1},{9,5},{13,9},{2,14},{6,2},{... | collective-permute-start | bytes 786440 | tf_op jit(solution)/shard_map/ppermute | solution.py:344
  8.1 21.5 %collective-permute-start.2 = (bf16[1,256,512]{2,1,0:T(8,128)(2,1)S(1)}, bf16[1,256,512]{2,1,0:T(8,128)(2,1)S(1)}, u32[]{:S(2)}, u32[]{:S(2)}) collective-permute-start(bf16[1,256,512]{2,1,0:T(8,128)(2,1)S(1)} %reshape_transpose.15.rest_3_), channel_id=1, source_target_pairs={{0,8},{4,12},{8,0},{12,4},{1,9},{5,13},{9,1},{13,5},{2,10},{6,14},... | collective-permute-start | bytes 786440 | tf_op jit(solution)/shard_map/ppermute | solution.py:344
  10.5 19.0 %copy-start.3 = (s32[4]{0:T(128)S(1)}, s32[4]{0:T(128)}, u32[]{:S(2)}) copy-start(s32[4]{0:T(128)} %flags_ref.1) | copy-start | bytes 52
  10.6 19.0 %copy-start.4 = (s32[4]{0:T(128)S(1)}, s32[4]{0:T(128)}, u32[]{:S(2)}) copy-start(s32[4]{0:T(128)} %ranks_ref.1) | copy-start | bytes 52
  34.0 6.9 %collective-permute-start.3 = (f32[4,256,128]{2,1,0:T(8,128)S(1)}, f32[4,256,128]{2,1,0:T(8,128)S(1)}, u32[]{:S(2)}, u32[]{:S(2)}) collective-permute-start(f32[4,256,128]{2,1,0:T(8,128)S(1)} %get-tuple-element.25), channel_id=1, source_target_pairs={{0,1},{1,0},{2,3},{3,2},{4,5},{5,4},{6,7},{7,6},{8,9},{9,8},{10,11... | collective-permute-start | bytes 1572872 | tf_op jit(solution)/shard_map/ppermute | solution.py:397
  34.1 4.7 %collective-permute-start.9 = (bf16[1,16,384]{2,1,0:T(8,128)(2,1)S(1)}, bf16[1,16,384]{2,1,0:T(8,128)(2,1)S(1)}, u32[]{:S(2)}, u32[]{:S(2)}) collective-permute-start(bf16[1,16,384]{2,1,0:T(8,128)(2,1)S(1)} %get-tuple-element.30), channel_id=1, source_target_pairs={{0,8},{4,12},{8,0},{12,4},{1,9},{5,13},{9,1},{13,5},{2,10},{6,14},... | collective-permute-start | bytes 36872 | tf_op jit(solution)/shard_map/ppermute | solution.py:401
  34.1 5.6 %collective-permute-start.7 = (bf16[1,16,384]{2,1,0:T(8,128)(2,1)S(1)}, bf16[1,16,384]{2,1,0:T(8,128)(2,1)S(1)}, u32[]{:S(2)}, u32[]{:S(2)}) collective-permute-start(bf16[1,16,384]{2,1,0:T(8,128)(2,1)S(1)} %get-tuple-element.29), channel_id=1, source_target_pairs={{0,12},{4,8},{8,4},{12,0},{1,13},{5,9},{9,5},{13,1},{2,14},{6,10},... | collective-permute-start | bytes 36872 | tf_op jit(solution)/shard_map/ppermute | solution.py:401
  35.8 3.9 %collective-permute-start.4 = (bf16[1,16,384]{2,1,0:T(8,128)(2,1)S(1)}, bf16[1,16,384]{2,1,0:T(8,128)(2,1)S(1)}, u32[]{:S(2)}, u32[]{:S(2)}) collective-permute-start(bf16[1,16,384]{2,1,0:T(8,128)(2,1)S(1)} %get-tuple-element.26), channel_id=1, source_target_pairs={{0,4},{4,0},{8,12},{12,8},{1,5},{5,1},{9,13},{13,9},{2,6},{6,2},{1... | collective-permute-start | bytes 36872 | tf_op jit(solution)/shard_map/ppermute | solution.py:401
  37.6 3.2 %collective-permute-start.6 = (bf16[1,16,384]{2,1,0:T(8,128)(2,1)S(1)}, bf16[1,16,384]{2,1,0:T(8,128)(2,1)S(1)}, u32[]{:S(2)}, u32[]{:S(2)}) collective-permute-start(bf16[1,16,384]{2,1,0:T(8,128)(2,1)S(1)} %get-tuple-element.28.rest_0_), channel_id=1, source_target_pairs={{0,1},{1,0},{2,3},{3,2},{4,5},{5,4},{6,7},{7,6},{8,9},{9,8},{10,11... | collective-permute-start | bytes 36872 | tf_op jit(solution)/shard_map/ppermute | solution.py:402
  38.8 2.1 %collective-permute-start.10 = (bf16[1,16,384]{2,1,0:T(8,128)(2,1)S(1)}, bf16[1,16,384]{2,1,0:T(8,128)(2,1)S(1)}, u32[]{:S(2)}, u32[]{:S(2)}) collective-permute-start(bf16[1,16,384]{2,1,0:T(8,128)(2,1)S(1)} %collective-permute-done.9.rest_1_), channel_id=1, source_target_pairs={{0,1},{1,0},{2,3},{3,2},{4,5},{5,4},{6,7},{7,6},{8,9},{9,8},{10,11... | collective-permute-start | bytes 36872 | tf_op jit(solution)/shard_map/ppermute | solution.py:402
  39.7 1.2 %collective-permute-start.8 = (bf16[1,16,384]{2,1,0:T(8,128)(2,1)S(1)}, bf16[1,16,384]{2,1,0:T(8,128)(2,1)S(1)}, u32[]{:S(2)}, u32[]{:S(2)}) collective-permute-start(bf16[1,16,384]{2,1,0:T(8,128)(2,1)S(1)} %collective-permute-done.7.rest_0_), channel_id=1, source_target_pairs={{0,1},{1,0},{2,3},{3,2},{4,5},{5,4},{6,7},{7,6},{8,9},{9,8},{10,11... | collective-permute-start | bytes 36872 | tf_op jit(solution)/shard_map/ppermute | solution.py:402
  39.7 1.5 %collective-permute-start.5 = (bf16[1,16,384]{2,1,0:T(8,128)(2,1)S(1)}, bf16[1,16,384]{2,1,0:T(8,128)(2,1)S(1)}, u32[]{:S(2)}, u32[]{:S(2)}) collective-permute-start(bf16[1,16,384]{2,1,0:T(8,128)(2,1)S(1)} %collective-permute-done.4.rest_0_), channel_id=1, source_target_pairs={{0,1},{1,0},{2,3},{3,2},{4,5},{5,4},{6,7},{7,6},{8,9},{9,8},{10,11... | collective-permute-start | bytes 36872 | tf_op jit(solution)/shard_map/ppermute | solution.py:402

commit v15 on v14

--- a/solution.py
+++ b/solution.py
@@ -17,6 +17,7 @@
 NN = (((1,), (0,)), ((), ()))
 TN = (((0,), (0,)), ((), ()))
 VMEM_LIMIT = 48 * 1024 * 1024
+FIRST_GRANT = 63 * 1024 * 1024
 CHUNK = 128
 
 
@@ -66,6 +67,13 @@
 def shifted(by):
     tm = lax.axis_size("tm")
     return lax.rem(lax.axis_index("tm") + tm + by, tm)
+
+
+def first_cut_kernel(own, voltages_ref, piece_ref, done):
+    channels = pl.ds(shifted(steps(lax.axis_size("tm"))[1]) * own, own)
+    copy = pltpu.make_async_copy(voltages_ref.at[:, 0, channels], piece_ref, done)
+    copy.start()
+    copy.wait()
 
 
 def cut_kernel(own, bys, voltages_ref, *rest):
@@ -263,10 +271,11 @@
         product = product[: 2 * vectors] + product[2 * vectors :]
         real_w = product[:vectors, :beams] - product[vectors:, beams:]
         imag_w = product[:vectors, beams:] + product[vectors:, :beams]
-        for i, by in enumerate(steps(tm)):
-            block = across_ref[o, :, i * rows : (i + 1) * rows] if i < tm - 1 else across
-            series = project(real_u, imag_u, block)[0]
-            series_ref[tm_index ^ shifted(-by)] = series
+        early = project(real_u, imag_u, across_ref[o])[0]
+        series = [early[:, i * rows : (i + 1) * rows] for i in range(tm - 1)]
+        series.append(project(real_u, imag_u, across)[0])
+        for by, values in zip(steps(tm), series):
+            series_ref[tm_index ^ shifted(-by)] = values
         steered = jnp.concatenate([real_w, imag_w], axis=0).astype(BF16)
         for x, out in enumerate(outs):
             series = series_ref[x]
@@ -337,13 +346,26 @@
         scratch_shapes=[pltpu.SemaphoreType.DMA((tm - 1,))],
         compiler_params=params,
     )(voltages)
-    urgent = lax.dynamic_slice_in_dim(voltages[:, 0], shifted(by[1]) * own, own, 1)
-    cut = [later[0], urgent, *later[1:]]
-    pieces = [piece.transpose(1, 0, 2, 3).reshape(own, rows, width) for piece in cut]
-    blocks = pieces[:1] + [
-        lax.ppermute(piece, "tm", [(z, (z + by) % tm) for z in range(tm)])
-        for by, piece in zip(steps(tm)[1:], pieces[1:])
-    ]
+    urgent = pl.pallas_call(
+        functools.partial(first_cut_kernel, own),
+        out_shape=jax.ShapeDtypeStruct((samples, own, 2, width), BF16),
+        in_specs=[pl.BlockSpec(memory_space=pltpu.HBM)],
+        out_specs=pl.BlockSpec(memory_space=pltpu.HBM),
+        scratch_shapes=[pltpu.SemaphoreType.DMA],
+        compiler_params=pltpu.CompilerParams(vmem_limit_bytes=FIRST_GRANT),
+    )(voltages)
+
+    def by_channel(piece):
+        return piece.transpose(1, 0, 2, 3).reshape(own, rows, width)
+
+    def send(piece, by):
+        return lax.ppermute(piece, "tm", [(z, (z + by) % tm) for z in range(tm)])
+
+    arrived = send(urgent, by[1])
+    home, *later = [by_channel(piece) for piece in later]
+    blocks = [home, None, *[send(piece, step) for piece, step in zip(later, by[2:])]]
+    blocks[1] = by_channel(arrived)
+    pieces = [home, by_channel(urgent), *later]
 
     raw = jax.ShapeDtypeStruct((chan_dev, rows, half), F32)
     mine, other = pl.pallas_call(
@@ -415,7 +437,7 @@
                 input_output_aliases={2 + len(used): 0} if power else {},
                 scratch_shapes=[pltpu.VMEM((rows, half), F32)],
                 compiler_params=params,
-                cost_estimate=cost(len(used) * own * rows * 2 * vectors * half, 8 * own * rows * half),
+                cost_estimate=cost(10**10 if later_xs else 10**6, 8 * own * rows * half),
             )(mine, theirs if later_xs else mine, *used, *power)
         ]
 

time: 42.6 us -> 50.6 us (1.19)
  Pallas kernels: 16.3 us -> 26.3 us
  waiting for transfers between devices: 12.7 us -> 9.16 us
  local copies, waits for them, and re-layouts: 2.85 us -> 4.36 us
    pallas_call x0 -> x1, Pallas kernels: none -> 9.05 us  [local(): pl.pallas_call(functools.partial(first_cut_kernel, own), out_shape=jax.Sh...]
    ppermute x3, waiting for transfers between devices: 10.6 us -> 7.04 us  [send(): return lax.ppermute(piece, 'tm', [(z, (z + by) % tm) for z in range(tm)])]
    another operation x4 -> x5, local copies, waits for them, and re-layouts: 0.41 us -> 2.16 us  [by_channel(): return piece.transpose(1, 0, 2, 3).reshape(own, rows, width)]
    dynamic_slice x1 -> x0, local copies, waits for them, and re-layouts: 1.19 us -> none  [local(): lax.dynamic_slice_in_dim(voltages[:, 0], shifted(by[1]) * own, own, 1)]
    pallas_call x1, Pallas kernels: 1.51 us -> 2.51 us  [local(): pl.pallas_call(early_kernel, out_shape=[jax.ShapeDtypeStruct((own, 2, wid...]
    unnamed x10 -> x14, local copies, waits for them, and re-layouts: 1.25 us -> 2.19 us
  transfers between devices with their start and end apart: 11 -> 11, of which waited for: 4 -> 3; matrix products, arithmetic and copies ran while one was open for 1% -> 4% of each run, Pallas kernels for 25% -> 23%
where the time goes in v15:
time: 50.6 us; the launch traced here: 50.4 us
  Pallas kernels  26.3 us (52%)
  starting transfers between devices  10.4 us (21%)
  waiting for transfers between devices  9.16 us (18%)
  local copies, waits for them, and re-layouts  4.36 us (9%)
    pallas_call x1, Pallas kernels, local(): pl.pallas_call(functools.partial(first_cut_kernel, own), out_shape=jax.Sh...  9.05 us
    ppermute x3, waiting for transfers between devices, send(): return lax.ppermute(piece, 'tm', [(z, (z + by) % tm) for z in range(tm)])  7.04 us
    pallas_call x1, Pallas kernels, local(): pl.pallas_call(functools.partial(raw_beams_kernel, tm, own), out_shape=[r...  6.82 us
    ppermute x3, starting transfers between devices, send(): return lax.ppermute(piece, 'tm', [(z, (z + by) % tm) for z in range(tm)])  6.23 us
    pallas_call x1, Pallas kernels, local(): pl.pallas_call(functools.partial(subspace_kernel, tm, own, factor), out_s...  4.41 us
    ppermute x3, starting transfers between devices, local(): arrived[x] = lax.ppermute(packets[x], 'tm', [(z, z ^ x) for z in range(tm)])  3.54 us
    pallas_call x1, Pallas kernels, local(): pl.pallas_call(early_kernel, out_shape=[jax.ShapeDtypeStruct((own, 2, wid...  2.51 us
    unnamed x14, local copies, waits for them, and re-layouts  2.19 us
  transfers between devices with their start and end apart: 11, of which 3 were waited for; matrix products, arithmetic and copies ran while one was open for 4% of the time, Pallas kernels for 23%

profile of v15, /device:TPU:0, one launch (start us, length us, event | category | flops | bytes accessed | tf_op | source)
XLA Modules:
  0.0 50.4 jit_solution(2630287089221030847)
XLA Ops:
  0.0 0.0 copy-start.1
  0.0 9.0 %shard_map.56 = bf16[128,1,2,512]{3,2,1,0:T(2,128)(2,1)} custom-call(bf16[128,1,4,2,512]{4,3,2,1,0:T(2,128)(2,1)} %voltages_ref.3), custom_call_target="tpu_custom_call" | custom-call | tf_op jit(solution)/shard_map/pallas_call | solution.py:349
  9.1 3.1 %collective-permute-start = (bf16[128,1,2,512]{3,2,1,0:T(2,128)(2,1)}, bf16[128,1,2,512]{3,2,1,0:T(2,128)(2,1)}, u32[]{:S(2)}, u32[]{:S(2)}) collective-permute-start(bf16[128,1,2,512]{3,2,1,0:T(2,128)(2,1)} %shard_map.56), channel_id=1, source_target_pairs={{0,4},{4,8},{8,12},{12,0},{1,5},{5,9},{9,13},{13,1},{2,6},{6,10},{... | collective-permute-start | bytes 786440 | tf_op jit(solution)/shard_map/ppermute | solution.py:362
  12.1 0.0 copy-start
  12.1 1.2 %copy-done = bf16[128,1,4,2,512]{4,3,2,1,0:T(2,128)(2,1)S(1)} copy-done((bf16[128,1,4,2,512]{4,3,2,1,0:T(2,128)(2,1)S(1)}, bf16[128,1,4,2,512]{4,3,2,1,0:T(2,128)(2,1)}, u32[]{:S(2)}) %copy-start) | copy-done | bytes 1048600
  13.4 0.0 copy-start.6
  13.4 0.2 shard_map.55
  13.5 0.1 reshape_transpose.17.rest_2_
  13.7 2.1 %collective-permute-start.1 = (bf16[1,256,512]{2,1,0:T(8,128)(2,1)S(1)}, bf16[1,256,512]{2,1,0:T(8,128)(2,1)}, u32[]{:S(2)}, u32[]{:S(2)}) collective-permute-start(bf16[1,256,512]{2,1,0:T(8,128)(2,1)S(1)} %reshape_transpose.17.rest_2_), channel_id=1, source_target_pairs={{0,12},{4,0},{8,4},{12,8},{1,13},{5,1},{9,5},{13,9},{2,14},{6,2},{... | collective-permute-start | bytes 786440 | tf_op jit(solution)/shard_map/ppermute | solution.py:362
  15.7 0.1 reshape_transpose.18.rest_3_
  15.9 1.1 %collective-permute-start.2 = (bf16[1,256,512]{2,1,0:T(8,128)(2,1)S(1)}, bf16[1,256,512]{2,1,0:T(8,128)(2,1)S(1)}, u32[]{:S(2)}, u32[]{:S(2)}) collective-permute-start(bf16[1,256,512]{2,1,0:T(8,128)(2,1)S(1)} %reshape_transpose.18.rest_3_), channel_id=1, source_target_pairs={{0,8},{4,12},{8,0},{12,4},{1,9},{5,13},{9,1},{13,5},{2,10},{6,14},... | collective-permute-start | bytes 786440 | tf_op jit(solution)/shard_map/ppermute | solution.py:362
  16.9 0.0 copy-done.6
  16.9 0.8 %reshape_transpose.16.rest_1_ = bf16[1,256,512]{2,1,0:T(8,128)(2,1)} reshape(bf16[128,1,2,512]{3,2,1,0:T(2,128)(2,1)S(1)} %copy-done.6) | data formatting | bytes 524288 | tf_op jit(solution)/shard_map/reshape;transpose | solution.py:359
  17.7 0.0 copy-start.3
  17.7 0.1 reshape_transpose.15.rest_0_.refs_0_
  17.8 0.0 copy-done.1
  17.8 1.3 %shard_map.58.weights_ref = bf16[1,512,512]{2,1,0:T(8,128)(2,1)S(1)} custom-call(s32[256,512]{1,0:T(8,128)S(1)} %copy-done.1), custom_call_target="tpu_custom_call" | custom-call | flops 5242880 | bytes 1048576 | tf_op jit(solution)/shard_map/pallas_call | solution.py:381
  19.1 0.0 copy-start.2
  19.1 0.9 %copy-done.2 = bf16[1,256,512]{2,1,0:T(8,128)(2,1)S(1)} copy-done((bf16[1,256,512]{2,1,0:T(8,128)(2,1)S(1)}, bf16[1,256,512]{2,1,0:T(8,128)(2,1)}, u32[]{:S(2)}) %copy-start.2) | copy-done | bytes 262168
  20.1 6.8 %shard_map.57 = (f32[4,256,128]{2,1,0:T(8,128)S(1)}, f32[4,256,128]{2,1,0:T(8,128)S(1)}) custom-call(s32[256,512]{1,0:T(8,128)S(1)} %copy-done.1, bf16[1,256,512]{2,1,0:T(8,128)(2,1)S(1)} %reshape_transpose.15.rest_0_.refs_0_, bf16[1,256,512]{2,1,0:T(8,128)(2,1)S(1)} %copy-done.2, bf16[1,256,512]{2,1,0:T(8,128)(2,1)S(1)} %reshape_transpose.17.rest_2_, ...), custom_call_target="tpu_custom_call" | custom-call | flops 536870912 | bytes 2097152 | tf_op jit(solution)/shard_map/pallas_call | solution.py:371
  26.9 0.0 copy-start.4
  26.9 0.0 copy-start.5
  26.9 0.0 collective-permute-done
  26.9 1.1 %reshape_transpose.19.refs_1_ = bf16[1,256,512]{2,1,0:T(8,128)(2,1)S(1)} reshape(bf16[128,1,2,512]{3,2,1,0:T(2,128)(2,1)} %collective-permute-done) | data formatting | bytes 524288 | tf_op jit(solution)/shard_map/reshape;transpose | solution.py:359
  28.0 0.0 collective-permute-done.1.refs_2_
  28.0 0.0 copy-done.3
  28.0 2.5 %shard_map.59 = (f32[1,2,512,512]{3,2,1,0:T(8,128)S(1)}, f32[1,16,512]{2,1,0:T(8,128)S(1)}, bf16[1,512,768]{2,1,0:T(8,128)(2,1)S(1)}) custom-call(f32[1,4,2,8,512]{4,3,2,1,0:T(8,128)S(1)} %copy-done.3, bf16[1,256,512]{2,1,0:T(8,128)(2,1)S(1)} %reshape_transpose.15.rest_0_.refs_0_, bf16[1,256,512]{2,1,0:T(8,128)(2,1)S(1)} %reshape_transpose.19.refs_1_, ...), custom_call_target="tpu_custom_call" | custom-call | flops 805306368 | bytes 2097152 | tf_op jit(solution)/shard_map/pallas_call | solution.py:392
  30.5 7.0 %collective-permute-done.2.last_ref = bf16[1,256,512]{2,1,0:T(8,128)(2,1)S(1)} collective-permute-done((bf16[1,256,512]{2,1,0:T(8,128)(2,1)S(1)}, bf16[1,256,512]{2,1,0:T(8,128)(2,1)S(1)}, u32[]{:S(2)}, u32[]{:S(2)}) %collective-permute-start.2) | collective-permute-done | bytes 262176 | tf_op jit(solution)/shard_map/ppermute | solution.py:362
  37.5 0.0 copy-done.4
  37.5 0.0 copy-done.5
  37.5 4.4 %shard_map.60 = (f32[4,256,128]{2,1,0:T(8,128)S(1)}, bf16[1,16,384]{2,1,0:T(8,128)(2,1)S(1)}, bf16[1,16,384]{2,1,0:T(8,128)(2,1)S(1)}, bf16[1,16,384]{2,1,0:T(8,128)(2,1)S(1)}, bf16[1,16,384]{2,1,0:T(8,128)(2,1)S(1)}) custom-call(f32[4,256,128]{2,1,0:T(8,128)S(1)} %get-tuple-element.21.beams_ref, ...), custom_call_target="tpu_custom_call", output_to_operand_aliasing={{0}: (0, {})} | custom-call | flops 134217728 | bytes 2097152 | tf_op jit(solution)/shard_map/pallas_call | solution.py:406
  41.9 0.1 collective-permute-start.3
  42.0 0.1 collective-permute-start.9
  42.1 1.7 %collective-permute-start.7 = (bf16[1,16,384]{2,1,0:T(8,128)(2,1)S(1)}, bf16[1,16,384]{2,1,0:T(8,128)(2,1)S(1)}, u32[]{:S(2)}, u32[]{:S(2)}) collective-permute-start(bf16[1,16,384]{2,1,0:T(8,128)(2,1)S(1)} %get-tuple-element.29), channel_id=1, source_target_pairs={{0,12},{4,8},{8,4},{12,0},{1,13},{5,9},{9,5},{13,1},{2,14},{6,10},... | collective-permute-start | bytes 36872 | tf_op jit(solution)/shard_map/ppermute | solution.py:423
  43.8 1.8 %collective-permute-start.4 = (bf16[1,16,384]{2,1,0:T(8,128)(2,1)S(1)}, bf16[1,16,384]{2,1,0:T(8,128)(2,1)S(1)}, u32[]{:S(2)}, u32[]{:S(2)}) collective-permute-start(bf16[1,16,384]{2,1,0:T(8,128)(2,1)S(1)} %get-tuple-element.26), channel_id=1, source_target_pairs={{0,4},{4,0},{8,12},{12,8},{1,5},{5,1},{9,13},{13,9},{2,6},{6,2},{1... | collective-permute-start | bytes 36872 | tf_op jit(solution)/shard_map/ppermute | solution.py:423
  45.6 0.0 collective-permute-start.6
  45.6 1.2 %collective-permute-done.9.rest_1_ = bf16[1,16,384]{2,1,0:T(8,128)(2,1)S(1)} collective-permute-done((bf16[1,16,384]{2,1,0:T(8,128)(2,1)S(1)}, bf16[1,16,384]{2,1,0:T(8,128)(2,1)S(1)}, u32[]{:S(2)}, u32[]{:S(2)}) %collective-permute-start.9) | collective-permute-done | bytes 12320 | tf_op jit(solution)/shard_map/ppermute | solution.py:423
  46.7 0.0 collective-permute-start.10
  46.7 0.9 %collective-permute-done.7.rest_0_ = bf16[1,16,384]{2,1,0:T(8,128)(2,1)S(1)} collective-permute-done((bf16[1,16,384]{2,1,0:T(8,128)(2,1)S(1)}, bf16[1,16,384]{2,1,0:T(8,128)(2,1)S(1)}, u32[]{:S(2)}, u32[]{:S(2)}) %collective-permute-start.7) | collective-permute-done | bytes 12320 | tf_op jit(solution)/shard_map/ppermute | solution.py:423
  47.7 0.0 collective-permute-start.8
  47.7 0.0 collective-permute-done.4.rest_0_
  47.7 0.5 %collective-permute-start.5 = (bf16[1,16,384]{2,1,0:T(8,128)(2,1)S(1)}, bf16[1,16,384]{2,1,0:T(8,128)(2,1)S(1)}, u32[]{:S(2)}, u32[]{:S(2)}) collective-permute-start(bf16[1,16,384]{2,1,0:T(8,128)(2,1)S(1)} %collective-permute-done.4.rest_0_), channel_id=1, source_target_pairs={{0,1},{1,0},{2,3},{3,2},{4,5},{5,4},{6,7},{7,6},{8,9},{9,8},{10,11... | collective-permute-start | bytes 36872 | tf_op jit(solution)/shard_map/ppermute | solution.py:424
  48.2 0.3 shard_map.61.rest_1_
  48.5 0.3 shard_map.62.rest_4_
  48.8 0.0 collective-permute-done.6.rest_1_
  48.8 0.0 collective-permute-done.10.rest_3_
  48.8 0.0 collective-permute-done.8.rest_2_
  48.8 0.0 collective-permute-done.3.theirs_ref
  48.8 0.4 shard_map.63.power_ref
  49.2 0.0 collective-permute-done.5.packet_ref
  49.2 1.1 %shard_map.64 = f32[128,4,128]{2,1,0:T(4,128)} custom-call(f32[4,256,128]{2,1,0:T(8,128)S(1)} %collective-permute-done.3.theirs_ref, bf16[1,16,384]{2,1,0:T(8,128)(2,1)S(1)} %collective-permute-done.5.packet_ref, f32[4,128,128]{2,1,0:T(8,128)S(1)} %shard_map.63.power_ref), custom_call_target="tpu_custom_call" | custom-call | flops 131072 | bytes 786432 | tf_op jit(solution)/shard_map/pallas_call | solution.py:444
Async XLA Ops:
  0.0 17.8 %copy-start.1 = (s32[256,512]{1,0:T(8,128)S(1)}, s32[256,512]{1,0:T(8,128)}, u32[]{:S(2)}) copy-start(s32[256,512]{1,0:T(8,128)} %phase_ref.3) | copy-start | bytes 1572868
  9.1 17.9 %collective-permute-start = (bf16[128,1,2,512]{3,2,1,0:T(2,128)(2,1)}, bf16[128,1,2,512]{3,2,1,0:T(2,128)(2,1)}, u32[]{:S(2)}, u32[]{:S(2)}) collective-permute-start(bf16[128,1,2,512]{3,2,1,0:T(2,128)(2,1)} %shard_map.56), channel_id=1, source_target_pairs={{0,4},{4,8},{8,12},{12,0},{1,5},{5,9},{9,13},{13,1},{2,6},{6,10},{... | collective-permute-start | bytes 786440 | tf_op jit(solution)/shard_map/ppermute | solution.py:362
  12.1 1.2 %copy-start = (bf16[128,1,4,2,512]{4,3,2,1,0:T(2,128)(2,1)S(1)}, bf16[128,1,4,2,512]{4,3,2,1,0:T(2,128)(2,1)}, u32[]{:S(2)}) copy-start(bf16[128,1,4,2,512]{4,3,2,1,0:T(2,128)(2,1)} %voltages_ref.3) | copy-start | bytes 3145732
  13.4 3.6 %copy-start.6 = (bf16[128,1,2,512]{3,2,1,0:T(2,128)(2,1)S(1)}, bf16[128,1,2,512]{3,2,1,0:T(2,128)(2,1)}, u32[]{:S(2)}) copy-start(bf16[128,1,2,512]{3,2,1,0:T(2,128)(2,1)} %shard_map.56) | copy-start | bytes 786436
  13.7 14.3 %collective-permute-start.1 = (bf16[1,256,512]{2,1,0:T(8,128)(2,1)S(1)}, bf16[1,256,512]{2,1,0:T(8,128)(2,1)}, u32[]{:S(2)}, u32[]{:S(2)}) collective-permute-start(bf16[1,256,512]{2,1,0:T(8,128)(2,1)S(1)} %reshape_transpose.17.rest_2_), channel_id=1, source_target_pairs={{0,12},{4,0},{8,4},{12,8},{1,13},{5,1},{9,5},{13,9},{2,14},{6,2},{... | collective-permute-start | bytes 786440 | tf_op jit(solution)/shard_map/ppermute | solution.py:362
  15.9 21.7 %collective-permute-start.2 = (bf16[1,256,512]{2,1,0:T(8,128)(2,1)S(1)}, bf16[1,256,512]{2,1,0:T(8,128)(2,1)S(1)}, u32[]{:S(2)}, u32[]{:S(2)}) collective-permute-start(bf16[1,256,512]{2,1,0:T(8,128)(2,1)S(1)} %reshape_transpose.18.rest_3_), channel_id=1, source_target_pairs={{0,8},{4,12},{8,0},{12,4},{1,9},{5,13},{9,1},{13,5},{2,10},{6,14},... | collective-permute-start | bytes 786440 | tf_op jit(solution)/shard_map/ppermute | solution.py:362
  17.7 10.3 %copy-start.3 = (f32[1,4,2,8,512]{4,3,2,1,0:T(8,128)S(1)}, f32[1,4,2,8,512]{4,3,2,1,0:T(8,128)}, u32[]{:S(2)}) copy-start(f32[1,4,2,8,512]{4,3,2,1,0:T(8,128)} %start_ref.3) | copy-start | bytes 393220
  19.1 1.0 %copy-start.2 = (bf16[1,256,512]{2,1,0:T(8,128)(2,1)S(1)}, bf16[1,256,512]{2,1,0:T(8,128)(2,1)}, u32[]{:S(2)}) copy-start(bf16[1,256,512]{2,1,0:T(8,128)(2,1)} %reshape_transpose.16.rest_1_) | copy-start | bytes 786436
  26.9 10.7 %copy-start.4 = (s32[4]{0:T(128)S(1)}, s32[4]{0:T(128)}, u32[]{:S(2)}) copy-start(s32[4]{0:T(128)} %flags_ref.1) | copy-start | bytes 52
  26.9 10.6 %copy-start.5 = (s32[4]{0:T(128)S(1)}, s32[4]{0:T(128)}, u32[]{:S(2)}) copy-start(s32[4]{0:T(128)} %ranks_ref.1) | copy-start | bytes 52
  41.9 6.9 %collective-permute-start.3 = (f32[4,256,128]{2,1,0:T(8,128)S(1)}, f32[4,256,128]{2,1,0:T(8,128)S(1)}, u32[]{:S(2)}, u32[]{:S(2)}) collective-permute-start(f32[4,256,128]{2,1,0:T(8,128)S(1)} %get-tuple-element.25), channel_id=1, source_target_pairs={{0,1},{1,0},{2,3},{3,2},{4,5},{5,4},{6,7},{7,6},{8,9},{9,8},{10,11... | collective-permute-start | bytes 1572872 | tf_op jit(solution)/shard_map/ppermute | solution.py:419
  42.0 4.7 %collective-permute-start.9 = (bf16[1,16,384]{2,1,0:T(8,128)(2,1)S(1)}, bf16[1,16,384]{2,1,0:T(8,128)(2,1)S(1)}, u32[]{:S(2)}, u32[]{:S(2)}) collective-permute-start(bf16[1,16,384]{2,1,0:T(8,128)(2,1)S(1)} %get-tuple-element.30), channel_id=1, source_target_pairs={{0,8},{4,12},{8,0},{12,4},{1,9},{5,13},{9,1},{13,5},{2,10},{6,14},... | collective-permute-start | bytes 36872 | tf_op jit(solution)/shard_map/ppermute | solution.py:423
  42.1 5.6 %collective-permute-start.7 = (bf16[1,16,384]{2,1,0:T(8,128)(2,1)S(1)}, bf16[1,16,384]{2,1,0:T(8,128)(2,1)S(1)}, u32[]{:S(2)}, u32[]{:S(2)}) collective-permute-start(bf16[1,16,384]{2,1,0:T(8,128)(2,1)S(1)} %get-tuple-element.29), channel_id=1, source_target_pairs={{0,12},{4,8},{8,4},{12,0},{1,13},{5,9},{9,5},{13,1},{2,14},{6,10},... | collective-permute-start | bytes 36872 | tf_op jit(solution)/shard_map/ppermute | solution.py:423
  43.8 3.9 %collective-permute-start.4 = (bf16[1,16,384]{2,1,0:T(8,128)(2,1)S(1)}, bf16[1,16,384]{2,1,0:T(8,128)(2,1)S(1)}, u32[]{:S(2)}, u32[]{:S(2)}) collective-permute-start(bf16[1,16,384]{2,1,0:T(8,128)(2,1)S(1)} %get-tuple-element.26), channel_id=1, source_target_pairs={{0,4},{4,0},{8,12},{12,8},{1,5},{5,1},{9,13},{13,9},{2,6},{6,2},{1... | collective-permute-start | bytes 36872 | tf_op jit(solution)/shard_map/ppermute | solution.py:423
  45.6 3.2 %collective-permute-start.6 = (bf16[1,16,384]{2,1,0:T(8,128)(2,1)S(1)}, bf16[1,16,384]{2,1,0:T(8,128)(2,1)S(1)}, u32[]{:S(2)}, u32[]{:S(2)}) collective-permute-start(bf16[1,16,384]{2,1,0:T(8,128)(2,1)S(1)} %get-tuple-element.28.rest_0_), channel_id=1, source_target_pairs={{0,1},{1,0},{2,3},{3,2},{4,5},{5,4},{6,7},{7,6},{8,9},{9,8},{10,11... | collective-permute-start | bytes 36872 | tf_op jit(solution)/shard_map/ppermute | solution.py:424
  46.7 2.1 %collective-permute-start.10 = (bf16[1,16,384]{2,1,0:T(8,128)(2,1)S(1)}, bf16[1,16,384]{2,1,0:T(8,128)(2,1)S(1)}, u32[]{:S(2)}, u32[]{:S(2)}) collective-permute-start(bf16[1,16,384]{2,1,0:T(8,128)(2,1)S(1)} %collective-permute-done.9.rest_1_), channel_id=1, source_target_pairs={{0,1},{1,0},{2,3},{3,2},{4,5},{5,4},{6,7},{7,6},{8,9},{9,8},{10,11... | collective-permute-start | bytes 36872 | tf_op jit(solution)/shard_map/ppermute | solution.py:424
  47.7 1.2 %collective-permute-start.8 = (bf16[1,16,384]{2,1,0:T(8,128)(2,1)S(1)}, bf16[1,16,384]{2,1,0:T(8,128)(2,1)S(1)}, u32[]{:S(2)}, u32[]{:S(2)}) collective-permute-start(bf16[1,16,384]{2,1,0:T(8,128)(2,1)S(1)} %collective-permute-done.7.rest_0_), channel_id=1, source_target_pairs={{0,1},{1,0},{2,3},{3,2},{4,5},{5,4},{6,7},{7,6},{8,9},{9,8},{10,11... | collective-permute-start | bytes 36872 | tf_op jit(solution)/shard_map/ppermute | solution.py:424
  47.7 1.5 %collective-permute-start.5 = (bf16[1,16,384]{2,1,0:T(8,128)(2,1)S(1)}, bf16[1,16,384]{2,1,0:T(8,128)(2,1)S(1)}, u32[]{:S(2)}, u32[]{:S(2)}) collective-permute-start(bf16[1,16,384]{2,1,0:T(8,128)(2,1)S(1)} %collective-permute-done.4.rest_0_), channel_id=1, source_target_pairs={{0,1},{1,0},{2,3},{3,2},{4,5},{5,4},{6,7},{7,6},{8,9},{9,8},{10,11... | collective-permute-start | bytes 36872 | tf_op jit(solution)/shard_map/ppermute | solution.py:424

commit v16 on v14

--- a/solution.py
+++ b/solution.py
@@ -185,7 +185,7 @@
     return real_v * factor, imag_v * factor
 
 
-def orthonormalize_by_gram(real_z, imag_z):
+def orthonormalize_by_gram(real_z, imag_z, riders=()):
     vectors = real_z.shape[0]
     row = lax.broadcasted_iota(jnp.int32, (vectors, 1), 0)
     by_z = []
@@ -199,7 +199,7 @@
             )
         )
     by_v = list(by_z)
-    real_v, imag_v = real_z, imag_z
+    pairs = [(real_z, imag_z), *riders]
     for n in range(vectors - 1):
         (real_d, imag_d), (real_p, imag_p) = by_z[n], by_v[n]
         square = jnp.maximum(real_p[n : n + 1], 0.0)
@@ -219,11 +219,16 @@
                 real - (real_s * real_d + imag_s * imag_d),
                 imag - (real_s * imag_d - imag_s * real_d),
             )
-        real_a, imag_a = real_v[n : n + 1], imag_v[n : n + 1]
-        real_v = real_v - (real_c * real_a - imag_c * imag_a)
-        imag_v = imag_v - (real_c * imag_a + imag_c * real_a)
+        pairs = [
+            (
+                real - (real_c * real[n : n + 1] - imag_c * imag[n : n + 1]),
+                imag - (real_c * imag[n : n + 1] + imag_c * real[n : n + 1]),
+            )
+            for real, imag in pairs
+        ]
+    real_v, imag_v = pairs[0]
     factor = 1.0 / jnp.sqrt(jnp.sum(real_v * real_v + imag_v * imag_v, axis=1, keepdims=True) + EPS)
-    return real_v * factor, imag_v * factor
+    return [(real * factor, imag * factor) for real, imag in pairs]
 
 
 def subspace_kernel(
@@ -251,22 +256,28 @@
         last = block_times(start_ref[0, chan, 0], start_ref[0, chan, 1], across, last_ref[o])
         both = (first_ref[o] + last) * factor
         real_q, imag_q = orthonormalize(both[:vectors], both[vectors:], chunks)
-        for sweep in range(1, ITERS):
+        for sweep in range(1, ITERS - 1):
             real_z, imag_z = cov_times(real_q, imag_q, high_ref, low_ref)
-            real_q, imag_q = orthonormalize_by_gram(real_z, imag_z)
-        rank = flags_ref[chan] * ranks_ref[chan]
-        keep = lax.broadcasted_iota(jnp.int32, (vectors, width), 0) < rank
-        real_u = jnp.where(keep, real_q, 0.0)
-        imag_u = jnp.where(keep, imag_q, 0.0)
-        both = jnp.concatenate(split(jnp.concatenate([real_u, imag_u], axis=0)), axis=0)
+            ((real_q, imag_q),) = orthonormalize_by_gram(real_z, imag_z)
+        real_z, imag_z = cov_times(real_q, imag_q, high_ref, low_ref)
+        both = jnp.concatenate(split(jnp.concatenate([real_z, imag_z], axis=0)), axis=0)
         product = dot(both, weights_ref[o], NN)
         product = product[: 2 * vectors] + product[2 * vectors :]
         real_w = product[:vectors, :beams] - product[vectors:, beams:]
         imag_w = product[:vectors, beams:] + product[vectors:, :beams]
-        for i, by in enumerate(steps(tm)):
-            block = across_ref[o, :, i * rows : (i + 1) * rows] if i < tm - 1 else across
-            series = project(real_u, imag_u, block)[0]
-            series_ref[tm_index ^ shifted(-by)] = series
+        riders = [
+            (real_w, imag_w),
+            project(real_z, imag_z, across_ref[o]),
+            project(real_z, imag_z, across),
+        ]
+        unused, (real_w, imag_w), (early, unused), (late, unused) = orthonormalize_by_gram(real_z, imag_z, riders)
+        rank = flags_ref[chan] * ranks_ref[chan]
+        keep = lax.broadcasted_iota(jnp.int32, (vectors, 1), 0) < rank
+        real_w = jnp.where(keep, real_w, 0.0)
+        imag_w = jnp.where(keep, imag_w, 0.0)
+        series = [early[:, i * rows : (i + 1) * rows] for i in range(tm - 1)] + [late]
+        for by, values in zip(steps(tm), series):
+            series_ref[tm_index ^ shifted(-by)] = jnp.where(keep, values, 0.0)
         steered = jnp.concatenate([real_w, imag_w], axis=0).astype(BF16)
         for x, out in enumerate(outs):
             series = series_ref[x]
@@ -402,7 +413,7 @@
     swapped = [lax.ppermute(packet, "pol", cores) for packet in arrived]
 
     shape = jax.ShapeDtypeStruct((chan_dev, samples, half), F32)
-    groups = [([0, order[0]], [])] + [([x], []) for x in order[1:-1]] + [(order[-1:], [0, *order[-2::-1]])]
+    groups = [([0, *order[:-1]], []), (order[-1:], [0, *order[-2::-1]])]
     power = []
     for xs, later_xs in groups:
         used = [arrived[x] for x in xs] + [swapped[x] for x in later_xs]

time: 42.6 us -> 42.3 us (level)
  Pallas kernels: 16.3 us -> 15.8 us
    pallas_call x3 -> x2, Pallas kernels: 0.95 us -> 0.69 us  [local(): pl.pallas_call(functools.partial(power_kernel, own, xs, later_xs), out_sh...]
  transfers between devices with their start and end apart: 11 -> 11, of which waited for: 4 -> 5; matrix products, arithmetic and copies ran while one was open for 1% -> 1% of each run, Pallas kernels for 25% -> 25%
where the time goes in v16:
time: 42.3 us; the launch traced here: 42.2 us
  Pallas kernels  15.8 us (37%)
  waiting for transfers between devices  13 us (31%)
  starting transfers between devices  10.4 us (25%)
  local copies, waits for them, and re-layouts  2.85 us (7%)
    ppermute x3, waiting for transfers between devices, local(): lax.ppermute(piece, 'tm', [(z, (z + by) % tm) for z in range(tm)])  10.6 us
    pallas_call x1, Pallas kernels, local(): pl.pallas_call(functools.partial(raw_beams_kernel, tm, own), out_shape=[r...  6.85 us
    ppermute x3, starting transfers between devices, local(): lax.ppermute(piece, 'tm', [(z, (z + by) % tm) for z in range(tm)])  6.23 us
    pallas_call x1, Pallas kernels, local(): pl.pallas_call(functools.partial(subspace_kernel, tm, own, factor), out_s...  4.19 us
    ppermute x3, starting transfers between devices, local(): arrived[x] = lax.ppermute(packets[x], 'tm', [(z, z ^ x) for z in range(tm)])  3.54 us
    ppermute x3, waiting for transfers between devices, local(): arrived[x] = lax.ppermute(packets[x], 'tm', [(z, z ^ x) for z in range(tm)])  2.08 us
    pallas_call x1, Pallas kernels, local(): pl.pallas_call(early_kernel, out_shape=[jax.ShapeDtypeStruct((own, 2, wid...  1.51 us
    pallas_call x1, Pallas kernels, local(): pl.pallas_call(functools.partial(own_weights_kernel, own, chan_dev), out_...  1.26 us
  transfers between devices with their start and end apart: 11, of which 5 were waited for; matrix products, arithmetic and copies ran while one was open for 1% of the time, Pallas kernels for 25%

profile of v16, /device:TPU:0, one launch (start us, length us, event | category | flops | bytes accessed | tf_op | source)
XLA Modules:
  0.0 42.2 jit_solution(1957627736238403657)
XLA Ops:
  0.0 0.0 copy-start.1
  0.0 1.2 %constant_dynamic-slice_fusion = bf16[128,1,1,2,512]{4,3,2,1,0:T(2,128)(2,1)S(1)} fusion(bf16[128,1,4,2,512]{4,3,2,1,0:T(2,128)(2,1)} %voltages_ref.1, s32[]{:T(128)S(6)} %select_n.3), kind=kLoop, calls=%fused_computation | loop fusion | bytes 524292 | tf_op jit(solution)/shard_map/dynamic_slice | solution.py:351
  1.2 0.1 reshape_transpose.13.rest_1_
  1.3 3.1 %collective-permute-start = (bf16[1,256,512]{2,1,0:T(8,128)(2,1)S(1)}, bf16[1,256,512]{2,1,0:T(8,128)(2,1)S(1)}, u32[]{:S(2)}, u32[]{:S(2)}) collective-permute-start(bf16[1,256,512]{2,1,0:T(8,128)(2,1)S(1)} %reshape_transpose.13.rest_1_), channel_id=1, source_target_pairs={{0,4},{4,8},{8,12},{12,0},{1,5},{5,9},{9,13},{13,1},{2,6},{6,10},{... | collective-permute-start | bytes 786440 | tf_op jit(solution)/shard_map/ppermute | solution.py:355
  4.4 0.0 copy-start
  4.4 1.2 %copy-done = bf16[128,1,4,2,512]{4,3,2,1,0:T(2,128)(2,1)S(1)} copy-done((bf16[128,1,4,2,512]{4,3,2,1,0:T(2,128)(2,1)S(1)}, bf16[128,1,4,2,512]{4,3,2,1,0:T(2,128)(2,1)}, u32[]{:S(2)}) %copy-start) | copy-done | bytes 1048600
  5.6 0.2 shard_map.55
  5.8 0.1 reshape_transpose.14.rest_2_
  5.9 0.0 copy-start.2
  5.9 2.1 %collective-permute-start.1 = (bf16[1,256,512]{2,1,0:T(8,128)(2,1)S(1)}, bf16[1,256,512]{2,1,0:T(8,128)(2,1)S(1)}, u32[]{:S(2)}, u32[]{:S(2)}) collective-permute-start(bf16[1,256,512]{2,1,0:T(8,128)(2,1)S(1)} %reshape_transpose.14.rest_2_), channel_id=1, source_target_pairs={{0,12},{4,0},{8,4},{12,8},{1,13},{5,1},{9,5},{13,9},{2,14},{6,2},{... | collective-permute-start | bytes 786440 | tf_op jit(solution)/shard_map/ppermute | solution.py:355
  8.0 0.1 reshape_transpose.15.rest_3_
  8.1 1.1 %collective-permute-start.2 = (bf16[1,256,512]{2,1,0:T(8,128)(2,1)S(1)}, bf16[1,256,512]{2,1,0:T(8,128)(2,1)S(1)}, u32[]{:S(2)}, u32[]{:S(2)}) collective-permute-start(bf16[1,256,512]{2,1,0:T(8,128)(2,1)S(1)} %reshape_transpose.15.rest_3_), channel_id=1, source_target_pairs={{0,8},{4,12},{8,0},{12,4},{1,9},{5,13},{9,1},{13,5},{2,10},{6,14},... | collective-permute-start | bytes 786440 | tf_op jit(solution)/shard_map/ppermute | solution.py:355
  9.2 0.1 reshape_transpose.12.rest_0_.refs_0_
  9.3 0.0 copy-done.1
  9.3 1.3 %shard_map.57.weights_ref = bf16[1,512,512]{2,1,0:T(8,128)(2,1)S(1)} custom-call(s32[256,512]{1,0:T(8,128)S(1)} %copy-done.1), custom_call_target="tpu_custom_call" | custom-call | flops 5242880 | bytes 1048576 | tf_op jit(solution)/shard_map/pallas_call | solution.py:370
  10.5 0.0 copy-start.3
  10.6 0.0 copy-start.4
  10.6 6.8 %shard_map.56 = (f32[4,256,128]{2,1,0:T(8,128)S(1)}, f32[4,256,128]{2,1,0:T(8,128)S(1)}) custom-call(s32[256,512]{1,0:T(8,128)S(1)} %copy-done.1, bf16[1,256,512]{2,1,0:T(8,128)(2,1)S(1)} %reshape_transpose.12.rest_0_.refs_0_, bf16[1,256,512]{2,1,0:T(8,128)(2,1)S(1)} %reshape_transpose.13.rest_1_, bf16[1,256,512]{2,1,0:T(8,128)(2,1)S(1)} %reshape_transpose.14.rest_2_, ...), custom_call_target="tpu_custom_call" | custom-call | flops 536870912 | bytes 2097152 | tf_op jit(solution)/shard_map/pallas_call | solution.py:360
  17.4 0.0 collective-permute-done.refs_1_
  17.4 0.9 %collective-permute-done.1.refs_2_ = bf16[1,256,512]{2,1,0:T(8,128)(2,1)S(1)} collective-permute-done((bf16[1,256,512]{2,1,0:T(8,128)(2,1)S(1)}, bf16[1,256,512]{2,1,0:T(8,128)(2,1)S(1)}, u32[]{:S(2)}, u32[]{:S(2)}) %collective-permute-start.1) | collective-permute-done | bytes 262176 | tf_op jit(solution)/shard_map/ppermute | solution.py:355
  18.3 0.0 copy-done.2
  18.3 1.5 %shard_map.58 = (f32[1,2,512,512]{3,2,1,0:T(8,128)S(1)}, f32[1,16,512]{2,1,0:T(8,128)S(1)}, bf16[1,512,768]{2,1,0:T(8,128)(2,1)S(1)}) custom-call(f32[1,4,2,8,512]{4,3,2,1,0:T(8,128)S(1)} %copy-done.2, bf16[1,256,512]{2,1,0:T(8,128)(2,1)S(1)} %reshape_transpose.12.rest_0_.refs_0_, bf16[1,256,512]{2,1,0:T(8,128)(2,1)S(1)} %collective-permute-done.refs_1_, ...), custom_call_target="tpu_custom_call" | custom-call | flops 805306368 | bytes 2097152 | tf_op jit(solution)/shard_map/pallas_call | solution.py:381
  19.8 9.7 %collective-permute-done.2.last_ref = bf16[1,256,512]{2,1,0:T(8,128)(2,1)S(1)} collective-permute-done((bf16[1,256,512]{2,1,0:T(8,128)(2,1)S(1)}, bf16[1,256,512]{2,1,0:T(8,128)(2,1)S(1)}, u32[]{:S(2)}, u32[]{:S(2)}) %collective-permute-start.2) | collective-permute-done | bytes 262176 | tf_op jit(solution)/shard_map/ppermute | solution.py:355
  29.6 0.0 copy-done.3
  29.6 0.0 copy-done.4
  29.6 4.2 %shard_map.59 = (f32[4,256,128]{2,1,0:T(8,128)S(1)}, bf16[1,16,384]{2,1,0:T(8,128)(2,1)S(1)}, bf16[1,16,384]{2,1,0:T(8,128)(2,1)S(1)}, bf16[1,16,384]{2,1,0:T(8,128)(2,1)S(1)}, bf16[1,16,384]{2,1,0:T(8,128)(2,1)S(1)}) custom-call(f32[4,256,128]{2,1,0:T(8,128)S(1)} %get-tuple-element.21.beams_ref, ...), custom_call_target="tpu_custom_call", output_to_operand_aliasing={{0}: (0, {})} | custom-call | flops 134217728 | bytes 2097152 | tf_op jit(solution)/shard_map/pallas_call | solution.py:395
  33.8 0.1 collective-permute-start.3
  33.8 0.1 collective-permute-start.9
  33.9 1.7 %collective-permute-start.7 = (bf16[1,16,384]{2,1,0:T(8,128)(2,1)S(1)}, bf16[1,16,384]{2,1,0:T(8,128)(2,1)S(1)}, u32[]{:S(2)}, u32[]{:S(2)}) collective-permute-start(bf16[1,16,384]{2,1,0:T(8,128)(2,1)S(1)} %get-tuple-element.29), channel_id=1, source_target_pairs={{0,12},{4,8},{8,4},{12,0},{1,13},{5,9},{9,5},{13,1},{2,14},{6,10},... | collective-permute-start | bytes 36872 | tf_op jit(solution)/shard_map/ppermute | solution.py:412
  35.6 1.8 %collective-permute-start.4 = (bf16[1,16,384]{2,1,0:T(8,128)(2,1)S(1)}, bf16[1,16,384]{2,1,0:T(8,128)(2,1)S(1)}, u32[]{:S(2)}, u32[]{:S(2)}) collective-permute-start(bf16[1,16,384]{2,1,0:T(8,128)(2,1)S(1)} %get-tuple-element.26), channel_id=1, source_target_pairs={{0,4},{4,0},{8,12},{12,8},{1,5},{5,1},{9,13},{13,9},{2,6},{6,2},{1... | collective-permute-start | bytes 36872 | tf_op jit(solution)/shard_map/ppermute | solution.py:412
  37.4 0.0 collective-permute-start.6
  37.4 1.2 %collective-permute-done.9.rest_1_ = bf16[1,16,384]{2,1,0:T(8,128)(2,1)S(1)} collective-permute-done((bf16[1,16,384]{2,1,0:T(8,128)(2,1)S(1)}, bf16[1,16,384]{2,1,0:T(8,128)(2,1)S(1)}, u32[]{:S(2)}, u32[]{:S(2)}) %collective-permute-start.9) | collective-permute-done | bytes 12320 | tf_op jit(solution)/shard_map/ppermute | solution.py:412
  38.6 0.0 collective-permute-start.10
  38.6 0.9 %collective-permute-done.7.rest_2_ = bf16[1,16,384]{2,1,0:T(8,128)(2,1)S(1)} collective-permute-done((bf16[1,16,384]{2,1,0:T(8,128)(2,1)S(1)}, bf16[1,16,384]{2,1,0:T(8,128)(2,1)S(1)}, u32[]{:S(2)}, u32[]{:S(2)}) %collective-permute-start.7) | collective-permute-done | bytes 12320 | tf_op jit(solution)/shard_map/ppermute | solution.py:412
  39.5 0.0 collective-permute-start.8
  39.5 0.0 collective-permute-done.4.rest_0_
  39.5 0.5 %collective-permute-start.5 = (bf16[1,16,384]{2,1,0:T(8,128)(2,1)S(1)}, bf16[1,16,384]{2,1,0:T(8,128)(2,1)S(1)}, u32[]{:S(2)}, u32[]{:S(2)}) collective-permute-start(bf16[1,16,384]{2,1,0:T(8,128)(2,1)S(1)} %collective-permute-done.4.rest_0_), channel_id=1, source_target_pairs={{0,1},{1,0},{2,3},{3,2},{4,5},{5,4},{6,7},{7,6},{8,9},{9,8},{10,11... | collective-permute-start | bytes 36872 | tf_op jit(solution)/shard_map/ppermute | solution.py:413
  40.0 0.3 shard_map.60.rest_4_
  40.3 0.0 collective-permute-done.6.rest_1_
  40.3 0.0 collective-permute-done.10.rest_3_
  40.4 0.3 collective-permute-done.8.rest_2_
  40.7 0.0 collective-permute-done.3.theirs_ref
  40.7 0.4 shard_map.61.power_ref
  41.0 0.0 collective-permute-done.5.packet_ref
  41.0 1.1 %shard_map.62 = f32[128,4,128]{2,1,0:T(4,128)} custom-call(f32[4,256,128]{2,1,0:T(8,128)S(1)} %collective-permute-done.3.theirs_ref, bf16[1,16,384]{2,1,0:T(8,128)(2,1)S(1)} %collective-permute-done.5.packet_ref, f32[4,128,128]{2,1,0:T(8,128)S(1)} %shard_map.61.power_ref), custom_call_target="tpu_custom_call" | custom-call | flops 131072 | bytes 786432 | tf_op jit(solution)/shard_map/pallas_call | solution.py:433
Async XLA Ops:
  0.0 9.3 %copy-start.1 = (s32[256,512]{1,0:T(8,128)S(1)}, s32[256,512]{1,0:T(8,128)}, u32[]{:S(2)}) copy-start(s32[256,512]{1,0:T(8,128)} %phase_ref.3) | copy-start | bytes 1572868
  1.3 16.1 %collective-permute-start = (bf16[1,256,512]{2,1,0:T(8,128)(2,1)S(1)}, bf16[1,256,512]{2,1,0:T(8,128)(2,1)S(1)}, u32[]{:S(2)}, u32[]{:S(2)}) collective-permute-start(bf16[1,256,512]{2,1,0:T(8,128)(2,1)S(1)} %reshape_transpose.13.rest_1_), channel_id=1, source_target_pairs={{0,4},{4,8},{8,12},{12,0},{1,5},{5,9},{9,13},{13,1},{2,6},{6,10},{... | collective-permute-start | bytes 786440 | tf_op jit(solution)/shard_map/ppermute | solution.py:355
  4.4 1.2 %copy-start = (bf16[128,1,4,2,512]{4,3,2,1,0:T(2,128)(2,1)S(1)}, bf16[128,1,4,2,512]{4,3,2,1,0:T(2,128)(2,1)}, u32[]{:S(2)}) copy-start(bf16[128,1,4,2,512]{4,3,2,1,0:T(2,128)(2,1)} %voltages_ref.1) | copy-start | bytes 3145732
  5.9 12.4 %copy-start.2 = (f32[1,4,2,8,512]{4,3,2,1,0:T(8,128)S(1)}, f32[1,4,2,8,512]{4,3,2,1,0:T(8,128)}, u32[]{:S(2)}) copy-start(f32[1,4,2,8,512]{4,3,2,1,0:T(8,128)} %start_ref.3) | copy-start | bytes 393220
  5.9 12.4 %collective-permute-start.1 = (bf16[1,256,512]{2,1,0:T(8,128)(2,1)S(1)}, bf16[1,256,512]{2,1,0:T(8,128)(2,1)S(1)}, u32[]{:S(2)}, u32[]{:S(2)}) collective-permute-start(bf16[1,256,512]{2,1,0:T(8,128)(2,1)S(1)} %reshape_transpose.14.rest_2_), channel_id=1, source_target_pairs={{0,12},{4,0},{8,4},{12,8},{1,13},{5,1},{9,5},{13,9},{2,14},{6,2},{... | collective-permute-start | bytes 786440 | tf_op jit(solution)/shard_map/ppermute | solution.py:355
  8.1 21.5 %collective-permute-start.2 = (bf16[1,256,512]{2,1,0:T(8,128)(2,1)S(1)}, bf16[1,256,512]{2,1,0:T(8,128)(2,1)S(1)}, u32[]{:S(2)}, u32[]{:S(2)}) collective-permute-start(bf16[1,256,512]{2,1,0:T(8,128)(2,1)S(1)} %reshape_transpose.15.rest_3_), channel_id=1, source_target_pairs={{0,8},{4,12},{8,0},{12,4},{1,9},{5,13},{9,1},{13,5},{2,10},{6,14},... | collective-permute-start | bytes 786440 | tf_op jit(solution)/shard_map/ppermute | solution.py:355
  10.5 19.0 %copy-start.3 = (s32[4]{0:T(128)S(1)}, s32[4]{0:T(128)}, u32[]{:S(2)}) copy-start(s32[4]{0:T(128)} %flags_ref.1) | copy-start | bytes 52
  10.6 19.0 %copy-start.4 = (s32[4]{0:T(128)S(1)}, s32[4]{0:T(128)}, u32[]{:S(2)}) copy-start(s32[4]{0:T(128)} %ranks_ref.1) | copy-start | bytes 52
  33.8 6.9 %collective-permute-start.3 = (f32[4,256,128]{2,1,0:T(8,128)S(1)}, f32[4,256,128]{2,1,0:T(8,128)S(1)}, u32[]{:S(2)}, u32[]{:S(2)}) collective-permute-start(f32[4,256,128]{2,1,0:T(8,128)S(1)} %get-tuple-element.25), channel_id=1, source_target_pairs={{0,1},{1,0},{2,3},{3,2},{4,5},{5,4},{6,7},{7,6},{8,9},{9,8},{10,11... | collective-permute-start | bytes 1572872 | tf_op jit(solution)/shard_map/ppermute | solution.py:408
  33.8 4.7 %collective-permute-start.9 = (bf16[1,16,384]{2,1,0:T(8,128)(2,1)S(1)}, bf16[1,16,384]{2,1,0:T(8,128)(2,1)S(1)}, u32[]{:S(2)}, u32[]{:S(2)}) collective-permute-start(bf16[1,16,384]{2,1,0:T(8,128)(2,1)S(1)} %get-tuple-element.30), channel_id=1, source_target_pairs={{0,8},{4,12},{8,0},{12,4},{1,9},{5,13},{9,1},{13,5},{2,10},{6,14},... | collective-permute-start | bytes 36872 | tf_op jit(solution)/shard_map/ppermute | solution.py:412
  33.9 5.6 %collective-permute-start.7 = (bf16[1,16,384]{2,1,0:T(8,128)(2,1)S(1)}, bf16[1,16,384]{2,1,0:T(8,128)(2,1)S(1)}, u32[]{:S(2)}, u32[]{:S(2)}) collective-permute-start(bf16[1,16,384]{2,1,0:T(8,128)(2,1)S(1)} %get-tuple-element.29), channel_id=1, source_target_pairs={{0,12},{4,8},{8,4},{12,0},{1,13},{5,9},{9,5},{13,1},{2,14},{6,10},... | collective-permute-start | bytes 36872 | tf_op jit(solution)/shard_map/ppermute | solution.py:412
  35.6 3.9 %collective-permute-start.4 = (bf16[1,16,384]{2,1,0:T(8,128)(2,1)S(1)}, bf16[1,16,384]{2,1,0:T(8,128)(2,1)S(1)}, u32[]{:S(2)}, u32[]{:S(2)}) collective-permute-start(bf16[1,16,384]{2,1,0:T(8,128)(2,1)S(1)} %get-tuple-element.26), channel_id=1, source_target_pairs={{0,4},{4,0},{8,12},{12,8},{1,5},{5,1},{9,13},{13,9},{2,6},{6,2},{1... | collective-permute-start | bytes 36872 | tf_op jit(solution)/shard_map/ppermute | solution.py:412
  37.4 2.9 %collective-permute-start.6 = (bf16[1,16,384]{2,1,0:T(8,128)(2,1)S(1)}, bf16[1,16,384]{2,1,0:T(8,128)(2,1)S(1)}, u32[]{:S(2)}, u32[]{:S(2)}) collective-permute-start(bf16[1,16,384]{2,1,0:T(8,128)(2,1)S(1)} %get-tuple-element.28.rest_0_), channel_id=1, source_target_pairs={{0,1},{1,0},{2,3},{3,2},{4,5},{5,4},{6,7},{7,6},{8,9},{9,8},{10,11... | collective-permute-start | bytes 36872 | tf_op jit(solution)/shard_map/ppermute | solution.py:413
  38.6 1.8 %collective-permute-start.10 = (bf16[1,16,384]{2,1,0:T(8,128)(2,1)S(1)}, bf16[1,16,384]{2,1,0:T(8,128)(2,1)S(1)}, u32[]{:S(2)}, u32[]{:S(2)}) collective-permute-start(bf16[1,16,384]{2,1,0:T(8,128)(2,1)S(1)} %collective-permute-done.9.rest_1_), channel_id=1, source_target_pairs={{0,1},{1,0},{2,3},{3,2},{4,5},{5,4},{6,7},{7,6},{8,9},{9,8},{10,11... | collective-permute-start | bytes 36872 | tf_op jit(solution)/shard_map/ppermute | solution.py:413
  39.5 1.2 %collective-permute-start.8 = (bf16[1,16,384]{2,1,0:T(8,128)(2,1)S(1)}, bf16[1,16,384]{2,1,0:T(8,128)(2,1)S(1)}, u32[]{:S(2)}, u32[]{:S(2)}) collective-permute-start(bf16[1,16,384]{2,1,0:T(8,128)(2,1)S(1)} %collective-permute-done.7.rest_2_), channel_id=1, source_target_pairs={{0,1},{1,0},{2,3},{3,2},{4,5},{5,4},{6,7},{7,6},{8,9},{9,8},{10,11... | collective-permute-start | bytes 36872 | tf_op jit(solution)/shard_map/ppermute | solution.py:413
  39.5 1.5 %collective-permute-start.5 = (bf16[1,16,384]{2,1,0:T(8,128)(2,1)S(1)}, bf16[1,16,384]{2,1,0:T(8,128)(2,1)S(1)}, u32[]{:S(2)}, u32[]{:S(2)}) collective-permute-start(bf16[1,16,384]{2,1,0:T(8,128)(2,1)S(1)} %collective-permute-done.4.rest_0_), channel_id=1, source_target_pairs={{0,1},{1,0},{2,3},{3,2},{4,5},{5,4},{6,7},{7,6},{8,9},{9,8},{10,11... | collective-permute-start | bytes 36872 | tf_op jit(solution)/shard_map/ppermute | solution.py:413

commit v17 on v16

--- a/solution.py
+++ b/solution.py
@@ -317,8 +317,9 @@
     for o in range(own):
         chan = (lax.axis_index("tm") ^ x) * own + o
         powers[chan] = power_ref[chan] + nulled_power(theirs_ref[chan], packet_ref.at[o], squares)
-    for chan in range(powers.shape[0]):
-        out_ref[:, chan, :] = powers[chan]
+    channels, samples = powers.shape[:2]
+    for chan in range(channels):
+        out_ref[pl.ds(chan, samples, channels), :] = powers[chan]
 
 
 def local(voltages, start_block, flags, ranks, phase_index):
@@ -430,15 +431,16 @@
             )(mine, theirs if later_xs else mine, *used, *power)
         ]
 
-    return pl.pallas_call(
+    rows_out = pl.pallas_call(
         functools.partial(last_kernel, own, order[-1]),
-        out_shape=jax.ShapeDtypeStruct((samples, chan_dev, half), F32),
+        out_shape=jax.ShapeDtypeStruct((samples * chan_dev, half), F32),
         in_specs=[whole] * 3,
         out_specs=whole,
         scratch_shapes=[pltpu.VMEM((chan_dev, samples, half), F32), pltpu.VMEM((rows, half), F32)],
         compiler_params=params,
         cost_estimate=cost(chan_dev * samples * half, 12 * chan_dev * samples * half),
     )(theirs, swapped[order[-1]], *power)
+    return rows_out.reshape(samples, chan_dev, half)
 
 
 def solution(mesh):

time: 42.3 us -> 42.2 us (level)
  no operation moved by 1% of the time
where the time goes in v17:
time: 42.2 us; the launch traced here: 42.1 us
  Pallas kernels  15.7 us (37%)
  waiting for transfers between devices  13 us (31%)
  starting transfers between devices  10.4 us (25%)
  local copies, waits for them, and re-layouts  2.85 us (7%)
    ppermute x3, waiting for transfers between devices, local(): lax.ppermute(piece, 'tm', [(z, (z + by) % tm) for z in range(tm)])  10.6 us
    pallas_call x1, Pallas kernels, local(): pl.pallas_call(functools.partial(raw_beams_kernel, tm, own), out_shape=[r...  6.85 us
    ppermute x3, starting transfers between devices, local(): lax.ppermute(piece, 'tm', [(z, (z + by) % tm) for z in range(tm)])  6.23 us
    pallas_call x1, Pallas kernels, local(): pl.pallas_call(functools.partial(subspace_kernel, tm, own, factor), out_s...  4.19 us
    ppermute x3, starting transfers between devices, local(): arrived[x] = lax.ppermute(packets[x], 'tm', [(z, z ^ x) for z in range(tm)])  3.54 us
    ppermute x3, waiting for transfers between devices, local(): arrived[x] = lax.ppermute(packets[x], 'tm', [(z, z ^ x) for z in range(tm)])  2.08 us
    pallas_call x1, Pallas kernels, local(): pl.pallas_call(early_kernel, out_shape=[jax.ShapeDtypeStruct((own, 2, wid...  1.51 us
    pallas_call x1, Pallas kernels, local(): pl.pallas_call(functools.partial(own_weights_kernel, own, chan_dev), out_...  1.26 us
  transfers between devices with their start and end apart: 11, of which 5 were waited for; matrix products, arithmetic and copies ran while one was open for 1% of the time, Pallas kernels for 25%

profile of v17, /device:TPU:0, one launch (start us, length us, event | category | flops | bytes accessed | tf_op | source)
XLA Modules:
  0.0 42.1 jit_solution(18146902756144206372)
XLA Ops:
  0.0 0.0 copy-start.1
  0.0 1.2 %constant_dynamic-slice_fusion = bf16[128,1,1,2,512]{4,3,2,1,0:T(2,128)(2,1)S(1)} fusion(bf16[128,1,4,2,512]{4,3,2,1,0:T(2,128)(2,1)} %voltages_ref.1, s32[]{:T(128)S(6)} %select_n.3), kind=kLoop, calls=%fused_computation | loop fusion | bytes 524292 | tf_op jit(solution)/shard_map/dynamic_slice | solution.py:352
  1.2 0.1 reshape_transpose.13.rest_1_
  1.3 3.1 %collective-permute-start = (bf16[1,256,512]{2,1,0:T(8,128)(2,1)S(1)}, bf16[1,256,512]{2,1,0:T(8,128)(2,1)S(1)}, u32[]{:S(2)}, u32[]{:S(2)}) collective-permute-start(bf16[1,256,512]{2,1,0:T(8,128)(2,1)S(1)} %reshape_transpose.13.rest_1_), channel_id=1, source_target_pairs={{0,4},{4,8},{8,12},{12,0},{1,5},{5,9},{9,13},{13,1},{2,6},{6,10},{... | collective-permute-start | bytes 786440 | tf_op jit(solution)/shard_map/ppermute | solution.py:356
  4.4 0.0 copy-start
  4.4 1.2 %copy-done = bf16[128,1,4,2,512]{4,3,2,1,0:T(2,128)(2,1)S(1)} copy-done((bf16[128,1,4,2,512]{4,3,2,1,0:T(2,128)(2,1)S(1)}, bf16[128,1,4,2,512]{4,3,2,1,0:T(2,128)(2,1)}, u32[]{:S(2)}) %copy-start) | copy-done | bytes 1048600
  5.6 0.2 shard_map.55
  5.8 0.1 reshape_transpose.14.rest_2_
  5.9 0.0 copy-start.2
  5.9 2.1 %collective-permute-start.1 = (bf16[1,256,512]{2,1,0:T(8,128)(2,1)S(1)}, bf16[1,256,512]{2,1,0:T(8,128)(2,1)S(1)}, u32[]{:S(2)}, u32[]{:S(2)}) collective-permute-start(bf16[1,256,512]{2,1,0:T(8,128)(2,1)S(1)} %reshape_transpose.14.rest_2_), channel_id=1, source_target_pairs={{0,12},{4,0},{8,4},{12,8},{1,13},{5,1},{9,5},{13,9},{2,14},{6,2},{... | collective-permute-start | bytes 786440 | tf_op jit(solution)/shard_map/ppermute | solution.py:356
  8.0 0.1 reshape_transpose.15.rest_3_
  8.1 1.1 %collective-permute-start.2 = (bf16[1,256,512]{2,1,0:T(8,128)(2,1)S(1)}, bf16[1,256,512]{2,1,0:T(8,128)(2,1)S(1)}, u32[]{:S(2)}, u32[]{:S(2)}) collective-permute-start(bf16[1,256,512]{2,1,0:T(8,128)(2,1)S(1)} %reshape_transpose.15.rest_3_), channel_id=1, source_target_pairs={{0,8},{4,12},{8,0},{12,4},{1,9},{5,13},{9,1},{13,5},{2,10},{6,14},... | collective-permute-start | bytes 786440 | tf_op jit(solution)/shard_map/ppermute | solution.py:356
  9.2 0.1 reshape_transpose.12.rest_0_.refs_0_
  9.3 0.0 copy-done.1
  9.3 1.3 %shard_map.57.weights_ref = bf16[1,512,512]{2,1,0:T(8,128)(2,1)S(1)} custom-call(s32[256,512]{1,0:T(8,128)S(1)} %copy-done.1), custom_call_target="tpu_custom_call" | custom-call | flops 5242880 | bytes 1048576 | tf_op jit(solution)/shard_map/pallas_call | solution.py:371
  10.5 0.0 copy-start.3
  10.6 0.0 copy-start.4
  10.6 6.8 %shard_map.56 = (f32[4,256,128]{2,1,0:T(8,128)S(1)}, f32[4,256,128]{2,1,0:T(8,128)S(1)}) custom-call(s32[256,512]{1,0:T(8,128)S(1)} %copy-done.1, bf16[1,256,512]{2,1,0:T(8,128)(2,1)S(1)} %reshape_transpose.12.rest_0_.refs_0_, bf16[1,256,512]{2,1,0:T(8,128)(2,1)S(1)} %reshape_transpose.13.rest_1_, bf16[1,256,512]{2,1,0:T(8,128)(2,1)S(1)} %reshape_transpose.14.rest_2_, ...), custom_call_target="tpu_custom_call" | custom-call | flops 536870912 | bytes 2097152 | tf_op jit(solution)/shard_map/pallas_call | solution.py:361
  17.4 0.0 collective-permute-done.refs_1_
  17.4 0.9 %collective-permute-done.1.refs_2_ = bf16[1,256,512]{2,1,0:T(8,128)(2,1)S(1)} collective-permute-done((bf16[1,256,512]{2,1,0:T(8,128)(2,1)S(1)}, bf16[1,256,512]{2,1,0:T(8,128)(2,1)S(1)}, u32[]{:S(2)}, u32[]{:S(2)}) %collective-permute-start.1) | collective-permute-done | bytes 262176 | tf_op jit(solution)/shard_map/ppermute | solution.py:356
  18.3 0.0 copy-done.2
  18.3 1.5 %shard_map.58 = (f32[1,2,512,512]{3,2,1,0:T(8,128)S(1)}, f32[1,16,512]{2,1,0:T(8,128)S(1)}, bf16[1,512,768]{2,1,0:T(8,128)(2,1)S(1)}) custom-call(f32[1,4,2,8,512]{4,3,2,1,0:T(8,128)S(1)} %copy-done.2, bf16[1,256,512]{2,1,0:T(8,128)(2,1)S(1)} %reshape_transpose.12.rest_0_.refs_0_, bf16[1,256,512]{2,1,0:T(8,128)(2,1)S(1)} %collective-permute-done.refs_1_, ...), custom_call_target="tpu_custom_call" | custom-call | flops 805306368 | bytes 2097152 | tf_op jit(solution)/shard_map/pallas_call | solution.py:382
  19.8 9.7 %collective-permute-done.2.last_ref = bf16[1,256,512]{2,1,0:T(8,128)(2,1)S(1)} collective-permute-done((bf16[1,256,512]{2,1,0:T(8,128)(2,1)S(1)}, bf16[1,256,512]{2,1,0:T(8,128)(2,1)S(1)}, u32[]{:S(2)}, u32[]{:S(2)}) %collective-permute-start.2) | collective-permute-done | bytes 262176 | tf_op jit(solution)/shard_map/ppermute | solution.py:356
  29.6 0.0 copy-done.3
  29.6 0.0 copy-done.4
  29.6 4.2 %shard_map.59 = (f32[4,256,128]{2,1,0:T(8,128)S(1)}, bf16[1,16,384]{2,1,0:T(8,128)(2,1)S(1)}, bf16[1,16,384]{2,1,0:T(8,128)(2,1)S(1)}, bf16[1,16,384]{2,1,0:T(8,128)(2,1)S(1)}, bf16[1,16,384]{2,1,0:T(8,128)(2,1)S(1)}) custom-call(f32[4,256,128]{2,1,0:T(8,128)S(1)} %get-tuple-element.21.beams_ref, ...), custom_call_target="tpu_custom_call", output_to_operand_aliasing={{0}: (0, {})} | custom-call | flops 134217728 | bytes 2097152 | tf_op jit(solution)/shard_map/pallas_call | solution.py:396
  33.8 0.1 collective-permute-start.3
  33.8 0.1 collective-permute-start.9
  33.9 1.7 %collective-permute-start.7 = (bf16[1,16,384]{2,1,0:T(8,128)(2,1)S(1)}, bf16[1,16,384]{2,1,0:T(8,128)(2,1)S(1)}, u32[]{:S(2)}, u32[]{:S(2)}) collective-permute-start(bf16[1,16,384]{2,1,0:T(8,128)(2,1)S(1)} %get-tuple-element.29), channel_id=1, source_target_pairs={{0,12},{4,8},{8,4},{12,0},{1,13},{5,9},{9,5},{13,1},{2,14},{6,10},... | collective-permute-start | bytes 36872 | tf_op jit(solution)/shard_map/ppermute | solution.py:413
  35.6 1.8 %collective-permute-start.4 = (bf16[1,16,384]{2,1,0:T(8,128)(2,1)S(1)}, bf16[1,16,384]{2,1,0:T(8,128)(2,1)S(1)}, u32[]{:S(2)}, u32[]{:S(2)}) collective-permute-start(bf16[1,16,384]{2,1,0:T(8,128)(2,1)S(1)} %get-tuple-element.26), channel_id=1, source_target_pairs={{0,4},{4,0},{8,12},{12,8},{1,5},{5,1},{9,13},{13,9},{2,6},{6,2},{1... | collective-permute-start | bytes 36872 | tf_op jit(solution)/shard_map/ppermute | solution.py:413
  37.4 0.0 collective-permute-start.6
  37.4 1.2 %collective-permute-done.9.rest_1_ = bf16[1,16,384]{2,1,0:T(8,128)(2,1)S(1)} collective-permute-done((bf16[1,16,384]{2,1,0:T(8,128)(2,1)S(1)}, bf16[1,16,384]{2,1,0:T(8,128)(2,1)S(1)}, u32[]{:S(2)}, u32[]{:S(2)}) %collective-permute-start.9) | collective-permute-done | bytes 12320 | tf_op jit(solution)/shard_map/ppermute | solution.py:413
  38.6 0.0 collective-permute-start.10
  38.6 0.9 %collective-permute-done.7.rest_2_ = bf16[1,16,384]{2,1,0:T(8,128)(2,1)S(1)} collective-permute-done((bf16[1,16,384]{2,1,0:T(8,128)(2,1)S(1)}, bf16[1,16,384]{2,1,0:T(8,128)(2,1)S(1)}, u32[]{:S(2)}, u32[]{:S(2)}) %collective-permute-start.7) | collective-permute-done | bytes 12320 | tf_op jit(solution)/shard_map/ppermute | solution.py:413
  39.5 0.0 collective-permute-start.8
  39.5 0.0 collective-permute-done.4.rest_0_
  39.5 0.5 %collective-permute-start.5 = (bf16[1,16,384]{2,1,0:T(8,128)(2,1)S(1)}, bf16[1,16,384]{2,1,0:T(8,128)(2,1)S(1)}, u32[]{:S(2)}, u32[]{:S(2)}) collective-permute-start(bf16[1,16,384]{2,1,0:T(8,128)(2,1)S(1)} %collective-permute-done.4.rest_0_), channel_id=1, source_target_pairs={{0,1},{1,0},{2,3},{3,2},{4,5},{5,4},{6,7},{7,6},{8,9},{9,8},{10,11... | collective-permute-start | bytes 36872 | tf_op jit(solution)/shard_map/ppermute | solution.py:414
  40.0 0.3 shard_map.60.rest_4_
  40.3 0.0 collective-permute-done.6.rest_1_
  40.3 0.0 collective-permute-done.10.rest_3_
  40.4 0.3 collective-permute-done.8.rest_2_
  40.7 0.0 collective-permute-done.3.theirs_ref
  40.7 0.4 shard_map.61.power_ref
  41.0 0.0 collective-permute-done.5.packet_ref
  41.0 1.0 %shard_map.62 = f32[512,128]{1,0:T(8,128)} custom-call(f32[4,256,128]{2,1,0:T(8,128)S(1)} %collective-permute-done.3.theirs_ref, bf16[1,16,384]{2,1,0:T(8,128)(2,1)S(1)} %collective-permute-done.5.packet_ref, f32[4,128,128]{2,1,0:T(8,128)S(1)} %shard_map.61.power_ref), custom_call_target="tpu_custom_call" | custom-call | flops 131072 | bytes 786432 | tf_op jit(solution)/shard_map/pallas_call | solution.py:434
Async XLA Ops:
  0.0 9.3 %copy-start.1 = (s32[256,512]{1,0:T(8,128)S(1)}, s32[256,512]{1,0:T(8,128)}, u32[]{:S(2)}) copy-start(s32[256,512]{1,0:T(8,128)} %phase_ref.3) | copy-start | bytes 1572868
  1.3 16.1 %collective-permute-start = (bf16[1,256,512]{2,1,0:T(8,128)(2,1)S(1)}, bf16[1,256,512]{2,1,0:T(8,128)(2,1)S(1)}, u32[]{:S(2)}, u32[]{:S(2)}) collective-permute-start(bf16[1,256,512]{2,1,0:T(8,128)(2,1)S(1)} %reshape_transpose.13.rest_1_), channel_id=1, source_target_pairs={{0,4},{4,8},{8,12},{12,0},{1,5},{5,9},{9,13},{13,1},{2,6},{6,10},{... | collective-permute-start | bytes 786440 | tf_op jit(solution)/shard_map/ppermute | solution.py:356
  4.4 1.2 %copy-start = (bf16[128,1,4,2,512]{4,3,2,1,0:T(2,128)(2,1)S(1)}, bf16[128,1,4,2,512]{4,3,2,1,0:T(2,128)(2,1)}, u32[]{:S(2)}) copy-start(bf16[128,1,4,2,512]{4,3,2,1,0:T(2,128)(2,1)} %voltages_ref.1) | copy-start | bytes 3145732
  5.9 12.4 %copy-start.2 = (f32[1,4,2,8,512]{4,3,2,1,0:T(8,128)S(1)}, f32[1,4,2,8,512]{4,3,2,1,0:T(8,128)}, u32[]{:S(2)}) copy-start(f32[1,4,2,8,512]{4,3,2,1,0:T(8,128)} %start_ref.3) | copy-start | bytes 393220
  5.9 12.4 %collective-permute-start.1 = (bf16[1,256,512]{2,1,0:T(8,128)(2,1)S(1)}, bf16[1,256,512]{2,1,0:T(8,128)(2,1)S(1)}, u32[]{:S(2)}, u32[]{:S(2)}) collective-permute-start(bf16[1,256,512]{2,1,0:T(8,128)(2,1)S(1)} %reshape_transpose.14.rest_2_), channel_id=1, source_target_pairs={{0,12},{4,0},{8,4},{12,8},{1,13},{5,1},{9,5},{13,9},{2,14},{6,2},{... | collective-permute-start | bytes 786440 | tf_op jit(solution)/shard_map/ppermute | solution.py:356
  8.1 21.5 %collective-permute-start.2 = (bf16[1,256,512]{2,1,0:T(8,128)(2,1)S(1)}, bf16[1,256,512]{2,1,0:T(8,128)(2,1)S(1)}, u32[]{:S(2)}, u32[]{:S(2)}) collective-permute-start(bf16[1,256,512]{2,1,0:T(8,128)(2,1)S(1)} %reshape_transpose.15.rest_3_), channel_id=1, source_target_pairs={{0,8},{4,12},{8,0},{12,4},{1,9},{5,13},{9,1},{13,5},{2,10},{6,14},... | collective-permute-start | bytes 786440 | tf_op jit(solution)/shard_map/ppermute | solution.py:356
  10.5 19.0 %copy-start.3 = (s32[4]{0:T(128)S(1)}, s32[4]{0:T(128)}, u32[]{:S(2)}) copy-start(s32[4]{0:T(128)} %flags_ref.1) | copy-start | bytes 52
  10.6 19.0 %copy-start.4 = (s32[4]{0:T(128)S(1)}, s32[4]{0:T(128)}, u32[]{:S(2)}) copy-start(s32[4]{0:T(128)} %ranks_ref.1) | copy-start | bytes 52
  33.8 6.9 %collective-permute-start.3 = (f32[4,256,128]{2,1,0:T(8,128)S(1)}, f32[4,256,128]{2,1,0:T(8,128)S(1)}, u32[]{:S(2)}, u32[]{:S(2)}) collective-permute-start(f32[4,256,128]{2,1,0:T(8,128)S(1)} %get-tuple-element.25), channel_id=1, source_target_pairs={{0,1},{1,0},{2,3},{3,2},{4,5},{5,4},{6,7},{7,6},{8,9},{9,8},{10,11... | collective-permute-start | bytes 1572872 | tf_op jit(solution)/shard_map/ppermute | solution.py:409
  33.8 4.7 %collective-permute-start.9 = (bf16[1,16,384]{2,1,0:T(8,128)(2,1)S(1)}, bf16[1,16,384]{2,1,0:T(8,128)(2,1)S(1)}, u32[]{:S(2)}, u32[]{:S(2)}) collective-permute-start(bf16[1,16,384]{2,1,0:T(8,128)(2,1)S(1)} %get-tuple-element.30), channel_id=1, source_target_pairs={{0,8},{4,12},{8,0},{12,4},{1,9},{5,13},{9,1},{13,5},{2,10},{6,14},... | collective-permute-start | bytes 36872 | tf_op jit(solution)/shard_map/ppermute | solution.py:413
  33.9 5.6 %collective-permute-start.7 = (bf16[1,16,384]{2,1,0:T(8,128)(2,1)S(1)}, bf16[1,16,384]{2,1,0:T(8,128)(2,1)S(1)}, u32[]{:S(2)}, u32[]{:S(2)}) collective-permute-start(bf16[1,16,384]{2,1,0:T(8,128)(2,1)S(1)} %get-tuple-element.29), channel_id=1, source_target_pairs={{0,12},{4,8},{8,4},{12,0},{1,13},{5,9},{9,5},{13,1},{2,14},{6,10},... | collective-permute-start | bytes 36872 | tf_op jit(solution)/shard_map/ppermute | solution.py:413
  35.6 3.9 %collective-permute-start.4 = (bf16[1,16,384]{2,1,0:T(8,128)(2,1)S(1)}, bf16[1,16,384]{2,1,0:T(8,128)(2,1)S(1)}, u32[]{:S(2)}, u32[]{:S(2)}) collective-permute-start(bf16[1,16,384]{2,1,0:T(8,128)(2,1)S(1)} %get-tuple-element.26), channel_id=1, source_target_pairs={{0,4},{4,0},{8,12},{12,8},{1,5},{5,1},{9,13},{13,9},{2,6},{6,2},{1... | collective-permute-start | bytes 36872 | tf_op jit(solution)/shard_map/ppermute | solution.py:413
  37.4 2.9 %collective-permute-start.6 = (bf16[1,16,384]{2,1,0:T(8,128)(2,1)S(1)}, bf16[1,16,384]{2,1,0:T(8,128)(2,1)S(1)}, u32[]{:S(2)}, u32[]{:S(2)}) collective-permute-start(bf16[1,16,384]{2,1,0:T(8,128)(2,1)S(1)} %get-tuple-element.28.rest_0_), channel_id=1, source_target_pairs={{0,1},{1,0},{2,3},{3,2},{4,5},{5,4},{6,7},{7,6},{8,9},{9,8},{10,11... | collective-permute-start | bytes 36872 | tf_op jit(solution)/shard_map/ppermute | solution.py:414
  38.6 1.8 %collective-permute-start.10 = (bf16[1,16,384]{2,1,0:T(8,128)(2,1)S(1)}, bf16[1,16,384]{2,1,0:T(8,128)(2,1)S(1)}, u32[]{:S(2)}, u32[]{:S(2)}) collective-permute-start(bf16[1,16,384]{2,1,0:T(8,128)(2,1)S(1)} %collective-permute-done.9.rest_1_), channel_id=1, source_target_pairs={{0,1},{1,0},{2,3},{3,2},{4,5},{5,4},{6,7},{7,6},{8,9},{9,8},{10,11... | collective-permute-start | bytes 36872 | tf_op jit(solution)/shard_map/ppermute | solution.py:414
  39.5 1.2 %collective-permute-start.8 = (bf16[1,16,384]{2,1,0:T(8,128)(2,1)S(1)}, bf16[1,16,384]{2,1,0:T(8,128)(2,1)S(1)}, u32[]{:S(2)}, u32[]{:S(2)}) collective-permute-start(bf16[1,16,384]{2,1,0:T(8,128)(2,1)S(1)} %collective-permute-done.7.rest_2_), channel_id=1, source_target_pairs={{0,1},{1,0},{2,3},{3,2},{4,5},{5,4},{6,7},{7,6},{8,9},{9,8},{10,11... | collective-permute-start | bytes 36872 | tf_op jit(solution)/shard_map/ppermute | solution.py:414
  39.5 1.5 %collective-permute-start.5 = (bf16[1,16,384]{2,1,0:T(8,128)(2,1)S(1)}, bf16[1,16,384]{2,1,0:T(8,128)(2,1)S(1)}, u32[]{:S(2)}, u32[]{:S(2)}) collective-permute-start(bf16[1,16,384]{2,1,0:T(8,128)(2,1)S(1)} %collective-permute-done.4.rest_0_), channel_id=1, source_target_pairs={{0,1},{1,0},{2,3},{3,2},{4,5},{5,4},{6,7},{7,6},{8,9},{9,8},{10,11... | collective-permute-start | bytes 36872 | tf_op jit(solution)/shard_map/ppermute | solution.py:414

commit v18 on v17

--- a/solution.py
+++ b/solution.py
@@ -63,17 +63,23 @@
     return [0, *[by for by in range(1, tm) if by != tm // 2], tm // 2]
 
 
+def parts(tm):
+    far = steps(tm)[1:]
+    return [(0, None)] + [(by, at) for at in range(2) for by in far]
+
+
 def shifted(by):
     tm = lax.axis_size("tm")
     return lax.rem(lax.axis_index("tm") + tm + by, tm)
 
 
-def cut_kernel(own, bys, voltages_ref, *rest):
+def cut_kernel(own, wanted, voltages_ref, *rest):
     pieces, done = rest[:-1], rest[-1]
     copies = []
-    for i, (by, piece) in enumerate(zip(bys, pieces)):
+    for i, ((by, at), piece) in enumerate(zip(wanted, pieces)):
+        times = pl.ds((at or 0) * piece.shape[0], piece.shape[0])
         channels = pl.ds(shifted(by) * own, own)
-        copy = pltpu.make_async_copy(voltages_ref.at[:, 0, channels], piece, done.at[i])
+        copy = pltpu.make_async_copy(voltages_ref.at[times, 0, channels], piece, done.at[i])
         copy.start()
         copies.append(copy)
     for copy in copies:
@@ -89,20 +95,22 @@
 
 
 def raw_beams_kernel(tm, own, phase_ref, *rest):
-    pieces, (mine_ref, other_ref, weights) = rest[:tm], rest[tm:]
+    pieces, (mine_ref, other_ref, weights) = dict(zip(parts(tm), rest[:-3])), rest[-3:]
     half = phase_ref.shape[0] // 2
-    rows = pieces[0].shape[1]
     pol = lax.axis_index("pol")
     start = lax.axis_index("chan") * tm * own
-    for by, piece in zip(steps(tm), pieces):
+    for by in steps(tm):
         for o in range(own):
             chan = shifted(by) * own + o
             for swap, out_ref in enumerate((mine_ref, other_ref)):
                 first = pl.multiple_of((pol ^ swap) * half, half)
                 fill_weights(phase_ref, first, half, start + chan + 1, weights)
-                product = dot(piece[o], weights[...], NT)
-                by_imag = turned(product[:, half:].reshape(rows // 8, 8, half), 1).reshape(rows, half)
-                out_ref[chan] = product[:, :half] - by_imag
+                for at in (0, 1) if by else (None,):
+                    piece = pieces[by, at]
+                    rows = piece.shape[1]
+                    product = dot(piece[o], weights[...], NT)
+                    by_imag = turned(product[:, half:].reshape(rows // 8, 8, half), 1).reshape(rows, half)
+                    out_ref[chan, (at or 0) * rows : (at or 0) * rows + rows] = product[:, :half] - by_imag
 
 
 def own_weights_kernel(own, chan_dev, phase_ref, out_ref, weights):
@@ -119,15 +127,16 @@
 
 def early_kernel(start_ref, *refs):
     blocks, (cov_ref, first_ref, across_ref, along_ref, rotated_ref) = refs[:-5], refs[-5:]
-    rows, width = blocks[0].shape[1:]
     own = cov_ref.shape[0]
     for o in range(own):
-        for i, block in enumerate(blocks):
+        first = 0
+        for block in blocks:
             x = block[o]
-            at = slice(i * rows, (i + 1) * rows)
+            at = slice(first, first + x.shape[0])
             along_ref[at] = x
             rotated_ref[at] = rotate(x)
             across_ref[o, :, at] = x.T
+            first += x.shape[0]
         cov_ref[o, 0] = dot(across_ref[o], along_ref[...], NN)
         cov_ref[o, 1] = dot(across_ref[o], rotated_ref[...], NN)
         chan = lax.axis_index("tm") * own + o
@@ -236,7 +245,7 @@
 ):
     outs, (high_ref, low_ref, series_ref) = rest[1 : tm + 1], rest[tm + 1 :]
     vectors, width = start_ref.shape[3], start_ref.shape[4]
-    rows = last_ref.shape[1]
+    rows = last_ref.shape[1] * 2
     tm_index = lax.axis_index("tm")
     beams = weights_ref.shape[2] // 2
     for o in range(own):
@@ -275,8 +284,14 @@
         keep = lax.broadcasted_iota(jnp.int32, (vectors, 1), 0) < rank
         real_w = jnp.where(keep, real_w, 0.0)
         imag_w = jnp.where(keep, imag_w, 0.0)
-        series = [early[:, i * rows : (i + 1) * rows] for i in range(tm - 1)] + [late]
-        for by, values in zip(steps(tm), series):
+        found, first = {}, 0
+        for part in parts(tm)[:-1]:
+            length = rows if part[1] is None else rows // 2
+            found[part] = early[:, first : first + length]
+            first += length
+        found[parts(tm)[-1]] = late
+        for by in steps(tm):
+            values = jnp.concatenate([found[by, 0], found[by, 1]], axis=1) if by else found[0, None]
             series_ref[tm_index ^ shifted(-by)] = jnp.where(keep, values, 0.0)
         steered = jnp.concatenate([real_w, imag_w], axis=0).astype(BF16)
         for x, out in enumerate(outs):
@@ -340,28 +355,36 @@
     def cost(multiplies, moved):
         return pl.CostEstimate(flops=2 * multiplies, bytes_accessed=moved, transcendentals=0)
 
-    by = steps(tm)
+    wanted = parts(tm)
+    first_by = wanted[1][0]
+    urgent = lax.dynamic_slice(
+        voltages, (0, 0, shifted(first_by) * own, 0, 0), (samples // 2, 1, own, 2, width)
+    )[:, 0]
     later = pl.pallas_call(
-        functools.partial(cut_kernel, own, [by[0], *by[2:]]),
-        out_shape=[jax.ShapeDtypeStruct((samples, own, 2, width), BF16)] * (tm - 1),
+        functools.partial(cut_kernel, own, wanted[:1] + wanted[2:]),
+        out_shape=[
+            jax.ShapeDtypeStruct((samples if at is None else samples // 2, own, 2, width), BF16)
+            for by, at in wanted[:1] + wanted[2:]
+        ],
         in_specs=[pl.BlockSpec(memory_space=pltpu.HBM)],
-        out_specs=[whole] * (tm - 1),
-        scratch_shapes=[pltpu.SemaphoreType.DMA((tm - 1,))],
+        out_specs=[whole] * (len(wanted) - 1),
+        scratch_shapes=[pltpu.SemaphoreType.DMA((len(wanted) - 1,))],
         compiler_params=params,
     )(voltages)
-    urgent = lax.dynamic_slice_in_dim(voltages[:, 0], shifted(by[1]) * own, own, 1)
-    cut = [later[0], urgent, *later[1:]]
-    pieces = [piece.transpose(1, 0, 2, 3).reshape(own, rows, width) for piece in cut]
+    pieces = [
+        piece.transpose(1, 0, 2, 3).reshape(own, 2 * piece.shape[0], width)
+        for piece in (later[0], urgent, *later[1:])
+    ]
     blocks = pieces[:1] + [
         lax.ppermute(piece, "tm", [(z, (z + by) % tm) for z in range(tm)])
-        for by, piece in zip(steps(tm)[1:], pieces[1:])
+        for (by, at), piece in list(zip(wanted, pieces))[1:]
     ]
 
     raw = jax.ShapeDtypeStruct((chan_dev, rows, half), F32)
     mine, other = pl.pallas_call(
         functools.partial(raw_beams_kernel, tm, own),
         out_shape=[raw] * 2,
-        in_specs=[whole] * (1 + tm),
+        in_specs=[whole] * (1 + len(pieces)),
         out_specs=[whole] * 2,
         scratch_shapes=[pltpu.VMEM((beams, width), BF16)],
         compiler_params=params,
@@ -378,7 +401,7 @@
         cost_estimate=cost(20 * own * beams * width, 8 * own * beams * width),
     )(phase_index)
 
-    early = (tm - 1) * rows
+    early = tm * rows - blocks[-1].shape[1]
     cov, first, across = pl.pallas_call(
         early_kernel,
         out_shape=[
@@ -386,7 +409,7 @@
             jax.ShapeDtypeStruct((own, 2 * vectors, width), F32),
             jax.ShapeDtypeStruct((own, width, early), BF16),
         ],
-        in_specs=[whole] * tm,
+        in_specs=[whole] * len(blocks),
         out_specs=[whole] * 3,
         scratch_shapes=[pltpu.VMEM((early, width), BF16)] * 2,
         compiler_params=params,

time: 42.2 us -> 43.3 us (1.026)
  starting transfers between devices: 10.4 us -> 15.4 us
  waiting for transfers between devices: 13 us -> 9.03 us
    ppermute x3 -> x6, waiting for transfers between devices: 10.6 us -> 6.19 us  [local(): lax.ppermute(piece, 'tm', [(z, (z + by) % tm) for z in range(tm)])]
    ppermute x3 -> x6, starting transfers between devices: 6.23 us -> 10.4 us  [local(): lax.ppermute(piece, 'tm', [(z, (z + by) % tm) for z in range(tm)])]
    ppermute x3, starting transfers between devices: 3.54 us -> 4.45 us  [local(): arrived[x] = lax.ppermute(packets[x], 'tm', [(z, z ^ x) for z in range(tm)])]
    ppermute x3, waiting for transfers between devices: 2.08 us -> 2.53 us  [local(): arrived[x] = lax.ppermute(packets[x], 'tm', [(z, z ^ x) for z in range(tm)])]
  transfers between devices with their start and end apart: 11 -> 14, of which waited for: 5 -> 5; matrix products, arithmetic and copies ran while one was open for 1% -> 1% of each run, Pallas kernels for 25% -> 25%
where the time goes in v18:
time: 43.3 us; the launch traced here: 43.2 us
  Pallas kernels  15.8 us (36%)
  starting transfers between devices  15.4 us (36%)
  waiting for transfers between devices  9.03 us (21%)
  local copies, waits for them, and re-layouts  2.75 us (6%)
    ppermute x6, starting transfers between devices, local(): lax.ppermute(piece, 'tm', [(z, (z + by) % tm) for z in range(tm)])  10.4 us
    pallas_call x1, Pallas kernels, local(): pl.pallas_call(functools.partial(raw_beams_kernel, tm, own), out_shape=[r...  6.76 us
    ppermute x6, waiting for transfers between devices, local(): lax.ppermute(piece, 'tm', [(z, (z + by) % tm) for z in range(tm)])  6.19 us
    ppermute x3, starting transfers between devices, local(): arrived[x] = lax.ppermute(packets[x], 'tm', [(z, z ^ x) for z in range(tm)])  4.45 us
    pallas_call x1, Pallas kernels, local(): pl.pallas_call(functools.partial(subspace_kernel, tm, own, factor), out_s...  4.13 us
    ppermute x3, waiting for transfers between devices, local(): arrived[x] = lax.ppermute(packets[x], 'tm', [(z, z ^ x) for z in range(tm)])  2.53 us
    pallas_call x1, Pallas kernels, local(): pl.pallas_call(early_kernel, out_shape=[jax.ShapeDtypeStruct((own, 2, wid...  1.74 us
    pallas_call x1, Pallas kernels, local(): pl.pallas_call(functools.partial(own_weights_kernel, own, chan_dev), out_...  1.26 us
  transfers between devices with their start and end apart: 14, of which 5 were waited for; matrix products, arithmetic and copies ran while one was open for 1% of the time, Pallas kernels for 25%

profile of v18, /device:TPU:0, one launch (start us, length us, event | category | flops | bytes accessed | tf_op | source)
XLA Modules:
  0.0 43.2 jit_solution(6398253016665898840)
XLA Ops:
  0.0 0.0 copy-start.1
  0.0 1.1 %constant_dynamic-slice_fusion = bf16[64,1,1,2,512]{4,3,2,1,0:T(2,128)(2,1)S(1)} fusion(bf16[128,1,4,2,512]{4,3,2,1,0:T(2,128)(2,1)} %voltages_ref.1, s32[]{:T(128)S(6)} %select_n.3), kind=kLoop, calls=%fused_computation | loop fusion | bytes 262148 | tf_op jit(solution)/shard_map/dynamic_slice | solution.py:360
  1.1 0.1 reshape_transpose_squeeze.3.rest_1_
  1.1 3.1 %collective-permute-start = (bf16[1,128,512]{2,1,0:T(8,128)(2,1)S(1)}, bf16[1,128,512]{2,1,0:T(8,128)(2,1)S(1)}, u32[]{:S(2)}, u32[]{:S(2)}) collective-permute-start(bf16[1,128,512]{2,1,0:T(8,128)(2,1)S(1)} %reshape_transpose_squeeze.3.rest_1_), channel_id=1, source_target_pairs={{0,4},{4,8},{8,12},{12,0},{1,5},{5,9},{9,13},{13,1},{2,6},{6,10},{... | collective-permute-start | bytes 393224 | tf_op jit(solution)/shard_map/ppermute | solution.py:379
  4.2 0.0 copy-start
  4.2 1.2 %copy-done = bf16[128,1,4,2,512]{4,3,2,1,0:T(2,128)(2,1)S(1)} copy-done((bf16[128,1,4,2,512]{4,3,2,1,0:T(2,128)(2,1)S(1)}, bf16[128,1,4,2,512]{4,3,2,1,0:T(2,128)(2,1)}, u32[]{:S(2)}) %copy-start) | copy-done | bytes 1048600
  5.4 0.2 shard_map.55
  5.7 0.1 reshape_transpose.19.rest_2_
  5.7 2.1 %collective-permute-start.1 = (bf16[1,128,512]{2,1,0:T(8,128)(2,1)S(1)}, bf16[1,128,512]{2,1,0:T(8,128)(2,1)S(1)}, u32[]{:S(2)}, u32[]{:S(2)}) collective-permute-start(bf16[1,128,512]{2,1,0:T(8,128)(2,1)S(1)} %reshape_transpose.19.rest_2_), channel_id=1, source_target_pairs={{0,12},{4,0},{8,4},{12,8},{1,13},{5,1},{9,5},{13,9},{2,14},{6,2},{... | collective-permute-start | bytes 393224 | tf_op jit(solution)/shard_map/ppermute | solution.py:379
  7.8 0.1 reshape_transpose.20.rest_3_
  7.9 1.1 %collective-permute-start.2 = (bf16[1,128,512]{2,1,0:T(8,128)(2,1)S(1)}, bf16[1,128,512]{2,1,0:T(8,128)(2,1)S(1)}, u32[]{:S(2)}, u32[]{:S(2)}) collective-permute-start(bf16[1,128,512]{2,1,0:T(8,128)(2,1)S(1)} %reshape_transpose.20.rest_3_), channel_id=1, source_target_pairs={{0,8},{4,12},{8,0},{12,4},{1,9},{5,13},{9,1},{13,5},{2,10},{6,14},... | collective-permute-start | bytes 393224 | tf_op jit(solution)/shard_map/ppermute | solution.py:379
  8.9 0.1 reshape_transpose.21.rest_4_
  9.0 0.0 copy-start.2
  9.0 1.6 %collective-permute-start.3 = (bf16[1,128,512]{2,1,0:T(8,128)(2,1)S(1)}, bf16[1,128,512]{2,1,0:T(8,128)(2,1)S(1)}, u32[]{:S(2)}, u32[]{:S(2)}) collective-permute-start(bf16[1,128,512]{2,1,0:T(8,128)(2,1)S(1)} %reshape_transpose.21.rest_4_), channel_id=1, source_target_pairs={{0,4},{4,8},{8,12},{12,0},{1,5},{5,9},{9,13},{13,1},{2,6},{6,10},{... | collective-permute-start | bytes 393224 | tf_op jit(solution)/shard_map/ppermute | solution.py:379
  10.6 0.1 reshape_transpose.22.rest_5_
  10.7 2.3 %collective-permute-start.4 = (bf16[1,128,512]{2,1,0:T(8,128)(2,1)S(1)}, bf16[1,128,512]{2,1,0:T(8,128)(2,1)S(1)}, u32[]{:S(2)}, u32[]{:S(2)}) collective-permute-start(bf16[1,128,512]{2,1,0:T(8,128)(2,1)S(1)} %reshape_transpose.22.rest_5_), channel_id=1, source_target_pairs={{0,12},{4,0},{8,4},{12,8},{1,13},{5,1},{9,5},{13,9},{2,14},{6,2},{... | collective-permute-start | bytes 393224 | tf_op jit(solution)/shard_map/ppermute | solution.py:379
  13.0 0.1 reshape_transpose.18.rest_0_.refs_0_
  13.1 0.1 reshape_transpose.23.rest_6_
  13.2 0.0 copy-done.1
  13.2 1.3 %shard_map.57.weights_ref = bf16[1,512,512]{2,1,0:T(8,128)(2,1)S(1)} custom-call(s32[256,512]{1,0:T(8,128)S(1)} %copy-done.1), custom_call_target="tpu_custom_call" | custom-call | flops 5242880 | bytes 1048576 | tf_op jit(solution)/shard_map/pallas_call | solution.py:394
  14.4 0.0 collective-permute-done.refs_1_
  14.5 0.2 collective-permute-start.5
  14.7 6.8 %shard_map.56 = (f32[4,256,128]{2,1,0:T(8,128)S(1)}, f32[4,256,128]{2,1,0:T(8,128)S(1)}) custom-call(s32[256,512]{1,0:T(8,128)S(1)} %copy-done.1, bf16[1,256,512]{2,1,0:T(8,128)(2,1)S(1)} %reshape_transpose.18.rest_0_.refs_0_, bf16[1,128,512]{2,1,0:T(8,128)(2,1)S(1)} %reshape_transpose_squeeze.3.rest_1_, bf16[1,128,512]{2,1,0:T(8,128)(2,1)S(1)} %reshape_transpose.19.rest_2_, ...), custom_call_target="tpu_custom_call" | custom-call | flops 536870912 | bytes 2097152 | tf_op jit(solution)/shard_map/pallas_call | solution.py:384
  21.4 0.0 copy-start.3
  21.4 0.0 copy-start.4
  21.4 0.0 collective-permute-done.1.refs_2_
  21.5 3.0 %collective-permute-done.2.refs_3_ = bf16[1,128,512]{2,1,0:T(8,128)(2,1)S(1)} collective-permute-done((bf16[1,128,512]{2,1,0:T(8,128)(2,1)S(1)}, bf16[1,128,512]{2,1,0:T(8,128)(2,1)S(1)}, u32[]{:S(2)}, u32[]{:S(2)}) %collective-permute-start.2) | collective-permute-done | bytes 131104 | tf_op jit(solution)/shard_map/ppermute | solution.py:379
  24.5 0.0 collective-permute-done.3.refs_4_
  24.5 0.0 collective-permute-done.4.refs_5_
  24.5 0.0 copy-done.2
  24.5 1.7 %shard_map.58 = (f32[1,2,512,512]{3,2,1,0:T(8,128)S(1)}, f32[1,16,512]{2,1,0:T(8,128)S(1)}, bf16[1,512,896]{2,1,0:T(8,128)(2,1)S(1)}) custom-call(f32[1,4,2,8,512]{4,3,2,1,0:T(8,128)S(1)} %copy-done.2, bf16[1,256,512]{2,1,0:T(8,128)(2,1)S(1)} %reshape_transpose.18.rest_0_.refs_0_, bf16[1,128,512]{2,1,0:T(8,128)(2,1)S(1)} %collective-permute-done.refs_1_, ...), custom_call_target="tpu_custom_call" | custom-call | flops 939524096 | bytes 2097152 | tf_op jit(solution)/shard_map/pallas_call | solution.py:405
  26.2 3.2 %collective-permute-done.5.last_ref = bf16[1,128,512]{2,1,0:T(8,128)(2,1)S(1)} collective-permute-done((bf16[1,128,512]{2,1,0:T(8,128)(2,1)S(1)}, bf16[1,128,512]{2,1,0:T(8,128)(2,1)S(1)}, u32[]{:S(2)}, u32[]{:S(2)}) %collective-permute-start.5) | collective-permute-done | bytes 131104 | tf_op jit(solution)/shard_map/ppermute | solution.py:379
  29.4 0.0 copy-done.3
  29.4 0.0 copy-done.4
  29.4 4.1 %shard_map.59 = (f32[4,256,128]{2,1,0:T(8,128)S(1)}, bf16[1,16,384]{2,1,0:T(8,128)(2,1)S(1)}, bf16[1,16,384]{2,1,0:T(8,128)(2,1)S(1)}, bf16[1,16,384]{2,1,0:T(8,128)(2,1)S(1)}, bf16[1,16,384]{2,1,0:T(8,128)(2,1)S(1)}) custom-call(f32[4,256,128]{2,1,0:T(8,128)S(1)} %get-tuple-element.27.beams_ref, ...), custom_call_target="tpu_custom_call", output_to_operand_aliasing={{0}: (0, {})} | custom-call | flops 134217728 | bytes 2097152 | tf_op jit(solution)/shard_map/pallas_call | solution.py:419
  33.5 0.1 collective-permute-start.6
  33.6 2.4 %collective-permute-start.10 = (bf16[1,16,384]{2,1,0:T(8,128)(2,1)S(1)}, bf16[1,16,384]{2,1,0:T(8,128)(2,1)S(1)}, u32[]{:S(2)}, u32[]{:S(2)}) collective-permute-start(bf16[1,16,384]{2,1,0:T(8,128)(2,1)S(1)} %get-tuple-element.35), channel_id=1, source_target_pairs={{0,12},{4,8},{8,4},{12,0},{1,13},{5,9},{9,5},{13,1},{2,14},{6,10},... | collective-permute-start | bytes 36872 | tf_op jit(solution)/shard_map/ppermute | solution.py:436
  36.0 0.0 collective-permute-start.12
  36.0 2.1 %collective-permute-start.7 = (bf16[1,16,384]{2,1,0:T(8,128)(2,1)S(1)}, bf16[1,16,384]{2,1,0:T(8,128)(2,1)S(1)}, u32[]{:S(2)}, u32[]{:S(2)}) collective-permute-start(bf16[1,16,384]{2,1,0:T(8,128)(2,1)S(1)} %get-tuple-element.32), channel_id=1, source_target_pairs={{0,4},{4,0},{8,12},{12,8},{1,5},{5,1},{9,13},{13,9},{2,6},{6,2},{1... | collective-permute-start | bytes 36872 | tf_op jit(solution)/shard_map/ppermute | solution.py:436
  38.1 0.0 collective-permute-start.9
  38.1 1.1 %collective-permute-done.10.rest_2_ = bf16[1,16,384]{2,1,0:T(8,128)(2,1)S(1)} collective-permute-done((bf16[1,16,384]{2,1,0:T(8,128)(2,1)S(1)}, bf16[1,16,384]{2,1,0:T(8,128)(2,1)S(1)}, u32[]{:S(2)}, u32[]{:S(2)}) %collective-permute-start.10) | collective-permute-done | bytes 12320 | tf_op jit(solution)/shard_map/ppermute | solution.py:436
  39.2 0.0 collective-permute-start.11
  39.2 1.4 %collective-permute-done.12.rest_1_ = bf16[1,16,384]{2,1,0:T(8,128)(2,1)S(1)} collective-permute-done((bf16[1,16,384]{2,1,0:T(8,128)(2,1)S(1)}, bf16[1,16,384]{2,1,0:T(8,128)(2,1)S(1)}, u32[]{:S(2)}, u32[]{:S(2)}) %collective-permute-start.12) | collective-permute-done | bytes 12320 | tf_op jit(solution)/shard_map/ppermute | solution.py:436
  40.6 0.0 collective-permute-start.13
  40.6 0.0 collective-permute-done.7.rest_0_
  40.6 0.5 %collective-permute-start.8 = (bf16[1,16,384]{2,1,0:T(8,128)(2,1)S(1)}, bf16[1,16,384]{2,1,0:T(8,128)(2,1)S(1)}, u32[]{:S(2)}, u32[]{:S(2)}) collective-permute-start(bf16[1,16,384]{2,1,0:T(8,128)(2,1)S(1)} %collective-permute-done.7.rest_0_), channel_id=1, source_target_pairs={{0,1},{1,0},{2,3},{3,2},{4,5},{5,4},{6,7},{7,6},{8,9},{9,8},{10,11... | collective-permute-start | bytes 36872 | tf_op jit(solution)/shard_map/ppermute | solution.py:437
  41.1 0.3 shard_map.60.rest_4_
  41.4 0.0 collective-permute-done.9.rest_1_
  41.4 0.0 collective-permute-done.11.rest_2_
  41.5 0.3 collective-permute-done.13.rest_3_
  41.8 0.0 collective-permute-done.6.theirs_ref
  41.8 0.4 shard_map.61.power_ref
  42.1 0.0 collective-permute-done.8.packet_ref
  42.1 1.0 %shard_map.62 = f32[512,128]{1,0:T(8,128)} custom-call(f32[4,256,128]{2,1,0:T(8,128)S(1)} %collective-permute-done.6.theirs_ref, bf16[1,16,384]{2,1,0:T(8,128)(2,1)S(1)} %collective-permute-done.8.packet_ref, f32[4,128,128]{2,1,0:T(8,128)S(1)} %shard_map.61.power_ref), custom_call_target="tpu_custom_call" | custom-call | flops 131072 | bytes 786432 | tf_op jit(solution)/shard_map/pallas_call | solution.py:457
Async XLA Ops:
  0.0 13.2 %copy-start.1 = (s32[256,512]{1,0:T(8,128)S(1)}, s32[256,512]{1,0:T(8,128)}, u32[]{:S(2)}) copy-start(s32[256,512]{1,0:T(8,128)} %phase_ref.3) | copy-start | bytes 1572868
  1.1 13.3 %collective-permute-start = (bf16[1,128,512]{2,1,0:T(8,128)(2,1)S(1)}, bf16[1,128,512]{2,1,0:T(8,128)(2,1)S(1)}, u32[]{:S(2)}, u32[]{:S(2)}) collective-permute-start(bf16[1,128,512]{2,1,0:T(8,128)(2,1)S(1)} %reshape_transpose_squeeze.3.rest_1_), channel_id=1, source_target_pairs={{0,4},{4,8},{8,12},{12,0},{1,5},{5,9},{9,13},{13,1},{2,6},{6,10},{... | collective-permute-start | bytes 393224 | tf_op jit(solution)/shard_map/ppermute | solution.py:379
  4.2 1.2 %copy-start = (bf16[128,1,4,2,512]{4,3,2,1,0:T(2,128)(2,1)S(1)}, bf16[128,1,4,2,512]{4,3,2,1,0:T(2,128)(2,1)}, u32[]{:S(2)}) copy-start(bf16[128,1,4,2,512]{4,3,2,1,0:T(2,128)(2,1)} %voltages_ref.1) | copy-start | bytes 3145732
  5.7 15.7 %collective-permute-start.1 = (bf16[1,128,512]{2,1,0:T(8,128)(2,1)S(1)}, bf16[1,128,512]{2,1,0:T(8,128)(2,1)S(1)}, u32[]{:S(2)}, u32[]{:S(2)}) collective-permute-start(bf16[1,128,512]{2,1,0:T(8,128)(2,1)S(1)} %reshape_transpose.19.rest_2_), channel_id=1, source_target_pairs={{0,12},{4,0},{8,4},{12,8},{1,13},{5,1},{9,5},{13,9},{2,14},{6,2},{... | collective-permute-start | bytes 393224 | tf_op jit(solution)/shard_map/ppermute | solution.py:379
  7.9 16.6 %collective-permute-start.2 = (bf16[1,128,512]{2,1,0:T(8,128)(2,1)S(1)}, bf16[1,128,512]{2,1,0:T(8,128)(2,1)S(1)}, u32[]{:S(2)}, u32[]{:S(2)}) collective-permute-start(bf16[1,128,512]{2,1,0:T(8,128)(2,1)S(1)} %reshape_transpose.20.rest_3_), channel_id=1, source_target_pairs={{0,8},{4,12},{8,0},{12,4},{1,9},{5,13},{9,1},{13,5},{2,10},{6,14},... | collective-permute-start | bytes 393224 | tf_op jit(solution)/shard_map/ppermute | solution.py:379
  9.0 15.5 %copy-start.2 = (f32[1,4,2,8,512]{4,3,2,1,0:T(8,128)S(1)}, f32[1,4,2,8,512]{4,3,2,1,0:T(8,128)}, u32[]{:S(2)}) copy-start(f32[1,4,2,8,512]{4,3,2,1,0:T(8,128)} %start_ref.3) | copy-start | bytes 393220
  9.0 15.4 %collective-permute-start.3 = (bf16[1,128,512]{2,1,0:T(8,128)(2,1)S(1)}, bf16[1,128,512]{2,1,0:T(8,128)(2,1)S(1)}, u32[]{:S(2)}, u32[]{:S(2)}) collective-permute-start(bf16[1,128,512]{2,1,0:T(8,128)(2,1)S(1)} %reshape_transpose.21.rest_4_), channel_id=1, source_target_pairs={{0,4},{4,8},{8,12},{12,0},{1,5},{5,9},{9,13},{13,1},{2,6},{6,10},{... | collective-permute-start | bytes 393224 | tf_op jit(solution)/shard_map/ppermute | solution.py:379
  10.7 13.8 %collective-permute-start.4 = (bf16[1,128,512]{2,1,0:T(8,128)(2,1)S(1)}, bf16[1,128,512]{2,1,0:T(8,128)(2,1)S(1)}, u32[]{:S(2)}, u32[]{:S(2)}) collective-permute-start(bf16[1,128,512]{2,1,0:T(8,128)(2,1)S(1)} %reshape_transpose.22.rest_5_), channel_id=1, source_target_pairs={{0,12},{4,0},{8,4},{12,8},{1,13},{5,1},{9,5},{13,9},{2,14},{6,2},{... | collective-permute-start | bytes 393224 | tf_op jit(solution)/shard_map/ppermute | solution.py:379
  14.5 14.9 %collective-permute-start.5 = (bf16[1,128,512]{2,1,0:T(8,128)(2,1)S(1)}, bf16[1,128,512]{2,1,0:T(8,128)(2,1)S(1)}, u32[]{:S(2)}, u32[]{:S(2)}) collective-permute-start(bf16[1,128,512]{2,1,0:T(8,128)(2,1)S(1)} %reshape_transpose.23.rest_6_), channel_id=1, source_target_pairs={{0,8},{4,12},{8,0},{12,4},{1,9},{5,13},{9,1},{13,5},{2,10},{6,14},... | collective-permute-start | bytes 393224 | tf_op jit(solution)/shard_map/ppermute | solution.py:379
  21.4 8.0 %copy-start.3 = (s32[4]{0:T(128)S(1)}, s32[4]{0:T(128)}, u32[]{:S(2)}) copy-start(s32[4]{0:T(128)} %flags_ref.1) | copy-start | bytes 52
  21.4 8.0 %copy-start.4 = (s32[4]{0:T(128)S(1)}, s32[4]{0:T(128)}, u32[]{:S(2)}) copy-start(s32[4]{0:T(128)} %ranks_ref.1) | copy-start | bytes 52
  33.5 8.2 %collective-permute-start.6 = (f32[4,256,128]{2,1,0:T(8,128)S(1)}, f32[4,256,128]{2,1,0:T(8,128)S(1)}, u32[]{:S(2)}, u32[]{:S(2)}) collective-permute-start(f32[4,256,128]{2,1,0:T(8,128)S(1)} %get-tuple-element.31), channel_id=1, source_target_pairs={{0,1},{1,0},{2,3},{3,2},{4,5},{5,4},{6,7},{7,6},{8,9},{9,8},{10,11... | collective-permute-start | bytes 1572872 | tf_op jit(solution)/shard_map/ppermute | solution.py:432
  33.6 5.6 %collective-permute-start.10 = (bf16[1,16,384]{2,1,0:T(8,128)(2,1)S(1)}, bf16[1,16,384]{2,1,0:T(8,128)(2,1)S(1)}, u32[]{:S(2)}, u32[]{:S(2)}) collective-permute-start(bf16[1,16,384]{2,1,0:T(8,128)(2,1)S(1)} %get-tuple-element.35), channel_id=1, source_target_pairs={{0,12},{4,8},{8,4},{12,0},{1,13},{5,9},{9,5},{13,1},{2,14},{6,10},... | collective-permute-start | bytes 36872 | tf_op jit(solution)/shard_map/ppermute | solution.py:436
  36.0 4.6 %collective-permute-start.12 = (bf16[1,16,384]{2,1,0:T(8,128)(2,1)S(1)}, bf16[1,16,384]{2,1,0:T(8,128)(2,1)S(1)}, u32[]{:S(2)}, u32[]{:S(2)}) collective-permute-start(bf16[1,16,384]{2,1,0:T(8,128)(2,1)S(1)} %get-tuple-element.36), channel_id=1, source_target_pairs={{0,8},{4,12},{8,0},{12,4},{1,9},{5,13},{9,1},{13,5},{2,10},{6,14},... | collective-permute-start | bytes 36872 | tf_op jit(solution)/shard_map/ppermute | solution.py:436
  36.0 4.6 %collective-permute-start.7 = (bf16[1,16,384]{2,1,0:T(8,128)(2,1)S(1)}, bf16[1,16,384]{2,1,0:T(8,128)(2,1)S(1)}, u32[]{:S(2)}, u32[]{:S(2)}) collective-permute-start(bf16[1,16,384]{2,1,0:T(8,128)(2,1)S(1)} %get-tuple-element.32), channel_id=1, source_target_pairs={{0,4},{4,0},{8,12},{12,8},{1,5},{5,1},{9,13},{13,9},{2,6},{6,2},{1... | collective-permute-start | bytes 36872 | tf_op jit(solution)/shard_map/ppermute | solution.py:436
  38.1 3.4 %collective-permute-start.9 = (bf16[1,16,384]{2,1,0:T(8,128)(2,1)S(1)}, bf16[1,16,384]{2,1,0:T(8,128)(2,1)S(1)}, u32[]{:S(2)}, u32[]{:S(2)}) collective-permute-start(bf16[1,16,384]{2,1,0:T(8,128)(2,1)S(1)} %get-tuple-element.34.rest_0_), channel_id=1, source_target_pairs={{0,1},{1,0},{2,3},{3,2},{4,5},{5,4},{6,7},{7,6},{8,9},{9,8},{10,11... | collective-permute-start | bytes 36872 | tf_op jit(solution)/shard_map/ppermute | solution.py:437
  39.2 2.3 %collective-permute-start.11 = (bf16[1,16,384]{2,1,0:T(8,128)(2,1)S(1)}, bf16[1,16,384]{2,1,0:T(8,128)(2,1)S(1)}, u32[]{:S(2)}, u32[]{:S(2)}) collective-permute-start(bf16[1,16,384]{2,1,0:T(8,128)(2,1)S(1)} %collective-permute-done.10.rest_2_), channel_id=1, source_target_pairs={{0,1},{1,0},{2,3},{3,2},{4,5},{5,4},{6,7},{7,6},{8,9},{9,8},{10,11... | collective-permute-start | bytes 36872 | tf_op jit(solution)/shard_map/ppermute | solution.py:437
  40.6 1.2 %collective-permute-start.13 = (bf16[1,16,384]{2,1,0:T(8,128)(2,1)S(1)}, bf16[1,16,384]{2,1,0:T(8,128)(2,1)S(1)}, u32[]{:S(2)}, u32[]{:S(2)}) collective-permute-start(bf16[1,16,384]{2,1,0:T(8,128)(2,1)S(1)} %collective-permute-done.12.rest_1_), channel_id=1, source_target_pairs={{0,1},{1,0},{2,3},{3,2},{4,5},{5,4},{6,7},{7,6},{8,9},{9,8},{10,11... | collective-permute-start | bytes 36872 | tf_op jit(solution)/shard_map/ppermute | solution.py:437
  40.6 1.5 %collective-permute-start.8 = (bf16[1,16,384]{2,1,0:T(8,128)(2,1)S(1)}, bf16[1,16,384]{2,1,0:T(8,128)(2,1)S(1)}, u32[]{:S(2)}, u32[]{:S(2)}) collective-permute-start(bf16[1,16,384]{2,1,0:T(8,128)(2,1)S(1)} %collective-permute-done.7.rest_0_), channel_id=1, source_target_pairs={{0,1},{1,0},{2,3},{3,2},{4,5},{5,4},{6,7},{7,6},{8,9},{9,8},{10,11... | collective-permute-start | bytes 36872 | tf_op jit(solution)/shard_map/ppermute | solution.py:437

commit v19 on v17

--- a/solution.py
+++ b/solution.py
@@ -18,6 +18,7 @@
 TN = (((0,), (0,)), ((), ()))
 VMEM_LIMIT = 48 * 1024 * 1024
 CHUNK = 128
+LEAST_PIVOT = 1e-4
 
 
 def dot(left, right, dims):
@@ -199,10 +200,14 @@
             )
         )
     by_v = list(by_z)
+    whole = [real[n : n + 1] for n, (real, imag) in enumerate(by_z)]
+    sound = jnp.ones((1, 1), F32)
     pairs = [(real_z, imag_z), *riders]
     for n in range(vectors - 1):
         (real_d, imag_d), (real_p, imag_p) = by_z[n], by_v[n]
         square = jnp.maximum(real_p[n : n + 1], 0.0)
+        fits = (square >= LEAST_PIVOT * whole[n]) & (square <= 4.0 * whole[n])
+        sound = jnp.where(fits, sound, 0.0)
         inverse = jnp.where(row > n, 1.0 / (square + EPS), 0.0)
         real_c, imag_c = real_d * inverse, imag_d * inverse
         real_b, imag_b = real_p - real_c * square, imag_p - imag_c * square
@@ -228,7 +233,7 @@
         ]
     real_v, imag_v = pairs[0]
     factor = 1.0 / jnp.sqrt(jnp.sum(real_v * real_v + imag_v * imag_v, axis=1, keepdims=True) + EPS)
-    return [(real * factor, imag * factor) for real, imag in pairs]
+    return [(real * factor, imag * factor) for real, imag in pairs], sound
 
 
 def subspace_kernel(
@@ -255,35 +260,55 @@
         ]
         last = block_times(start_ref[0, chan, 0], start_ref[0, chan, 1], across, last_ref[o])
         both = (first_ref[o] + last) * factor
-        real_q, imag_q = orthonormalize(both[:vectors], both[vectors:], chunks)
+        start = orthonormalize(both[:vectors], both[vectors:], chunks)
+        rank = flags_ref[chan] * ranks_ref[chan]
+        keep = lax.broadcasted_iota(jnp.int32, (vectors, 1), 0) < rank
+
+        def steered_by(real, imag):
+            rows_in = jnp.concatenate(split(jnp.concatenate([real, imag], axis=0)), axis=0)
+            product = dot(rows_in, weights_ref[o], NN)
+            product = product[: 2 * vectors] + product[2 * vectors :]
+            return (
+                product[:vectors, :beams] - product[vectors:, beams:],
+                product[:vectors, beams:] + product[vectors:, :beams],
+            )
+
+        def write(real_w, imag_w, early, late):
+            series = [early[:, i * rows : (i + 1) * rows] for i in range(tm - 1)] + [late]
+            for by, values in zip(steps(tm), series):
+                series_ref[tm_index ^ shifted(-by)] = jnp.where(keep, values, 0.0)
+            kept = [jnp.where(keep, real_w, 0.0), jnp.where(keep, imag_w, 0.0)]
+            for x, out in enumerate(outs):
+                values = series_ref[x]
+                values = jnp.concatenate([values[:, : rows // 2], values[:, rows // 2 :]], axis=0)
+                out[o, :, :beams] = jnp.concatenate(kept, axis=0).astype(BF16)
+                out[o, :, beams:] = values.astype(BF16)
+
+        real_q, imag_q = start
+        sound = jnp.ones((1, 1), F32)
         for sweep in range(1, ITERS - 1):
             real_z, imag_z = cov_times(real_q, imag_q, high_ref, low_ref)
-            ((real_q, imag_q),) = orthonormalize_by_gram(real_z, imag_z)
+            ((real_q, imag_q),), now = orthonormalize_by_gram(real_z, imag_z)
+            sound = jnp.minimum(sound, now)
         real_z, imag_z = cov_times(real_q, imag_q, high_ref, low_ref)
-        both = jnp.concatenate(split(jnp.concatenate([real_z, imag_z], axis=0)), axis=0)
-        product = dot(both, weights_ref[o], NN)
-        product = product[: 2 * vectors] + product[2 * vectors :]
-        real_w = product[:vectors, :beams] - product[vectors:, beams:]
-        imag_w = product[:vectors, beams:] + product[vectors:, :beams]
         riders = [
-            (real_w, imag_w),
+            steered_by(real_z, imag_z),
             project(real_z, imag_z, across_ref[o]),
             project(real_z, imag_z, across),
         ]
-        unused, (real_w, imag_w), (early, unused), (late, unused) = orthonormalize_by_gram(real_z, imag_z, riders)
-        rank = flags_ref[chan] * ranks_ref[chan]
-        keep = lax.broadcasted_iota(jnp.int32, (vectors, 1), 0) < rank
-        real_w = jnp.where(keep, real_w, 0.0)
-        imag_w = jnp.where(keep, imag_w, 0.0)
-        series = [early[:, i * rows : (i + 1) * rows] for i in range(tm - 1)] + [late]
-        for by, values in zip(steps(tm), series):
-            series_ref[tm_index ^ shifted(-by)] = jnp.where(keep, values, 0.0)
-        steered = jnp.concatenate([real_w, imag_w], axis=0).astype(BF16)
-        for x, out in enumerate(outs):
-            series = series_ref[x]
-            series = jnp.concatenate([series[:, : rows // 2], series[:, rows // 2 :]], axis=0)
-            out[o, :, :beams] = steered
-            out[o, :, beams:] = series.astype(BF16)
+        (unused, steered, early, late), now = orthonormalize_by_gram(real_z, imag_z, riders)
+        write(*steered, early[0], late[0])
+
+        @pl.when(jnp.min(jnp.minimum(sound, now)) < 0.5)
+        def plainly():
+            real, imag = start
+            for sweep in range(1, ITERS):
+                real, imag = orthonormalize(*cov_times(real, imag, high_ref, low_ref))
+            write(
+                *steered_by(real, imag),
+                project(real, imag, across_ref[o])[0],
+                project(real, imag, last_ref[o].T)[0],
+            )
 
 
 def nulled_power(raw, packet_ref, squares):

time: 42.2 us -> 42.3 us (level)
  no operation moved by 1% of the time
where the time goes in v19:
time: 42.3 us; the launch traced here: 42.1 us
  Pallas kernels  15.7 us (37%)
  waiting for transfers between devices  13 us (31%)
  starting transfers between devices  10.4 us (25%)
  local copies, waits for them, and re-layouts  2.85 us (7%)
    ppermute x3, waiting for transfers between devices, local(): lax.ppermute(piece, 'tm', [(z, (z + by) % tm) for z in range(tm)])  10.6 us
    pallas_call x1, Pallas kernels, local(): pl.pallas_call(functools.partial(raw_beams_kernel, tm, own), out_shape=[r...  6.85 us
    ppermute x3, starting transfers between devices, local(): lax.ppermute(piece, 'tm', [(z, (z + by) % tm) for z in range(tm)])  6.23 us
    pallas_call x1, Pallas kernels, local(): pl.pallas_call(functools.partial(subspace_kernel, tm, own, factor), out_s...  4.22 us
    ppermute x3, starting transfers between devices, local(): arrived[x] = lax.ppermute(packets[x], 'tm', [(z, z ^ x) for z in range(tm)])  3.54 us
    ppermute x3, waiting for transfers between devices, local(): arrived[x] = lax.ppermute(packets[x], 'tm', [(z, z ^ x) for z in range(tm)])  2.08 us
    pallas_call x1, Pallas kernels, local(): pl.pallas_call(early_kernel, out_shape=[jax.ShapeDtypeStruct((own, 2, wid...  1.51 us
    pallas_call x1, Pallas kernels, local(): pl.pallas_call(functools.partial(own_weights_kernel, own, chan_dev), out_...  1.26 us
  transfers between devices with their start and end apart: 11, of which 5 were waited for; matrix products, arithmetic and copies ran while one was open for 1% of the time, Pallas kernels for 25%

profile of v19, /device:TPU:0, one launch (start us, length us, event | category | flops | bytes accessed | tf_op | source)
XLA Modules:
  0.0 42.1 jit_solution(6194351567276816905)
XLA Ops:
  0.0 0.0 copy-start.1
  0.0 1.2 %constant_dynamic-slice_fusion = bf16[128,1,1,2,512]{4,3,2,1,0:T(2,128)(2,1)S(1)} fusion(bf16[128,1,4,2,512]{4,3,2,1,0:T(2,128)(2,1)} %voltages_ref.1, s32[]{:T(128)S(6)} %select_n.3), kind=kLoop, calls=%fused_computation | loop fusion | bytes 524292 | tf_op jit(solution)/shard_map/dynamic_slice | solution.py:377
  1.2 0.1 reshape_transpose.13.rest_1_
  1.3 3.1 %collective-permute-start = (bf16[1,256,512]{2,1,0:T(8,128)(2,1)S(1)}, bf16[1,256,512]{2,1,0:T(8,128)(2,1)S(1)}, u32[]{:S(2)}, u32[]{:S(2)}) collective-permute-start(bf16[1,256,512]{2,1,0:T(8,128)(2,1)S(1)} %reshape_transpose.13.rest_1_), channel_id=1, source_target_pairs={{0,4},{4,8},{8,12},{12,0},{1,5},{5,9},{9,13},{13,1},{2,6},{6,10},{... | collective-permute-start | bytes 786440 | tf_op jit(solution)/shard_map/ppermute | solution.py:381
  4.4 0.0 copy-start
  4.4 1.2 %copy-done = bf16[128,1,4,2,512]{4,3,2,1,0:T(2,128)(2,1)S(1)} copy-done((bf16[128,1,4,2,512]{4,3,2,1,0:T(2,128)(2,1)S(1)}, bf16[128,1,4,2,512]{4,3,2,1,0:T(2,128)(2,1)}, u32[]{:S(2)}) %copy-start) | copy-done | bytes 1048600
  5.6 0.2 shard_map.55
  5.8 0.1 reshape_transpose.14.rest_2_
  5.9 0.0 copy-start.2
  5.9 2.1 %collective-permute-start.1 = (bf16[1,256,512]{2,1,0:T(8,128)(2,1)S(1)}, bf16[1,256,512]{2,1,0:T(8,128)(2,1)S(1)}, u32[]{:S(2)}, u32[]{:S(2)}) collective-permute-start(bf16[1,256,512]{2,1,0:T(8,128)(2,1)S(1)} %reshape_transpose.14.rest_2_), channel_id=1, source_target_pairs={{0,12},{4,0},{8,4},{12,8},{1,13},{5,1},{9,5},{13,9},{2,14},{6,2},{... | collective-permute-start | bytes 786440 | tf_op jit(solution)/shard_map/ppermute | solution.py:381
  8.0 0.1 reshape_transpose.15.rest_3_
  8.1 1.1 %collective-permute-start.2 = (bf16[1,256,512]{2,1,0:T(8,128)(2,1)S(1)}, bf16[1,256,512]{2,1,0:T(8,128)(2,1)S(1)}, u32[]{:S(2)}, u32[]{:S(2)}) collective-permute-start(bf16[1,256,512]{2,1,0:T(8,128)(2,1)S(1)} %reshape_transpose.15.rest_3_), channel_id=1, source_target_pairs={{0,8},{4,12},{8,0},{12,4},{1,9},{5,13},{9,1},{13,5},{2,10},{6,14},... | collective-permute-start | bytes 786440 | tf_op jit(solution)/shard_map/ppermute | solution.py:381
  9.2 0.1 reshape_transpose.12.rest_0_.refs_0_
  9.3 0.0 copy-done.1
  9.3 1.3 %shard_map.57.weights_ref = bf16[1,512,512]{2,1,0:T(8,128)(2,1)S(1)} custom-call(s32[256,512]{1,0:T(8,128)S(1)} %copy-done.1), custom_call_target="tpu_custom_call" | custom-call | flops 5242880 | bytes 1048576 | tf_op jit(solution)/shard_map/pallas_call | solution.py:396
  10.5 0.0 copy-start.3
  10.6 0.0 copy-start.4
  10.6 6.8 %shard_map.56 = (f32[4,256,128]{2,1,0:T(8,128)S(1)}, f32[4,256,128]{2,1,0:T(8,128)S(1)}) custom-call(s32[256,512]{1,0:T(8,128)S(1)} %copy-done.1, bf16[1,256,512]{2,1,0:T(8,128)(2,1)S(1)} %reshape_transpose.12.rest_0_.refs_0_, bf16[1,256,512]{2,1,0:T(8,128)(2,1)S(1)} %reshape_transpose.13.rest_1_, bf16[1,256,512]{2,1,0:T(8,128)(2,1)S(1)} %reshape_transpose.14.rest_2_, ...), custom_call_target="tpu_custom_call" | custom-call | flops 536870912 | bytes 2097152 | tf_op jit(solution)/shard_map/pallas_call | solution.py:386
  17.4 0.0 collective-permute-done.refs_1_
  17.4 0.9 %collective-permute-done.1.refs_2_ = bf16[1,256,512]{2,1,0:T(8,128)(2,1)S(1)} collective-permute-done((bf16[1,256,512]{2,1,0:T(8,128)(2,1)S(1)}, bf16[1,256,512]{2,1,0:T(8,128)(2,1)S(1)}, u32[]{:S(2)}, u32[]{:S(2)}) %collective-permute-start.1) | collective-permute-done | bytes 262176 | tf_op jit(solution)/shard_map/ppermute | solution.py:381
  18.3 0.0 copy-done.2
  18.3 1.5 %shard_map.58 = (f32[1,2,512,512]{3,2,1,0:T(8,128)S(1)}, f32[1,16,512]{2,1,0:T(8,128)S(1)}, bf16[1,512,768]{2,1,0:T(8,128)(2,1)S(1)}) custom-call(f32[1,4,2,8,512]{4,3,2,1,0:T(8,128)S(1)} %copy-done.2, bf16[1,256,512]{2,1,0:T(8,128)(2,1)S(1)} %reshape_transpose.12.rest_0_.refs_0_, bf16[1,256,512]{2,1,0:T(8,128)(2,1)S(1)} %collective-permute-done.refs_1_, ...), custom_call_target="tpu_custom_call" | custom-call | flops 805306368 | bytes 2097152 | tf_op jit(solution)/shard_map/pallas_call | solution.py:407
  19.8 9.7 %collective-permute-done.2.last_ref = bf16[1,256,512]{2,1,0:T(8,128)(2,1)S(1)} collective-permute-done((bf16[1,256,512]{2,1,0:T(8,128)(2,1)S(1)}, bf16[1,256,512]{2,1,0:T(8,128)(2,1)S(1)}, u32[]{:S(2)}, u32[]{:S(2)}) %collective-permute-start.2) | collective-permute-done | bytes 262176 | tf_op jit(solution)/shard_map/ppermute | solution.py:381
  29.6 0.0 copy-done.3
  29.6 0.0 copy-done.4
  29.6 4.2 %shard_map.59 = (f32[4,256,128]{2,1,0:T(8,128)S(1)}, bf16[1,16,384]{2,1,0:T(8,128)(2,1)S(1)}, bf16[1,16,384]{2,1,0:T(8,128)(2,1)S(1)}, bf16[1,16,384]{2,1,0:T(8,128)(2,1)S(1)}, bf16[1,16,384]{2,1,0:T(8,128)(2,1)S(1)}) custom-call(f32[4,256,128]{2,1,0:T(8,128)S(1)} %get-tuple-element.21.beams_ref, ...), custom_call_target="tpu_custom_call", output_to_operand_aliasing={{0}: (0, {})} | custom-call | flops 134217728 | bytes 2097152 | tf_op jit(solution)/shard_map/pallas_call | solution.py:421
  33.8 0.1 collective-permute-start.3
  33.9 0.1 collective-permute-start.9
  34.0 1.7 %collective-permute-start.7 = (bf16[1,16,384]{2,1,0:T(8,128)(2,1)S(1)}, bf16[1,16,384]{2,1,0:T(8,128)(2,1)S(1)}, u32[]{:S(2)}, u32[]{:S(2)}) collective-permute-start(bf16[1,16,384]{2,1,0:T(8,128)(2,1)S(1)} %get-tuple-element.29), channel_id=1, source_target_pairs={{0,12},{4,8},{8,4},{12,0},{1,13},{5,9},{9,5},{13,1},{2,14},{6,10},... | collective-permute-start | bytes 36872 | tf_op jit(solution)/shard_map/ppermute | solution.py:438
  35.6 1.8 %collective-permute-start.4 = (bf16[1,16,384]{2,1,0:T(8,128)(2,1)S(1)}, bf16[1,16,384]{2,1,0:T(8,128)(2,1)S(1)}, u32[]{:S(2)}, u32[]{:S(2)}) collective-permute-start(bf16[1,16,384]{2,1,0:T(8,128)(2,1)S(1)} %get-tuple-element.26), channel_id=1, source_target_pairs={{0,4},{4,0},{8,12},{12,8},{1,5},{5,1},{9,13},{13,9},{2,6},{6,2},{1... | collective-permute-start | bytes 36872 | tf_op jit(solution)/shard_map/ppermute | solution.py:438
  37.4 0.0 collective-permute-start.6
  37.4 1.2 %collective-permute-done.9.rest_1_ = bf16[1,16,384]{2,1,0:T(8,128)(2,1)S(1)} collective-permute-done((bf16[1,16,384]{2,1,0:T(8,128)(2,1)S(1)}, bf16[1,16,384]{2,1,0:T(8,128)(2,1)S(1)}, u32[]{:S(2)}, u32[]{:S(2)}) %collective-permute-start.9) | collective-permute-done | bytes 12320 | tf_op jit(solution)/shard_map/ppermute | solution.py:438
  38.6 0.0 collective-permute-start.10
  38.6 0.9 %collective-permute-done.7.rest_2_ = bf16[1,16,384]{2,1,0:T(8,128)(2,1)S(1)} collective-permute-done((bf16[1,16,384]{2,1,0:T(8,128)(2,1)S(1)}, bf16[1,16,384]{2,1,0:T(8,128)(2,1)S(1)}, u32[]{:S(2)}, u32[]{:S(2)}) %collective-permute-start.7) | collective-permute-done | bytes 12320 | tf_op jit(solution)/shard_map/ppermute | solution.py:438
  39.5 0.0 collective-permute-start.8
  39.5 0.0 collective-permute-done.4.rest_0_
  39.5 0.5 %collective-permute-start.5 = (bf16[1,16,384]{2,1,0:T(8,128)(2,1)S(1)}, bf16[1,16,384]{2,1,0:T(8,128)(2,1)S(1)}, u32[]{:S(2)}, u32[]{:S(2)}) collective-permute-start(bf16[1,16,384]{2,1,0:T(8,128)(2,1)S(1)} %collective-permute-done.4.rest_0_), channel_id=1, source_target_pairs={{0,1},{1,0},{2,3},{3,2},{4,5},{5,4},{6,7},{7,6},{8,9},{9,8},{10,11... | collective-permute-start | bytes 36872 | tf_op jit(solution)/shard_map/ppermute | solution.py:439
  40.0 0.3 shard_map.60.rest_4_
  40.4 0.0 collective-permute-done.6.rest_1_
  40.4 0.0 collective-permute-done.10.rest_3_
  40.4 0.3 collective-permute-done.8.rest_2_
  40.7 0.0 collective-permute-done.3.theirs_ref
  40.7 0.4 shard_map.61.power_ref
  41.1 0.0 collective-permute-done.5.packet_ref
  41.1 1.0 %shard_map.62 = f32[512,128]{1,0:T(8,128)} custom-call(f32[4,256,128]{2,1,0:T(8,128)S(1)} %collective-permute-done.3.theirs_ref, bf16[1,16,384]{2,1,0:T(8,128)(2,1)S(1)} %collective-permute-done.5.packet_ref, f32[4,128,128]{2,1,0:T(8,128)S(1)} %shard_map.61.power_ref), custom_call_target="tpu_custom_call" | custom-call | flops 131072 | bytes 786432 | tf_op jit(solution)/shard_map/pallas_call | solution.py:459
Async XLA Ops:
  0.0 9.3 %copy-start.1 = (s32[256,512]{1,0:T(8,128)S(1)}, s32[256,512]{1,0:T(8,128)}, u32[]{:S(2)}) copy-start(s32[256,512]{1,0:T(8,128)} %phase_ref.3) | copy-start | bytes 1572868
  1.3 16.1 %collective-permute-start = (bf16[1,256,512]{2,1,0:T(8,128)(2,1)S(1)}, bf16[1,256,512]{2,1,0:T(8,128)(2,1)S(1)}, u32[]{:S(2)}, u32[]{:S(2)}) collective-permute-start(bf16[1,256,512]{2,1,0:T(8,128)(2,1)S(1)} %reshape_transpose.13.rest_1_), channel_id=1, source_target_pairs={{0,4},{4,8},{8,12},{12,0},{1,5},{5,9},{9,13},{13,1},{2,6},{6,10},{... | collective-permute-start | bytes 786440 | tf_op jit(solution)/shard_map/ppermute | solution.py:381
  4.4 1.2 %copy-start = (bf16[128,1,4,2,512]{4,3,2,1,0:T(2,128)(2,1)S(1)}, bf16[128,1,4,2,512]{4,3,2,1,0:T(2,128)(2,1)}, u32[]{:S(2)}) copy-start(bf16[128,1,4,2,512]{4,3,2,1,0:T(2,128)(2,1)} %voltages_ref.1) | copy-start | bytes 3145732
  5.9 12.4 %copy-start.2 = (f32[1,4,2,8,512]{4,3,2,1,0:T(8,128)S(1)}, f32[1,4,2,8,512]{4,3,2,1,0:T(8,128)}, u32[]{:S(2)}) copy-start(f32[1,4,2,8,512]{4,3,2,1,0:T(8,128)} %start_ref.3) | copy-start | bytes 393220
  5.9 12.4 %collective-permute-start.1 = (bf16[1,256,512]{2,1,0:T(8,128)(2,1)S(1)}, bf16[1,256,512]{2,1,0:T(8,128)(2,1)S(1)}, u32[]{:S(2)}, u32[]{:S(2)}) collective-permute-start(bf16[1,256,512]{2,1,0:T(8,128)(2,1)S(1)} %reshape_transpose.14.rest_2_), channel_id=1, source_target_pairs={{0,12},{4,0},{8,4},{12,8},{1,13},{5,1},{9,5},{13,9},{2,14},{6,2},{... | collective-permute-start | bytes 786440 | tf_op jit(solution)/shard_map/ppermute | solution.py:381
  8.1 21.5 %collective-permute-start.2 = (bf16[1,256,512]{2,1,0:T(8,128)(2,1)S(1)}, bf16[1,256,512]{2,1,0:T(8,128)(2,1)S(1)}, u32[]{:S(2)}, u32[]{:S(2)}) collective-permute-start(bf16[1,256,512]{2,1,0:T(8,128)(2,1)S(1)} %reshape_transpose.15.rest_3_), channel_id=1, source_target_pairs={{0,8},{4,12},{8,0},{12,4},{1,9},{5,13},{9,1},{13,5},{2,10},{6,14},... | collective-permute-start | bytes 786440 | tf_op jit(solution)/shard_map/ppermute | solution.py:381
  10.5 19.0 %copy-start.3 = (s32[4]{0:T(128)S(1)}, s32[4]{0:T(128)}, u32[]{:S(2)}) copy-start(s32[4]{0:T(128)} %flags_ref.1) | copy-start | bytes 52
  10.6 19.0 %copy-start.4 = (s32[4]{0:T(128)S(1)}, s32[4]{0:T(128)}, u32[]{:S(2)}) copy-start(s32[4]{0:T(128)} %ranks_ref.1) | copy-start | bytes 52
  33.8 6.9 %collective-permute-start.3 = (f32[4,256,128]{2,1,0:T(8,128)S(1)}, f32[4,256,128]{2,1,0:T(8,128)S(1)}, u32[]{:S(2)}, u32[]{:S(2)}) collective-permute-start(f32[4,256,128]{2,1,0:T(8,128)S(1)} %get-tuple-element.25), channel_id=1, source_target_pairs={{0,1},{1,0},{2,3},{3,2},{4,5},{5,4},{6,7},{7,6},{8,9},{9,8},{10,11... | collective-permute-start | bytes 1572872 | tf_op jit(solution)/shard_map/ppermute | solution.py:434
  33.9 4.7 %collective-permute-start.9 = (bf16[1,16,384]{2,1,0:T(8,128)(2,1)S(1)}, bf16[1,16,384]{2,1,0:T(8,128)(2,1)S(1)}, u32[]{:S(2)}, u32[]{:S(2)}) collective-permute-start(bf16[1,16,384]{2,1,0:T(8,128)(2,1)S(1)} %get-tuple-element.30), channel_id=1, source_target_pairs={{0,8},{4,12},{8,0},{12,4},{1,9},{5,13},{9,1},{13,5},{2,10},{6,14},... | collective-permute-start | bytes 36872 | tf_op jit(solution)/shard_map/ppermute | solution.py:438
  34.0 5.6 %collective-permute-start.7 = (bf16[1,16,384]{2,1,0:T(8,128)(2,1)S(1)}, bf16[1,16,384]{2,1,0:T(8,128)(2,1)S(1)}, u32[]{:S(2)}, u32[]{:S(2)}) collective-permute-start(bf16[1,16,384]{2,1,0:T(8,128)(2,1)S(1)} %get-tuple-element.29), channel_id=1, source_target_pairs={{0,12},{4,8},{8,4},{12,0},{1,13},{5,9},{9,5},{13,1},{2,14},{6,10},... | collective-permute-start | bytes 36872 | tf_op jit(solution)/shard_map/ppermute | solution.py:438
  35.6 3.9 %collective-permute-start.4 = (bf16[1,16,384]{2,1,0:T(8,128)(2,1)S(1)}, bf16[1,16,384]{2,1,0:T(8,128)(2,1)S(1)}, u32[]{:S(2)}, u32[]{:S(2)}) collective-permute-start(bf16[1,16,384]{2,1,0:T(8,128)(2,1)S(1)} %get-tuple-element.26), channel_id=1, source_target_pairs={{0,4},{4,0},{8,12},{12,8},{1,5},{5,1},{9,13},{13,9},{2,6},{6,2},{1... | collective-permute-start | bytes 36872 | tf_op jit(solution)/shard_map/ppermute | solution.py:438
  37.4 2.9 %collective-permute-start.6 = (bf16[1,16,384]{2,1,0:T(8,128)(2,1)S(1)}, bf16[1,16,384]{2,1,0:T(8,128)(2,1)S(1)}, u32[]{:S(2)}, u32[]{:S(2)}) collective-permute-start(bf16[1,16,384]{2,1,0:T(8,128)(2,1)S(1)} %get-tuple-element.28.rest_0_), channel_id=1, source_target_pairs={{0,1},{1,0},{2,3},{3,2},{4,5},{5,4},{6,7},{7,6},{8,9},{9,8},{10,11... | collective-permute-start | bytes 36872 | tf_op jit(solution)/shard_map/ppermute | solution.py:439
  38.6 1.8 %collective-permute-start.10 = (bf16[1,16,384]{2,1,0:T(8,128)(2,1)S(1)}, bf16[1,16,384]{2,1,0:T(8,128)(2,1)S(1)}, u32[]{:S(2)}, u32[]{:S(2)}) collective-permute-start(bf16[1,16,384]{2,1,0:T(8,128)(2,1)S(1)} %collective-permute-done.9.rest_1_), channel_id=1, source_target_pairs={{0,1},{1,0},{2,3},{3,2},{4,5},{5,4},{6,7},{7,6},{8,9},{9,8},{10,11... | collective-permute-start | bytes 36872 | tf_op jit(solution)/shard_map/ppermute | solution.py:439
  39.5 1.2 %collective-permute-start.8 = (bf16[1,16,384]{2,1,0:T(8,128)(2,1)S(1)}, bf16[1,16,384]{2,1,0:T(8,128)(2,1)S(1)}, u32[]{:S(2)}, u32[]{:S(2)}) collective-permute-start(bf16[1,16,384]{2,1,0:T(8,128)(2,1)S(1)} %collective-permute-done.7.rest_2_), channel_id=1, source_target_pairs={{0,1},{1,0},{2,3},{3,2},{4,5},{5,4},{6,7},{7,6},{8,9},{9,8},{10,11... | collective-permute-start | bytes 36872 | tf_op jit(solution)/shard_map/ppermute | solution.py:439
  39.5 1.5 %collective-permute-start.5 = (bf16[1,16,384]{2,1,0:T(8,128)(2,1)S(1)}, bf16[1,16,384]{2,1,0:T(8,128)(2,1)S(1)}, u32[]{:S(2)}, u32[]{:S(2)}) collective-permute-start(bf16[1,16,384]{2,1,0:T(8,128)(2,1)S(1)} %collective-permute-done.4.rest_0_), channel_id=1, source_target_pairs={{0,1},{1,0},{2,3},{3,2},{4,5},{5,4},{6,7},{7,6},{8,9},{9,8},{10,11... | collective-permute-start | bytes 36872 | tf_op jit(solution)/shard_map/ppermute | solution.py:439

commit v20 on v19

--- a/solution.py
+++ b/solution.py
@@ -61,7 +61,7 @@
 
 
 def steps(tm):
-    return [0, *[by for by in range(1, tm) if by != tm // 2], tm // 2]
+    return [0, *[by for by in reversed(range(1, tm)) if by != tm // 2], tm // 2]
 
 
 def shifted(by):
@@ -432,7 +432,7 @@
 
     cores = [(0, 1), (1, 0)]
     theirs = lax.ppermute(other, "pol", cores)
-    order = [*range(2, tm), 1]
+    order = [*reversed(range(1, tm))]
     arrived = list(packets)
     for x in order:
         arrived[x] = lax.ppermute(packets[x], "tm", [(z, z ^ x) for z in range(tm)])

time: 42.3 us -> 44.7 us (1.057)
  starting transfers between devices: 10.4 us -> 11.7 us
  waiting for transfers between devices: 13 us -> 14 us
    ppermute x3, waiting for transfers between devices: 2.08 us -> 3.95 us  [local(): arrived[x] = lax.ppermute(packets[x], 'tm', [(z, z ^ x) for z in range(tm)])]
    ppermute x3, starting transfers between devices: 3.54 us -> 4.93 us  [local(): arrived[x] = lax.ppermute(packets[x], 'tm', [(z, z ^ x) for z in range(tm)])]
    ppermute x3, waiting for transfers between devices: 10.6 us -> 9.76 us  [local(): lax.ppermute(piece, 'tm', [(z, (z + by) % tm) for z in range(tm)])]
  transfers between devices with their start and end apart: 11 -> 11, of which waited for: 5 -> 5; matrix products, arithmetic and copies ran while one was open for 1% -> 1% of each run, Pallas kernels for 25% -> 24%
where the time goes in v20:
time: 44.7 us; the launch traced here: 44.5 us
  Pallas kernels  15.7 us (35%)
  waiting for transfers between devices  14 us (31%)
  starting transfers between devices  11.7 us (26%)
  local copies, waits for them, and re-layouts  2.85 us (6%)
    ppermute x3, waiting for transfers between devices, local(): lax.ppermute(piece, 'tm', [(z, (z + by) % tm) for z in range(tm)])  9.76 us
    pallas_call x1, Pallas kernels, local(): pl.pallas_call(functools.partial(raw_beams_kernel, tm, own), out_shape=[r...  6.85 us
    ppermute x3, starting transfers between devices, local(): lax.ppermute(piece, 'tm', [(z, (z + by) % tm) for z in range(tm)])  6.22 us
    ppermute x3, starting transfers between devices, local(): arrived[x] = lax.ppermute(packets[x], 'tm', [(z, z ^ x) for z in range(tm)])  4.93 us
    pallas_call x1, Pallas kernels, local(): pl.pallas_call(functools.partial(subspace_kernel, tm, own, factor), out_s...  4.22 us
    ppermute x3, waiting for transfers between devices, local(): arrived[x] = lax.ppermute(packets[x], 'tm', [(z, z ^ x) for z in range(tm)])  3.95 us
    pallas_call x1, Pallas kernels, local(): pl.pallas_call(early_kernel, out_shape=[jax.ShapeDtypeStruct((own, 2, wid...  1.52 us
    pallas_call x1, Pallas kernels, local(): pl.pallas_call(functools.partial(own_weights_kernel, own, chan_dev), out_...  1.26 us
  transfers between devices with their start and end apart: 11, of which 5 were waited for; matrix products, arithmetic and copies ran while one was open for 1% of the time, Pallas kernels for 24%

profile of v20, /device:TPU:0, one launch (start us, length us, event | category | flops | bytes accessed | tf_op | source)
XLA Modules:
  0.0 44.5 jit_solution(9500999458916538327)
XLA Ops:
  0.0 0.0 copy-start.1
  0.0 1.2 %constant_dynamic-slice_fusion = bf16[128,1,1,2,512]{4,3,2,1,0:T(2,128)(2,1)S(1)} fusion(bf16[128,1,4,2,512]{4,3,2,1,0:T(2,128)(2,1)} %voltages_ref.1, s32[]{:T(128)S(6)} %select_n.3), kind=kLoop, calls=%fused_computation | loop fusion | bytes 524292 | tf_op jit(solution)/shard_map/dynamic_slice | solution.py:377
  1.2 0.1 reshape_transpose.13.rest_1_
  1.3 5.1 %collective-permute-start = (bf16[1,256,512]{2,1,0:T(8,128)(2,1)S(1)}, bf16[1,256,512]{2,1,0:T(8,128)(2,1)S(1)}, u32[]{:S(2)}, u32[]{:S(2)}) collective-permute-start(bf16[1,256,512]{2,1,0:T(8,128)(2,1)S(1)} %reshape_transpose.13.rest_1_), channel_id=1, source_target_pairs={{0,12},{4,0},{8,4},{12,8},{1,13},{5,1},{9,5},{13,9},{2,14},{6,2},{... | collective-permute-start | bytes 786440 | tf_op jit(solution)/shard_map/ppermute | solution.py:381
  6.4 0.0 copy-start
  6.4 1.2 %copy-done = bf16[128,1,4,2,512]{4,3,2,1,0:T(2,128)(2,1)S(1)} copy-done((bf16[128,1,4,2,512]{4,3,2,1,0:T(2,128)(2,1)S(1)}, bf16[128,1,4,2,512]{4,3,2,1,0:T(2,128)(2,1)}, u32[]{:S(2)}) %copy-start) | copy-done | bytes 1048600
  7.6 0.2 shard_map.55
  7.8 0.1 reshape_transpose.14.rest_2_
  7.9 0.0 copy-start.2
  7.9 0.1 collective-permute-start.1
  8.0 0.1 reshape_transpose.15.rest_3_
  8.1 1.1 %collective-permute-start.2 = (bf16[1,256,512]{2,1,0:T(8,128)(2,1)S(1)}, bf16[1,256,512]{2,1,0:T(8,128)(2,1)S(1)}, u32[]{:S(2)}, u32[]{:S(2)}) collective-permute-start(bf16[1,256,512]{2,1,0:T(8,128)(2,1)S(1)} %reshape_transpose.15.rest_3_), channel_id=1, source_target_pairs={{0,8},{4,12},{8,0},{12,4},{1,9},{5,13},{9,1},{13,5},{2,10},{6,14},... | collective-permute-start | bytes 786440 | tf_op jit(solution)/shard_map/ppermute | solution.py:381
  9.2 0.1 reshape_transpose.12.rest_0_.refs_0_
  9.3 0.0 copy-done.1
  9.3 1.3 %shard_map.57.weights_ref = bf16[1,512,512]{2,1,0:T(8,128)(2,1)S(1)} custom-call(s32[256,512]{1,0:T(8,128)S(1)} %copy-done.1), custom_call_target="tpu_custom_call" | custom-call | flops 5242880 | bytes 1048576 | tf_op jit(solution)/shard_map/pallas_call | solution.py:396
  10.5 0.0 copy-start.3
  10.6 0.0 copy-start.4
  10.6 6.8 %shard_map.56 = (f32[4,256,128]{2,1,0:T(8,128)S(1)}, f32[4,256,128]{2,1,0:T(8,128)S(1)}) custom-call(s32[256,512]{1,0:T(8,128)S(1)} %copy-done.1, bf16[1,256,512]{2,1,0:T(8,128)(2,1)S(1)} %reshape_transpose.12.rest_0_.refs_0_, bf16[1,256,512]{2,1,0:T(8,128)(2,1)S(1)} %reshape_transpose.13.rest_1_, bf16[1,256,512]{2,1,0:T(8,128)(2,1)S(1)} %reshape_transpose.14.rest_2_, ...), custom_call_target="tpu_custom_call" | custom-call | flops 536870912 | bytes 2097152 | tf_op jit(solution)/shard_map/pallas_call | solution.py:386
  17.4 0.0 collective-permute-done.refs_1_
  17.4 2.0 %collective-permute-done.1.refs_2_ = bf16[1,256,512]{2,1,0:T(8,128)(2,1)S(1)} collective-permute-done((bf16[1,256,512]{2,1,0:T(8,128)(2,1)S(1)}, bf16[1,256,512]{2,1,0:T(8,128)(2,1)S(1)}, u32[]{:S(2)}, u32[]{:S(2)}) %collective-permute-start.1) | collective-permute-done | bytes 262176 | tf_op jit(solution)/shard_map/ppermute | solution.py:381
  19.5 0.0 copy-done.2
  19.5 1.5 %shard_map.58 = (f32[1,2,512,512]{3,2,1,0:T(8,128)S(1)}, f32[1,16,512]{2,1,0:T(8,128)S(1)}, bf16[1,512,768]{2,1,0:T(8,128)(2,1)S(1)}) custom-call(f32[1,4,2,8,512]{4,3,2,1,0:T(8,128)S(1)} %copy-done.2, bf16[1,256,512]{2,1,0:T(8,128)(2,1)S(1)} %reshape_transpose.12.rest_0_.refs_0_, bf16[1,256,512]{2,1,0:T(8,128)(2,1)S(1)} %collective-permute-done.refs_1_, ...), custom_call_target="tpu_custom_call" | custom-call | flops 805306368 | bytes 2097152 | tf_op jit(solution)/shard_map/pallas_call | solution.py:407
  21.0 7.7 %collective-permute-done.2.last_ref = bf16[1,256,512]{2,1,0:T(8,128)(2,1)S(1)} collective-permute-done((bf16[1,256,512]{2,1,0:T(8,128)(2,1)S(1)}, bf16[1,256,512]{2,1,0:T(8,128)(2,1)S(1)}, u32[]{:S(2)}, u32[]{:S(2)}) %collective-permute-start.2) | collective-permute-done | bytes 262176 | tf_op jit(solution)/shard_map/ppermute | solution.py:381
  28.7 0.0 copy-done.3
  28.7 0.0 copy-done.4
  28.7 4.2 %shard_map.59 = (f32[4,256,128]{2,1,0:T(8,128)S(1)}, bf16[1,16,384]{2,1,0:T(8,128)(2,1)S(1)}, bf16[1,16,384]{2,1,0:T(8,128)(2,1)S(1)}, bf16[1,16,384]{2,1,0:T(8,128)(2,1)S(1)}, bf16[1,16,384]{2,1,0:T(8,128)(2,1)S(1)}) custom-call(f32[4,256,128]{2,1,0:T(8,128)S(1)} %get-tuple-element.21.beams_ref, ...), custom_call_target="tpu_custom_call", output_to_operand_aliasing={{0}: (0, {})} | custom-call | flops 134217728 | bytes 2097152 | tf_op jit(solution)/shard_map/pallas_call | solution.py:421
  32.9 0.1 collective-permute-start.3
  33.0 4.3 %collective-permute-start.9 = (bf16[1,16,384]{2,1,0:T(8,128)(2,1)S(1)}, bf16[1,16,384]{2,1,0:T(8,128)(2,1)S(1)}, u32[]{:S(2)}, u32[]{:S(2)}) collective-permute-start(bf16[1,16,384]{2,1,0:T(8,128)(2,1)S(1)} %get-tuple-element.30), channel_id=1, source_target_pairs={{0,12},{4,8},{8,4},{12,0},{1,13},{5,9},{9,5},{13,1},{2,14},{6,10},... | collective-permute-start | bytes 36872 | tf_op jit(solution)/shard_map/ppermute | solution.py:438
  37.3 0.0 collective-permute-start.7
  37.3 0.6 %collective-permute-start.4 = (bf16[1,16,384]{2,1,0:T(8,128)(2,1)S(1)}, bf16[1,16,384]{2,1,0:T(8,128)(2,1)S(1)}, u32[]{:S(2)}, u32[]{:S(2)}) collective-permute-start(bf16[1,16,384]{2,1,0:T(8,128)(2,1)S(1)} %get-tuple-element.26), channel_id=1, source_target_pairs={{0,4},{4,0},{8,12},{12,8},{1,5},{5,1},{9,13},{13,9},{2,6},{6,2},{1... | collective-permute-start | bytes 36872 | tf_op jit(solution)/shard_map/ppermute | solution.py:438
  38.0 0.0 collective-permute-start.6
  38.0 1.0 %collective-permute-done.9.rest_1_ = bf16[1,16,384]{2,1,0:T(8,128)(2,1)S(1)} collective-permute-done((bf16[1,16,384]{2,1,0:T(8,128)(2,1)S(1)}, bf16[1,16,384]{2,1,0:T(8,128)(2,1)S(1)}, u32[]{:S(2)}, u32[]{:S(2)}) %collective-permute-start.9) | collective-permute-done | bytes 12320 | tf_op jit(solution)/shard_map/ppermute | solution.py:438
  39.0 0.0 collective-permute-start.10
  39.0 2.9 %collective-permute-done.7.rest_2_ = bf16[1,16,384]{2,1,0:T(8,128)(2,1)S(1)} collective-permute-done((bf16[1,16,384]{2,1,0:T(8,128)(2,1)S(1)}, bf16[1,16,384]{2,1,0:T(8,128)(2,1)S(1)}, u32[]{:S(2)}, u32[]{:S(2)}) %collective-permute-start.7) | collective-permute-done | bytes 12320 | tf_op jit(solution)/shard_map/ppermute | solution.py:438
  41.9 0.0 collective-permute-start.8
  41.9 0.0 collective-permute-done.4.rest_0_
  41.9 0.5 %collective-permute-start.5 = (bf16[1,16,384]{2,1,0:T(8,128)(2,1)S(1)}, bf16[1,16,384]{2,1,0:T(8,128)(2,1)S(1)}, u32[]{:S(2)}, u32[]{:S(2)}) collective-permute-start(bf16[1,16,384]{2,1,0:T(8,128)(2,1)S(1)} %collective-permute-done.4.rest_0_), channel_id=1, source_target_pairs={{0,1},{1,0},{2,3},{3,2},{4,5},{5,4},{6,7},{7,6},{8,9},{9,8},{10,11... | collective-permute-start | bytes 36872 | tf_op jit(solution)/shard_map/ppermute | solution.py:439
  42.4 0.3 shard_map.60.rest_4_
  42.8 0.0 collective-permute-done.6.rest_1_
  42.8 0.0 collective-permute-done.10.rest_3_
  42.8 0.3 collective-permute-done.8.rest_2_
  43.1 0.0 collective-permute-done.3.theirs_ref
  43.1 0.4 shard_map.61.power_ref
  43.5 0.0 collective-permute-done.5.packet_ref
  43.5 1.0 %shard_map.62 = f32[512,128]{1,0:T(8,128)} custom-call(f32[4,256,128]{2,1,0:T(8,128)S(1)} %collective-permute-done.3.theirs_ref, bf16[1,16,384]{2,1,0:T(8,128)(2,1)S(1)} %collective-permute-done.5.packet_ref, f32[4,128,128]{2,1,0:T(8,128)S(1)} %shard_map.61.power_ref), custom_call_target="tpu_custom_call" | custom-call | flops 131072 | bytes 786432 | tf_op jit(solution)/shard_map/pallas_call | solution.py:459
Async XLA Ops:
  0.0 9.3 %copy-start.1 = (s32[256,512]{1,0:T(8,128)S(1)}, s32[256,512]{1,0:T(8,128)}, u32[]{:S(2)}) copy-start(s32[256,512]{1,0:T(8,128)} %phase_ref.3) | copy-start | bytes 1572868
  1.3 16.1 %collective-permute-start = (bf16[1,256,512]{2,1,0:T(8,128)(2,1)S(1)}, bf16[1,256,512]{2,1,0:T(8,128)(2,1)S(1)}, u32[]{:S(2)}, u32[]{:S(2)}) collective-permute-start(bf16[1,256,512]{2,1,0:T(8,128)(2,1)S(1)} %reshape_transpose.13.rest_1_), channel_id=1, source_target_pairs={{0,12},{4,0},{8,4},{12,8},{1,13},{5,1},{9,5},{13,9},{2,14},{6,2},{... | collective-permute-start | bytes 786440 | tf_op jit(solution)/shard_map/ppermute | solution.py:381
  6.4 1.2 %copy-start = (bf16[128,1,4,2,512]{4,3,2,1,0:T(2,128)(2,1)S(1)}, bf16[128,1,4,2,512]{4,3,2,1,0:T(2,128)(2,1)}, u32[]{:S(2)}) copy-start(bf16[128,1,4,2,512]{4,3,2,1,0:T(2,128)(2,1)} %voltages_ref.1) | copy-start | bytes 3145732
  7.9 11.6 %copy-start.2 = (f32[1,4,2,8,512]{4,3,2,1,0:T(8,128)S(1)}, f32[1,4,2,8,512]{4,3,2,1,0:T(8,128)}, u32[]{:S(2)}) copy-start(f32[1,4,2,8,512]{4,3,2,1,0:T(8,128)} %start_ref.3) | copy-start | bytes 393220
  7.9 11.5 %collective-permute-start.1 = (bf16[1,256,512]{2,1,0:T(8,128)(2,1)S(1)}, bf16[1,256,512]{2,1,0:T(8,128)(2,1)S(1)}, u32[]{:S(2)}, u32[]{:S(2)}) collective-permute-start(bf16[1,256,512]{2,1,0:T(8,128)(2,1)S(1)} %reshape_transpose.14.rest_2_), channel_id=1, source_target_pairs={{0,4},{4,8},{8,12},{12,0},{1,5},{5,9},{9,13},{13,1},{2,6},{6,10},{... | collective-permute-start | bytes 786440 | tf_op jit(solution)/shard_map/ppermute | solution.py:381
  8.1 20.6 %collective-permute-start.2 = (bf16[1,256,512]{2,1,0:T(8,128)(2,1)S(1)}, bf16[1,256,512]{2,1,0:T(8,128)(2,1)S(1)}, u32[]{:S(2)}, u32[]{:S(2)}) collective-permute-start(bf16[1,256,512]{2,1,0:T(8,128)(2,1)S(1)} %reshape_transpose.15.rest_3_), channel_id=1, source_target_pairs={{0,8},{4,12},{8,0},{12,4},{1,9},{5,13},{9,1},{13,5},{2,10},{6,14},... | collective-permute-start | bytes 786440 | tf_op jit(solution)/shard_map/ppermute | solution.py:381
  10.5 18.2 %copy-start.3 = (s32[4]{0:T(128)S(1)}, s32[4]{0:T(128)}, u32[]{:S(2)}) copy-start(s32[4]{0:T(128)} %flags_ref.1) | copy-start | bytes 52
  10.6 18.2 %copy-start.4 = (s32[4]{0:T(128)S(1)}, s32[4]{0:T(128)}, u32[]{:S(2)}) copy-start(s32[4]{0:T(128)} %ranks_ref.1) | copy-start | bytes 52
  32.9 10.1 %collective-permute-start.3 = (f32[4,256,128]{2,1,0:T(8,128)S(1)}, f32[4,256,128]{2,1,0:T(8,128)S(1)}, u32[]{:S(2)}, u32[]{:S(2)}) collective-permute-start(f32[4,256,128]{2,1,0:T(8,128)S(1)} %get-tuple-element.25), channel_id=1, source_target_pairs={{0,1},{1,0},{2,3},{3,2},{4,5},{5,4},{6,7},{7,6},{8,9},{9,8},{10,11... | collective-permute-start | bytes 1572872 | tf_op jit(solution)/shard_map/ppermute | solution.py:434
  33.0 6.0 %collective-permute-start.9 = (bf16[1,16,384]{2,1,0:T(8,128)(2,1)S(1)}, bf16[1,16,384]{2,1,0:T(8,128)(2,1)S(1)}, u32[]{:S(2)}, u32[]{:S(2)}) collective-permute-start(bf16[1,16,384]{2,1,0:T(8,128)(2,1)S(1)} %get-tuple-element.30), channel_id=1, source_target_pairs={{0,12},{4,8},{8,4},{12,0},{1,13},{5,9},{9,5},{13,1},{2,14},{6,10},... | collective-permute-start | bytes 36872 | tf_op jit(solution)/shard_map/ppermute | solution.py:438
  37.3 4.6 %collective-permute-start.7 = (bf16[1,16,384]{2,1,0:T(8,128)(2,1)S(1)}, bf16[1,16,384]{2,1,0:T(8,128)(2,1)S(1)}, u32[]{:S(2)}, u32[]{:S(2)}) collective-permute-start(bf16[1,16,384]{2,1,0:T(8,128)(2,1)S(1)} %get-tuple-element.29), channel_id=1, source_target_pairs={{0,8},{4,12},{8,0},{12,4},{1,9},{5,13},{9,1},{13,5},{2,10},{6,14},... | collective-permute-start | bytes 36872 | tf_op jit(solution)/shard_map/ppermute | solution.py:438
  37.3 4.6 %collective-permute-start.4 = (bf16[1,16,384]{2,1,0:T(8,128)(2,1)S(1)}, bf16[1,16,384]{2,1,0:T(8,128)(2,1)S(1)}, u32[]{:S(2)}, u32[]{:S(2)}) collective-permute-start(bf16[1,16,384]{2,1,0:T(8,128)(2,1)S(1)} %get-tuple-element.26), channel_id=1, source_target_pairs={{0,4},{4,0},{8,12},{12,8},{1,5},{5,1},{9,13},{13,9},{2,6},{6,2},{1... | collective-permute-start | bytes 36872 | tf_op jit(solution)/shard_map/ppermute | solution.py:438
  38.0 4.8 %collective-permute-start.6 = (bf16[1,16,384]{2,1,0:T(8,128)(2,1)S(1)}, bf16[1,16,384]{2,1,0:T(8,128)(2,1)S(1)}, u32[]{:S(2)}, u32[]{:S(2)}) collective-permute-start(bf16[1,16,384]{2,1,0:T(8,128)(2,1)S(1)} %get-tuple-element.28.rest_0_), channel_id=1, source_target_pairs={{0,1},{1,0},{2,3},{3,2},{4,5},{5,4},{6,7},{7,6},{8,9},{9,8},{10,11... | collective-permute-start | bytes 36872 | tf_op jit(solution)/shard_map/ppermute | solution.py:439
  39.0 3.8 %collective-permute-start.10 = (bf16[1,16,384]{2,1,0:T(8,128)(2,1)S(1)}, bf16[1,16,384]{2,1,0:T(8,128)(2,1)S(1)}, u32[]{:S(2)}, u32[]{:S(2)}) collective-permute-start(bf16[1,16,384]{2,1,0:T(8,128)(2,1)S(1)} %collective-permute-done.9.rest_1_), channel_id=1, source_target_pairs={{0,1},{1,0},{2,3},{3,2},{4,5},{5,4},{6,7},{7,6},{8,9},{9,8},{10,11... | collective-permute-start | bytes 36872 | tf_op jit(solution)/shard_map/ppermute | solution.py:439
  41.9 1.2 %collective-permute-start.8 = (bf16[1,16,384]{2,1,0:T(8,128)(2,1)S(1)}, bf16[1,16,384]{2,1,0:T(8,128)(2,1)S(1)}, u32[]{:S(2)}, u32[]{:S(2)}) collective-permute-start(bf16[1,16,384]{2,1,0:T(8,128)(2,1)S(1)} %collective-permute-done.7.rest_2_), channel_id=1, source_target_pairs={{0,1},{1,0},{2,3},{3,2},{4,5},{5,4},{6,7},{7,6},{8,9},{9,8},{10,11... | collective-permute-start | bytes 36872 | tf_op jit(solution)/shard_map/ppermute | solution.py:439
  41.9 1.5 %collective-permute-start.5 = (bf16[1,16,384]{2,1,0:T(8,128)(2,1)S(1)}, bf16[1,16,384]{2,1,0:T(8,128)(2,1)S(1)}, u32[]{:S(2)}, u32[]{:S(2)}) collective-permute-start(bf16[1,16,384]{2,1,0:T(8,128)(2,1)S(1)} %collective-permute-done.4.rest_0_), channel_id=1, source_target_pairs={{0,1},{1,0},{2,3},{3,2},{4,5},{5,4},{6,7},{7,6},{8,9},{9,8},{10,11... | collective-permute-start | bytes 36872 | tf_op jit(solution)/shard_map/ppermute | solution.py:439

commit v21 on v19

--- a/solution.py
+++ b/solution.py
@@ -17,7 +17,7 @@
 NN = (((1,), (0,)), ((), ()))
 TN = (((0,), (0,)), ((), ()))
 VMEM_LIMIT = 48 * 1024 * 1024
-CHUNK = 128
+CHUNK = 256
 LEAST_PIVOT = 1e-4
 
 

time: 42.3 us -> 42.3 us (level)
  no operation moved by 1% of the time
where the time goes in v21:
time: 42.3 us; the launch traced here: 42.1 us
  Pallas kernels  15.7 us (37%)
  waiting for transfers between devices  13 us (31%)
  starting transfers between devices  10.4 us (25%)
  local copies, waits for them, and re-layouts  2.85 us (7%)
    ppermute x3, waiting for transfers between devices, local(): lax.ppermute(piece, 'tm', [(z, (z + by) % tm) for z in range(tm)])  10.6 us
    pallas_call x1, Pallas kernels, local(): pl.pallas_call(functools.partial(raw_beams_kernel, tm, own), out_shape=[r...  6.85 us
    ppermute x3, starting transfers between devices, local(): lax.ppermute(piece, 'tm', [(z, (z + by) % tm) for z in range(tm)])  6.23 us
    pallas_call x1, Pallas kernels, local(): pl.pallas_call(functools.partial(subspace_kernel, tm, own, factor), out_s...  4.22 us
    ppermute x3, starting transfers between devices, local(): arrived[x] = lax.ppermute(packets[x], 'tm', [(z, z ^ x) for z in range(tm)])  3.54 us
    ppermute x3, waiting for transfers between devices, local(): arrived[x] = lax.ppermute(packets[x], 'tm', [(z, z ^ x) for z in range(tm)])  2.08 us
    pallas_call x1, Pallas kernels, local(): pl.pallas_call(early_kernel, out_shape=[jax.ShapeDtypeStruct((own, 2, wid...  1.51 us
    pallas_call x1, Pallas kernels, local(): pl.pallas_call(functools.partial(own_weights_kernel, own, chan_dev), out_...  1.26 us
  transfers between devices with their start and end apart: 11, of which 5 were waited for; matrix products, arithmetic and copies ran while one was open for 1% of the time, Pallas kernels for 25%

profile of v21, /device:TPU:0, one launch (start us, length us, event | category | flops | bytes accessed | tf_op | source)
XLA Modules:
  0.0 42.1 jit_solution(623051957243319380)
XLA Ops:
  0.0 0.0 copy-start.1
  0.0 1.2 %constant_dynamic-slice_fusion = bf16[128,1,1,2,512]{4,3,2,1,0:T(2,128)(2,1)S(1)} fusion(bf16[128,1,4,2,512]{4,3,2,1,0:T(2,128)(2,1)} %voltages_ref.1, s32[]{:T(128)S(6)} %select_n.3), kind=kLoop, calls=%fused_computation | loop fusion | bytes 524292 | tf_op jit(solution)/shard_map/dynamic_slice | solution.py:377
  1.2 0.1 reshape_transpose.13.rest_1_
  1.3 3.1 %collective-permute-start = (bf16[1,256,512]{2,1,0:T(8,128)(2,1)S(1)}, bf16[1,256,512]{2,1,0:T(8,128)(2,1)S(1)}, u32[]{:S(2)}, u32[]{:S(2)}) collective-permute-start(bf16[1,256,512]{2,1,0:T(8,128)(2,1)S(1)} %reshape_transpose.13.rest_1_), channel_id=1, source_target_pairs={{0,4},{4,8},{8,12},{12,0},{1,5},{5,9},{9,13},{13,1},{2,6},{6,10},{... | collective-permute-start | bytes 786440 | tf_op jit(solution)/shard_map/ppermute | solution.py:381
  4.4 0.0 copy-start
  4.4 1.2 %copy-done = bf16[128,1,4,2,512]{4,3,2,1,0:T(2,128)(2,1)S(1)} copy-done((bf16[128,1,4,2,512]{4,3,2,1,0:T(2,128)(2,1)S(1)}, bf16[128,1,4,2,512]{4,3,2,1,0:T(2,128)(2,1)}, u32[]{:S(2)}) %copy-start) | copy-done | bytes 1048600
  5.6 0.2 shard_map.55
  5.8 0.1 reshape_transpose.14.rest_2_
  5.9 0.0 copy-start.2
  5.9 2.1 %collective-permute-start.1 = (bf16[1,256,512]{2,1,0:T(8,128)(2,1)S(1)}, bf16[1,256,512]{2,1,0:T(8,128)(2,1)S(1)}, u32[]{:S(2)}, u32[]{:S(2)}) collective-permute-start(bf16[1,256,512]{2,1,0:T(8,128)(2,1)S(1)} %reshape_transpose.14.rest_2_), channel_id=1, source_target_pairs={{0,12},{4,0},{8,4},{12,8},{1,13},{5,1},{9,5},{13,9},{2,14},{6,2},{... | collective-permute-start | bytes 786440 | tf_op jit(solution)/shard_map/ppermute | solution.py:381
  8.0 0.1 reshape_transpose.15.rest_3_
  8.1 1.1 %collective-permute-start.2 = (bf16[1,256,512]{2,1,0:T(8,128)(2,1)S(1)}, bf16[1,256,512]{2,1,0:T(8,128)(2,1)S(1)}, u32[]{:S(2)}, u32[]{:S(2)}) collective-permute-start(bf16[1,256,512]{2,1,0:T(8,128)(2,1)S(1)} %reshape_transpose.15.rest_3_), channel_id=1, source_target_pairs={{0,8},{4,12},{8,0},{12,4},{1,9},{5,13},{9,1},{13,5},{2,10},{6,14},... | collective-permute-start | bytes 786440 | tf_op jit(solution)/shard_map/ppermute | solution.py:381
  9.2 0.1 reshape_transpose.12.rest_0_.refs_0_
  9.3 0.0 copy-done.1
  9.3 1.3 %shard_map.57.weights_ref = bf16[1,512,512]{2,1,0:T(8,128)(2,1)S(1)} custom-call(s32[256,512]{1,0:T(8,128)S(1)} %copy-done.1), custom_call_target="tpu_custom_call" | custom-call | flops 5242880 | bytes 1048576 | tf_op jit(solution)/shard_map/pallas_call | solution.py:396
  10.5 0.0 copy-start.3
  10.6 0.0 copy-start.4
  10.6 6.8 %shard_map.56 = (f32[4,256,128]{2,1,0:T(8,128)S(1)}, f32[4,256,128]{2,1,0:T(8,128)S(1)}) custom-call(s32[256,512]{1,0:T(8,128)S(1)} %copy-done.1, bf16[1,256,512]{2,1,0:T(8,128)(2,1)S(1)} %reshape_transpose.12.rest_0_.refs_0_, bf16[1,256,512]{2,1,0:T(8,128)(2,1)S(1)} %reshape_transpose.13.rest_1_, bf16[1,256,512]{2,1,0:T(8,128)(2,1)S(1)} %reshape_transpose.14.rest_2_, ...), custom_call_target="tpu_custom_call" | custom-call | flops 536870912 | bytes 2097152 | tf_op jit(solution)/shard_map/pallas_call | solution.py:386
  17.4 0.0 collective-permute-done.refs_1_
  17.4 0.9 %collective-permute-done.1.refs_2_ = bf16[1,256,512]{2,1,0:T(8,128)(2,1)S(1)} collective-permute-done((bf16[1,256,512]{2,1,0:T(8,128)(2,1)S(1)}, bf16[1,256,512]{2,1,0:T(8,128)(2,1)S(1)}, u32[]{:S(2)}, u32[]{:S(2)}) %collective-permute-start.1) | collective-permute-done | bytes 262176 | tf_op jit(solution)/shard_map/ppermute | solution.py:381
  18.3 0.0 copy-done.2
  18.3 1.5 %shard_map.58 = (f32[1,2,512,512]{3,2,1,0:T(8,128)S(1)}, f32[1,16,512]{2,1,0:T(8,128)S(1)}, bf16[1,512,768]{2,1,0:T(8,128)(2,1)S(1)}) custom-call(f32[1,4,2,8,512]{4,3,2,1,0:T(8,128)S(1)} %copy-done.2, bf16[1,256,512]{2,1,0:T(8,128)(2,1)S(1)} %reshape_transpose.12.rest_0_.refs_0_, bf16[1,256,512]{2,1,0:T(8,128)(2,1)S(1)} %collective-permute-done.refs_1_, ...), custom_call_target="tpu_custom_call" | custom-call | flops 805306368 | bytes 2097152 | tf_op jit(solution)/shard_map/pallas_call | solution.py:407
  19.8 9.7 %collective-permute-done.2.last_ref = bf16[1,256,512]{2,1,0:T(8,128)(2,1)S(1)} collective-permute-done((bf16[1,256,512]{2,1,0:T(8,128)(2,1)S(1)}, bf16[1,256,512]{2,1,0:T(8,128)(2,1)S(1)}, u32[]{:S(2)}, u32[]{:S(2)}) %collective-permute-start.2) | collective-permute-done | bytes 262176 | tf_op jit(solution)/shard_map/ppermute | solution.py:381
  29.6 0.0 copy-done.3
  29.6 0.0 copy-done.4
  29.6 4.2 %shard_map.59 = (f32[4,256,128]{2,1,0:T(8,128)S(1)}, bf16[1,16,384]{2,1,0:T(8,128)(2,1)S(1)}, bf16[1,16,384]{2,1,0:T(8,128)(2,1)S(1)}, bf16[1,16,384]{2,1,0:T(8,128)(2,1)S(1)}, bf16[1,16,384]{2,1,0:T(8,128)(2,1)S(1)}) custom-call(f32[4,256,128]{2,1,0:T(8,128)S(1)} %get-tuple-element.21.beams_ref, ...), custom_call_target="tpu_custom_call", output_to_operand_aliasing={{0}: (0, {})} | custom-call | flops 134217728 | bytes 2097152 | tf_op jit(solution)/shard_map/pallas_call | solution.py:421
  33.8 0.1 collective-permute-start.3
  33.9 0.1 collective-permute-start.9
  34.0 1.7 %collective-permute-start.7 = (bf16[1,16,384]{2,1,0:T(8,128)(2,1)S(1)}, bf16[1,16,384]{2,1,0:T(8,128)(2,1)S(1)}, u32[]{:S(2)}, u32[]{:S(2)}) collective-permute-start(bf16[1,16,384]{2,1,0:T(8,128)(2,1)S(1)} %get-tuple-element.29), channel_id=1, source_target_pairs={{0,12},{4,8},{8,4},{12,0},{1,13},{5,9},{9,5},{13,1},{2,14},{6,10},... | collective-permute-start | bytes 36872 | tf_op jit(solution)/shard_map/ppermute | solution.py:438
  35.6 1.8 %collective-permute-start.4 = (bf16[1,16,384]{2,1,0:T(8,128)(2,1)S(1)}, bf16[1,16,384]{2,1,0:T(8,128)(2,1)S(1)}, u32[]{:S(2)}, u32[]{:S(2)}) collective-permute-start(bf16[1,16,384]{2,1,0:T(8,128)(2,1)S(1)} %get-tuple-element.26), channel_id=1, source_target_pairs={{0,4},{4,0},{8,12},{12,8},{1,5},{5,1},{9,13},{13,9},{2,6},{6,2},{1... | collective-permute-start | bytes 36872 | tf_op jit(solution)/shard_map/ppermute | solution.py:438
  37.4 0.0 collective-permute-start.6
  37.4 1.2 %collective-permute-done.9.rest_1_ = bf16[1,16,384]{2,1,0:T(8,128)(2,1)S(1)} collective-permute-done((bf16[1,16,384]{2,1,0:T(8,128)(2,1)S(1)}, bf16[1,16,384]{2,1,0:T(8,128)(2,1)S(1)}, u32[]{:S(2)}, u32[]{:S(2)}) %collective-permute-start.9) | collective-permute-done | bytes 12320 | tf_op jit(solution)/shard_map/ppermute | solution.py:438
  38.6 0.0 collective-permute-start.10
  38.6 0.9 %collective-permute-done.7.rest_2_ = bf16[1,16,384]{2,1,0:T(8,128)(2,1)S(1)} collective-permute-done((bf16[1,16,384]{2,1,0:T(8,128)(2,1)S(1)}, bf16[1,16,384]{2,1,0:T(8,128)(2,1)S(1)}, u32[]{:S(2)}, u32[]{:S(2)}) %collective-permute-start.7) | collective-permute-done | bytes 12320 | tf_op jit(solution)/shard_map/ppermute | solution.py:438
  39.5 0.0 collective-permute-start.8
  39.5 0.0 collective-permute-done.4.rest_0_
  39.5 0.5 %collective-permute-start.5 = (bf16[1,16,384]{2,1,0:T(8,128)(2,1)S(1)}, bf16[1,16,384]{2,1,0:T(8,128)(2,1)S(1)}, u32[]{:S(2)}, u32[]{:S(2)}) collective-permute-start(bf16[1,16,384]{2,1,0:T(8,128)(2,1)S(1)} %collective-permute-done.4.rest_0_), channel_id=1, source_target_pairs={{0,1},{1,0},{2,3},{3,2},{4,5},{5,4},{6,7},{7,6},{8,9},{9,8},{10,11... | collective-permute-start | bytes 36872 | tf_op jit(solution)/shard_map/ppermute | solution.py:439
  40.0 0.3 shard_map.60.rest_4_
  40.4 0.0 collective-permute-done.6.rest_1_
  40.4 0.0 collective-permute-done.10.rest_3_
  40.4 0.3 collective-permute-done.8.rest_2_
  40.7 0.0 collective-permute-done.3.theirs_ref
  40.7 0.4 shard_map.61.power_ref
  41.1 0.0 collective-permute-done.5.packet_ref
  41.1 1.0 %shard_map.62 = f32[512,128]{1,0:T(8,128)} custom-call(f32[4,256,128]{2,1,0:T(8,128)S(1)} %collective-permute-done.3.theirs_ref, bf16[1,16,384]{2,1,0:T(8,128)(2,1)S(1)} %collective-permute-done.5.packet_ref, f32[4,128,128]{2,1,0:T(8,128)S(1)} %shard_map.61.power_ref), custom_call_target="tpu_custom_call" | custom-call | flops 131072 | bytes 786432 | tf_op jit(solution)/shard_map/pallas_call | solution.py:459
Async XLA Ops:
  0.0 9.3 %copy-start.1 = (s32[256,512]{1,0:T(8,128)S(1)}, s32[256,512]{1,0:T(8,128)}, u32[]{:S(2)}) copy-start(s32[256,512]{1,0:T(8,128)} %phase_ref.3) | copy-start | bytes 1572868
  1.3 16.1 %collective-permute-start = (bf16[1,256,512]{2,1,0:T(8,128)(2,1)S(1)}, bf16[1,256,512]{2,1,0:T(8,128)(2,1)S(1)}, u32[]{:S(2)}, u32[]{:S(2)}) collective-permute-start(bf16[1,256,512]{2,1,0:T(8,128)(2,1)S(1)} %reshape_transpose.13.rest_1_), channel_id=1, source_target_pairs={{0,4},{4,8},{8,12},{12,0},{1,5},{5,9},{9,13},{13,1},{2,6},{6,10},{... | collective-permute-start | bytes 786440 | tf_op jit(solution)/shard_map/ppermute | solution.py:381
  4.4 1.2 %copy-start = (bf16[128,1,4,2,512]{4,3,2,1,0:T(2,128)(2,1)S(1)}, bf16[128,1,4,2,512]{4,3,2,1,0:T(2,128)(2,1)}, u32[]{:S(2)}) copy-start(bf16[128,1,4,2,512]{4,3,2,1,0:T(2,128)(2,1)} %voltages_ref.1) | copy-start | bytes 3145732
  5.9 12.4 %copy-start.2 = (f32[1,4,2,8,512]{4,3,2,1,0:T(8,128)S(1)}, f32[1,4,2,8,512]{4,3,2,1,0:T(8,128)}, u32[]{:S(2)}) copy-start(f32[1,4,2,8,512]{4,3,2,1,0:T(8,128)} %start_ref.3) | copy-start | bytes 393220
  5.9 12.4 %collective-permute-start.1 = (bf16[1,256,512]{2,1,0:T(8,128)(2,1)S(1)}, bf16[1,256,512]{2,1,0:T(8,128)(2,1)S(1)}, u32[]{:S(2)}, u32[]{:S(2)}) collective-permute-start(bf16[1,256,512]{2,1,0:T(8,128)(2,1)S(1)} %reshape_transpose.14.rest_2_), channel_id=1, source_target_pairs={{0,12},{4,0},{8,4},{12,8},{1,13},{5,1},{9,5},{13,9},{2,14},{6,2},{... | collective-permute-start | bytes 786440 | tf_op jit(solution)/shard_map/ppermute | solution.py:381
  8.1 21.5 %collective-permute-start.2 = (bf16[1,256,512]{2,1,0:T(8,128)(2,1)S(1)}, bf16[1,256,512]{2,1,0:T(8,128)(2,1)S(1)}, u32[]{:S(2)}, u32[]{:S(2)}) collective-permute-start(bf16[1,256,512]{2,1,0:T(8,128)(2,1)S(1)} %reshape_transpose.15.rest_3_), channel_id=1, source_target_pairs={{0,8},{4,12},{8,0},{12,4},{1,9},{5,13},{9,1},{13,5},{2,10},{6,14},... | collective-permute-start | bytes 786440 | tf_op jit(solution)/shard_map/ppermute | solution.py:381
  10.5 19.0 %copy-start.3 = (s32[4]{0:T(128)S(1)}, s32[4]{0:T(128)}, u32[]{:S(2)}) copy-start(s32[4]{0:T(128)} %flags_ref.1) | copy-start | bytes 52
  10.6 19.0 %copy-start.4 = (s32[4]{0:T(128)S(1)}, s32[4]{0:T(128)}, u32[]{:S(2)}) copy-start(s32[4]{0:T(128)} %ranks_ref.1) | copy-start | bytes 52
  33.8 6.9 %collective-permute-start.3 = (f32[4,256,128]{2,1,0:T(8,128)S(1)}, f32[4,256,128]{2,1,0:T(8,128)S(1)}, u32[]{:S(2)}, u32[]{:S(2)}) collective-permute-start(f32[4,256,128]{2,1,0:T(8,128)S(1)} %get-tuple-element.25), channel_id=1, source_target_pairs={{0,1},{1,0},{2,3},{3,2},{4,5},{5,4},{6,7},{7,6},{8,9},{9,8},{10,11... | collective-permute-start | bytes 1572872 | tf_op jit(solution)/shard_map/ppermute | solution.py:434
  33.9 4.7 %collective-permute-start.9 = (bf16[1,16,384]{2,1,0:T(8,128)(2,1)S(1)}, bf16[1,16,384]{2,1,0:T(8,128)(2,1)S(1)}, u32[]{:S(2)}, u32[]{:S(2)}) collective-permute-start(bf16[1,16,384]{2,1,0:T(8,128)(2,1)S(1)} %get-tuple-element.30), channel_id=1, source_target_pairs={{0,8},{4,12},{8,0},{12,4},{1,9},{5,13},{9,1},{13,5},{2,10},{6,14},... | collective-permute-start | bytes 36872 | tf_op jit(solution)/shard_map/ppermute | solution.py:438
  34.0 5.6 %collective-permute-start.7 = (bf16[1,16,384]{2,1,0:T(8,128)(2,1)S(1)}, bf16[1,16,384]{2,1,0:T(8,128)(2,1)S(1)}, u32[]{:S(2)}, u32[]{:S(2)}) collective-permute-start(bf16[1,16,384]{2,1,0:T(8,128)(2,1)S(1)} %get-tuple-element.29), channel_id=1, source_target_pairs={{0,12},{4,8},{8,4},{12,0},{1,13},{5,9},{9,5},{13,1},{2,14},{6,10},... | collective-permute-start | bytes 36872 | tf_op jit(solution)/shard_map/ppermute | solution.py:438
  35.6 3.9 %collective-permute-start.4 = (bf16[1,16,384]{2,1,0:T(8,128)(2,1)S(1)}, bf16[1,16,384]{2,1,0:T(8,128)(2,1)S(1)}, u32[]{:S(2)}, u32[]{:S(2)}) collective-permute-start(bf16[1,16,384]{2,1,0:T(8,128)(2,1)S(1)} %get-tuple-element.26), channel_id=1, source_target_pairs={{0,4},{4,0},{8,12},{12,8},{1,5},{5,1},{9,13},{13,9},{2,6},{6,2},{1... | collective-permute-start | bytes 36872 | tf_op jit(solution)/shard_map/ppermute | solution.py:438
  37.4 2.9 %collective-permute-start.6 = (bf16[1,16,384]{2,1,0:T(8,128)(2,1)S(1)}, bf16[1,16,384]{2,1,0:T(8,128)(2,1)S(1)}, u32[]{:S(2)}, u32[]{:S(2)}) collective-permute-start(bf16[1,16,384]{2,1,0:T(8,128)(2,1)S(1)} %get-tuple-element.28.rest_0_), channel_id=1, source_target_pairs={{0,1},{1,0},{2,3},{3,2},{4,5},{5,4},{6,7},{7,6},{8,9},{9,8},{10,11... | collective-permute-start | bytes 36872 | tf_op jit(solution)/shard_map/ppermute | solution.py:439
  38.6 1.8 %collective-permute-start.10 = (bf16[1,16,384]{2,1,0:T(8,128)(2,1)S(1)}, bf16[1,16,384]{2,1,0:T(8,128)(2,1)S(1)}, u32[]{:S(2)}, u32[]{:S(2)}) collective-permute-start(bf16[1,16,384]{2,1,0:T(8,128)(2,1)S(1)} %collective-permute-done.9.rest_1_), channel_id=1, source_target_pairs={{0,1},{1,0},{2,3},{3,2},{4,5},{5,4},{6,7},{7,6},{8,9},{9,8},{10,11... | collective-permute-start | bytes 36872 | tf_op jit(solution)/shard_map/ppermute | solution.py:439
  39.5 1.2 %collective-permute-start.8 = (bf16[1,16,384]{2,1,0:T(8,128)(2,1)S(1)}, bf16[1,16,384]{2,1,0:T(8,128)(2,1)S(1)}, u32[]{:S(2)}, u32[]{:S(2)}) collective-permute-start(bf16[1,16,384]{2,1,0:T(8,128)(2,1)S(1)} %collective-permute-done.7.rest_2_), channel_id=1, source_target_pairs={{0,1},{1,0},{2,3},{3,2},{4,5},{5,4},{6,7},{7,6},{8,9},{9,8},{10,11... | collective-permute-start | bytes 36872 | tf_op jit(solution)/shard_map/ppermute | solution.py:439
  39.5 1.5 %collective-permute-start.5 = (bf16[1,16,384]{2,1,0:T(8,128)(2,1)S(1)}, bf16[1,16,384]{2,1,0:T(8,128)(2,1)S(1)}, u32[]{:S(2)}, u32[]{:S(2)}) collective-permute-start(bf16[1,16,384]{2,1,0:T(8,128)(2,1)S(1)} %collective-permute-done.4.rest_0_), channel_id=1, source_target_pairs={{0,1},{1,0},{2,3},{3,2},{4,5},{5,4},{6,7},{7,6},{8,9},{9,8},{10,11... | collective-permute-start | bytes 36872 | tf_op jit(solution)/shard_map/ppermute | solution.py:439

commit v22 on v19

--- a/solution.py
+++ b/solution.py
@@ -337,11 +337,13 @@
             power_ref[chan] = power_ref[chan] + nulled_power(theirs_ref[chan], ref.at[o], squares)
 
 
-def last_kernel(own, x, theirs_ref, packet_ref, power_ref, out_ref, powers, squares):
+def last_kernel(own, xs, theirs_ref, *rest):
+    packets, (power_ref, out_ref, powers, squares) = rest[: len(xs)], rest[len(xs) :]
     powers[...] = power_ref[...]
-    for o in range(own):
-        chan = (lax.axis_index("tm") ^ x) * own + o
-        powers[chan] = power_ref[chan] + nulled_power(theirs_ref[chan], packet_ref.at[o], squares)
+    for x, ref in zip(xs, packets):
+        for o in range(own):
+            chan = (lax.axis_index("tm") ^ x) * own + o
+            powers[chan] = power_ref[chan] + nulled_power(theirs_ref[chan], ref.at[o], squares)
     channels, samples = powers.shape[:2]
     for chan in range(channels):
         out_ref[pl.ds(chan, samples, channels), :] = powers[chan]
@@ -439,7 +441,7 @@
     swapped = [lax.ppermute(packet, "pol", cores) for packet in arrived]
 
     shape = jax.ShapeDtypeStruct((chan_dev, samples, half), F32)
-    groups = [([0, *order[:-1]], []), (order[-1:], [0, *order[-2::-1]])]
+    groups = [([0, *order], [0, *order[:-2]])]
     power = []
     for xs, later_xs in groups:
         used = [arrived[x] for x in xs] + [swapped[x] for x in later_xs]
@@ -457,14 +459,14 @@
         ]
 
     rows_out = pl.pallas_call(
-        functools.partial(last_kernel, own, order[-1]),
+        functools.partial(last_kernel, own, order[-2:]),
         out_shape=jax.ShapeDtypeStruct((samples * chan_dev, half), F32),
-        in_specs=[whole] * 3,
+        in_specs=[whole] * 4,
         out_specs=whole,
         scratch_shapes=[pltpu.VMEM((chan_dev, samples, half), F32), pltpu.VMEM((rows, half), F32)],
         compiler_params=params,
         cost_estimate=cost(chan_dev * samples * half, 12 * chan_dev * samples * half),
-    )(theirs, swapped[order[-1]], *power)
+    )(theirs, *[swapped[x] for x in order[-2:]], *power)
     return rows_out.reshape(samples, chan_dev, half)
 
 

time: 42.3 us -> 42.1 us (level)
  transfers between devices with their start and end apart: 11 -> 11, of which waited for: 5 -> 6; matrix products, arithmetic and copies ran while one was open for 1% -> 1% of each run, Pallas kernels for 25% -> 24%
where the time goes in v22:
time: 42.1 us; the launch traced here: 41.9 us
  Pallas kernels  15.5 us (37%)
  waiting for transfers between devices  13.1 us (31%)
  starting transfers between devices  10.4 us (25%)
  local copies, waits for them, and re-layouts  2.85 us (7%)
    ppermute x3, waiting for transfers between devices, local(): lax.ppermute(piece, 'tm', [(z, (z + by) % tm) for z in range(tm)])  10.6 us
    pallas_call x1, Pallas kernels, local(): pl.pallas_call(functools.partial(raw_beams_kernel, tm, own), out_shape=[r...  6.85 us
    ppermute x3, starting transfers between devices, local(): lax.ppermute(piece, 'tm', [(z, (z + by) % tm) for z in range(tm)])  6.23 us
    pallas_call x1, Pallas kernels, local(): pl.pallas_call(functools.partial(subspace_kernel, tm, own, factor), out_s...  4.22 us
    ppermute x3, starting transfers between devices, local(): arrived[x] = lax.ppermute(packets[x], 'tm', [(z, z ^ x) for z in range(tm)])  3.54 us
    ppermute x3, waiting for transfers between devices, local(): arrived[x] = lax.ppermute(packets[x], 'tm', [(z, z ^ x) for z in range(tm)])  2.08 us
    pallas_call x1, Pallas kernels, local(): pl.pallas_call(early_kernel, out_shape=[jax.ShapeDtypeStruct((own, 2, wid...  1.51 us
    pallas_call x1, Pallas kernels, local(): pl.pallas_call(functools.partial(own_weights_kernel, own, chan_dev), out_...  1.26 us
  transfers between devices with their start and end apart: 11, of which 6 were waited for; matrix products, arithmetic and copies ran while one was open for 1% of the time, Pallas kernels for 24%

profile of v22, /device:TPU:0, one launch (start us, length us, event | category | flops | bytes accessed | tf_op | source)
XLA Modules:
  0.0 41.9 jit_solution(10281802993461663635)
XLA Ops:
  0.0 0.0 copy-start.1
  0.0 1.2 %constant_dynamic-slice_fusion = bf16[128,1,1,2,512]{4,3,2,1,0:T(2,128)(2,1)S(1)} fusion(bf16[128,1,4,2,512]{4,3,2,1,0:T(2,128)(2,1)} %voltages_ref.1, s32[]{:T(128)S(6)} %select_n.3), kind=kLoop, calls=%fused_computation | loop fusion | bytes 524292 | tf_op jit(solution)/shard_map/dynamic_slice | solution.py:379
  1.2 0.1 reshape_transpose.13.rest_1_
  1.3 3.1 %collective-permute-start = (bf16[1,256,512]{2,1,0:T(8,128)(2,1)S(1)}, bf16[1,256,512]{2,1,0:T(8,128)(2,1)S(1)}, u32[]{:S(2)}, u32[]{:S(2)}) collective-permute-start(bf16[1,256,512]{2,1,0:T(8,128)(2,1)S(1)} %reshape_transpose.13.rest_1_), channel_id=1, source_target_pairs={{0,4},{4,8},{8,12},{12,0},{1,5},{5,9},{9,13},{13,1},{2,6},{6,10},{... | collective-permute-start | bytes 786440 | tf_op jit(solution)/shard_map/ppermute | solution.py:383
  4.4 0.0 copy-start
  4.4 1.2 %copy-done = bf16[128,1,4,2,512]{4,3,2,1,0:T(2,128)(2,1)S(1)} copy-done((bf16[128,1,4,2,512]{4,3,2,1,0:T(2,128)(2,1)S(1)}, bf16[128,1,4,2,512]{4,3,2,1,0:T(2,128)(2,1)}, u32[]{:S(2)}) %copy-start) | copy-done | bytes 1048600
  5.6 0.2 shard_map.55
  5.8 0.1 reshape_transpose.14.rest_2_
  5.9 0.0 copy-start.2
  5.9 2.1 %collective-permute-start.1 = (bf16[1,256,512]{2,1,0:T(8,128)(2,1)S(1)}, bf16[1,256,512]{2,1,0:T(8,128)(2,1)S(1)}, u32[]{:S(2)}, u32[]{:S(2)}) collective-permute-start(bf16[1,256,512]{2,1,0:T(8,128)(2,1)S(1)} %reshape_transpose.14.rest_2_), channel_id=1, source_target_pairs={{0,12},{4,0},{8,4},{12,8},{1,13},{5,1},{9,5},{13,9},{2,14},{6,2},{... | collective-permute-start | bytes 786440 | tf_op jit(solution)/shard_map/ppermute | solution.py:383
  8.0 0.1 reshape_transpose.15.rest_3_
  8.1 1.1 %collective-permute-start.2 = (bf16[1,256,512]{2,1,0:T(8,128)(2,1)S(1)}, bf16[1,256,512]{2,1,0:T(8,128)(2,1)S(1)}, u32[]{:S(2)}, u32[]{:S(2)}) collective-permute-start(bf16[1,256,512]{2,1,0:T(8,128)(2,1)S(1)} %reshape_transpose.15.rest_3_), channel_id=1, source_target_pairs={{0,8},{4,12},{8,0},{12,4},{1,9},{5,13},{9,1},{13,5},{2,10},{6,14},... | collective-permute-start | bytes 786440 | tf_op jit(solution)/shard_map/ppermute | solution.py:383
  9.2 0.1 reshape_transpose.12.rest_0_.refs_0_
  9.3 0.0 copy-done.1
  9.3 1.3 %shard_map.57.weights_ref = bf16[1,512,512]{2,1,0:T(8,128)(2,1)S(1)} custom-call(s32[256,512]{1,0:T(8,128)S(1)} %copy-done.1), custom_call_target="tpu_custom_call" | custom-call | flops 5242880 | bytes 1048576 | tf_op jit(solution)/shard_map/pallas_call | solution.py:398
  10.5 0.0 copy-start.3
  10.6 0.0 copy-start.4
  10.6 6.8 %shard_map.56 = (f32[4,256,128]{2,1,0:T(8,128)S(1)}, f32[4,256,128]{2,1,0:T(8,128)S(1)}) custom-call(s32[256,512]{1,0:T(8,128)S(1)} %copy-done.1, bf16[1,256,512]{2,1,0:T(8,128)(2,1)S(1)} %reshape_transpose.12.rest_0_.refs_0_, bf16[1,256,512]{2,1,0:T(8,128)(2,1)S(1)} %reshape_transpose.13.rest_1_, bf16[1,256,512]{2,1,0:T(8,128)(2,1)S(1)} %reshape_transpose.14.rest_2_, ...), custom_call_target="tpu_custom_call" | custom-call | flops 536870912 | bytes 2097152 | tf_op jit(solution)/shard_map/pallas_call | solution.py:388
  17.4 0.0 collective-permute-done.refs_1_
  17.4 0.9 %collective-permute-done.1.refs_2_ = bf16[1,256,512]{2,1,0:T(8,128)(2,1)S(1)} collective-permute-done((bf16[1,256,512]{2,1,0:T(8,128)(2,1)S(1)}, bf16[1,256,512]{2,1,0:T(8,128)(2,1)S(1)}, u32[]{:S(2)}, u32[]{:S(2)}) %collective-permute-start.1) | collective-permute-done | bytes 262176 | tf_op jit(solution)/shard_map/ppermute | solution.py:383
  18.3 0.0 copy-done.2
  18.3 1.5 %shard_map.58 = (f32[1,2,512,512]{3,2,1,0:T(8,128)S(1)}, f32[1,16,512]{2,1,0:T(8,128)S(1)}, bf16[1,512,768]{2,1,0:T(8,128)(2,1)S(1)}) custom-call(f32[1,4,2,8,512]{4,3,2,1,0:T(8,128)S(1)} %copy-done.2, bf16[1,256,512]{2,1,0:T(8,128)(2,1)S(1)} %reshape_transpose.12.rest_0_.refs_0_, bf16[1,256,512]{2,1,0:T(8,128)(2,1)S(1)} %collective-permute-done.refs_1_, ...), custom_call_target="tpu_custom_call" | custom-call | flops 805306368 | bytes 2097152 | tf_op jit(solution)/shard_map/pallas_call | solution.py:409
  19.8 9.7 %collective-permute-done.2.last_ref = bf16[1,256,512]{2,1,0:T(8,128)(2,1)S(1)} collective-permute-done((bf16[1,256,512]{2,1,0:T(8,128)(2,1)S(1)}, bf16[1,256,512]{2,1,0:T(8,128)(2,1)S(1)}, u32[]{:S(2)}, u32[]{:S(2)}) %collective-permute-start.2) | collective-permute-done | bytes 262176 | tf_op jit(solution)/shard_map/ppermute | solution.py:383
  29.6 0.0 copy-done.3
  29.6 0.0 copy-done.4
  29.6 4.2 %shard_map.59 = (f32[4,256,128]{2,1,0:T(8,128)S(1)}, bf16[1,16,384]{2,1,0:T(8,128)(2,1)S(1)}, bf16[1,16,384]{2,1,0:T(8,128)(2,1)S(1)}, bf16[1,16,384]{2,1,0:T(8,128)(2,1)S(1)}, bf16[1,16,384]{2,1,0:T(8,128)(2,1)S(1)}) custom-call(f32[4,256,128]{2,1,0:T(8,128)S(1)} %get-tuple-element.21.beams_ref, ...), custom_call_target="tpu_custom_call", output_to_operand_aliasing={{0}: (0, {})} | custom-call | flops 134217728 | bytes 2097152 | tf_op jit(solution)/shard_map/pallas_call | solution.py:423
  33.8 0.1 collective-permute-start.3
  33.9 0.1 collective-permute-start.8
  34.0 1.7 %collective-permute-start.4 = (bf16[1,16,384]{2,1,0:T(8,128)(2,1)S(1)}, bf16[1,16,384]{2,1,0:T(8,128)(2,1)S(1)}, u32[]{:S(2)}, u32[]{:S(2)}) collective-permute-start(bf16[1,16,384]{2,1,0:T(8,128)(2,1)S(1)} %get-tuple-element.26), channel_id=1, source_target_pairs={{0,12},{4,8},{8,4},{12,0},{1,13},{5,9},{9,5},{13,1},{2,14},{6,10},... | collective-permute-start | bytes 36872 | tf_op jit(solution)/shard_map/ppermute | solution.py:440
  35.6 1.8 %collective-permute-start.6 = (bf16[1,16,384]{2,1,0:T(8,128)(2,1)S(1)}, bf16[1,16,384]{2,1,0:T(8,128)(2,1)S(1)}, u32[]{:S(2)}, u32[]{:S(2)}) collective-permute-start(bf16[1,16,384]{2,1,0:T(8,128)(2,1)S(1)} %get-tuple-element.27), channel_id=1, source_target_pairs={{0,4},{4,0},{8,12},{12,8},{1,5},{5,1},{9,13},{13,9},{2,6},{6,2},{1... | collective-permute-start | bytes 36872 | tf_op jit(solution)/shard_map/ppermute | solution.py:440
  37.4 0.0 collective-permute-start.9
  37.4 1.2 %collective-permute-done.8.rest_1_ = bf16[1,16,384]{2,1,0:T(8,128)(2,1)S(1)} collective-permute-done((bf16[1,16,384]{2,1,0:T(8,128)(2,1)S(1)}, bf16[1,16,384]{2,1,0:T(8,128)(2,1)S(1)}, u32[]{:S(2)}, u32[]{:S(2)}) %collective-permute-start.8) | collective-permute-done | bytes 12320 | tf_op jit(solution)/shard_map/ppermute | solution.py:440
  38.6 0.0 collective-permute-start.10
  38.6 0.9 %collective-permute-done.4.rest_2_ = bf16[1,16,384]{2,1,0:T(8,128)(2,1)S(1)} collective-permute-done((bf16[1,16,384]{2,1,0:T(8,128)(2,1)S(1)}, bf16[1,16,384]{2,1,0:T(8,128)(2,1)S(1)}, u32[]{:S(2)}, u32[]{:S(2)}) %collective-permute-start.4) | collective-permute-done | bytes 12320 | tf_op jit(solution)/shard_map/ppermute | solution.py:440
  39.5 0.0 collective-permute-start.5
  39.5 0.0 collective-permute-done.6.rest_3_
  39.5 0.5 %collective-permute-start.7 = (bf16[1,16,384]{2,1,0:T(8,128)(2,1)S(1)}, bf16[1,16,384]{2,1,0:T(8,128)(2,1)S(1)}, u32[]{:S(2)}, u32[]{:S(2)}) collective-permute-start(bf16[1,16,384]{2,1,0:T(8,128)(2,1)S(1)} %collective-permute-done.6.rest_3_), channel_id=1, source_target_pairs={{0,1},{1,0},{2,3},{3,2},{4,5},{5,4},{6,7},{7,6},{8,9},{9,8},{10,11... | collective-permute-start | bytes 36872 | tf_op jit(solution)/shard_map/ppermute | solution.py:441
  40.0 0.0 collective-permute-done.9.rest_4_
  40.0 0.0 collective-permute-done.10.rest_5_
  40.0 0.0 collective-permute-done.3.theirs_ref
  40.0 0.4 %shard_map.60.rest_2_ = f32[4,128,128]{2,1,0:T(8,128)S(1)} custom-call(f32[4,256,128]{2,1,0:T(8,128)S(1)} %get-tuple-element.28.mine_ref, f32[4,256,128]{2,1,0:T(8,128)S(1)} %collective-permute-done.3.theirs_ref, bf16[1,16,384]{2,1,0:T(8,128)(2,1)S(1)} %get-tuple-element.29.rest_0_, bf16[1,16,384]{2,1,0:T(8,128)(2,1)S(1)} %collective-permute-done.8.rest_1_, ...), custom_call_target="tpu_custom_call" | custom-call | flops 6291456 | bytes 262144 | tf_op jit(solution)/shard_map/pallas_call | solution.py:449
  40.5 0.2 collective-permute-done.5.rest_0_
  40.7 0.2 collective-permute-done.7.rest_1_
  40.9 1.0 %shard_map.61 = f32[512,128]{1,0:T(8,128)} custom-call(f32[4,256,128]{2,1,0:T(8,128)S(1)} %collective-permute-done.3.theirs_ref, bf16[1,16,384]{2,1,0:T(8,128)(2,1)S(1)} %collective-permute-done.5.rest_0_, bf16[1,16,384]{2,1,0:T(8,128)(2,1)S(1)} %collective-permute-done.7.rest_1_, f32[4,128,128]{2,1,0:T(8,128)S(1)} %shard_map.60.rest_2_), custom_call_target="tpu_custom_call" | custom-call | flops 131072 | bytes 786432 | tf_op jit(solution)/shard_map/pallas_call | solution.py:461
Async XLA Ops:
  0.0 9.3 %copy-start.1 = (s32[256,512]{1,0:T(8,128)S(1)}, s32[256,512]{1,0:T(8,128)}, u32[]{:S(2)}) copy-start(s32[256,512]{1,0:T(8,128)} %phase_ref.3) | copy-start | bytes 1572868
  1.3 16.1 %collective-permute-start = (bf16[1,256,512]{2,1,0:T(8,128)(2,1)S(1)}, bf16[1,256,512]{2,1,0:T(8,128)(2,1)S(1)}, u32[]{:S(2)}, u32[]{:S(2)}) collective-permute-start(bf16[1,256,512]{2,1,0:T(8,128)(2,1)S(1)} %reshape_transpose.13.rest_1_), channel_id=1, source_target_pairs={{0,4},{4,8},{8,12},{12,0},{1,5},{5,9},{9,13},{13,1},{2,6},{6,10},{... | collective-permute-start | bytes 786440 | tf_op jit(solution)/shard_map/ppermute | solution.py:383
  4.4 1.2 %copy-start = (bf16[128,1,4,2,512]{4,3,2,1,0:T(2,128)(2,1)S(1)}, bf16[128,1,4,2,512]{4,3,2,1,0:T(2,128)(2,1)}, u32[]{:S(2)}) copy-start(bf16[128,1,4,2,512]{4,3,2,1,0:T(2,128)(2,1)} %voltages_ref.1) | copy-start | bytes 3145732
  5.9 12.4 %copy-start.2 = (f32[1,4,2,8,512]{4,3,2,1,0:T(8,128)S(1)}, f32[1,4,2,8,512]{4,3,2,1,0:T(8,128)}, u32[]{:S(2)}) copy-start(f32[1,4,2,8,512]{4,3,2,1,0:T(8,128)} %start_ref.3) | copy-start | bytes 393220
  5.9 12.4 %collective-permute-start.1 = (bf16[1,256,512]{2,1,0:T(8,128)(2,1)S(1)}, bf16[1,256,512]{2,1,0:T(8,128)(2,1)S(1)}, u32[]{:S(2)}, u32[]{:S(2)}) collective-permute-start(bf16[1,256,512]{2,1,0:T(8,128)(2,1)S(1)} %reshape_transpose.14.rest_2_), channel_id=1, source_target_pairs={{0,12},{4,0},{8,4},{12,8},{1,13},{5,1},{9,5},{13,9},{2,14},{6,2},{... | collective-permute-start | bytes 786440 | tf_op jit(solution)/shard_map/ppermute | solution.py:383
  8.1 21.5 %collective-permute-start.2 = (bf16[1,256,512]{2,1,0:T(8,128)(2,1)S(1)}, bf16[1,256,512]{2,1,0:T(8,128)(2,1)S(1)}, u32[]{:S(2)}, u32[]{:S(2)}) collective-permute-start(bf16[1,256,512]{2,1,0:T(8,128)(2,1)S(1)} %reshape_transpose.15.rest_3_), channel_id=1, source_target_pairs={{0,8},{4,12},{8,0},{12,4},{1,9},{5,13},{9,1},{13,5},{2,10},{6,14},... | collective-permute-start | bytes 786440 | tf_op jit(solution)/shard_map/ppermute | solution.py:383
  10.5 19.0 %copy-start.3 = (s32[4]{0:T(128)S(1)}, s32[4]{0:T(128)}, u32[]{:S(2)}) copy-start(s32[4]{0:T(128)} %flags_ref.1) | copy-start | bytes 52
  10.6 19.0 %copy-start.4 = (s32[4]{0:T(128)S(1)}, s32[4]{0:T(128)}, u32[]{:S(2)}) copy-start(s32[4]{0:T(128)} %ranks_ref.1) | copy-start | bytes 52
  33.8 6.2 %collective-permute-start.3 = (f32[4,256,128]{2,1,0:T(8,128)S(1)}, f32[4,256,128]{2,1,0:T(8,128)S(1)}, u32[]{:S(2)}, u32[]{:S(2)}) collective-permute-start(f32[4,256,128]{2,1,0:T(8,128)S(1)} %get-tuple-element.25), channel_id=1, source_target_pairs={{0,1},{1,0},{2,3},{3,2},{4,5},{5,4},{6,7},{7,6},{8,9},{9,8},{10,11... | collective-permute-start | bytes 1572872 | tf_op jit(solution)/shard_map/ppermute | solution.py:436
  33.9 4.7 %collective-permute-start.8 = (bf16[1,16,384]{2,1,0:T(8,128)(2,1)S(1)}, bf16[1,16,384]{2,1,0:T(8,128)(2,1)S(1)}, u32[]{:S(2)}, u32[]{:S(2)}) collective-permute-start(bf16[1,16,384]{2,1,0:T(8,128)(2,1)S(1)} %get-tuple-element.30), channel_id=1, source_target_pairs={{0,8},{4,12},{8,0},{12,4},{1,9},{5,13},{9,1},{13,5},{2,10},{6,14},... | collective-permute-start | bytes 36872 | tf_op jit(solution)/shard_map/ppermute | solution.py:440
  34.0 5.6 %collective-permute-start.4 = (bf16[1,16,384]{2,1,0:T(8,128)(2,1)S(1)}, bf16[1,16,384]{2,1,0:T(8,128)(2,1)S(1)}, u32[]{:S(2)}, u32[]{:S(2)}) collective-permute-start(bf16[1,16,384]{2,1,0:T(8,128)(2,1)S(1)} %get-tuple-element.26), channel_id=1, source_target_pairs={{0,12},{4,8},{8,4},{12,0},{1,13},{5,9},{9,5},{13,1},{2,14},{6,10},... | collective-permute-start | bytes 36872 | tf_op jit(solution)/shard_map/ppermute | solution.py:440
  35.6 3.9 %collective-permute-start.6 = (bf16[1,16,384]{2,1,0:T(8,128)(2,1)S(1)}, bf16[1,16,384]{2,1,0:T(8,128)(2,1)S(1)}, u32[]{:S(2)}, u32[]{:S(2)}) collective-permute-start(bf16[1,16,384]{2,1,0:T(8,128)(2,1)S(1)} %get-tuple-element.27), channel_id=1, source_target_pairs={{0,4},{4,0},{8,12},{12,8},{1,5},{5,1},{9,13},{13,9},{2,6},{6,2},{1... | collective-permute-start | bytes 36872 | tf_op jit(solution)/shard_map/ppermute | solution.py:440
  37.4 2.6 %collective-permute-start.9 = (bf16[1,16,384]{2,1,0:T(8,128)(2,1)S(1)}, bf16[1,16,384]{2,1,0:T(8,128)(2,1)S(1)}, u32[]{:S(2)}, u32[]{:S(2)}) collective-permute-start(bf16[1,16,384]{2,1,0:T(8,128)(2,1)S(1)} %get-tuple-element.29.rest_0_), channel_id=1, source_target_pairs={{0,1},{1,0},{2,3},{3,2},{4,5},{5,4},{6,7},{7,6},{8,9},{9,8},{10,11... | collective-permute-start | bytes 36872 | tf_op jit(solution)/shard_map/ppermute | solution.py:441
  38.6 1.4 %collective-permute-start.10 = (bf16[1,16,384]{2,1,0:T(8,128)(2,1)S(1)}, bf16[1,16,384]{2,1,0:T(8,128)(2,1)S(1)}, u32[]{:S(2)}, u32[]{:S(2)}) collective-permute-start(bf16[1,16,384]{2,1,0:T(8,128)(2,1)S(1)} %collective-permute-done.8.rest_1_), channel_id=1, source_target_pairs={{0,1},{1,0},{2,3},{3,2},{4,5},{5,4},{6,7},{7,6},{8,9},{9,8},{10,11... | collective-permute-start | bytes 36872 | tf_op jit(solution)/shard_map/ppermute | solution.py:441
  39.5 1.2 %collective-permute-start.5 = (bf16[1,16,384]{2,1,0:T(8,128)(2,1)S(1)}, bf16[1,16,384]{2,1,0:T(8,128)(2,1)S(1)}, u32[]{:S(2)}, u32[]{:S(2)}) collective-permute-start(bf16[1,16,384]{2,1,0:T(8,128)(2,1)S(1)} %collective-permute-done.4.rest_2_), channel_id=1, source_target_pairs={{0,1},{1,0},{2,3},{3,2},{4,5},{5,4},{6,7},{7,6},{8,9},{9,8},{10,11... | collective-permute-start | bytes 36872 | tf_op jit(solution)/shard_map/ppermute | solution.py:441
  39.5 1.3 %collective-permute-start.7 = (bf16[1,16,384]{2,1,0:T(8,128)(2,1)S(1)}, bf16[1,16,384]{2,1,0:T(8,128)(2,1)S(1)}, u32[]{:S(2)}, u32[]{:S(2)}) collective-permute-start(bf16[1,16,384]{2,1,0:T(8,128)(2,1)S(1)} %collective-permute-done.6.rest_3_), channel_id=1, source_target_pairs={{0,1},{1,0},{2,3},{3,2},{4,5},{5,4},{6,7},{7,6},{8,9},{9,8},{10,11... | collective-permute-start | bytes 36872 | tf_op jit(solution)/shard_map/ppermute | solution.py:441

commit v23 on v21

--- a/solution.py
+++ b/solution.py
@@ -17,7 +17,7 @@
 NN = (((1,), (0,)), ((), ()))
 TN = (((0,), (0,)), ((), ()))
 VMEM_LIMIT = 48 * 1024 * 1024
-CHUNK = 256
+CHUNK = 64
 LEAST_PIVOT = 1e-4
 
 

time: 42.3 us -> 42.4 us (level)
  no operation moved by 1% of the time
where the time goes in v23:
time: 42.4 us; the launch traced here: 42.2 us
  Pallas kernels  15.9 us (38%)
  waiting for transfers between devices  13 us (31%)
  starting transfers between devices  10.4 us (25%)
  local copies, waits for them, and re-layouts  2.85 us (7%)
    ppermute x3, waiting for transfers between devices, local(): lax.ppermute(piece, 'tm', [(z, (z + by) % tm) for z in range(tm)])  10.6 us
    pallas_call x1, Pallas kernels, local(): pl.pallas_call(functools.partial(raw_beams_kernel, tm, own), out_shape=[r...  6.85 us
    ppermute x3, starting transfers between devices, local(): lax.ppermute(piece, 'tm', [(z, (z + by) % tm) for z in range(tm)])  6.23 us
    pallas_call x1, Pallas kernels, local(): pl.pallas_call(functools.partial(subspace_kernel, tm, own, factor), out_s...  4.36 us
    ppermute x3, starting transfers between devices, local(): arrived[x] = lax.ppermute(packets[x], 'tm', [(z, z ^ x) for z in range(tm)])  3.55 us
    ppermute x3, waiting for transfers between devices, local(): arrived[x] = lax.ppermute(packets[x], 'tm', [(z, z ^ x) for z in range(tm)])  2.08 us
    pallas_call x1, Pallas kernels, local(): pl.pallas_call(early_kernel, out_shape=[jax.ShapeDtypeStruct((own, 2, wid...  1.51 us
    pallas_call x1, Pallas kernels, local(): pl.pallas_call(functools.partial(own_weights_kernel, own, chan_dev), out_...  1.26 us
  transfers between devices with their start and end apart: 11, of which 5 were waited for; matrix products, arithmetic and copies ran while one was open for 1% of the time, Pallas kernels for 25%

profile of v23, /device:TPU:0, one launch (start us, length us, event | category | flops | bytes accessed | tf_op | source)
XLA Modules:
  0.0 42.2 jit_solution(2455895208990599666)
XLA Ops:
  0.0 0.0 copy-start.1
  0.0 1.2 %constant_dynamic-slice_fusion = bf16[128,1,1,2,512]{4,3,2,1,0:T(2,128)(2,1)S(1)} fusion(bf16[128,1,4,2,512]{4,3,2,1,0:T(2,128)(2,1)} %voltages_ref.1, s32[]{:T(128)S(6)} %select_n.3), kind=kLoop, calls=%fused_computation | loop fusion | bytes 524292 | tf_op jit(solution)/shard_map/dynamic_slice | solution.py:377
  1.2 0.1 reshape_transpose.13.rest_1_
  1.3 3.1 %collective-permute-start = (bf16[1,256,512]{2,1,0:T(8,128)(2,1)S(1)}, bf16[1,256,512]{2,1,0:T(8,128)(2,1)S(1)}, u32[]{:S(2)}, u32[]{:S(2)}) collective-permute-start(bf16[1,256,512]{2,1,0:T(8,128)(2,1)S(1)} %reshape_transpose.13.rest_1_), channel_id=1, source_target_pairs={{0,4},{4,8},{8,12},{12,0},{1,5},{5,9},{9,13},{13,1},{2,6},{6,10},{... | collective-permute-start | bytes 786440 | tf_op jit(solution)/shard_map/ppermute | solution.py:381
  4.4 0.0 copy-start
  4.4 1.2 %copy-done = bf16[128,1,4,2,512]{4,3,2,1,0:T(2,128)(2,1)S(1)} copy-done((bf16[128,1,4,2,512]{4,3,2,1,0:T(2,128)(2,1)S(1)}, bf16[128,1,4,2,512]{4,3,2,1,0:T(2,128)(2,1)}, u32[]{:S(2)}) %copy-start) | copy-done | bytes 1048600
  5.6 0.2 shard_map.55
  5.8 0.1 reshape_transpose.14.rest_2_
  5.9 0.0 copy-start.2
  5.9 2.1 %collective-permute-start.1 = (bf16[1,256,512]{2,1,0:T(8,128)(2,1)S(1)}, bf16[1,256,512]{2,1,0:T(8,128)(2,1)S(1)}, u32[]{:S(2)}, u32[]{:S(2)}) collective-permute-start(bf16[1,256,512]{2,1,0:T(8,128)(2,1)S(1)} %reshape_transpose.14.rest_2_), channel_id=1, source_target_pairs={{0,12},{4,0},{8,4},{12,8},{1,13},{5,1},{9,5},{13,9},{2,14},{6,2},{... | collective-permute-start | bytes 786440 | tf_op jit(solution)/shard_map/ppermute | solution.py:381
  8.0 0.1 reshape_transpose.15.rest_3_
  8.1 1.1 %collective-permute-start.2 = (bf16[1,256,512]{2,1,0:T(8,128)(2,1)S(1)}, bf16[1,256,512]{2,1,0:T(8,128)(2,1)S(1)}, u32[]{:S(2)}, u32[]{:S(2)}) collective-permute-start(bf16[1,256,512]{2,1,0:T(8,128)(2,1)S(1)} %reshape_transpose.15.rest_3_), channel_id=1, source_target_pairs={{0,8},{4,12},{8,0},{12,4},{1,9},{5,13},{9,1},{13,5},{2,10},{6,14},... | collective-permute-start | bytes 786440 | tf_op jit(solution)/shard_map/ppermute | solution.py:381
  9.2 0.1 reshape_transpose.12.rest_0_.refs_0_
  9.3 0.0 copy-done.1
  9.3 1.3 %shard_map.57.weights_ref = bf16[1,512,512]{2,1,0:T(8,128)(2,1)S(1)} custom-call(s32[256,512]{1,0:T(8,128)S(1)} %copy-done.1), custom_call_target="tpu_custom_call" | custom-call | flops 5242880 | bytes 1048576 | tf_op jit(solution)/shard_map/pallas_call | solution.py:396
  10.5 0.0 copy-start.3
  10.6 0.0 copy-start.4
  10.6 6.8 %shard_map.56 = (f32[4,256,128]{2,1,0:T(8,128)S(1)}, f32[4,256,128]{2,1,0:T(8,128)S(1)}) custom-call(s32[256,512]{1,0:T(8,128)S(1)} %copy-done.1, bf16[1,256,512]{2,1,0:T(8,128)(2,1)S(1)} %reshape_transpose.12.rest_0_.refs_0_, bf16[1,256,512]{2,1,0:T(8,128)(2,1)S(1)} %reshape_transpose.13.rest_1_, bf16[1,256,512]{2,1,0:T(8,128)(2,1)S(1)} %reshape_transpose.14.rest_2_, ...), custom_call_target="tpu_custom_call" | custom-call | flops 536870912 | bytes 2097152 | tf_op jit(solution)/shard_map/pallas_call | solution.py:386
  17.4 0.0 collective-permute-done.refs_1_
  17.4 0.9 %collective-permute-done.1.refs_2_ = bf16[1,256,512]{2,1,0:T(8,128)(2,1)S(1)} collective-permute-done((bf16[1,256,512]{2,1,0:T(8,128)(2,1)S(1)}, bf16[1,256,512]{2,1,0:T(8,128)(2,1)S(1)}, u32[]{:S(2)}, u32[]{:S(2)}) %collective-permute-start.1) | collective-permute-done | bytes 262176 | tf_op jit(solution)/shard_map/ppermute | solution.py:381
  18.3 0.0 copy-done.2
  18.3 1.5 %shard_map.58 = (f32[1,2,512,512]{3,2,1,0:T(8,128)S(1)}, f32[1,16,512]{2,1,0:T(8,128)S(1)}, bf16[1,512,768]{2,1,0:T(8,128)(2,1)S(1)}) custom-call(f32[1,4,2,8,512]{4,3,2,1,0:T(8,128)S(1)} %copy-done.2, bf16[1,256,512]{2,1,0:T(8,128)(2,1)S(1)} %reshape_transpose.12.rest_0_.refs_0_, bf16[1,256,512]{2,1,0:T(8,128)(2,1)S(1)} %collective-permute-done.refs_1_, ...), custom_call_target="tpu_custom_call" | custom-call | flops 805306368 | bytes 2097152 | tf_op jit(solution)/shard_map/pallas_call | solution.py:407
  19.8 9.7 %collective-permute-done.2.last_ref = bf16[1,256,512]{2,1,0:T(8,128)(2,1)S(1)} collective-permute-done((bf16[1,256,512]{2,1,0:T(8,128)(2,1)S(1)}, bf16[1,256,512]{2,1,0:T(8,128)(2,1)S(1)}, u32[]{:S(2)}, u32[]{:S(2)}) %collective-permute-start.2) | collective-permute-done | bytes 262176 | tf_op jit(solution)/shard_map/ppermute | solution.py:381
  29.6 0.0 copy-done.3
  29.6 0.0 copy-done.4
  29.6 4.4 %shard_map.59 = (f32[4,256,128]{2,1,0:T(8,128)S(1)}, bf16[1,16,384]{2,1,0:T(8,128)(2,1)S(1)}, bf16[1,16,384]{2,1,0:T(8,128)(2,1)S(1)}, bf16[1,16,384]{2,1,0:T(8,128)(2,1)S(1)}, bf16[1,16,384]{2,1,0:T(8,128)(2,1)S(1)}) custom-call(f32[4,256,128]{2,1,0:T(8,128)S(1)} %get-tuple-element.21.beams_ref, ...), custom_call_target="tpu_custom_call", output_to_operand_aliasing={{0}: (0, {})} | custom-call | flops 134217728 | bytes 2097152 | tf_op jit(solution)/shard_map/pallas_call | solution.py:421
  33.9 0.1 collective-permute-start.3
  34.0 0.1 collective-permute-start.9
  34.1 1.7 %collective-permute-start.7 = (bf16[1,16,384]{2,1,0:T(8,128)(2,1)S(1)}, bf16[1,16,384]{2,1,0:T(8,128)(2,1)S(1)}, u32[]{:S(2)}, u32[]{:S(2)}) collective-permute-start(bf16[1,16,384]{2,1,0:T(8,128)(2,1)S(1)} %get-tuple-element.29), channel_id=1, source_target_pairs={{0,12},{4,8},{8,4},{12,0},{1,13},{5,9},{9,5},{13,1},{2,14},{6,10},... | collective-permute-start | bytes 36872 | tf_op jit(solution)/shard_map/ppermute | solution.py:438
  35.8 1.8 %collective-permute-start.4 = (bf16[1,16,384]{2,1,0:T(8,128)(2,1)S(1)}, bf16[1,16,384]{2,1,0:T(8,128)(2,1)S(1)}, u32[]{:S(2)}, u32[]{:S(2)}) collective-permute-start(bf16[1,16,384]{2,1,0:T(8,128)(2,1)S(1)} %get-tuple-element.26), channel_id=1, source_target_pairs={{0,4},{4,0},{8,12},{12,8},{1,5},{5,1},{9,13},{13,9},{2,6},{6,2},{1... | collective-permute-start | bytes 36872 | tf_op jit(solution)/shard_map/ppermute | solution.py:438
  37.6 0.0 collective-permute-start.6
  37.6 1.2 %collective-permute-done.9.rest_1_ = bf16[1,16,384]{2,1,0:T(8,128)(2,1)S(1)} collective-permute-done((bf16[1,16,384]{2,1,0:T(8,128)(2,1)S(1)}, bf16[1,16,384]{2,1,0:T(8,128)(2,1)S(1)}, u32[]{:S(2)}, u32[]{:S(2)}) %collective-permute-start.9) | collective-permute-done | bytes 12320 | tf_op jit(solution)/shard_map/ppermute | solution.py:438
  38.7 0.0 collective-permute-start.10
  38.7 0.9 %collective-permute-done.7.rest_2_ = bf16[1,16,384]{2,1,0:T(8,128)(2,1)S(1)} collective-permute-done((bf16[1,16,384]{2,1,0:T(8,128)(2,1)S(1)}, bf16[1,16,384]{2,1,0:T(8,128)(2,1)S(1)}, u32[]{:S(2)}, u32[]{:S(2)}) %collective-permute-start.7) | collective-permute-done | bytes 12320 | tf_op jit(solution)/shard_map/ppermute | solution.py:438
  39.7 0.0 collective-permute-start.8
  39.7 0.0 collective-permute-done.4.rest_0_
  39.7 0.5 %collective-permute-start.5 = (bf16[1,16,384]{2,1,0:T(8,128)(2,1)S(1)}, bf16[1,16,384]{2,1,0:T(8,128)(2,1)S(1)}, u32[]{:S(2)}, u32[]{:S(2)}) collective-permute-start(bf16[1,16,384]{2,1,0:T(8,128)(2,1)S(1)} %collective-permute-done.4.rest_0_), channel_id=1, source_target_pairs={{0,1},{1,0},{2,3},{3,2},{4,5},{5,4},{6,7},{7,6},{8,9},{9,8},{10,11... | collective-permute-start | bytes 36872 | tf_op jit(solution)/shard_map/ppermute | solution.py:439
  40.2 0.3 shard_map.60.rest_4_
  40.5 0.0 collective-permute-done.6.rest_1_
  40.5 0.0 collective-permute-done.10.rest_3_
  40.5 0.3 collective-permute-done.8.rest_2_
  40.8 0.0 collective-permute-done.3.theirs_ref
  40.8 0.4 shard_map.61.power_ref
  41.2 0.0 collective-permute-done.5.packet_ref
  41.2 1.0 %shard_map.62 = f32[512,128]{1,0:T(8,128)} custom-call(f32[4,256,128]{2,1,0:T(8,128)S(1)} %collective-permute-done.3.theirs_ref, bf16[1,16,384]{2,1,0:T(8,128)(2,1)S(1)} %collective-permute-done.5.packet_ref, f32[4,128,128]{2,1,0:T(8,128)S(1)} %shard_map.61.power_ref), custom_call_target="tpu_custom_call" | custom-call | flops 131072 | bytes 786432 | tf_op jit(solution)/shard_map/pallas_call | solution.py:459
Async XLA Ops:
  0.0 9.3 %copy-start.1 = (s32[256,512]{1,0:T(8,128)S(1)}, s32[256,512]{1,0:T(8,128)}, u32[]{:S(2)}) copy-start(s32[256,512]{1,0:T(8,128)} %phase_ref.3) | copy-start | bytes 1572868
  1.3 16.1 %collective-permute-start = (bf16[1,256,512]{2,1,0:T(8,128)(2,1)S(1)}, bf16[1,256,512]{2,1,0:T(8,128)(2,1)S(1)}, u32[]{:S(2)}, u32[]{:S(2)}) collective-permute-start(bf16[1,256,512]{2,1,0:T(8,128)(2,1)S(1)} %reshape_transpose.13.rest_1_), channel_id=1, source_target_pairs={{0,4},{4,8},{8,12},{12,0},{1,5},{5,9},{9,13},{13,1},{2,6},{6,10},{... | collective-permute-start | bytes 786440 | tf_op jit(solution)/shard_map/ppermute | solution.py:381
  4.4 1.2 %copy-start = (bf16[128,1,4,2,512]{4,3,2,1,0:T(2,128)(2,1)S(1)}, bf16[128,1,4,2,512]{4,3,2,1,0:T(2,128)(2,1)}, u32[]{:S(2)}) copy-start(bf16[128,1,4,2,512]{4,3,2,1,0:T(2,128)(2,1)} %voltages_ref.1) | copy-start | bytes 3145732
  5.9 12.4 %copy-start.2 = (f32[1,4,2,8,512]{4,3,2,1,0:T(8,128)S(1)}, f32[1,4,2,8,512]{4,3,2,1,0:T(8,128)}, u32[]{:S(2)}) copy-start(f32[1,4,2,8,512]{4,3,2,1,0:T(8,128)} %start_ref.3) | copy-start | bytes 393220
  5.9 12.4 %collective-permute-start.1 = (bf16[1,256,512]{2,1,0:T(8,128)(2,1)S(1)}, bf16[1,256,512]{2,1,0:T(8,128)(2,1)S(1)}, u32[]{:S(2)}, u32[]{:S(2)}) collective-permute-start(bf16[1,256,512]{2,1,0:T(8,128)(2,1)S(1)} %reshape_transpose.14.rest_2_), channel_id=1, source_target_pairs={{0,12},{4,0},{8,4},{12,8},{1,13},{5,1},{9,5},{13,9},{2,14},{6,2},{... | collective-permute-start | bytes 786440 | tf_op jit(solution)/shard_map/ppermute | solution.py:381
  8.1 21.5 %collective-permute-start.2 = (bf16[1,256,512]{2,1,0:T(8,128)(2,1)S(1)}, bf16[1,256,512]{2,1,0:T(8,128)(2,1)S(1)}, u32[]{:S(2)}, u32[]{:S(2)}) collective-permute-start(bf16[1,256,512]{2,1,0:T(8,128)(2,1)S(1)} %reshape_transpose.15.rest_3_), channel_id=1, source_target_pairs={{0,8},{4,12},{8,0},{12,4},{1,9},{5,13},{9,1},{13,5},{2,10},{6,14},... | collective-permute-start | bytes 786440 | tf_op jit(solution)/shard_map/ppermute | solution.py:381
  10.5 19.0 %copy-start.3 = (s32[4]{0:T(128)S(1)}, s32[4]{0:T(128)}, u32[]{:S(2)}) copy-start(s32[4]{0:T(128)} %flags_ref.1) | copy-start | bytes 52
  10.6 19.0 %copy-start.4 = (s32[4]{0:T(128)S(1)}, s32[4]{0:T(128)}, u32[]{:S(2)}) copy-start(s32[4]{0:T(128)} %ranks_ref.1) | copy-start | bytes 52
  33.9 6.9 %collective-permute-start.3 = (f32[4,256,128]{2,1,0:T(8,128)S(1)}, f32[4,256,128]{2,1,0:T(8,128)S(1)}, u32[]{:S(2)}, u32[]{:S(2)}) collective-permute-start(f32[4,256,128]{2,1,0:T(8,128)S(1)} %get-tuple-element.25), channel_id=1, source_target_pairs={{0,1},{1,0},{2,3},{3,2},{4,5},{5,4},{6,7},{7,6},{8,9},{9,8},{10,11... | collective-permute-start | bytes 1572872 | tf_op jit(solution)/shard_map/ppermute | solution.py:434
  34.0 4.7 %collective-permute-start.9 = (bf16[1,16,384]{2,1,0:T(8,128)(2,1)S(1)}, bf16[1,16,384]{2,1,0:T(8,128)(2,1)S(1)}, u32[]{:S(2)}, u32[]{:S(2)}) collective-permute-start(bf16[1,16,384]{2,1,0:T(8,128)(2,1)S(1)} %get-tuple-element.30), channel_id=1, source_target_pairs={{0,8},{4,12},{8,0},{12,4},{1,9},{5,13},{9,1},{13,5},{2,10},{6,14},... | collective-permute-start | bytes 36872 | tf_op jit(solution)/shard_map/ppermute | solution.py:438
  34.1 5.6 %collective-permute-start.7 = (bf16[1,16,384]{2,1,0:T(8,128)(2,1)S(1)}, bf16[1,16,384]{2,1,0:T(8,128)(2,1)S(1)}, u32[]{:S(2)}, u32[]{:S(2)}) collective-permute-start(bf16[1,16,384]{2,1,0:T(8,128)(2,1)S(1)} %get-tuple-element.29), channel_id=1, source_target_pairs={{0,12},{4,8},{8,4},{12,0},{1,13},{5,9},{9,5},{13,1},{2,14},{6,10},... | collective-permute-start | bytes 36872 | tf_op jit(solution)/shard_map/ppermute | solution.py:438
  35.8 3.9 %collective-permute-start.4 = (bf16[1,16,384]{2,1,0:T(8,128)(2,1)S(1)}, bf16[1,16,384]{2,1,0:T(8,128)(2,1)S(1)}, u32[]{:S(2)}, u32[]{:S(2)}) collective-permute-start(bf16[1,16,384]{2,1,0:T(8,128)(2,1)S(1)} %get-tuple-element.26), channel_id=1, source_target_pairs={{0,4},{4,0},{8,12},{12,8},{1,5},{5,1},{9,13},{13,9},{2,6},{6,2},{1... | collective-permute-start | bytes 36872 | tf_op jit(solution)/shard_map/ppermute | solution.py:438
  37.6 2.9 %collective-permute-start.6 = (bf16[1,16,384]{2,1,0:T(8,128)(2,1)S(1)}, bf16[1,16,384]{2,1,0:T(8,128)(2,1)S(1)}, u32[]{:S(2)}, u32[]{:S(2)}) collective-permute-start(bf16[1,16,384]{2,1,0:T(8,128)(2,1)S(1)} %get-tuple-element.28.rest_0_), channel_id=1, source_target_pairs={{0,1},{1,0},{2,3},{3,2},{4,5},{5,4},{6,7},{7,6},{8,9},{9,8},{10,11... | collective-permute-start | bytes 36872 | tf_op jit(solution)/shard_map/ppermute | solution.py:439
  38.7 1.8 %collective-permute-start.10 = (bf16[1,16,384]{2,1,0:T(8,128)(2,1)S(1)}, bf16[1,16,384]{2,1,0:T(8,128)(2,1)S(1)}, u32[]{:S(2)}, u32[]{:S(2)}) collective-permute-start(bf16[1,16,384]{2,1,0:T(8,128)(2,1)S(1)} %collective-permute-done.9.rest_1_), channel_id=1, source_target_pairs={{0,1},{1,0},{2,3},{3,2},{4,5},{5,4},{6,7},{7,6},{8,9},{9,8},{10,11... | collective-permute-start | bytes 36872 | tf_op jit(solution)/shard_map/ppermute | solution.py:439
  39.7 1.2 %collective-permute-start.8 = (bf16[1,16,384]{2,1,0:T(8,128)(2,1)S(1)}, bf16[1,16,384]{2,1,0:T(8,128)(2,1)S(1)}, u32[]{:S(2)}, u32[]{:S(2)}) collective-permute-start(bf16[1,16,384]{2,1,0:T(8,128)(2,1)S(1)} %collective-permute-done.7.rest_2_), channel_id=1, source_target_pairs={{0,1},{1,0},{2,3},{3,2},{4,5},{5,4},{6,7},{7,6},{8,9},{9,8},{10,11... | collective-permute-start | bytes 36872 | tf_op jit(solution)/shard_map/ppermute | solution.py:439
  39.7 1.5 %collective-permute-start.5 = (bf16[1,16,384]{2,1,0:T(8,128)(2,1)S(1)}, bf16[1,16,384]{2,1,0:T(8,128)(2,1)S(1)}, u32[]{:S(2)}, u32[]{:S(2)}) collective-permute-start(bf16[1,16,384]{2,1,0:T(8,128)(2,1)S(1)} %collective-permute-done.4.rest_0_), channel_id=1, source_target_pairs={{0,1},{1,0},{2,3},{3,2},{4,5},{5,4},{6,7},{7,6},{8,9},{9,8},{10,11... | collective-permute-start | bytes 36872 | tf_op jit(solution)/shard_map/ppermute | solution.py:439
